TPU v7x, 256 devices: a whole 4x4x8 slice. The times are simulated.
256 devices in a mesh: dp: 64 (over z, y_hi, x), tensor: 4 (over y_lo, core).
Axes of the slice: x: 4, y: 4 (y_hi: 2, y_lo: 2; y = y_hi * 2 + y_lo), z: 8, core: 2. Of those that a mesh axis runs over, the one named last changes fastest.
Arguments:
- tokens: bfloat16 [16384, 8192], P('dp'), may hold values from -16 to 16
- gate_weight: bfloat16 [8192, 512], P('dp', 'tensor'), may hold values from -0.0625 to 0.0625
- up_weight: bfloat16 [8192, 512], P('dp', 'tensor'), may hold values from -0.0625 to 0.0625
- down_weight: bfloat16 [512, 8192], P('tensor', 'dp'), may hold values from -0.25 to 0.25
- cotangent: bfloat16 [16384, 8192], P('dp', 'tensor'), may hold values from -16 to 16
Outputs:
- layer_out: bfloat16 [16384, 8192], P('dp', 'tensor')
- token_grad: bfloat16 [16384, 8192], P('dp', 'tensor')
- gate_grad: float32 [8192, 512], P('dp', 'tensor')
- up_grad: float32 [8192, 512], P('dp', 'tensor')
- down_grad: float32 [512, 8192], P('tensor', 'dp')
All inputs are finite; a program needn't handle non-finite values.
Results may differ from a plain program's by a relative error of at most 0.013.
Values may be sent and summed in bfloat16 or wider, within the bound.
No kernel may reach another device: no remote copies, remote signals or barrier semaphores. Data moves between devices by JAX's collectives and lax.ppermute only.
A program may use at most 128 MiB of HBM per device.

v0:
```python
import jax
import jax.numpy as jnp
from jax import lax
from jax.sharding import PartitionSpec as P


def contract_first(left, right):
    return lax.dot_general(
        left, right, (((0,), (0,)), ((), ())), preferred_element_type=jnp.float32
    )


def contract_last(left, right):
    return lax.dot_general(
        left, right, (((1,), (1,)), ((), ())), preferred_element_type=jnp.float32
    )


def shards(tokens, gate_weight, up_weight, down_weight, cotangent):
    gate_full = lax.all_gather(gate_weight, "dp", axis=0, tiled=True)
    up_full = lax.all_gather(up_weight, "dp", axis=0, tiled=True)
    down_full = lax.all_gather(down_weight, "dp", axis=1, tiled=True)
    gate_pre = jnp.dot(tokens, gate_full, preferred_element_type=jnp.float32)
    up_pre = jnp.dot(tokens, up_full, preferred_element_type=jnp.float32)
    sig_val = jax.nn.sigmoid(gate_pre)
    act_val = gate_pre * sig_val
    hidden = (act_val * up_pre).astype(jnp.bfloat16)
    out_terms = jnp.dot(hidden, down_full, preferred_element_type=jnp.float32)
    layer_out = lax.psum_scatter(
        out_terms.astype(jnp.bfloat16), "tensor", scatter_dimension=1, tiled=True
    )
    cot_full = lax.all_gather(cotangent, "tensor", axis=1, tiled=True)
    down_term = contract_first(cot_full, hidden)
    d_hidden = contract_last(cot_full, down_full)
    d_gate = (d_hidden * up_pre * sig_val * (1.0 + gate_pre * (1.0 - sig_val))).astype(jnp.bfloat16)
    d_up = (d_hidden * act_val).astype(jnp.bfloat16)
    gate_term = contract_first(tokens, d_gate)
    up_term = contract_first(tokens, d_up)
    down_part, gate_part, up_part = (
        lax.psum_scatter(down_term, "dp", scatter_dimension=0, tiled=True),
        lax.psum_scatter(gate_term, "dp", scatter_dimension=0, tiled=True),
        lax.psum_scatter(up_term, "dp", scatter_dimension=0, tiled=True),
    )
    grad_terms = contract_last(d_gate, gate_full) + contract_last(d_up, up_full)
    token_grad = lax.psum_scatter(
        grad_terms.astype(jnp.bfloat16), "tensor", scatter_dimension=1, tiled=True
    )
    return (layer_out, token_grad, gate_part, up_part, down_part.T)


def solution(mesh):
    placed = (
        P("dp", None),
        P("dp", "tensor"),
        P("dp", "tensor"),
        P("tensor", "dp"),
        P("dp", "tensor"),
    )
    return jax.shard_map(
        shards,
        mesh=mesh,
        in_specs=placed,
        out_specs=(
            P("dp", "tensor"),
            P("dp", "tensor"),
            P("dp", "tensor"),
            P("dp", "tensor"),
            P("tensor", "dp"),
        ),
        check_vma=False,
    )
```

profile of v0, /device:TPU:9, one launch (start us, length us, event | category | flops | bytes accessed | tf_op | source)
XLA Modules:
  0.0 1615.0 jit_solution(13091805836469833592)
XLA Ops:
  7.2 0.0 all-gather.7.cloned.1.call-start
  7.2 0.7 all-gather.7.cloned.1.call-update
  7.9 0.0 all-gather.5.cloned.1.call-start
  7.9 0.7 all-gather.5.cloned.1.call-update
  8.6 0.0 all-gather.9.cloned.1.call-start
  8.7 0.7 all-gather.9.cloned.1.call-update
  9.4 0.0 all-gather.11.cloned.1.call-start
  9.4 0.5 all-gather.11.cloned.1.call-update
  10.0 0.0 reduce-scatter.12.cloned.1.call-start
  10.0 117.8 %all-gather.7.cloned.1.call-done = bf16[8192,128]{1,0:T(8,128)(2,1)} async-done(((bf16[128,128]{1,0:T(8,128)(2,1)}), bf16[8192,128]{1,0:T(8,128)(2,1)}) %all-gather.7.cloned.1.call-update) | async-done | bytes 2097168 | tf_op jit(solution)/shard_map/all_gather | solution.py:21
  127.8 4.1 fusion.3
  131.9 113.9 %all-gather.5.cloned.1.call-done = bf16[8192,128]{1,0:T(8,128)(2,1)} async-done(((bf16[128,128]{1,0:T(8,128)(2,1)}), bf16[8192,128]{1,0:T(8,128)(2,1)}) %all-gather.5.cloned.1.call-update) | async-done | bytes 2097168 | tf_op jit(solution)/shard_map/all_gather | solution.py:20
  245.8 4.1 fusion.2
  249.9 96.8 %all-gather.9.cloned.1.call-done = bf16[128,8192]{1,0:T(8,128)(2,1)} async-done(((bf16[128,128]{1,0:T(8,128)(2,1)}), bf16[128,8192]{1,0:T(8,128)(2,1)}) %all-gather.9.cloned.1.call-update) | async-done | bytes 2097168 | tf_op jit(solution)/shard_map/all_gather | solution.py:22
  346.7 52.4 %all-gather.11.cloned.1.call-done = bf16[256,8192]{1,0:T(8,128)(2,1)} async-done(((bf16[256,2048]{1,0:T(8,128)(2,1)}), bf16[256,8192]{1,0:T(8,128)(2,1)}) %all-gather.11.cloned.1.call-update) | async-done | bytes 4194320 | tf_op jit(solution)/shard_map/all_gather | solution.py:32
  399.1 0.0 copy-start
  399.1 4.2 multiply_convert_fusion
  403.4 0.0 copy-done
  403.4 2.7 convolution_bitcast_fusion.1
  406.1 0.0 reduce-scatter.12.cloned.1.call-update
  406.1 0.0 reduce-scatter.10.cloned.1.call-start
  406.2 4.9 convolution_bitcast_fusion.2
  411.1 0.0 reduce-scatter.10.cloned.1.call-update
  411.1 0.0 reduce-scatter.14.cloned.1.call-start
  411.2 4.9 convolution_bitcast_fusion
  416.1 0.0 copy-start.2
  416.1 0.0 reduce-scatter.14.cloned.1.call-update
  416.1 0.0 reduce-scatter.6.cloned.1.call-start
  416.1 1.5 copy-done.2
  417.6 3.2 convolution_convert_fusion
  420.8 0.0 reduce-scatter.6.cloned.1.call-update
  420.9 0.0 copy-start.1
  420.9 0.0 reduce-scatter.8.cloned.1.call-start
  420.9 3.0 fusion.4
  423.9 0.0 copy-done.1
  423.9 3.3 fusion
  427.2 0.0 reduce-scatter.8.cloned.1.call-update
  427.2 299.1 %reduce-scatter.12.cloned.1.call-done = f32[128,128]{0,1:T(8,128)} async-done(((f32[8192,128]{0,1:T(8,128)}), f32[128,128]{0,1:T(8,128)}) %reduce-scatter.12.cloned.1.call-update) | async-done | bytes 65552 | tf_op jit(solution)/shard_map/reduce_scatter | solution.py:42
  726.4 1.6 copy.11
  727.9 364.9 %reduce-scatter.10.cloned.1.call-done = f32[128,128]{0,1:T(8,128)} async-done(((f32[8192,128]{0,1:T(8,128)}), f32[128,128]{0,1:T(8,128)}) %reduce-scatter.10.cloned.1.call-update) | async-done | bytes 65552 | tf_op jit(solution)/shard_map/reduce_scatter | solution.py:41
  1092.8 1.6 copy.10
  1094.4 365.7 %reduce-scatter.14.cloned.1.call-done = f32[128,128]{0,1:T(8,128)} async-done(((f32[8192,128]{0,1:T(8,128)}), f32[128,128]{0,1:T(8,128)}) %reduce-scatter.14.cloned.1.call-update) | async-done | bytes 65552 | tf_op jit(solution)/shard_map/reduce_scatter | solution.py:40
  1460.1 96.3 %reduce-scatter.6.cloned.1.call-done = bf16[256,2048]{1,0:T(8,128)(2,1)} async-done(((bf16[256,8192]{1,0:T(8,128)(2,1)}), bf16[256,2048]{1,0:T(8,128)(2,1)}) %reduce-scatter.6.cloned.1.call-update) | async-done | bytes 1048592 | tf_op jit(solution)/shard_map/reduce_scatter | solution.py:29
  1556.4 52.1 %reduce-scatter.8.cloned.1.call-done = bf16[256,2048]{1,0:T(8,128)(2,1)} async-done(((bf16[256,8192]{1,0:T(8,128)(2,1)}), bf16[256,2048]{1,0:T(8,128)(2,1)}) %reduce-scatter.8.cloned.1.call-update) | async-done | bytes 1048592 | tf_op jit(solution)/shard_map/reduce_scatter | solution.py:45
Async XLA Ops:
  7.2 120.6 %all-gather.7.cloned.1.call-start = ((), (), s32[]{:S(2)}) async-start(), calls=%async_computation.6 | async-start | bytes 2129920 | tf_op jit(solution)/shard_map/all_gather | solution.py:21
  7.9 237.9 %all-gather.5.cloned.1.call-start = ((), (), s32[]{:S(2)}) async-start(), calls=%async_computation.5 | async-start | bytes 2129920 | tf_op jit(solution)/shard_map/all_gather | solution.py:20
  8.6 338.1 %all-gather.9.cloned.1.call-start = ((), (), s32[]{:S(2)}) async-start(), calls=%async_computation.7 | async-start | bytes 2129920 | tf_op jit(solution)/shard_map/all_gather | solution.py:22
  9.4 389.7 %all-gather.11.cloned.1.call-start = ((), (), s32[]{:S(2)}) async-start(), calls=%async_computation.9 | async-start | bytes 5242880 | tf_op jit(solution)/shard_map/all_gather | solution.py:32
  10.0 716.4 %reduce-scatter.12.cloned.1.call-start = ((), (), s32[]{:S(2)}) async-start(), calls=%async_computation.12 | async-start | bytes 4259840 | tf_op jit(solution)/shard_map/reduce_scatter | solution.py:42
  399.1 4.3 copy-start
  406.1 686.7 %reduce-scatter.10.cloned.1.call-start = ((), (), s32[]{:S(2)}) async-start(), calls=%async_computation.11 | async-start | bytes 4259840 | tf_op jit(solution)/shard_map/reduce_scatter | solution.py:41
  411.1 1049.0 %reduce-scatter.14.cloned.1.call-start = ((), (), s32[]{:S(2)}) async-start(), calls=%async_computation.13 | async-start | bytes 4259840 | tf_op jit(solution)/shard_map/reduce_scatter | solution.py:40
  416.1 1.6 copy-start.2
  416.1 1140.3 %reduce-scatter.6.cloned.1.call-start = ((), (), s32[]{:S(2)}) async-start(), calls=%async_computation.8 | async-start | bytes 5242880 | tf_op jit(solution)/shard_map/reduce_scatter | solution.py:29
  420.9 3.0 copy-start.1
  420.9 1187.6 %reduce-scatter.8.cloned.1.call-start = ((), (), s32[]{:S(2)}) async-start(), calls=%async_computation.10 | async-start | bytes 5242880 | tf_op jit(solution)/shard_map/reduce_scatter | solution.py:45
Sparse Core Ops, SparseCore 0:
  11.6 116.1 all-gather.6
  131.4 114.3 all-gather.4
  249.2 97.4 all-gather.8
  348.4 50.6 all-gather.10
  406.2 320.0 reduce-scatter.11
  728.9 363.8 reduce-scatter.9
  1095.9 364.1 reduce-scatter.13
  1463.4 93.0 reduce-scatter.5
  1559.5 48.8 reduce-scatter.7
where the time goes:
time: 1620 us
  waiting for transfers between devices  1560 us (96%)
  matrix products  34.5 us (2%)
    reduce_scatter x1, waiting for transfers between devices, shards(): lax.psum_scatter(down_term, 'dp', scatter_dimension=0, tiled=True)  366 us
    reduce_scatter x1, waiting for transfers between devices, shards(): lax.psum_scatter(gate_term, 'dp', scatter_dimension=0, tiled=True)  365 us
    reduce_scatter x1, waiting for transfers between devices, shards(): lax.psum_scatter(up_term, 'dp', scatter_dimension=0, tiled=True)  299 us
    all_gather x1, waiting for transfers between devices, shards(): up_full = lax.all_gather(up_weight, 'dp', axis=0, tiled=True)  118 us
    all_gather x1, waiting for transfers between devices, shards(): gate_full = lax.all_gather(gate_weight, 'dp', axis=0, tiled=True)  114 us
    all_gather x1, waiting for transfers between devices, shards(): down_full = lax.all_gather(down_weight, 'dp', axis=1, tiled=True)  96.8 us
    reduce_scatter x1, waiting for transfers between devices, shards(): lax.psum_scatter(out_terms.astype(jnp.bfloat16), 'tensor', scatter_dimens...  96.3 us
    all_gather x1, waiting for transfers between devices, shards(): cot_full = lax.all_gather(cotangent, 'tensor', axis=1, tiled=True)  52.4 us
  transfers between devices with their start and end apart: 9, of which 9 were waited for; matrix products, arithmetic and copies ran while one was open for 2% of the time, Pallas kernels for 0%

commit v1 on v0

v1 whole, which is shorter than its diff:
```python
import functools

import jax
import jax.numpy as jnp
from jax import lax
from jax.experimental import pallas as pl
from jax.experimental.pallas import tpu as pltpu
from jax.sharding import PartitionSpec as P

NZ, NH, NX, NL, NC = 8, 2, 4, 2, 2
AXES = ("dp", "tensor")
BF = jnp.bfloat16
F32 = jnp.float32
VMEM_BYTES = 32 * 1024 * 1024


def index_of(z, h, x, l, c):
    return (((z * NH + h) * NX + x) * NL + l) * NC + c


def pairs_of(move):
    pairs = []
    for z in range(NZ):
        for h in range(NH):
            for x in range(NX):
                for l in range(NL):
                    for c in range(NC):
                        pairs.append((index_of(z, h, x, l, c), index_of(*move(z, h, x, l, c))))
    return pairs


def send(value, move):
    return lax.ppermute(value, AXES, pairs_of(move))


def send_back(value, move):
    return lax.ppermute(value, AXES, [(b, a) for a, b in pairs_of(move)])


def swap_hi(z, h, x, l, c):
    return z, 1 - h, x, l, c


def swap_core(z, h, x, l, c):
    return z, h, x, l, 1 - c


def along_x(step):
    return lambda z, h, x, l, c: (z, h, (x + step) % NX, l, c)


def along_y(k):
    return lambda z, h, x, l, c: (z, h ^ (k // 2), x, l ^ (k % 2), c)


def turn(f, g):
    def move(z, h, x, l, c):
        return 4 * ((z % 2) ^ f) + 2 * (l ^ g) + c, h, x, z // 4, (z // 2) % 2

    return move


PARTNERS = [[(z * NH + h) * NX + x for h in range(NH)] for z in range(NZ) for x in range(NX)]


def nn(a, b):
    return jnp.dot(a, b, preferred_element_type=F32)


def tn(a, b):
    return lax.dot_general(a, b, (((0,), (0,)), ((), ())), preferred_element_type=F32)


def nt(a, b):
    return lax.dot_general(a, b, (((1,), (1,)), ((), ())), preferred_element_type=F32)


def call(body, shapes, args, flops=0):
    moved = sum(a.size * a.dtype.itemsize for a in args)
    moved += sum(functools.reduce(lambda p, q: p * q, s, 1) * jnp.dtype(d).itemsize for s, d in shapes)
    return pl.pallas_call(
        body,
        out_shape=[jax.ShapeDtypeStruct(s, d) for s, d in shapes],
        in_specs=[pl.BlockSpec(memory_space=pltpu.VMEM)] * len(args),
        out_specs=[pl.BlockSpec(memory_space=pltpu.VMEM)] * len(shapes),
        compiler_params=pltpu.CompilerParams(vmem_limit_bytes=VMEM_BYTES),
        cost_estimate=pl.CostEstimate(flops=flops, bytes_accessed=moved, transcendentals=0),
    )(*args)


def call_at(body, where, args, shapes, flops=0):
    def at(block, shifted):
        zeros = (0,) * (len(block) - 1)
        return pl.BlockSpec(block, lambda i, where: (*zeros, where[0] if shifted else 0))

    moved = sum(functools.reduce(lambda p, q: p * q, b, 1) * 2 for _, b, _ in args)
    moved += sum(functools.reduce(lambda p, q: p * q, s, 1) * jnp.dtype(d).itemsize for s, d in shapes)
    return pl.pallas_call(
        body,
        grid_spec=pltpu.PrefetchScalarGridSpec(
            num_scalar_prefetch=1,
            grid=(1,),
            in_specs=[at(block, shifted) for _, block, shifted in args],
            out_specs=[at(shape, False) for shape, _ in shapes],
        ),
        out_shape=[jax.ShapeDtypeStruct(s, d) for s, d in shapes],
        compiler_params=pltpu.CompilerParams(vmem_limit_bytes=VMEM_BYTES),
        cost_estimate=pl.CostEstimate(flops=flops, bytes_accessed=moved, transcendentals=0),
    )(where, *[a for a, _, _ in args])


def blocks_of(where, fb, sub):
    t, x, b = where[0], where[2], where[3]
    for oc in range(2):
        for ol in range(2):
            rows = pl.multiple_of((t ^ (2 * ol + oc)) * sub, sub)
            for r in range(2):
                for j in range(NX):
                    s = lax.rem(x + j, NX)

                    def lanes(half, r=r, s=s):
                        return pl.multiple_of((((r ^ b) * NH + half) * NX + s) * fb, fb)

                    yield (oc * 2 + ol) * sub, (r * NX + j) * fb, rows, lanes


def pick_body(where, tok, cot, own, oth):
    sub = tok.shape[0] // 4
    fb = tok.shape[1] // 16
    h = where[1]
    for m, source in enumerate((tok, cot)):
        for to_row, to_lane, row, lanes in blocks_of(where, fb, sub):
            oth[m, to_row : to_row + sub, to_lane : to_lane + fb] = source[pl.ds(row, sub), pl.ds(lanes(1 - h), fb)]
            own[m, to_row : to_row + sub, to_lane : to_lane + fb] = source[pl.ds(row, sub), pl.ds(lanes(h), fb)]


def place_body(where, own, both, layer_out, token_grad):
    sub = own.shape[1] // 4
    fb = own.shape[2] // 8
    h = where[1]
    for m, out in enumerate((layer_out, token_grad)):
        for at_row, at_lane, row, lanes in blocks_of(where, fb, sub):
            out[pl.ds(row, sub), pl.ds(lanes(h), fb)] = own[m, at_row : at_row + sub, at_lane : at_lane + fb]
            out[pl.ds(row, sub), pl.ds(lanes(1 - h), fb)] = both[1 - h, m, at_row : at_row + sub, at_lane : at_lane + fb]


def forward_body(where, own, both, *refs):
    columns, (gu, dn, tok, cot, keep, away) = refs[:8], refs[8:]
    fb = columns[0].shape[-1]
    tb = own.shape[1]
    half = tb // 2
    h = where[1]
    for m, full in enumerate((tok, cot)):
        for oc in range(2):
            full[oc * tb : oc * tb + half, :] = own[m, oc * half : (oc + 1) * half, :]
            full[oc * tb + half : (oc + 1) * tb, :] = both[1 - h, m, oc * half : (oc + 1) * half, :]
    for f in range(2):
        for j in range(NX):
            column = columns[f * NX + j]
            at = (f * NX + j) * fb
            for g in range(2):
                for e in range(2):
                    unit = (g * 2 + e) * fb
                    gu[at : at + fb, unit : unit + fb] = column[g, e, 0]
                    gu[at : at + fb, 4 * fb + unit : 4 * fb + unit + fb] = column[g, e, 1]
                    dn[unit : unit + fb, at : at + fb] = column[g, e, 2]
    wide = gu.shape[1]
    away[:, :wide] = nn(tok[tb:, :], gu[...]).astype(BF)
    away[:, wide:] = nt(cot[tb:, :], dn[...]).astype(BF)
    keep[:, :wide] = nn(tok[:tb, :], gu[...])
    keep[:, wide:] = nt(cot[:tb, :], dn[...])


def grad_body(f, da, dc, tok, cot, p1, p3, p2, p0):
    tb = da.shape[0]
    fb = p0.shape[-1]
    hid = 4 * fb
    for j, piece in ((1, p1), (3, p3), (2, p2), (0, p0)):
        at = (f * NX + j) * fb
        gu = tn(tok[:tb, at : at + fb], da[:, : 2 * hid]) + tn(tok[tb:, at : at + fb], dc[:, : 2 * hid])
        dn = tn(da[:, 2 * hid :], cot[:tb, at : at + fb]) + tn(dc[:, 2 * hid :], cot[tb:, at : at + fb])
        for g in range(2):
            for e in range(2):
                unit = (g * 2 + e) * fb
                piece[g, e, 0] = gu[:, unit : unit + fb].astype(piece.dtype)
                piece[g, e, 1] = gu[:, hid + unit : hid + unit + fb].astype(piece.dtype)
                piece[g, e, 2] = dn[unit : unit + fb].astype(piece.dtype)


def output_body(da, dc, gu, dn, own, oth):
    tb, wide = da.shape[0], gu.shape[1]
    half = tb // 2
    for oc, part in ((0, da), (1, dc)):
        out = nn(part[:, wide:], dn[...]).astype(BF)
        grad = nt(part[:, :wide], gu[...]).astype(BF)
        for m, rows in ((0, out), (1, grad)):
            own[m, oc * half : (oc + 1) * half, :] = rows[:half]
            oth[m, oc * half : (oc + 1) * half, :] = rows[half:]


def shards(tokens, gate_weight, up_weight, down_weight, cotangent):
    dp, t = lax.axis_index("dp"), lax.axis_index("tensor")
    z, h, x = dp // (NH * NX), (dp // NX) % NH, dp % NX
    where = jnp.stack([t, h, x, z // 4]).astype(jnp.int32)
    fb = gate_weight.shape[0]
    tb = tokens.shape[0]
    sub = tb // 4
    quarter = cotangent.shape[1]
    wide, hid = 8 * fb, 4 * fb

    own, oth = call_at(
        pick_body,
        where,
        [(tokens, (tb, quarter), True), (cotangent, (tb, quarter), False)],
        [((2, tb, wide), BF)] * 2,
    )
    both = lax.all_gather(oth, "dp", axis_index_groups=PARTNERS)

    block = jnp.stack([gate_weight, up_weight, down_weight])
    pair = jnp.stack([block, send(block, swap_core)])

    def column_of(f, value):
        return [send(value, turn(f, g)) for g in range(2)]

    def along(column):
        return [column] + [send(column, along_x(-j)) for j in range(1, NX)]

    near = column_of(0, pair)
    pair, *near = lax.optimization_barrier((pair, *near))
    near = along(jnp.stack(near))
    far = along(jnp.stack(column_of(1, pair)))

    product = 2 * 2 * tb * wide * hid
    gu, dn, tok, cot, keep, away = call_at(
        forward_body,
        where,
        [(a, a.shape, False) for a in (own, both, *near, *far)],
        [((wide, 2 * hid), BF), ((hid, wide), BF), ((2 * tb, wide), BF), ((2 * tb, wide), BF), ((tb, 3 * hid), F32), ((tb, 3 * hid), BF)],
        3 * product,
    )
    part = keep + send(away, swap_core).astype(F32)
    pre = part[:sub]
    for k in range(1, 4):
        pre = pre + send(part[k * sub : (k + 1) * sub].astype(BF), along_y(k)).astype(F32)
    gate_pre, up_pre, d_hidden = pre[:, :hid], pre[:, hid : 2 * hid], pre[:, 2 * hid :]
    sig = jax.nn.sigmoid(gate_pre)
    act = gate_pre * sig
    hidden = (act * up_pre).astype(BF)
    d_gate = (d_hidden * up_pre * sig * (1.0 + gate_pre * (1.0 - sig))).astype(BF)
    d_up = (d_hidden * act).astype(BF)
    mine = jnp.concatenate([d_gate, d_up, hidden], axis=1)
    four = jnp.concatenate([mine] + [send(mine, along_y(k)) for k in range(1, 4)], axis=0)
    terms = (four, send(four, swap_core))

    shape = (2, 2, 3, fb, fb)

    def pieces_of(f):
        return call(functools.partial(grad_body, f), [(shape, BF)] * 3 + [(shape, F32)], [*terms, tok, cot], 3 * product // 2)

    def summed(moved, kept):
        total = kept
        for piece in moved:
            total = total + piece.astype(F32)
        return total.astype(BF)

    def returned(f, total):
        return [send_back(total[g], turn(f, g)) for g in range(2)]

    p1, p3, p2, p0 = pieces_of(0)
    q1, q3, q2, q0 = pieces_of(1)
    p1, p3, p2 = send(p1, along_x(1)), send(p3, along_x(3)), send(p2, along_x(2))
    p1, p3, q1, q3, q2 = lax.optimization_barrier((p1, p3, q1, q3, q2))
    back = returned(0, summed((p1, p3, p2), p0))
    q1, q3, q2 = send(q1, along_x(1)), send(q3, along_x(3)), send(q2, along_x(2))

    own, oth = call(output_body, [((2, tb, wide), BF)] * 2, [*terms, gu, dn], 3 * product)
    both = lax.all_gather(oth, "dp", axis_index_groups=PARTNERS)
    layer_out, token_grad = call_at(
        place_body,
        where,
        [(own, own.shape, False), (both, both.shape, False)],
        [((tb, quarter), BF)] * 2,
    )

    back = back + returned(1, summed((q1, q3, q2), q0))
    total = sum(piece.astype(F32) for piece in back)
    kept, moved, layer_out, token_grad = lax.optimization_barrier((total[0], total[1], layer_out, token_grad))
    total = kept + send(moved, swap_core)
    return layer_out, token_grad, total[0], total[1], total[2]


def solution(mesh):
    placed = (
        P("dp", None),
        P("dp", "tensor"),
        P("dp", "tensor"),
        P("tensor", "dp"),
        P("dp", "tensor"),
    )
    return jax.shard_map(
        shards,
        mesh=mesh,
        in_specs=placed,
        out_specs=(
            P("dp", "tensor"),
            P("dp", "tensor"),
            P("dp", "tensor"),
            P("dp", "tensor"),
            P("tensor", "dp"),
        ),
        check_vma=False,
    )
```

time: 1620 us -> 207 us (0.13)
  the two profiles are of different devices: /device:TPU:9 before, /device:TPU:1 now
where the time goes in v1:
time: 207 us; the launch traced here: 206 us
  waiting for transfers between devices  101 us (49%)
  starting transfers between devices  53.9 us (26%)
  local copies, waits for them, and re-layouts  22.3 us (11%)
  between operations  14.4 us (7%)
  Pallas kernels  12.1 us (6%)
  other arithmetic  2.42 us (1%)
    ppermute x26, waiting for transfers between devices, send(): return lax.ppermute(value, AXES, pairs_of(move))  74.4 us
    ppermute x26, starting transfers between devices, send(): return lax.ppermute(value, AXES, pairs_of(move))  46.7 us
    ppermute x4, waiting for transfers between devices, send_back(): return lax.ppermute(value, AXES, [(b, a) for a, b in pairs_of(move)])  26.6 us
    unnamed x52, local copies, waits for them, and re-layouts  21.5 us
    ppermute x4, starting transfers between devices, send_back(): return lax.ppermute(value, AXES, [(b, a) for a, b in pairs_of(move)])  7.19 us
    pallas_call x3, Pallas kernels, call_at(): pl.pallas_call(body, grid_spec=pltpu.PrefetchScalarGridSpec(num_scalar_pr...  6.97 us
    pallas_call x3, Pallas kernels, call(): pl.pallas_call(body, out_shape=[jax.ShapeDtypeStruct(s, d) for s, d in sh...  5.1 us
  transfers between devices with their start and end apart: 32, of which 24 were waited for; matrix products, arithmetic and copies ran while one was open for 1% of the time, Pallas kernels for 1%

profile of v1, /device:TPU:1, one launch (start us, length us, event | category | flops | bytes accessed | tf_op | source)
XLA Modules:
  0.0 206.2 jit_solution(11458957742112750441)
XLA Ops:
  7.4 2.2 %copy-done = bf16[256,8192]{1,0:T(8,128)(2,1)S(1)} copy-done((bf16[256,8192]{1,0:T(8,128)(2,1)S(1)}, bf16[256,8192]{1,0:T(8,128)(2,1)}, u32[]{:S(2)}) %copy-start) | copy-done | bytes 4194328
  9.5 1.2 copy-done.10
  10.8 2.2 %shard_map.92 = (bf16[2,256,1024]{2,1,0:T(8,128)(2,1)S(1)}, bf16[2,256,1024]{2,1,0:T(8,128)(2,1)}) custom-call(s32[4]{0:T(128)S(1)} %pad_add_fusion.where, bf16[256,8192]{1,0:T(8,128)(2,1)S(1)} %copy-done, bf16[256,2048]{1,0:T(8,128)(2,1)S(1)} %copy-done.10), custom_call_target="tpu_custom_call" | custom-call | bytes 4194304 | tf_op jit(solution)/shard_map/pallas_call | solution.py:98
  13.0 1.0 copy-done.5
  14.1 3.3 %collective-permute-start = (bf16[3,128,128]{2,1,0:T(8,128)(2,1)S(1)}, bf16[3,128,128]{2,1,0:T(8,128)(2,1)S(1)}, u32[]{:S(2)}, u32[]{:S(2)}) collective-permute-start(bf16[3,128,128]{2,1,0:T(8,128)(2,1)S(1)} %get-tuple-element.87), channel_id=1, source_target_pairs={{0,1},{1,0},{2,3},{3,2},{4,5},{5,4},{6,7},{7,6},{8,9},{9,8},{10,11... | collective-permute-start | bytes 294920 | tf_op jit(solution)/shard_map/ppermute | solution.py:33
  18.4 2.9 %collective-permute-start.2 = (bf16[2,3,128,128]{3,2,1,0:T(8,128)(2,1)S(1)}, bf16[2,3,128,128]{3,2,1,0:T(8,128)(2,1)S(1)}, u32[]{:S(2)}, u32[]{:S(2)}) collective-permute-start(bf16[2,3,128,128]{3,2,1,0:T(8,128)(2,1)S(1)} %pad_maximum_fusion.3), channel_id=1, source_target_pairs={{0,64},{1,96},{2,0},{3,32},{4,68},{5,100},{6,4},{7,36},{8,72},{9,1... | collective-permute-start | bytes 589832 | tf_op jit(solution)/shard_map/ppermute | solution.py:33
  21.3 5.0 %collective-permute-start.1 = (bf16[2,3,128,128]{3,2,1,0:T(8,128)(2,1)S(1)}, bf16[2,3,128,128]{3,2,1,0:T(8,128)(2,1)S(1)}, u32[]{:S(2)}, u32[]{:S(2)}) collective-permute-start(bf16[2,3,128,128]{3,2,1,0:T(8,128)(2,1)S(1)} %pad_maximum_fusion.3), channel_id=1, source_target_pairs={{0,0},{1,32},{2,64},{3,96},{4,4},{5,36},{6,68},{7,100},{8,8},{9,40... | collective-permute-start | bytes 589832 | tf_op jit(solution)/shard_map/ppermute | solution.py:33
  26.3 2.1 %collective-permute-done.2 = bf16[2,3,128,128]{3,2,1,0:T(8,128)(2,1)S(1)} collective-permute-done((bf16[2,3,128,128]{3,2,1,0:T(8,128)(2,1)S(1)}, bf16[2,3,128,128]{3,2,1,0:T(8,128)(2,1)S(1)}, u32[]{:S(2)}, u32[]{:S(2)}) %collective-permute-start.2) | collective-permute-done | bytes 196640 | tf_op jit(solution)/shard_map/ppermute | solution.py:33
  28.4 6.5 %collective-permute-done.1 = bf16[2,3,128,128]{3,2,1,0:T(8,128)(2,1)S(1)} collective-permute-done((bf16[2,3,128,128]{3,2,1,0:T(8,128)(2,1)S(1)}, bf16[2,3,128,128]{3,2,1,0:T(8,128)(2,1)S(1)}, u32[]{:S(2)}, u32[]{:S(2)}) %collective-permute-start.1) | collective-permute-done | bytes 196640 | tf_op jit(solution)/shard_map/ppermute | solution.py:33
  35.0 1.2 collective-permute-start.5
  36.2 5.3 %collective-permute-start.7 = (bf16[2,3,128,128]{3,2,1,0:T(8,128)(2,1)S(1)}, bf16[2,3,128,128]{3,2,1,0:T(8,128)(2,1)S(1)}, u32[]{:S(2)}, u32[]{:S(2)}) collective-permute-start(bf16[2,3,128,128]{3,2,1,0:T(8,128)(2,1)S(1)} %pad_maximum_fusion.3), channel_id=1, source_target_pairs={{0,192},{1,224},{2,128},{3,160},{4,196},{5,228},{6,132},{7,164},{8... | collective-permute-start | bytes 589832 | tf_op jit(solution)/shard_map/ppermute | solution.py:33
  41.5 2.0 collective-permute-start.6
  43.5 2.5 %collective-permute-start.4 = (bf16[2,2,3,128,128]{4,3,2,1,0:T(8,128)(2,1)S(1)}, bf16[2,2,3,128,128]{4,3,2,1,0:T(8,128)(2,1)S(1)}, u32[]{:S(2)}, u32[]{:S(2)}) collective-permute-start(bf16[2,2,3,128,128]{4,3,2,1,0:T(8,128)(2,1)S(1)} %pad_maximum_fusion.1.refs_0_), channel_id=1, source_target_pairs={{0,8},{1,9},{2,10},{3,11},{4,12},{5,13},{6,14},{7,15},{8,0},{9,1},... | collective-permute-start | bytes 1179656 | tf_op jit(solution)/shard_map/ppermute | solution.py:33
  46.0 1.1 collective-permute-start.3
  47.1 1.2 collective-permute-done.7
  49.0 1.3 collective-permute-start.10
  50.2 2.0 collective-permute-start.9
  52.2 1.4 collective-permute-start.8
  53.6 2.3 %collective-permute-done.4.refs_2_ = bf16[2,2,3,128,128]{4,3,2,1,0:T(8,128)(2,1)S(1)} collective-permute-done((bf16[2,2,3,128,128]{4,3,2,1,0:T(8,128)(2,1)S(1)}, bf16[2,2,3,128,128]{4,3,2,1,0:T(8,128)(2,1)S(1)}, u32[]{:S(2)}, u32[]{:S(2)}) %collective-permute-start.4) | collective-permute-done | bytes 393248 | tf_op jit(solution)/shard_map/ppermute | solution.py:33
  56.7 6.7 %collective-permute-done.3.refs_1_ = bf16[2,2,3,128,128]{4,3,2,1,0:T(8,128)(2,1)S(1)} collective-permute-done((bf16[2,2,3,128,128]{4,3,2,1,0:T(8,128)(2,1)S(1)}, bf16[2,2,3,128,128]{4,3,2,1,0:T(8,128)(2,1)S(1)}, u32[]{:S(2)}, u32[]{:S(2)}) %collective-permute-start.3) | collective-permute-done | bytes 393248 | tf_op jit(solution)/shard_map/ppermute | solution.py:33
  65.5 7.2 %collective-permute-done.9.refs_6_ = bf16[2,2,3,128,128]{4,3,2,1,0:T(8,128)(2,1)S(1)} collective-permute-done((bf16[2,2,3,128,128]{4,3,2,1,0:T(8,128)(2,1)S(1)}, bf16[2,2,3,128,128]{4,3,2,1,0:T(8,128)(2,1)S(1)}, u32[]{:S(2)}, u32[]{:S(2)}) %collective-permute-start.9) | collective-permute-done | bytes 393248 | tf_op jit(solution)/shard_map/ppermute | solution.py:33
  73.4 6.9 %collective-permute-done.8.refs_5_ = bf16[2,2,3,128,128]{4,3,2,1,0:T(8,128)(2,1)S(1)} collective-permute-done((bf16[2,2,3,128,128]{4,3,2,1,0:T(8,128)(2,1)S(1)}, bf16[2,2,3,128,128]{4,3,2,1,0:T(8,128)(2,1)S(1)}, u32[]{:S(2)}, u32[]{:S(2)}) %collective-permute-start.8) | collective-permute-done | bytes 393248 | tf_op jit(solution)/shard_map/ppermute | solution.py:33
  81.1 1.6 copy-done.3
  82.7 1.2 copy-done.6
  83.9 1.0 copy-done.14
  84.9 1.0 copy-done.16
  85.9 1.0 copy-done.18
  86.9 1.0 copy-done.20
  87.9 1.0 copy-done.22
  88.9 2.4 %shard_map.93 = (bf16[1024,1024]{1,0:T(8,128)(2,1)S(1)}, bf16[512,1024]{1,0:T(8,128)(2,1)S(1)}, bf16[512,1024]{1,0:T(8,128)(2,1)S(1)}, bf16[512,1024]{1,0:T(8,12...) custom-call(s32[4]{0:T(128)S(1)} %pad_add_fusion.where, bf16[2,256,1024]{2,1,0:T(8,128)(2,1)S(1)} %copy-done.6, ...), custom_call_target="tpu_custom_call" | custom-call | flops 1610612736 | bytes 13893632 | tf_op jit(solution)/shard_map/pallas_call | solution.py:98
  92.1 1.9 collective-permute-done.11
  94.3 1.3 collective-permute-start.12
  95.7 2.0 collective-permute-start.14
  97.6 1.0 collective-permute-start.13
  98.6 1.9 collective-permute-done.12
  100.5 4.8 %collective-permute-done.14 = bf16[64,1536]{1,0:T(8,128)(2,1)S(1)} collective-permute-done((bf16[64,1536]{1,0:T(8,128)(2,1)S(1)}, bf16[64,1536]{1,0:T(8,128)(2,1)S(1)}, u32[]{:S(2)}, u32[]{:S(2)}) %collective-permute-start.14) | collective-permute-done | bytes 196640 | tf_op jit(solution)/shard_map/ppermute | solution.py:33
  105.3 2.2 %collective-permute-done.13 = bf16[64,1536]{1,0:T(8,128)(2,1)S(1)} collective-permute-done((bf16[64,1536]{1,0:T(8,128)(2,1)S(1)}, bf16[64,1536]{1,0:T(8,128)(2,1)S(1)}, u32[]{:S(2)}, u32[]{:S(2)}) %collective-permute-start.13) | collective-permute-done | bytes 196640 | tf_op jit(solution)/shard_map/ppermute | solution.py:33
  107.7 1.5 collective-permute-start.17
  109.2 1.8 collective-permute-start.15
  111.0 5.8 %collective-permute-done.17 = bf16[64,1536]{1,0:T(8,128)(2,1)S(1)} collective-permute-done((bf16[64,1536]{1,0:T(8,128)(2,1)S(1)}, bf16[64,1536]{1,0:T(8,128)(2,1)S(1)}, u32[]{:S(2)}, u32[]{:S(2)}) %collective-permute-start.17) | collective-permute-done | bytes 196640 | tf_op jit(solution)/shard_map/ppermute | solution.py:33
  116.8 1.9 collective-permute-done.15
  118.8 2.4 %collective-permute-start.18 = (bf16[256,1536]{1,0:T(8,128)(2,1)S(1)}, bf16[256,1536]{1,0:T(8,128)(2,1)S(1)}, u32[]{:S(2)}, u32[]{:S(2)}) collective-permute-start(bf16[256,1536]{1,0:T(8,128)(2,1)S(1)} %pad_maximum_fusion.da), channel_id=1, source_target_pairs={{0,1},{1,0},{2,3},{3,2},{4,5},{5,4},{6,7},{7,6},{8,9},{9,8},{10,11... | collective-permute-start | bytes 2359304 | tf_op jit(solution)/shard_map/ppermute | solution.py:33
  121.2 1.9 collective-permute-done.18.dc
  123.2 2.0 shard_map.94
  126.1 1.4 collective-permute-start.19
  127.5 1.3 collective-permute-start.20
  128.7 1.5 collective-permute-start.21
  130.2 1.8 shard_map.96
  133.0 1.0 copy-done.9
  134.0 1.1 copy-done.2
  135.1 1.3 shard_map.95
  136.4 1.5 collective-permute-done.19
  138.8 1.8 collective-permute-start.25
  141.5 5.7 %collective-permute-done.21 = bf16[2,2,3,128,128]{4,3,2,1,0:T(8,128)(2,1)} collective-permute-done((bf16[2,2,3,128,128]{4,3,2,1,0:T(8,128)(2,1)S(1)}, bf16[2,2,3,128,128]{4,3,2,1,0:T(8,128)(2,1)}, u32[]{:S(2)}, u32[]{:S(2)}) %collective-permute-start.21) | collective-permute-done | bytes 393248 | tf_op jit(solution)/shard_map/ppermute | solution.py:33
  147.2 1.4 add_convert_fusion.1
  148.7 4.4 %collective-permute-start.22 = (bf16[2,3,128,128]{3,2,1,0:T(8,128)(2,1)S(1)}, bf16[2,3,128,128]{3,2,1,0:T(8,128)(2,1)S(1)}, u32[]{:S(2)}, u32[]{:S(2)}) collective-permute-start(bf16[2,3,128,128]{3,2,1,0:T(8,128)(2,1)S(1)} %get-tuple-element.76), channel_id=1, source_target_pairs={{0,0},{32,1},{64,2},{96,3},{4,4},{36,5},{68,6},{100,7},{8,8},{40,9... | collective-permute-start | bytes 589832 | tf_op jit(solution)/shard_map/ppermute | solution.py:37
  153.7 3.2 %collective-permute-done.24 = bf16[2,2,3,128,128]{4,3,2,1,0:T(8,128)(2,1)S(1)} collective-permute-done((bf16[2,2,3,128,128]{4,3,2,1,0:T(8,128)(2,1)S(1)}, bf16[2,2,3,128,128]{4,3,2,1,0:T(8,128)(2,1)S(1)}, u32[]{:S(2)}, u32[]{:S(2)}) %collective-permute-start.24) | collective-permute-done | bytes 393248 | tf_op jit(solution)/shard_map/ppermute | solution.py:33
  157.0 7.1 %collective-permute-done.26 = bf16[2,2,3,128,128]{4,3,2,1,0:T(8,128)(2,1)S(1)} collective-permute-done((bf16[2,2,3,128,128]{4,3,2,1,0:T(8,128)(2,1)S(1)}, bf16[2,2,3,128,128]{4,3,2,1,0:T(8,128)(2,1)S(1)}, u32[]{:S(2)}, u32[]{:S(2)}) %collective-permute-start.26) | collective-permute-done | bytes 393248 | tf_op jit(solution)/shard_map/ppermute | solution.py:33
  164.4 2.1 collective-permute-start.28
  166.5 8.3 %collective-permute-done.27 = bf16[2,3,128,128]{3,2,1,0:T(8,128)(2,1)S(1)} collective-permute-done((bf16[2,3,128,128]{3,2,1,0:T(8,128)(2,1)S(1)}, bf16[2,3,128,128]{3,2,1,0:T(8,128)(2,1)S(1)}, u32[]{:S(2)}, u32[]{:S(2)}) %collective-permute-start.27) | collective-permute-done | bytes 196640 | tf_op jit(solution)/shard_map/ppermute | solution.py:37
  174.8 18.3 %collective-permute-done.28 = bf16[2,3,128,128]{3,2,1,0:T(8,128)(2,1)S(1)} collective-permute-done((bf16[2,3,128,128]{3,2,1,0:T(8,128)(2,1)S(1)}, bf16[2,3,128,128]{3,2,1,0:T(8,128)(2,1)S(1)}, u32[]{:S(2)}, u32[]{:S(2)}) %collective-permute-start.28) | collective-permute-done | bytes 196640 | tf_op jit(solution)/shard_map/ppermute | solution.py:37
  193.2 1.6 copy-done.4
  194.8 2.4 %shard_map.97 = (bf16[256,2048]{1,0:T(8,128)(2,1)}, bf16[256,2048]{1,0:T(8,128)(2,1)}) custom-call(s32[4]{0:T(128)S(1)} %pad_add_fusion.where, bf16[2,256,1024]{2,1,0:T(8,128)(2,1)S(1)} %copy-done.8, bf16[2,2,256,1024]{3,2,1,0:T(8,128)(2,1)S(1)} %bitcast.35), custom_call_target="tpu_custom_call" | custom-call | bytes 5242880 | tf_op jit(solution)/shard_map/pallas_call | solution.py:98
  197.2 1.4 collective-permute-done.29
  (79 shorter events, 13.1 us)
Async XLA Ops:
  7.2 73.9 %all-gather.5.cloned.1.call-start = ((), (), s32[]{:S(2)}) async-start(), calls=%async_computation | async-start | bytes 3145728 | tf_op jit(solution)/shard_map/all_gather | solution.py:217
  7.4 2.2 %copy-start = (bf16[256,8192]{1,0:T(8,128)(2,1)S(1)}, bf16[256,8192]{1,0:T(8,128)(2,1)}, u32[]{:S(2)}) copy-start(bf16[256,8192]{1,0:T(8,128)(2,1)} %tok.1) | copy-start | bytes 12582916
  9.5 1.2 copy-start.10
  10.8 3.2 %copy-start.23 = (bf16[128,128]{1,0:T(8,128)(2,1)S(1)}, bf16[128,128]{1,0:T(8,128)(2,1)}, u32[]{:S(2)}) copy-start(bf16[128,128]{1,0:T(8,128)(2,1)} %param.8) | copy-start | bytes 98308
  10.8 3.3 %copy-start.24 = (bf16[128,128]{1,0:T(8,128)(2,1)S(1)}, bf16[128,128]{1,0:T(8,128)(2,1)}, u32[]{:S(2)}) copy-start(bf16[128,128]{1,0:T(8,128)(2,1)} %param.7) | copy-start | bytes 98308
  10.8 3.3 %copy-start.25 = (bf16[128,128]{1,0:T(8,128)(2,1)S(1)}, bf16[128,128]{1,0:T(8,128)(2,1)}, u32[]{:S(2)}) copy-start(bf16[128,128]{1,0:T(8,128)(2,1)} %param.6) | copy-start | bytes 98308
  13.0 1.0 copy-start.5
  14.0 179.3 %all-gather.7.cloned.1.call-start = ((), (), s32[]{:S(2)}) async-start(), calls=%async_computation.1 | async-start | bytes 3145728 | tf_op jit(solution)/shard_map/all_gather | solution.py:277
  14.1 4.3 %collective-permute-start = (bf16[3,128,128]{2,1,0:T(8,128)(2,1)S(1)}, bf16[3,128,128]{2,1,0:T(8,128)(2,1)S(1)}, u32[]{:S(2)}, u32[]{:S(2)}) collective-permute-start(bf16[3,128,128]{2,1,0:T(8,128)(2,1)S(1)} %get-tuple-element.87), channel_id=1, source_target_pairs={{0,1},{1,0},{2,3},{3,2},{4,5},{5,4},{6,7},{7,6},{8,9},{9,8},{10,11... | collective-permute-start | bytes 294920 | tf_op jit(solution)/shard_map/ppermute | solution.py:33
  18.4 10.1 %collective-permute-start.2 = (bf16[2,3,128,128]{3,2,1,0:T(8,128)(2,1)S(1)}, bf16[2,3,128,128]{3,2,1,0:T(8,128)(2,1)S(1)}, u32[]{:S(2)}, u32[]{:S(2)}) collective-permute-start(bf16[2,3,128,128]{3,2,1,0:T(8,128)(2,1)S(1)} %pad_maximum_fusion.3), channel_id=1, source_target_pairs={{0,64},{1,96},{2,0},{3,32},{4,68},{5,100},{6,4},{7,36},{8,72},{9,1... | collective-permute-start | bytes 589832 | tf_op jit(solution)/shard_map/ppermute | solution.py:33
  21.3 13.6 %collective-permute-start.1 = (bf16[2,3,128,128]{3,2,1,0:T(8,128)(2,1)S(1)}, bf16[2,3,128,128]{3,2,1,0:T(8,128)(2,1)S(1)}, u32[]{:S(2)}, u32[]{:S(2)}) collective-permute-start(bf16[2,3,128,128]{3,2,1,0:T(8,128)(2,1)S(1)} %pad_maximum_fusion.3), channel_id=1, source_target_pairs={{0,0},{1,32},{2,64},{3,96},{4,4},{5,36},{6,68},{7,100},{8,8},{9,40... | collective-permute-start | bytes 589832 | tf_op jit(solution)/shard_map/ppermute | solution.py:33
  35.0 17.3 %collective-permute-start.5 = (bf16[2,2,3,128,128]{4,3,2,1,0:T(8,128)(2,1)S(1)}, bf16[2,2,3,128,128]{4,3,2,1,0:T(8,128)(2,1)S(1)}, u32[]{:S(2)}, u32[]{:S(2)}) collective-permute-start(bf16[2,2,3,128,128]{4,3,2,1,0:T(8,128)(2,1)S(1)} %pad_maximum_fusion.1.refs_0_), channel_id=1, source_target_pairs={{0,4},{1,5},{2,6},{3,7},{4,8},{5,9},{6,10},{7,11},{8,12},{9,13},{1... | collective-permute-start | bytes 1179656 | tf_op jit(solution)/shard_map/ppermute | solution.py:33
  36.2 12.1 %collective-permute-start.7 = (bf16[2,3,128,128]{3,2,1,0:T(8,128)(2,1)S(1)}, bf16[2,3,128,128]{3,2,1,0:T(8,128)(2,1)S(1)}, u32[]{:S(2)}, u32[]{:S(2)}) collective-permute-start(bf16[2,3,128,128]{3,2,1,0:T(8,128)(2,1)S(1)} %pad_maximum_fusion.3), channel_id=1, source_target_pairs={{0,192},{1,224},{2,128},{3,160},{4,196},{5,228},{6,132},{7,164},{8... | collective-permute-start | bytes 589832 | tf_op jit(solution)/shard_map/ppermute | solution.py:33
  41.5 7.4 %collective-permute-start.6 = (bf16[2,3,128,128]{3,2,1,0:T(8,128)(2,1)S(1)}, bf16[2,3,128,128]{3,2,1,0:T(8,128)(2,1)S(1)}, u32[]{:S(2)}, u32[]{:S(2)}) collective-permute-start(bf16[2,3,128,128]{3,2,1,0:T(8,128)(2,1)S(1)} %pad_maximum_fusion.3), channel_id=1, source_target_pairs={{0,128},{1,160},{2,192},{3,224},{4,132},{5,164},{6,196},{7,228},{8... | collective-permute-start | bytes 589832 | tf_op jit(solution)/shard_map/ppermute | solution.py:33
  43.5 12.4 %collective-permute-start.4 = (bf16[2,2,3,128,128]{4,3,2,1,0:T(8,128)(2,1)S(1)}, bf16[2,2,3,128,128]{4,3,2,1,0:T(8,128)(2,1)S(1)}, u32[]{:S(2)}, u32[]{:S(2)}) collective-permute-start(bf16[2,2,3,128,128]{4,3,2,1,0:T(8,128)(2,1)S(1)} %pad_maximum_fusion.1.refs_0_), channel_id=1, source_target_pairs={{0,8},{1,9},{2,10},{3,11},{4,12},{5,13},{6,14},{7,15},{8,0},{9,1},... | collective-permute-start | bytes 1179656 | tf_op jit(solution)/shard_map/ppermute | solution.py:33
  46.0 17.5 %collective-permute-start.3 = (bf16[2,2,3,128,128]{4,3,2,1,0:T(8,128)(2,1)S(1)}, bf16[2,2,3,128,128]{4,3,2,1,0:T(8,128)(2,1)S(1)}, u32[]{:S(2)}, u32[]{:S(2)}) collective-permute-start(bf16[2,2,3,128,128]{4,3,2,1,0:T(8,128)(2,1)S(1)} %pad_maximum_fusion.1.refs_0_), channel_id=1, source_target_pairs={{0,12},{1,13},{2,14},{3,15},{4,0},{5,1},{6,2},{7,3},{8,4},{9,5},{1... | collective-permute-start | bytes 1179656 | tf_op jit(solution)/shard_map/ppermute | solution.py:33
  49.0 15.7 %collective-permute-start.10 = (bf16[2,2,3,128,128]{4,3,2,1,0:T(8,128)(2,1)S(1)}, bf16[2,2,3,128,128]{4,3,2,1,0:T(8,128)(2,1)S(1)}, u32[]{:S(2)}, u32[]{:S(2)}) collective-permute-start(bf16[2,2,3,128,128]{4,3,2,1,0:T(8,128)(2,1)S(1)} %pad_maximum_fusion.2.refs_4_), channel_id=1, source_target_pairs={{0,4},{1,5},{2,6},{3,7},{4,8},{5,9},{6,10},{7,11},{8,12},{9,13},{1... | collective-permute-start | bytes 1179656 | tf_op jit(solution)/shard_map/ppermute | solution.py:33
  50.2 22.4 %collective-permute-start.9 = (bf16[2,2,3,128,128]{4,3,2,1,0:T(8,128)(2,1)S(1)}, bf16[2,2,3,128,128]{4,3,2,1,0:T(8,128)(2,1)S(1)}, u32[]{:S(2)}, u32[]{:S(2)}) collective-permute-start(bf16[2,2,3,128,128]{4,3,2,1,0:T(8,128)(2,1)S(1)} %pad_maximum_fusion.2.refs_4_), channel_id=1, source_target_pairs={{0,8},{1,9},{2,10},{3,11},{4,12},{5,13},{6,14},{7,15},{8,0},{9,1},... | collective-permute-start | bytes 1179656 | tf_op jit(solution)/shard_map/ppermute | solution.py:33
  52.2 28.1 %collective-permute-start.8 = (bf16[2,2,3,128,128]{4,3,2,1,0:T(8,128)(2,1)S(1)}, bf16[2,2,3,128,128]{4,3,2,1,0:T(8,128)(2,1)S(1)}, u32[]{:S(2)}, u32[]{:S(2)}) collective-permute-start(bf16[2,2,3,128,128]{4,3,2,1,0:T(8,128)(2,1)S(1)} %pad_maximum_fusion.2.refs_4_), channel_id=1, source_target_pairs={{0,12},{1,13},{2,14},{3,15},{4,0},{5,1},{6,2},{7,3},{8,4},{9,5},{1... | collective-permute-start | bytes 1179656 | tf_op jit(solution)/shard_map/ppermute | solution.py:33
  55.9 0.8 copy-start.13
  63.4 0.7 copy-start.15
  64.7 0.8 copy-start.17
  72.7 0.8 copy-start.19
  80.3 0.7 copy-start.21
  81.1 1.6 copy-start.3
  82.7 1.2 copy-start.6
  83.9 1.0 copy-start.14
  84.9 1.0 copy-start.16
  85.9 1.0 copy-start.18
  86.9 1.0 copy-start.20
  87.9 1.0 copy-start.22
  91.3 2.7 %collective-permute-start.11 = (bf16[256,1536]{1,0:T(8,128)(2,1)S(1)}, bf16[256,1536]{1,0:T(8,128)(2,1)S(1)}, u32[]{:S(2)}, u32[]{:S(2)}) collective-permute-start(bf16[256,1536]{1,0:T(8,128)(2,1)S(1)} %get-tuple-element.43), channel_id=1, source_target_pairs={{0,1},{1,0},{2,3},{3,2},{4,5},{5,4},{6,7},{7,6},{8,9},{9,8},{10,11... | collective-permute-start | bytes 2359304 | tf_op jit(solution)/shard_map/ppermute | solution.py:33
  94.3 6.2 %collective-permute-start.12 = (bf16[64,1536]{1,0:T(8,128)(2,1)S(1)}, bf16[64,1536]{1,0:T(8,128)(2,1)S(1)}, u32[]{:S(2)}, u32[]{:S(2)}) collective-permute-start(bf16[64,1536]{1,0:T(8,128)(2,1)S(1)} %get-tuple-element.71), channel_id=1, source_target_pairs={{0,2},{1,3},{2,0},{3,1},{4,6},{5,7},{6,4},{7,5},{8,10},{9,11},{10,... | collective-permute-start | bytes 589832 | tf_op jit(solution)/shard_map/ppermute | solution.py:33
  95.7 9.6 %collective-permute-start.14 = (bf16[64,1536]{1,0:T(8,128)(2,1)S(1)}, bf16[64,1536]{1,0:T(8,128)(2,1)S(1)}, u32[]{:S(2)}, u32[]{:S(2)}) collective-permute-start(bf16[64,1536]{1,0:T(8,128)(2,1)S(1)} %get-tuple-element.72), channel_id=1, source_target_pairs={{0,18},{1,19},{2,16},{3,17},{4,22},{5,23},{6,20},{7,21},{8,26},{9,... | collective-permute-start | bytes 589832 | tf_op jit(solution)/shard_map/ppermute | solution.py:33
  97.6 9.8 %collective-permute-start.13 = (bf16[64,1536]{1,0:T(8,128)(2,1)S(1)}, bf16[64,1536]{1,0:T(8,128)(2,1)S(1)}, u32[]{:S(2)}, u32[]{:S(2)}) collective-permute-start(bf16[64,1536]{1,0:T(8,128)(2,1)S(1)} %get-tuple-element.73), channel_id=1, source_target_pairs={{0,16},{1,17},{2,18},{3,19},{4,20},{5,21},{6,22},{7,23},{8,24},{9,... | collective-permute-start | bytes 589832 | tf_op jit(solution)/shard_map/ppermute | solution.py:33
  107.7 9.2 %collective-permute-start.17 = (bf16[64,1536]{1,0:T(8,128)(2,1)S(1)}, bf16[64,1536]{1,0:T(8,128)(2,1)S(1)}, u32[]{:S(2)}, u32[]{:S(2)}) collective-permute-start(bf16[64,1536]{1,0:T(8,128)(2,1)S(1)} %pad_maximum_fusion.4), channel_id=1, source_target_pairs={{0,18},{1,19},{2,16},{3,17},{4,22},{5,23},{6,20},{7,21},{8,26},{9,... | collective-permute-start | bytes 589832 | tf_op jit(solution)/shard_map/ppermute | solution.py:33
  109.1 7.7 %collective-permute-start.16 = (bf16[64,1536]{1,0:T(8,128)(2,1)S(1)}, bf16[64,1536]{1,0:T(8,128)(2,1)S(1)}, u32[]{:S(2)}, u32[]{:S(2)}) collective-permute-start(bf16[64,1536]{1,0:T(8,128)(2,1)S(1)} %pad_maximum_fusion.4), channel_id=1, source_target_pairs={{0,16},{1,17},{2,18},{3,19},{4,20},{5,21},{6,22},{7,23},{8,24},{9,... | collective-permute-start | bytes 589832 | tf_op jit(solution)/shard_map/ppermute | solution.py:33
  109.2 9.6 %collective-permute-start.15 = (bf16[64,1536]{1,0:T(8,128)(2,1)S(1)}, bf16[64,1536]{1,0:T(8,128)(2,1)S(1)}, u32[]{:S(2)}, u32[]{:S(2)}) collective-permute-start(bf16[64,1536]{1,0:T(8,128)(2,1)S(1)} %pad_maximum_fusion.4), channel_id=1, source_target_pairs={{0,2},{1,3},{2,0},{3,1},{4,6},{5,7},{6,4},{7,5},{8,10},{9,11},{10,... | collective-permute-start | bytes 589832 | tf_op jit(solution)/shard_map/ppermute | solution.py:33
  118.8 4.4 %collective-permute-start.18 = (bf16[256,1536]{1,0:T(8,128)(2,1)S(1)}, bf16[256,1536]{1,0:T(8,128)(2,1)S(1)}, u32[]{:S(2)}, u32[]{:S(2)}) collective-permute-start(bf16[256,1536]{1,0:T(8,128)(2,1)S(1)} %pad_maximum_fusion.da), channel_id=1, source_target_pairs={{0,1},{1,0},{2,3},{3,2},{4,5},{5,4},{6,7},{7,6},{8,9},{9,8},{10,11... | collective-permute-start | bytes 2359304 | tf_op jit(solution)/shard_map/ppermute | solution.py:33
  123.2 7.1 %copy-start.1 = (bf16[256,1536]{1,0:T(8,128)(2,1)}, bf16[256,1536]{1,0:T(8,128)(2,1)S(1)}, u32[]{:S(2)}) copy-start(bf16[256,1536]{1,0:T(8,128)(2,1)S(1)} %collective-permute-done.18.dc) | copy-start | bytes 2359300
  125.2 0.9 copy-start.11
  126.1 11.8 %collective-permute-start.19 = (bf16[2,2,3,128,128]{4,3,2,1,0:T(8,128)(2,1)}, bf16[2,2,3,128,128]{4,3,2,1,0:T(8,128)(2,1)}, u32[]{:S(2)}, u32[]{:S(2)}) collective-permute-start(bf16[2,2,3,128,128]{4,3,2,1,0:T(8,128)(2,1)} %get-tuple-element.47), channel_id=1, source_target_pairs={{0,4},{1,5},{2,6},{3,7},{4,8},{5,9},{6,10},{7,11},{8,12},{9,13},{1... | collective-permute-start | bytes 1179656 | tf_op jit(solution)/shard_map/ppermute | solution.py:33
  127.5 10.4 %collective-permute-start.20 = (bf16[2,2,3,128,128]{4,3,2,1,0:T(8,128)(2,1)}, bf16[2,2,3,128,128]{4,3,2,1,0:T(8,128)(2,1)}, u32[]{:S(2)}, u32[]{:S(2)}) collective-permute-start(bf16[2,2,3,128,128]{4,3,2,1,0:T(8,128)(2,1)} %get-tuple-element.48), channel_id=1, source_target_pairs={{0,12},{1,13},{2,14},{3,15},{4,0},{5,1},{6,2},{7,3},{8,4},{9,5},{1... | collective-permute-start | bytes 1179656 | tf_op jit(solution)/shard_map/ppermute | solution.py:33
  128.7 18.5 %collective-permute-start.21 = (bf16[2,2,3,128,128]{4,3,2,1,0:T(8,128)(2,1)S(1)}, bf16[2,2,3,128,128]{4,3,2,1,0:T(8,128)(2,1)}, u32[]{:S(2)}, u32[]{:S(2)}) collective-permute-start(bf16[2,2,3,128,128]{4,3,2,1,0:T(8,128)(2,1)S(1)} %get-tuple-element.54), channel_id=1, source_target_pairs={{0,8},{1,9},{2,10},{3,11},{4,12},{5,13},{6,14},{7,15},{8,0},{9,1},... | collective-permute-start | bytes 1179656 | tf_op jit(solution)/shard_map/ppermute | solution.py:33
  132.0 1.0 copy-start.7
  133.0 1.0 copy-start.9
  134.0 1.1 copy-start.2
  135.1 12.1 %copy-start.12 = (f32[2,2,3,128,128]{4,3,2,1,0:T(8,128)S(1)}, f32[2,2,3,128,128]{4,3,2,1,0:T(8,128)}, u32[]{:S(2)}) copy-start(f32[2,2,3,128,128]{4,3,2,1,0:T(8,128)} %copy-done.11) | copy-start | bytes 2359300
  137.9 19.0 %collective-permute-start.24 = (bf16[2,2,3,128,128]{4,3,2,1,0:T(8,128)(2,1)S(1)}, bf16[2,2,3,128,128]{4,3,2,1,0:T(8,128)(2,1)S(1)}, u32[]{:S(2)}, u32[]{:S(2)}) collective-permute-start(bf16[2,2,3,128,128]{4,3,2,1,0:T(8,128)(2,1)S(1)} %get-tuple-element.56), channel_id=1, source_target_pairs={{0,4},{1,5},{2,6},{3,7},{4,8},{5,9},{6,10},{7,11},{8,12},{9,13},{1... | collective-permute-start | bytes 1179656 | tf_op jit(solution)/shard_map/ppermute | solution.py:33
  138.8 18.2 %collective-permute-start.25 = (bf16[2,2,3,128,128]{4,3,2,1,0:T(8,128)(2,1)S(1)}, bf16[2,2,3,128,128]{4,3,2,1,0:T(8,128)(2,1)S(1)}, u32[]{:S(2)}, u32[]{:S(2)}) collective-permute-start(bf16[2,2,3,128,128]{4,3,2,1,0:T(8,128)(2,1)S(1)} %get-tuple-element.57), channel_id=1, source_target_pairs={{0,12},{1,13},{2,14},{3,15},{4,0},{5,1},{6,2},{7,3},{8,4},{9,5},{1... | collective-permute-start | bytes 1179656 | tf_op jit(solution)/shard_map/ppermute | solution.py:33
  140.6 23.5 %collective-permute-start.26 = (bf16[2,2,3,128,128]{4,3,2,1,0:T(8,128)(2,1)S(1)}, bf16[2,2,3,128,128]{4,3,2,1,0:T(8,128)(2,1)S(1)}, u32[]{:S(2)}, u32[]{:S(2)}) collective-permute-start(bf16[2,2,3,128,128]{4,3,2,1,0:T(8,128)(2,1)S(1)} %get-tuple-element.58), channel_id=1, source_target_pairs={{0,8},{1,9},{2,10},{3,11},{4,12},{5,13},{6,14},{7,15},{8,0},{9,1},... | collective-permute-start | bytes 1179656 | tf_op jit(solution)/shard_map/ppermute | solution.py:33
  148.7 17.8 %collective-permute-start.22 = (bf16[2,3,128,128]{3,2,1,0:T(8,128)(2,1)S(1)}, bf16[2,3,128,128]{3,2,1,0:T(8,128)(2,1)S(1)}, u32[]{:S(2)}, u32[]{:S(2)}) collective-permute-start(bf16[2,3,128,128]{3,2,1,0:T(8,128)(2,1)S(1)} %get-tuple-element.76), channel_id=1, source_target_pairs={{0,0},{32,1},{64,2},{96,3},{4,4},{36,5},{68,6},{100,7},{8,8},{40,9... | collective-permute-start | bytes 589832 | tf_op jit(solution)/shard_map/ppermute | solution.py:37
  153.1 13.4 %collective-permute-start.23 = (bf16[2,3,128,128]{3,2,1,0:T(8,128)(2,1)S(1)}, bf16[2,3,128,128]{3,2,1,0:T(8,128)(2,1)S(1)}, u32[]{:S(2)}, u32[]{:S(2)}) collective-permute-start(bf16[2,3,128,128]{3,2,1,0:T(8,128)(2,1)S(1)} %get-tuple-element.77), channel_id=1, source_target_pairs={{64,0},{96,1},{0,2},{32,3},{68,4},{100,5},{4,6},{36,7},{72,8},{104... | collective-permute-start | bytes 589832 | tf_op jit(solution)/shard_map/ppermute | solution.py:37
  164.2 29.0 %copy-start.8 = (bf16[2,256,1024]{2,1,0:T(8,128)(2,1)S(1)}, bf16[2,256,1024]{2,1,0:T(8,128)(2,1)}, u32[]{:S(2)}) copy-start(bf16[2,256,1024]{2,1,0:T(8,128)(2,1)} %copy-done.7) | copy-start | bytes 3145732
  164.3 10.5 %collective-permute-start.27 = (bf16[2,3,128,128]{3,2,1,0:T(8,128)(2,1)S(1)}, bf16[2,3,128,128]{3,2,1,0:T(8,128)(2,1)S(1)}, u32[]{:S(2)}, u32[]{:S(2)}) collective-permute-start(bf16[2,3,128,128]{3,2,1,0:T(8,128)(2,1)S(1)} %get-tuple-element.78), channel_id=1, source_target_pairs={{128,0},{160,1},{192,2},{224,3},{132,4},{164,5},{196,6},{228,7},{1... | collective-permute-start | bytes 589832 | tf_op jit(solution)/shard_map/ppermute | solution.py:37
  164.4 28.7 %collective-permute-start.28 = (bf16[2,3,128,128]{3,2,1,0:T(8,128)(2,1)S(1)}, bf16[2,3,128,128]{3,2,1,0:T(8,128)(2,1)S(1)}, u32[]{:S(2)}, u32[]{:S(2)}) collective-permute-start(bf16[2,3,128,128]{3,2,1,0:T(8,128)(2,1)S(1)} %get-tuple-element.79), channel_id=1, source_target_pairs={{192,0},{224,1},{128,2},{160,3},{196,4},{228,5},{132,6},{164,7},{2... | collective-permute-start | bytes 589832 | tf_op jit(solution)/shard_map/ppermute | solution.py:37
  193.2 1.6 copy-start.4
  197.2 1.4 collective-permute-start.29
Sparse Core Ops, SparseCore 0:
  14.1 48.0 all-gather.4
  134.1 51.5 all-gather.6

commit v2 on v0

v2 whole, which is shorter than its diff:
```python
import functools

import jax
import jax.numpy as jnp
from jax import lax
from jax.experimental import pallas as pl
from jax.experimental.pallas import tpu as pltpu
from jax.sharding import PartitionSpec as P

NZ, NH, NX, NL, NC = 8, 2, 4, 2, 2
AXES = ("dp", "tensor")
BF = jnp.bfloat16
F32 = jnp.float32
VMEM_BYTES = 32 * 1024 * 1024


def index_of(z, h, x, l, c):
    return (((z * NH + h) * NX + x) * NL + l) * NC + c


def pairs_of(move):
    pairs = []
    for z in range(NZ):
        for h in range(NH):
            for x in range(NX):
                for l in range(NL):
                    for c in range(NC):
                        pairs.append((index_of(z, h, x, l, c), index_of(*move(z, h, x, l, c))))
    return pairs


def send(value, move):
    return lax.ppermute(value, AXES, pairs_of(move))


def send_back(value, move):
    return lax.ppermute(value, AXES, [(b, a) for a, b in pairs_of(move)])


def swap_hi(z, h, x, l, c):
    return z, 1 - h, x, l, c


def swap_core(z, h, x, l, c):
    return z, h, x, l, 1 - c


def along_x(step):
    return lambda z, h, x, l, c: (z, h, (x + step) % NX, l, c)


def turn(f, g):
    def move(z, h, x, l, c):
        return 4 * ((z % 2) ^ f) + 2 * (l ^ g) + c, h, x, z // 4, (z // 2) % 2

    return move


def after(value, *others):
    return lax.optimization_barrier((value, *others))[0]


def along_y(k):
    return lambda z, h, x, l, c: (z, h ^ (k // 2), x, l ^ (k % 2), c)


RING = [[index_of(z, h, x, l, c) for h in range(NH) for l in range(NL) for c in range(NC)] for z in range(NZ) for x in range(NX)]


def nn(a, b):
    return jnp.dot(a, b, preferred_element_type=F32)


def tn(a, b):
    return lax.dot_general(a, b, (((0,), (0,)), ((), ())), preferred_element_type=F32)


def nt(a, b):
    return lax.dot_general(a, b, (((1,), (1,)), ((), ())), preferred_element_type=F32)


def call(body, shapes, args, flops=0, where=None):
    moved = sum(a.size * a.dtype.itemsize for a in args)
    moved += sum(functools.reduce(lambda p, q: p * q, s, 1) * jnp.dtype(d).itemsize for s, d in shapes)
    scalars = [] if where is None else [where]
    return pl.pallas_call(
        body,
        out_shape=[jax.ShapeDtypeStruct(s, d) for s, d in shapes],
        in_specs=[pl.BlockSpec(memory_space=pltpu.SMEM)] * len(scalars) + [pl.BlockSpec(memory_space=pltpu.VMEM)] * len(args),
        out_specs=[pl.BlockSpec(memory_space=pltpu.VMEM)] * len(shapes),
        compiler_params=pltpu.CompilerParams(vmem_limit_bytes=VMEM_BYTES),
        cost_estimate=pl.CostEstimate(flops=flops, bytes_accessed=moved, transcendentals=0),
    )(*scalars, *args)


def blocks_of(where, fb):
    x, b = where[1], where[2]
    for r in range(2):
        for j in range(NX):
            s = lax.rem(x + j, NX)

            def lanes(half, r=r, s=s):
                return pl.multiple_of((((r ^ b) * NH + half) * NX + s) * fb, fb)

            yield (r * NX + j) * fb, lanes


def pick_body(where, tok, cot, own, oth):
    fb = tok.shape[1] // 16
    h = where[0]
    for m, source in enumerate((tok, cot)):
        for at, lanes in blocks_of(where, fb):
            oth[m, :, at : at + fb] = source[:, pl.ds(lanes(1 - h), fb)]
            own[m, :, at : at + fb] = source[:, pl.ds(lanes(h), fb)]


def place_body(where, own, far, layer_out, token_grad):
    fb = own.shape[2] // 8
    h = where[0]
    for m, out in enumerate((layer_out, token_grad)):
        for at, lanes in blocks_of(where, fb):
            out[:, pl.ds(lanes(h), fb)] = own[m, :, at : at + fb]
            out[:, pl.ds(lanes(1 - h), fb)] = far[m, :, at : at + fb]


def join_body(where, own, far, tok, cot):
    tb = own.shape[1]
    h = where[0]
    for m, full in enumerate((tok, cot)):
        full[pl.ds(pl.multiple_of(h * tb, tb), tb), :] = own[m]
        full[pl.ds(pl.multiple_of((1 - h) * tb, tb), tb), :] = far[m]


def forward_body(tok, cot, c0, c1, c2, c3, gu, dn, part):
    fb = c0.shape[-1]
    for f in range(2):
        for j, column in enumerate((c0, c1, c2, c3)):
            at = (f * NX + j) * fb
            for e in range(2):
                gu[at : at + fb, e * fb : e * fb + fb] = column[f, e, 0]
                gu[at : at + fb, (2 + e) * fb : (2 + e) * fb + fb] = column[f, e, 1]
                dn[e * fb : e * fb + fb, at : at + fb] = column[f, e, 2]
    wide = gu.shape[1]
    part[:, :wide] = nn(tok[...], gu[...]).astype(BF)
    part[:, wide:] = nt(cot[...], dn[...]).astype(BF)


def ordered_body(where, mine, twin, tok, cot, d, p1, p3, p2, p0):
    sub = mine.shape[0] // 4
    h, l, c = where[0], where[3], where[4]
    for k in range(4):
        for flip, part in ((0, mine), (1, twin)):
            row = (((h ^ (k // 2)) * NL + (l ^ (k % 2))) * NC + (c ^ flip)) * sub
            d[pl.ds(pl.multiple_of(row, sub), sub), :] = part[k * sub : (k + 1) * sub, :]
    grad_body(d, tok, cot, p1, p3, p2, p0)


def grad_body(d, tok, cot, p1, p3, p2, p0):
    fb = p0.shape[-1]
    wide = 4 * fb
    for j, piece in ((1, p1), (3, p3), (2, p2), (0, p0)):
        for f in range(2):
            at = (f * NX + j) * fb
            gu = tn(tok[:, at : at + fb], d[:, :wide])
            dn = tn(d[:, wide:], cot[:, at : at + fb])
            for e in range(2):
                piece[f, e, 0] = gu[:, e * fb : e * fb + fb].astype(piece.dtype)
                piece[f, e, 1] = gu[:, (2 + e) * fb : (2 + e) * fb + fb].astype(piece.dtype)
                piece[f, e, 2] = dn[e * fb : e * fb + fb].astype(piece.dtype)


def output_body(where, d, e, gu_d, dn_d, gu_e, dn_e, own, oth):
    wide = gu_d.shape[1]
    tb = own.shape[1]
    h = where[0]
    for half, to in ((h, own), (1 - h, oth)):
        rows = pl.ds(pl.multiple_of(half * tb, tb), tb)
        to[0] = (nn(d[rows, wide:], dn_d[...]) + nn(e[rows, wide:], dn_e[...])).astype(BF)
        to[1] = (nt(d[rows, :wide], gu_d[...]) + nt(e[rows, :wide], gu_e[...])).astype(BF)


def shards(tokens, gate_weight, up_weight, down_weight, cotangent):
    dp, t = lax.axis_index("dp"), lax.axis_index("tensor")
    z, h, x = dp // (NH * NX), (dp // NX) % NH, dp % NX
    where = jnp.stack([h, x, z // 4, t // 2, t % 2]).astype(jnp.int32)
    fb = gate_weight.shape[0]
    tb = tokens.shape[0]
    quarter = cotangent.shape[1]
    wide, unit = 8 * fb, 2 * fb

    with jax.named_scope("weights_core"):
        block = jnp.stack([gate_weight, up_weight, down_weight])
        pair = jnp.stack([block, send(block, swap_core)])

    def turned(g, value):
        with jax.named_scope(f"weights_turn_{g}"):
            return [send(value, turn(f, g)) for f in range(2)]

    def along(g, column):
        with jax.named_scope(f"weights_x_{g}"):
            return [column] + [send(column, along_x(-j)) for j in range(1, NX)]

    first = turned(0, pair)
    where, tokens, cotangent, _ = lax.optimization_barrier((where, tokens, cotangent, pair))
    picked = lax.dynamic_slice(tokens, (0, t * quarter), (tb, quarter))
    with jax.named_scope("pick"):
        own, oth = call(pick_body, [((2, tb, wide), BF)] * 2, [picked, cotangent], 0, where)
    with jax.named_scope("input_swap"):
        far = send(oth, swap_hi)
    with jax.named_scope("join"):
        tok, cot = call(join_body, [((2 * tb, wide), BF)] * 2, [own, far], 0, where)
    pair, *first = lax.optimization_barrier((pair, *first))
    first = along(0, jnp.stack(first))
    second = jnp.stack(turned(1, after(pair, far)))
    first[0] = after(first[0], second)
    second = along(1, after(second, first[1], first[2], first[3]))

    product = 2 * 2 * tb * wide * unit

    def forward(g, columns, rows):
        with jax.named_scope(f"forward_{g}"):
            return call(
                forward_body,
                [((wide, 2 * unit), BF), ((unit, wide), BF), ((2 * tb, 3 * unit), BF)],
                [rows, cot, *columns],
                3 * product,
            )

    def reduced(g, part):
        with jax.named_scope(f"reduce_ring_{g}"):
            parts = lax.all_to_all(part.reshape(8, -1, part.shape[1]), AXES, 0, 0, axis_index_groups=RING, tiled=True)
            return jnp.sum(parts.astype(F32), axis=0)

    def activations(pre):
        gate_pre, up_pre, d_hidden = pre[:, :unit], pre[:, unit : 2 * unit], pre[:, 2 * unit :]
        sig = jax.nn.sigmoid(gate_pre)
        act = gate_pre * sig
        hidden = (act * up_pre).astype(BF)
        d_gate = (d_hidden * up_pre * sig * (1.0 + gate_pre * (1.0 - sig))).astype(BF)
        d_up = (d_hidden * act).astype(BF)
        return jnp.concatenate([d_gate, d_up, hidden], axis=1)

    def gathered(g, mine):
        with jax.named_scope(f"gather_ring_{g}"):
            four = jnp.concatenate([mine] + [send(mine, along_y(k)) for k in range(1, 4)], axis=0)
        with jax.named_scope(f"gather_core_{g}"):
            return four, send(four, swap_core)

    def gathered_at_once(g, mine):
        with jax.named_scope(f"gather_ring_{g}"):
            copies = jnp.broadcast_to(mine, (8, *mine.shape))
            return (lax.all_to_all(copies, AXES, 0, 0, axis_index_groups=RING, tiled=True).reshape(-1, mine.shape[1]),)

    shape = (2, 2, 3, fb, fb)

    def pieces_of(g, terms):
        shapes = [(shape, BF)] * 3 + [(shape, F32)]
        with jax.named_scope(f"grads_{g}"):
            if len(terms) == 1:
                return [*terms, *call(grad_body, shapes, [*terms, tok, cot], 3 * product)]
            return call(ordered_body, [((2 * tb, 3 * unit), BF)] + shapes, [*terms, tok, cot], 3 * product, where)

    def summed(moved, kept):
        total = kept
        for piece in moved:
            total = total + piece.astype(F32)
        return total.astype(BF)

    def returned(g, total):
        with jax.named_scope(f"grads_turn_{g}"):
            return [send_back(total[f], turn(f, g)) for f in range(2)]

    gu_0, dn_0, part_0 = forward(0, first, tok)
    mine_0 = activations(reduced(0, part_0))
    gu_1, dn_1, part_1 = forward(1, second, after(tok, mine_0))
    terms_0 = gathered(0, mine_0)
    d_0, p1, p3, p2, p0 = pieces_of(0, terms_0)
    with jax.named_scope("grads_x_0"):
        p1, p3, p2 = send(p1, along_x(1)), send(p3, along_x(3)), send(p2, along_x(2))

    terms_1 = gathered_at_once(1, after(activations(reduced(1, part_1)), d_0))
    d_1, q1, q3, q2, q0 = pieces_of(1, terms_1)
    with jax.named_scope("outputs"):
        own, oth = call(output_body, [((2, tb, wide), BF)] * 2, [d_0, d_1, gu_0, dn_0, gu_1, dn_1], 6 * product, where)
    p1, p3, q1, q3, q2, oth = lax.optimization_barrier((p1, p3, q1, q3, q2, oth))
    back = returned(0, summed((p1, p3, p2), p0))
    with jax.named_scope("grads_x_1"):
        q1, q3, q2 = send(q1, along_x(1)), send(q3, along_x(3)), send(q2, along_x(2))

    with jax.named_scope("output_swap"):
        far = send(oth, swap_hi)
    with jax.named_scope("place"):
        layer_out, token_grad = call(place_body, [((tb, quarter), BF)] * 2, [own, far], 0, where)

    back = back + returned(1, after(summed((q1, q3, q2), q0), far))
    total = sum(piece.astype(F32) for piece in back)
    kept, moved, layer_out, token_grad = lax.optimization_barrier((total[0], total[1], layer_out, token_grad))
    with jax.named_scope("grads_core"):
        total = kept + send(moved, swap_core)
    return layer_out, token_grad, total[0], total[1], total[2]


def solution(mesh):
    placed = (
        P("dp", None),
        P("dp", "tensor"),
        P("dp", "tensor"),
        P("tensor", "dp"),
        P("dp", "tensor"),
    )
    return jax.shard_map(
        shards,
        mesh=mesh,
        in_specs=placed,
        out_specs=(
            P("dp", "tensor"),
            P("dp", "tensor"),
            P("dp", "tensor"),
            P("dp", "tensor"),
            P("tensor", "dp"),
        ),
        check_vma=False,
    )
```

time: 1620 us -> 208 us (0.13)
  the two profiles are of different devices: /device:TPU:9 before, /device:TPU:1 now
where the time goes in v2:
time: 208 us; the launch traced here: 207 us
  waiting for transfers between devices  87.7 us (42%)
  starting transfers between devices  81.2 us (39%)
  local copies, waits for them, and re-layouts  16.8 us (8%)
  Pallas kernels  14.7 us (7%)
  other arithmetic  5.73 us (3%)
    ppermute x24, waiting for transfers between devices, send(): return lax.ppermute(value, AXES, pairs_of(move))  45.8 us
    ppermute x24, starting transfers between devices, send(): return lax.ppermute(value, AXES, pairs_of(move))  43.5 us
    ppermute x4, waiting for transfers between devices, send_back(): return lax.ppermute(value, AXES, [(b, a) for a, b in pairs_of(move)])  18.8 us
    ppermute x4, starting transfers between devices, send_back(): return lax.ppermute(value, AXES, [(b, a) for a, b in pairs_of(move)])  18 us
    all_to_all x2, starting transfers between devices, reduced(): lax.all_to_all(part.reshape(8, -1, part.shape[1]), AXES, 0, 0, axis_index...  15.3 us
    pallas_call x8, Pallas kernels, call(): pl.pallas_call(body, out_shape=[jax.ShapeDtypeStruct(s, d) for s, d in sh...  14.7 us
    unnamed x30, local copies, waits for them, and re-layouts  13.7 us
    all_to_all x2, waiting for transfers between devices, reduced(): lax.all_to_all(part.reshape(8, -1, part.shape[1]), AXES, 0, 0, axis_index...  13.5 us
  transfers between devices with their start and end apart: 31, of which 16 were waited for; matrix products, arithmetic and copies ran while one was open for 2% of the time, Pallas kernels for 6%

profile of v2, /device:TPU:1, one launch (start us, length us, event | category | flops | bytes accessed | tf_op | source)
XLA Modules:
  0.0 207.1 jit_solution(2220800851203494737)
XLA Ops:
  0.6 0.8 fusion.2
  1.4 3.3 %collective-permute-start = (bf16[3,128,128]{2,1,0:T(8,128)(2,1)S(1)}, bf16[3,128,128]{2,1,0:T(8,128)(2,1)S(1)}, u32[]{:S(2)}, u32[]{:S(2)}) collective-permute-start(bf16[3,128,128]{2,1,0:T(8,128)(2,1)S(1)} %get-tuple-element.111), channel_id=1, source_target_pairs={{0,1},{1,0},{2,3},{3,2},{4,5},{5,4},{6,7},{7,6},{8,9},{9,8},{10,11... | collective-permute-start | bytes 294920 | tf_op jit(solution)/shard_map/weights_core/ppermute | solution.py:33
  4.9 0.9 collective-permute-done
  5.7 1.3 constant_dynamic-slice_fusion.tok
  7.1 1.2 copy-done
  8.3 1.2 pick.1
  9.5 1.3 collective-permute-start.1
  10.8 4.1 %collective-permute-start.2 = (bf16[2,3,128,128]{3,2,1,0:T(8,128)(2,1)S(1)}, bf16[2,3,128,128]{3,2,1,0:T(8,128)(2,1)S(1)}, u32[]{:S(2)}, u32[]{:S(2)}) collective-permute-start(bf16[2,3,128,128]{3,2,1,0:T(8,128)(2,1)S(1)} %pad_maximum_fusion.3), channel_id=1, source_target_pairs={{0,0},{1,32},{2,64},{3,96},{4,4},{5,36},{6,68},{7,100},{8,8},{9,40... | collective-permute-start | bytes 589832 | tf_op jit(solution)/shard_map/weights_turn_0/ppermute | solution.py:33
  14.8 6.0 %collective-permute-start.3 = (bf16[2,3,128,128]{3,2,1,0:T(8,128)(2,1)S(1)}, bf16[2,3,128,128]{3,2,1,0:T(8,128)(2,1)S(1)}, u32[]{:S(2)}, u32[]{:S(2)}) collective-permute-start(bf16[2,3,128,128]{3,2,1,0:T(8,128)(2,1)S(1)} %pad_maximum_fusion.3), channel_id=1, source_target_pairs={{0,128},{1,160},{2,192},{3,224},{4,132},{5,164},{6,196},{7,228},{8... | collective-permute-start | bytes 589832 | tf_op jit(solution)/shard_map/weights_turn_0/ppermute | solution.py:33
  20.9 1.4 collective-permute-done.2
  22.3 5.1 %collective-permute-done.3 = bf16[2,3,128,128]{3,2,1,0:T(8,128)(2,1)S(1)} collective-permute-done((bf16[2,3,128,128]{3,2,1,0:T(8,128)(2,1)S(1)}, bf16[2,3,128,128]{3,2,1,0:T(8,128)(2,1)S(1)}, u32[]{:S(2)}, u32[]{:S(2)}) %collective-permute-start.3) | collective-permute-done | bytes 196640 | tf_op jit(solution)/shard_map/weights_turn_0/ppermute | solution.py:33
  27.4 2.5 %collective-permute-start.6 = (bf16[2,2,3,128,128]{4,3,2,1,0:T(8,128)(2,1)S(1)}, bf16[2,2,3,128,128]{4,3,2,1,0:T(8,128)(2,1)S(1)}, u32[]{:S(2)}, u32[]{:S(2)}) collective-permute-start(bf16[2,2,3,128,128]{4,3,2,1,0:T(8,128)(2,1)S(1)} %pad_maximum_fusion.c0), channel_id=1, source_target_pairs={{0,12},{1,13},{2,14},{3,15},{4,0},{5,1},{6,2},{7,3},{8,4},{9,5},{1... | collective-permute-start | bytes 1179656 | tf_op jit(solution)/shard_map/weights_x_0/ppermute | solution.py:33
  31.0 12.9 %collective-permute-done.1.far = bf16[2,256,1024]{2,1,0:T(8,128)(2,1)S(1)} collective-permute-done((bf16[2,256,1024]{2,1,0:T(8,128)(2,1)S(1)}, bf16[2,256,1024]{2,1,0:T(8,128)(2,1)S(1)}, u32[]{:S(2)}, u32[]{:S(2)}) %collective-permute-start.1) | collective-permute-done | bytes 1048608 | tf_op jit(solution)/shard_map/input_swap/ppermute | solution.py:33
  43.9 1.9 collective-permute-start.5
  45.8 7.5 %collective-permute-start.4 = (bf16[2,3,128,128]{3,2,1,0:T(8,128)(2,1)S(1)}, bf16[2,3,128,128]{3,2,1,0:T(8,128)(2,1)S(1)}, u32[]{:S(2)}, u32[]{:S(2)}) collective-permute-start(bf16[2,3,128,128]{3,2,1,0:T(8,128)(2,1)S(1)} %pad_maximum_fusion.3), channel_id=1, source_target_pairs={{0,64},{1,96},{2,0},{3,32},{4,68},{5,100},{6,4},{7,36},{8,72},{9,1... | collective-permute-start | bytes 589832 | tf_op jit(solution)/shard_map/weights_turn_1/ppermute | solution.py:33
  53.4 0.7 join.1
  54.1 4.2 %collective-permute-done.4 = bf16[2,3,128,128]{3,2,1,0:T(8,128)(2,1)S(1)} collective-permute-done((bf16[2,3,128,128]{3,2,1,0:T(8,128)(2,1)S(1)}, bf16[2,3,128,128]{3,2,1,0:T(8,128)(2,1)S(1)}, u32[]{:S(2)}, u32[]{:S(2)}) %collective-permute-start.4) | collective-permute-done | bytes 196640 | tf_op jit(solution)/shard_map/weights_turn_1/ppermute | solution.py:33
  58.4 2.0 forward_0.1
  60.4 1.0 copy-done.3
  61.3 0.8 copy-done.7
  62.1 10.4 %all-to-all-start = ((bf16[8,64,768]{2,1,0:T(8,128)(2,1)}), bf16[8,64,768]{2,1,0:T(8,128)(2,1)}, u32[]{:S(2)}, u32[]{:S(2)}) async-start(bf16[8,64,768]{2,1,0:T(8,128)(2,1)} %bitcast.14), calls=%async_computation | async-start | bytes 1572864 | tf_op jit(solution)/shard_map/reduce_ring_0/all_to_all | solution.py:231
  72.6 2.2 %collective-permute-start.15 = (bf16[2,2,3,128,128]{4,3,2,1,0:T(8,128)(2,1)S(1)}, bf16[2,2,3,128,128]{4,3,2,1,0:T(8,128)(2,1)S(1)}, u32[]{:S(2)}, u32[]{:S(2)}) collective-permute-start(bf16[2,2,3,128,128]{4,3,2,1,0:T(8,128)(2,1)S(1)} %pad_maximum_fusion.1.c0), channel_id=1, source_target_pairs={{0,12},{1,13},{2,14},{3,15},{4,0},{5,1},{6,2},{7,3},{8,4},{9,5},{1... | collective-permute-start | bytes 1179656 | tf_op jit(solution)/shard_map/weights_x_1/ppermute | solution.py:33
  74.7 1.0 collective-permute-start.16
  75.8 9.2 %all-to-all-done = bf16[8,64,768]{2,1,0:T(8,128)(2,1)} async-done(((bf16[8,64,768]{2,1,0:T(8,128)(2,1)}), bf16[8,64,768]{2,1,0:T(8,128)(2,1)}, u32[]{:S(2)}, u32[]{:S(2)}) %all-to-all-start) | async-done | bytes 786464 | tf_op jit(solution)/shard_map/reduce_ring_0/all_to_all | solution.py:231
  85.0 1.3 convert_reduce_fusion.1
  87.2 1.8 collective-permute-start.10
  89.0 2.6 %collective-permute-done.15.c1 = bf16[2,2,3,128,128]{4,3,2,1,0:T(8,128)(2,1)S(1)} collective-permute-done((bf16[2,2,3,128,128]{4,3,2,1,0:T(8,128)(2,1)S(1)}, bf16[2,2,3,128,128]{4,3,2,1,0:T(8,128)(2,1)S(1)}, u32[]{:S(2)}, u32[]{:S(2)}) %collective-permute-start.15) | collective-permute-done | bytes 393248 | tf_op jit(solution)/shard_map/weights_x_1/ppermute | solution.py:33
  91.6 4.2 %collective-permute-done.17.c3 = bf16[2,2,3,128,128]{4,3,2,1,0:T(8,128)(2,1)} collective-permute-done((bf16[2,2,3,128,128]{4,3,2,1,0:T(8,128)(2,1)S(1)}, bf16[2,2,3,128,128]{4,3,2,1,0:T(8,128)(2,1)}, u32[]{:S(2)}, u32[]{:S(2)}) %collective-permute-start.17) | collective-permute-done | bytes 393248 | tf_op jit(solution)/shard_map/weights_x_1/ppermute | solution.py:33
  95.8 3.0 %forward_1.1 = (bf16[1024,512]{1,0:T(8,128)(2,1)S(1)}, bf16[256,1024]{1,0:T(8,128)(2,1)S(1)}, bf16[512,768]{1,0:T(8,128)(2,1)}) custom-call(bf16[512,1024]{1,0:T(8,128)(2,1)S(1)} %get-tuple-element.66.tok, bf16[512,1024]{1,0:T(8,128)(2,1)S(1)} %get-tuple-element.56.cot, bf16[2,2,3,128,128]{4,3,2,1,0:T(8,128)(2,1)S(1)} %pad_maximum_fusion.1.c0, ...), custom_call_target="tpu_custom_call" | custom-call | flops 805306368 | bytes 6029312 | tf_op jit(solution)/shard_map/forward_1/pallas_call | solution.py:86
  98.8 1.0 copy-done.5
  99.8 0.8 copy-done.9
  100.5 4.9 %all-to-all-start.1 = ((bf16[8,64,768]{2,1,0:T(8,128)(2,1)}), bf16[8,64,768]{2,1,0:T(8,128)(2,1)S(1)}, u32[]{:S(2)}, u32[]{:S(2)}) async-start(bf16[8,64,768]{2,1,0:T(8,128)(2,1)} %bitcast.15), calls=%async_computation.1 | async-start | bytes 1572864 | tf_op jit(solution)/shard_map/reduce_ring_1/all_to_all | solution.py:231
  105.5 1.0 pad_maximum_fusion.2.mine
  106.6 1.7 collective-permute-done.12.twin
  108.3 1.9 grads_0.1
  110.2 0.9 copy-done.1
  111.1 0.7 copy-done.11
  111.8 0.8 copy-done.12
  112.6 0.9 copy-done.13
  113.5 4.3 %all-to-all-done.1 = bf16[8,64,768]{2,1,0:T(8,128)(2,1)S(1)} async-done(((bf16[8,64,768]{2,1,0:T(8,128)(2,1)}), bf16[8,64,768]{2,1,0:T(8,128)(2,1)S(1)}, u32[]{:S(2)}, u32[]{:S(2)}) %all-to-all-start.1) | async-done | bytes 786464 | tf_op jit(solution)/shard_map/reduce_ring_1/all_to_all | solution.py:231
  117.9 0.9 broadcast_in_dim.3
  118.9 4.3 %all-to-all-start.2 = ((bf16[8,64,768]{2,1,0:T(8,128)(2,1)}), bf16[8,64,768]{2,1,0:T(8,128)(2,1)S(1)}, u32[]{:S(2)}, u32[]{:S(2)}) async-start(bf16[8,64,768]{2,1,0:T(8,128)(2,1)} %broadcast_in_dim.3), calls=%async_computation.2 | async-start | bytes 1572864 | tf_op jit(solution)/shard_map/gather_ring_1/all_to_all | solution.py:252
  123.2 2.7 %collective-permute-start.14 = (bf16[2,2,3,128,128]{4,3,2,1,0:T(8,128)(2,1)}, bf16[2,2,3,128,128]{4,3,2,1,0:T(8,128)(2,1)}, u32[]{:S(2)}, u32[]{:S(2)}) collective-permute-start(bf16[2,2,3,128,128]{4,3,2,1,0:T(8,128)(2,1)} %copy-done.11), channel_id=1, source_target_pairs={{0,12},{1,13},{2,14},{3,15},{4,0},{5,1},{6,2},{7,3},{8,4},{9,5},{1... | collective-permute-start | bytes 1179656 | tf_op jit(solution)/shard_map/grads_x_0/ppermute | solution.py:33
  125.9 9.6 %all-to-all-done.2 = bf16[8,64,768]{2,1,0:T(8,128)(2,1)S(1)} async-done(((bf16[8,64,768]{2,1,0:T(8,128)(2,1)}), bf16[8,64,768]{2,1,0:T(8,128)(2,1)S(1)}, u32[]{:S(2)}, u32[]{:S(2)}) %all-to-all-start.2) | async-done | bytes 786464 | tf_op jit(solution)/shard_map/gather_ring_1/all_to_all | solution.py:252
  135.5 1.3 grads_1.1
  136.8 1.2 copy-done.4
  138.0 1.2 copy-done.6
  139.3 1.0 copy-done.8
  140.3 1.0 copy-done.10
  141.3 1.1 copy-done.14
  142.5 2.3 %outputs.1 = (bf16[2,256,1024]{2,1,0:T(8,128)(2,1)S(1)}, bf16[2,256,1024]{2,1,0:T(8,128)(2,1)S(1)}) custom-call(s32[5]{0:T(128)S(1)} %stack.62.where, bf16[512,768]{1,0:T(8,128)(2,1)S(1)} %copy-done.14, bf16[512,768]{1,0:T(8,128)(2,1)S(1)} %bitcast.37, bf16[1024,512]{1,0:T(8,128)(2,1)S(1)} %copy-done.4, bf16[256,1024]{1,0:T(8,128)(2,1)S(1)} %copy-done.8, ...), custom_call_target="tpu_custom_call" | custom-call | flops 1610612736 | bytes 6815744 | tf_op jit(solution)/shard_map/outputs/pallas_call | solution.py:86
  145.3 0.9 collective-permute-start.23
  146.2 2.5 %collective-permute-start.22 = (bf16[2,2,3,128,128]{4,3,2,1,0:T(8,128)(2,1)S(1)}, bf16[2,2,3,128,128]{4,3,2,1,0:T(8,128)(2,1)S(1)}, u32[]{:S(2)}, u32[]{:S(2)}) collective-permute-start(bf16[2,2,3,128,128]{4,3,2,1,0:T(8,128)(2,1)S(1)} %get-tuple-element.84), channel_id=1, source_target_pairs={{0,12},{1,13},{2,14},{3,15},{4,0},{5,1},{6,2},{7,3},{8,4},{9,5},{1... | collective-permute-start | bytes 1179656 | tf_op jit(solution)/shard_map/grads_x_1/ppermute | solution.py:33
  149.3 1.4 add_convert_fusion.1
  150.8 5.4 %collective-permute-start.20 = (bf16[2,3,128,128]{3,2,1,0:T(8,128)(2,1)S(1)}, bf16[2,3,128,128]{3,2,1,0:T(8,128)(2,1)S(1)}, u32[]{:S(2)}, u32[]{:S(2)}) collective-permute-start(bf16[2,3,128,128]{3,2,1,0:T(8,128)(2,1)S(1)} %get-tuple-element.98), channel_id=1, source_target_pairs={{128,0},{160,1},{192,2},{224,3},{132,4},{164,5},{196,6},{228,7},{1... | collective-permute-start | bytes 589832 | tf_op jit(solution)/shard_map/grads_turn_0/ppermute | solution.py:37
  156.3 10.6 %collective-permute-start.19 = (bf16[2,3,128,128]{3,2,1,0:T(8,128)(2,1)S(1)}, bf16[2,3,128,128]{3,2,1,0:T(8,128)(2,1)S(1)}, u32[]{:S(2)}, u32[]{:S(2)}) collective-permute-start(bf16[2,3,128,128]{3,2,1,0:T(8,128)(2,1)S(1)} %get-tuple-element.97), channel_id=1, source_target_pairs={{0,0},{32,1},{64,2},{96,3},{4,4},{36,5},{68,6},{100,7},{8,8},{40,9... | collective-permute-start | bytes 589832 | tf_op jit(solution)/shard_map/grads_turn_0/ppermute | solution.py:37
  167.1 11.6 %collective-permute-done.24.far = bf16[2,256,1024]{2,1,0:T(8,128)(2,1)S(1)} collective-permute-done((bf16[2,256,1024]{2,1,0:T(8,128)(2,1)S(1)}, bf16[2,256,1024]{2,1,0:T(8,128)(2,1)S(1)}, u32[]{:S(2)}, u32[]{:S(2)}) %collective-permute-start.24) | collective-permute-done | bytes 1048608 | tf_op jit(solution)/shard_map/output_swap/ppermute | solution.py:33
  178.7 1.9 collective-permute-start.26
  180.7 2.4 %place.1 = (bf16[256,2048]{1,0:T(8,128)(2,1)}, bf16[256,2048]{1,0:T(8,128)(2,1)}) custom-call(s32[5]{0:T(128)S(1)} %stack.62.where, bf16[2,256,1024]{2,1,0:T(8,128)(2,1)S(1)} %get-tuple-element.88.own, bf16[2,256,1024]{2,1,0:T(8,128)(2,1)S(1)} %collective-permute-done.24.far), custom_call_target="tpu_custom_call" | custom-call | bytes 4194304 | tf_op jit(solution)/shard_map/place/pallas_call | solution.py:86
  183.1 5.3 %collective-permute-done.26 = bf16[2,3,128,128]{3,2,1,0:T(8,128)(2,1)S(1)} collective-permute-done((bf16[2,3,128,128]{3,2,1,0:T(8,128)(2,1)S(1)}, bf16[2,3,128,128]{3,2,1,0:T(8,128)(2,1)S(1)}, u32[]{:S(2)}, u32[]{:S(2)}) %collective-permute-start.26) | collective-permute-done | bytes 196640 | tf_op jit(solution)/shard_map/grads_turn_1/ppermute | solution.py:37
  188.4 13.5 %collective-permute-done.25 = bf16[2,3,128,128]{3,2,1,0:T(8,128)(2,1)S(1)} collective-permute-done((bf16[2,3,128,128]{3,2,1,0:T(8,128)(2,1)S(1)}, bf16[2,3,128,128]{3,2,1,0:T(8,128)(2,1)S(1)}, u32[]{:S(2)}, u32[]{:S(2)}) %collective-permute-start.25) | collective-permute-done | bytes 196640 | tf_op jit(solution)/shard_map/grads_turn_1/ppermute | solution.py:37
  202.1 3.2 %collective-permute-start.27 = (f32[3,128,128]{2,1,0:T(8,128)S(1)}, f32[3,128,128]{2,1,0:T(8,128)S(1)}, u32[]{:S(2)}, u32[]{:S(2)}) collective-permute-start(f32[3,128,128]{2,1,0:T(8,128)S(1)} %get-tuple-element.94), channel_id=1, source_target_pairs={{0,1},{1,0},{2,3},{3,2},{4,5},{5,4},{6,7},{7,6},{8,9},{9,8},{10,11... | collective-permute-start | bytes 589832 | tf_op jit(solution)/shard_map/grads_core/ppermute | solution.py:33
  205.3 1.1 collective-permute-done.27
  206.4 0.7 slice_bitcast_fusion.6
  (58 shorter events, 4.2 us)
Async XLA Ops:
  1.4 4.3 %collective-permute-start = (bf16[3,128,128]{2,1,0:T(8,128)(2,1)S(1)}, bf16[3,128,128]{2,1,0:T(8,128)(2,1)S(1)}, u32[]{:S(2)}, u32[]{:S(2)}) collective-permute-start(bf16[3,128,128]{2,1,0:T(8,128)(2,1)S(1)} %get-tuple-element.111), channel_id=1, source_target_pairs={{0,1},{1,0},{2,3},{3,2},{4,5},{5,4},{6,7},{7,6},{8,9},{9,8},{10,11... | collective-permute-start | bytes 294920 | tf_op jit(solution)/shard_map/weights_core/ppermute | solution.py:33
  7.1 1.2 copy-start
  9.5 34.4 %collective-permute-start.1 = (bf16[2,256,1024]{2,1,0:T(8,128)(2,1)S(1)}, bf16[2,256,1024]{2,1,0:T(8,128)(2,1)S(1)}, u32[]{:S(2)}, u32[]{:S(2)}) collective-permute-start(bf16[2,256,1024]{2,1,0:T(8,128)(2,1)S(1)} %get-tuple-element.54), channel_id=1, source_target_pairs={{0,16},{1,17},{2,18},{3,19},{4,20},{5,21},{6,22},{7,23},{8,24},{9,... | collective-permute-start | bytes 3145736 | tf_op jit(solution)/shard_map/input_swap/ppermute | solution.py:33
  10.8 11.5 %collective-permute-start.2 = (bf16[2,3,128,128]{3,2,1,0:T(8,128)(2,1)S(1)}, bf16[2,3,128,128]{3,2,1,0:T(8,128)(2,1)S(1)}, u32[]{:S(2)}, u32[]{:S(2)}) collective-permute-start(bf16[2,3,128,128]{3,2,1,0:T(8,128)(2,1)S(1)} %pad_maximum_fusion.3), channel_id=1, source_target_pairs={{0,0},{1,32},{2,64},{3,96},{4,4},{5,36},{6,68},{7,100},{8,8},{9,40... | collective-permute-start | bytes 589832 | tf_op jit(solution)/shard_map/weights_turn_0/ppermute | solution.py:33
  14.8 12.5 %collective-permute-start.3 = (bf16[2,3,128,128]{3,2,1,0:T(8,128)(2,1)S(1)}, bf16[2,3,128,128]{3,2,1,0:T(8,128)(2,1)S(1)}, u32[]{:S(2)}, u32[]{:S(2)}) collective-permute-start(bf16[2,3,128,128]{3,2,1,0:T(8,128)(2,1)S(1)} %pad_maximum_fusion.3), channel_id=1, source_target_pairs={{0,128},{1,160},{2,192},{3,224},{4,132},{5,164},{6,196},{7,228},{8... | collective-permute-start | bytes 589832 | tf_op jit(solution)/shard_map/weights_turn_0/ppermute | solution.py:33
  27.4 31.0 %collective-permute-start.6 = (bf16[2,2,3,128,128]{4,3,2,1,0:T(8,128)(2,1)S(1)}, bf16[2,2,3,128,128]{4,3,2,1,0:T(8,128)(2,1)S(1)}, u32[]{:S(2)}, u32[]{:S(2)}) collective-permute-start(bf16[2,2,3,128,128]{4,3,2,1,0:T(8,128)(2,1)S(1)} %pad_maximum_fusion.c0), channel_id=1, source_target_pairs={{0,12},{1,13},{2,14},{3,15},{4,0},{5,1},{6,2},{7,3},{8,4},{9,5},{1... | collective-permute-start | bytes 1179656 | tf_op jit(solution)/shard_map/weights_x_0/ppermute | solution.py:33
  29.9 28.5 %collective-permute-start.7 = (bf16[2,2,3,128,128]{4,3,2,1,0:T(8,128)(2,1)S(1)}, bf16[2,2,3,128,128]{4,3,2,1,0:T(8,128)(2,1)S(1)}, u32[]{:S(2)}, u32[]{:S(2)}) collective-permute-start(bf16[2,2,3,128,128]{4,3,2,1,0:T(8,128)(2,1)S(1)} %pad_maximum_fusion.c0), channel_id=1, source_target_pairs={{0,8},{1,9},{2,10},{3,11},{4,12},{5,13},{6,14},{7,15},{8,0},{9,1},... | collective-permute-start | bytes 1179656 | tf_op jit(solution)/shard_map/weights_x_0/ppermute | solution.py:33
  30.4 28.0 %collective-permute-start.8 = (bf16[2,2,3,128,128]{4,3,2,1,0:T(8,128)(2,1)S(1)}, bf16[2,2,3,128,128]{4,3,2,1,0:T(8,128)(2,1)S(1)}, u32[]{:S(2)}, u32[]{:S(2)}) collective-permute-start(bf16[2,2,3,128,128]{4,3,2,1,0:T(8,128)(2,1)S(1)} %pad_maximum_fusion.c0), channel_id=1, source_target_pairs={{0,4},{1,5},{2,6},{3,7},{4,8},{5,9},{6,10},{7,11},{8,12},{9,13},{1... | collective-permute-start | bytes 1179656 | tf_op jit(solution)/shard_map/weights_x_0/ppermute | solution.py:33
  43.9 10.2 %collective-permute-start.5 = (bf16[2,3,128,128]{3,2,1,0:T(8,128)(2,1)S(1)}, bf16[2,3,128,128]{3,2,1,0:T(8,128)(2,1)S(1)}, u32[]{:S(2)}, u32[]{:S(2)}) collective-permute-start(bf16[2,3,128,128]{3,2,1,0:T(8,128)(2,1)S(1)} %pad_maximum_fusion.3), channel_id=1, source_target_pairs={{0,192},{1,224},{2,128},{3,160},{4,196},{5,228},{6,132},{7,164},{8... | collective-permute-start | bytes 589832 | tf_op jit(solution)/shard_map/weights_turn_1/ppermute | solution.py:33
  45.8 12.5 %collective-permute-start.4 = (bf16[2,3,128,128]{3,2,1,0:T(8,128)(2,1)S(1)}, bf16[2,3,128,128]{3,2,1,0:T(8,128)(2,1)S(1)}, u32[]{:S(2)}, u32[]{:S(2)}) collective-permute-start(bf16[2,3,128,128]{3,2,1,0:T(8,128)(2,1)S(1)} %pad_maximum_fusion.3), channel_id=1, source_target_pairs={{0,64},{1,96},{2,0},{3,32},{4,68},{5,100},{6,4},{7,36},{8,72},{9,1... | collective-permute-start | bytes 589832 | tf_op jit(solution)/shard_map/weights_turn_1/ppermute | solution.py:33
  60.4 1.0 copy-start.3
  61.3 0.8 copy-start.7
  62.1 22.8 %all-to-all-start = ((bf16[8,64,768]{2,1,0:T(8,128)(2,1)}), bf16[8,64,768]{2,1,0:T(8,128)(2,1)}, u32[]{:S(2)}, u32[]{:S(2)}) async-start(bf16[8,64,768]{2,1,0:T(8,128)(2,1)} %bitcast.14), calls=%async_computation | async-start | bytes 1572864 | tf_op jit(solution)/shard_map/reduce_ring_0/all_to_all | solution.py:231
  72.6 19.0 %collective-permute-start.15 = (bf16[2,2,3,128,128]{4,3,2,1,0:T(8,128)(2,1)S(1)}, bf16[2,2,3,128,128]{4,3,2,1,0:T(8,128)(2,1)S(1)}, u32[]{:S(2)}, u32[]{:S(2)}) collective-permute-start(bf16[2,2,3,128,128]{4,3,2,1,0:T(8,128)(2,1)S(1)} %pad_maximum_fusion.1.c0), channel_id=1, source_target_pairs={{0,12},{1,13},{2,14},{3,15},{4,0},{5,1},{6,2},{7,3},{8,4},{9,5},{1... | collective-permute-start | bytes 1179656 | tf_op jit(solution)/shard_map/weights_x_1/ppermute | solution.py:33
  74.7 16.8 %collective-permute-start.16 = (bf16[2,2,3,128,128]{4,3,2,1,0:T(8,128)(2,1)S(1)}, bf16[2,2,3,128,128]{4,3,2,1,0:T(8,128)(2,1)S(1)}, u32[]{:S(2)}, u32[]{:S(2)}) collective-permute-start(bf16[2,2,3,128,128]{4,3,2,1,0:T(8,128)(2,1)S(1)} %pad_maximum_fusion.1.c0), channel_id=1, source_target_pairs={{0,8},{1,9},{2,10},{3,11},{4,12},{5,13},{6,14},{7,15},{8,0},{9,1},... | collective-permute-start | bytes 1179656 | tf_op jit(solution)/shard_map/weights_x_1/ppermute | solution.py:33
  75.8 20.0 %collective-permute-start.17 = (bf16[2,2,3,128,128]{4,3,2,1,0:T(8,128)(2,1)S(1)}, bf16[2,2,3,128,128]{4,3,2,1,0:T(8,128)(2,1)}, u32[]{:S(2)}, u32[]{:S(2)}) collective-permute-start(bf16[2,2,3,128,128]{4,3,2,1,0:T(8,128)(2,1)S(1)} %pad_maximum_fusion.1.c0), channel_id=1, source_target_pairs={{0,4},{1,5},{2,6},{3,7},{4,8},{5,9},{6,10},{7,11},{8,12},{9,13},{1... | collective-permute-start | bytes 1179656 | tf_op jit(solution)/shard_map/weights_x_1/ppermute | solution.py:33
  86.9 18.6 %collective-permute-start.11 = (bf16[64,768]{1,0:T(8,128)(2,1)}, bf16[64,768]{1,0:T(8,128)(2,1)S(1)}, u32[]{:S(2)}, u32[]{:S(2)}) collective-permute-start(bf16[64,768]{1,0:T(8,128)(2,1)} %pad_maximum_fusion.5), channel_id=1, source_target_pairs={{0,18},{1,19},{2,16},{3,17},{4,22},{5,23},{6,20},{7,21},{8,26},{9,... | collective-permute-start | bytes 294920 | tf_op jit(solution)/shard_map/gather_ring_0/ppermute | solution.py:33
  87.2 18.3 %collective-permute-start.10 = (bf16[64,768]{1,0:T(8,128)(2,1)}, bf16[64,768]{1,0:T(8,128)(2,1)}, u32[]{:S(2)}, u32[]{:S(2)}) collective-permute-start(bf16[64,768]{1,0:T(8,128)(2,1)} %pad_maximum_fusion.5), channel_id=1, source_target_pairs={{0,16},{1,17},{2,18},{3,19},{4,20},{5,21},{6,22},{7,23},{8,24},{9,... | collective-permute-start | bytes 294920 | tf_op jit(solution)/shard_map/gather_ring_0/ppermute | solution.py:33
  91.6 13.9 %collective-permute-start.9 = (bf16[64,768]{1,0:T(8,128)(2,1)}, bf16[64,768]{1,0:T(8,128)(2,1)}, u32[]{:S(2)}, u32[]{:S(2)}) collective-permute-start(bf16[64,768]{1,0:T(8,128)(2,1)} %pad_maximum_fusion.5), channel_id=1, source_target_pairs={{0,2},{1,3},{2,0},{3,1},{4,6},{5,7},{6,4},{7,5},{8,10},{9,11},{10,... | collective-permute-start | bytes 294920 | tf_op jit(solution)/shard_map/gather_ring_0/ppermute | solution.py:33
  98.8 1.0 copy-start.5
  99.8 0.8 copy-start.9
  100.5 17.2 %all-to-all-start.1 = ((bf16[8,64,768]{2,1,0:T(8,128)(2,1)}), bf16[8,64,768]{2,1,0:T(8,128)(2,1)S(1)}, u32[]{:S(2)}, u32[]{:S(2)}) async-start(bf16[8,64,768]{2,1,0:T(8,128)(2,1)} %bitcast.15), calls=%async_computation.1 | async-start | bytes 1572864 | tf_op jit(solution)/shard_map/reduce_ring_1/all_to_all | solution.py:231
  106.5 1.8 collective-permute-start.12
  110.2 0.9 copy-start.1
  111.1 0.7 copy-start.11
  111.8 0.8 copy-start.12
  112.6 0.9 copy-start.13
  118.9 16.6 %all-to-all-start.2 = ((bf16[8,64,768]{2,1,0:T(8,128)(2,1)}), bf16[8,64,768]{2,1,0:T(8,128)(2,1)S(1)}, u32[]{:S(2)}, u32[]{:S(2)}) async-start(bf16[8,64,768]{2,1,0:T(8,128)(2,1)} %broadcast_in_dim.3), calls=%async_computation.2 | async-start | bytes 1572864 | tf_op jit(solution)/shard_map/gather_ring_1/all_to_all | solution.py:252
  123.2 21.6 %collective-permute-start.13 = (bf16[2,2,3,128,128]{4,3,2,1,0:T(8,128)(2,1)}, bf16[2,2,3,128,128]{4,3,2,1,0:T(8,128)(2,1)}, u32[]{:S(2)}, u32[]{:S(2)}) collective-permute-start(bf16[2,2,3,128,128]{4,3,2,1,0:T(8,128)(2,1)} %copy-done.12), channel_id=1, source_target_pairs={{0,4},{1,5},{2,6},{3,7},{4,8},{5,9},{6,10},{7,11},{8,12},{9,13},{1... | collective-permute-start | bytes 1179656 | tf_op jit(solution)/shard_map/grads_x_0/ppermute | solution.py:33
  123.2 21.6 %collective-permute-start.14 = (bf16[2,2,3,128,128]{4,3,2,1,0:T(8,128)(2,1)}, bf16[2,2,3,128,128]{4,3,2,1,0:T(8,128)(2,1)}, u32[]{:S(2)}, u32[]{:S(2)}) collective-permute-start(bf16[2,2,3,128,128]{4,3,2,1,0:T(8,128)(2,1)} %copy-done.11), channel_id=1, source_target_pairs={{0,12},{1,13},{2,14},{3,15},{4,0},{5,1},{6,2},{7,3},{8,4},{9,5},{1... | collective-permute-start | bytes 1179656 | tf_op jit(solution)/shard_map/grads_x_0/ppermute | solution.py:33
  125.9 23.5 %collective-permute-start.18 = (bf16[2,2,3,128,128]{4,3,2,1,0:T(8,128)(2,1)S(1)}, bf16[2,2,3,128,128]{4,3,2,1,0:T(8,128)(2,1)}, u32[]{:S(2)}, u32[]{:S(2)}) collective-permute-start(bf16[2,2,3,128,128]{4,3,2,1,0:T(8,128)(2,1)S(1)} %get-tuple-element.81), channel_id=1, source_target_pairs={{0,8},{1,9},{2,10},{3,11},{4,12},{5,13},{6,14},{7,15},{8,0},{9,1},... | collective-permute-start | bytes 1179656 | tf_op jit(solution)/shard_map/grads_x_0/ppermute | solution.py:33
  135.5 13.8 %copy-start.2 = (f32[2,2,3,128,128]{4,3,2,1,0:T(8,128)S(1)}, f32[2,2,3,128,128]{4,3,2,1,0:T(8,128)}, u32[]{:S(2)}) copy-start(f32[2,2,3,128,128]{4,3,2,1,0:T(8,128)} %copy-done.1) | copy-start | bytes 2359300
  136.8 1.2 copy-start.4
  138.0 1.2 copy-start.6
  139.3 1.0 copy-start.8
  140.3 1.0 copy-start.10
  141.3 1.1 copy-start.14
  144.8 33.8 %collective-permute-start.24 = (bf16[2,256,1024]{2,1,0:T(8,128)(2,1)S(1)}, bf16[2,256,1024]{2,1,0:T(8,128)(2,1)S(1)}, u32[]{:S(2)}, u32[]{:S(2)}) collective-permute-start(bf16[2,256,1024]{2,1,0:T(8,128)(2,1)S(1)} %get-tuple-element.86), channel_id=1, source_target_pairs={{0,16},{1,17},{2,18},{3,19},{4,20},{5,21},{6,22},{7,23},{8,24},{9,... | collective-permute-start | bytes 3145736 | tf_op jit(solution)/shard_map/output_swap/ppermute | solution.py:33
  145.3 10.9 %collective-permute-start.23 = (bf16[2,2,3,128,128]{4,3,2,1,0:T(8,128)(2,1)S(1)}, bf16[2,2,3,128,128]{4,3,2,1,0:T(8,128)(2,1)S(1)}, u32[]{:S(2)}, u32[]{:S(2)}) collective-permute-start(bf16[2,2,3,128,128]{4,3,2,1,0:T(8,128)(2,1)S(1)} %get-tuple-element.85), channel_id=1, source_target_pairs={{0,8},{1,9},{2,10},{3,11},{4,12},{5,13},{6,14},{7,15},{8,0},{9,1},... | collective-permute-start | bytes 1179656 | tf_op jit(solution)/shard_map/grads_x_1/ppermute | solution.py:33
  146.2 20.6 %collective-permute-start.22 = (bf16[2,2,3,128,128]{4,3,2,1,0:T(8,128)(2,1)S(1)}, bf16[2,2,3,128,128]{4,3,2,1,0:T(8,128)(2,1)S(1)}, u32[]{:S(2)}, u32[]{:S(2)}) collective-permute-start(bf16[2,2,3,128,128]{4,3,2,1,0:T(8,128)(2,1)S(1)} %get-tuple-element.84), channel_id=1, source_target_pairs={{0,12},{1,13},{2,14},{3,15},{4,0},{5,1},{6,2},{7,3},{8,4},{9,5},{1... | collective-permute-start | bytes 1179656 | tf_op jit(solution)/shard_map/grads_x_1/ppermute | solution.py:33
  148.8 18.1 %collective-permute-start.21 = (bf16[2,2,3,128,128]{4,3,2,1,0:T(8,128)(2,1)S(1)}, bf16[2,2,3,128,128]{4,3,2,1,0:T(8,128)(2,1)S(1)}, u32[]{:S(2)}, u32[]{:S(2)}) collective-permute-start(bf16[2,2,3,128,128]{4,3,2,1,0:T(8,128)(2,1)S(1)} %get-tuple-element.83), channel_id=1, source_target_pairs={{0,4},{1,5},{2,6},{3,7},{4,8},{5,9},{6,10},{7,11},{8,12},{9,13},{1... | collective-permute-start | bytes 1179656 | tf_op jit(solution)/shard_map/grads_x_1/ppermute | solution.py:33
  150.8 32.3 %collective-permute-start.20 = (bf16[2,3,128,128]{3,2,1,0:T(8,128)(2,1)S(1)}, bf16[2,3,128,128]{3,2,1,0:T(8,128)(2,1)S(1)}, u32[]{:S(2)}, u32[]{:S(2)}) collective-permute-start(bf16[2,3,128,128]{3,2,1,0:T(8,128)(2,1)S(1)} %get-tuple-element.98), channel_id=1, source_target_pairs={{128,0},{160,1},{192,2},{224,3},{132,4},{164,5},{196,6},{228,7},{1... | collective-permute-start | bytes 589832 | tf_op jit(solution)/shard_map/grads_turn_0/ppermute | solution.py:37
  156.3 26.8 %collective-permute-start.19 = (bf16[2,3,128,128]{3,2,1,0:T(8,128)(2,1)S(1)}, bf16[2,3,128,128]{3,2,1,0:T(8,128)(2,1)S(1)}, u32[]{:S(2)}, u32[]{:S(2)}) collective-permute-start(bf16[2,3,128,128]{3,2,1,0:T(8,128)(2,1)S(1)} %get-tuple-element.97), channel_id=1, source_target_pairs={{0,0},{32,1},{64,2},{96,3},{4,4},{36,5},{68,6},{100,7},{8,8},{40,9... | collective-permute-start | bytes 589832 | tf_op jit(solution)/shard_map/grads_turn_0/ppermute | solution.py:37
  178.7 9.7 %collective-permute-start.26 = (bf16[2,3,128,128]{3,2,1,0:T(8,128)(2,1)S(1)}, bf16[2,3,128,128]{3,2,1,0:T(8,128)(2,1)S(1)}, u32[]{:S(2)}, u32[]{:S(2)}) collective-permute-start(bf16[2,3,128,128]{3,2,1,0:T(8,128)(2,1)S(1)} %get-tuple-element.100), channel_id=1, source_target_pairs={{192,0},{224,1},{128,2},{160,3},{196,4},{228,5},{132,6},{164,7},{2... | collective-permute-start | bytes 589832 | tf_op jit(solution)/shard_map/grads_turn_1/ppermute | solution.py:37
  180.6 21.3 %collective-permute-start.25 = (bf16[2,3,128,128]{3,2,1,0:T(8,128)(2,1)S(1)}, bf16[2,3,128,128]{3,2,1,0:T(8,128)(2,1)S(1)}, u32[]{:S(2)}, u32[]{:S(2)}) collective-permute-start(bf16[2,3,128,128]{3,2,1,0:T(8,128)(2,1)S(1)} %get-tuple-element.99), channel_id=1, source_target_pairs={{64,0},{96,1},{0,2},{32,3},{68,4},{100,5},{4,6},{36,7},{72,8},{104... | collective-permute-start | bytes 589832 | tf_op jit(solution)/shard_map/grads_turn_1/ppermute | solution.py:37
  202.1 4.3 %collective-permute-start.27 = (f32[3,128,128]{2,1,0:T(8,128)S(1)}, f32[3,128,128]{2,1,0:T(8,128)S(1)}, u32[]{:S(2)}, u32[]{:S(2)}) collective-permute-start(f32[3,128,128]{2,1,0:T(8,128)S(1)} %get-tuple-element.94), channel_id=1, source_target_pairs={{0,1},{1,0},{2,3},{3,2},{4,5},{5,4},{6,7},{7,6},{8,9},{9,8},{10,11... | collective-permute-start | bytes 589832 | tf_op jit(solution)/shard_map/grads_core/ppermute | solution.py:33

commit v3 on v1

--- a/solution.py
+++ b/solution.py
@@ -11,7 +11,7 @@
 AXES = ("dp", "tensor")
 BF = jnp.bfloat16
 F32 = jnp.float32
-VMEM_BYTES = 32 * 1024 * 1024
+VMEM_BYTES = 16 * 1024 * 1024
 
 
 def index_of(z, h, x, l, c):
@@ -60,7 +60,8 @@
     return move
 
 
-PARTNERS = [[(z * NH + h) * NX + x for h in range(NH)] for z in range(NZ) for x in range(NX)]
+def after(value, *others):
+    return lax.optimization_barrier((value, *others))[0]
 
 
 def nn(a, b):
@@ -75,38 +76,18 @@
     return lax.dot_general(a, b, (((1,), (1,)), ((), ())), preferred_element_type=F32)
 
 
-def call(body, shapes, args, flops=0):
+def call(body, shapes, args, flops=0, where=None):
     moved = sum(a.size * a.dtype.itemsize for a in args)
     moved += sum(functools.reduce(lambda p, q: p * q, s, 1) * jnp.dtype(d).itemsize for s, d in shapes)
+    scalars = [] if where is None else [where]
     return pl.pallas_call(
         body,
         out_shape=[jax.ShapeDtypeStruct(s, d) for s, d in shapes],
-        in_specs=[pl.BlockSpec(memory_space=pltpu.VMEM)] * len(args),
+        in_specs=[pl.BlockSpec(memory_space=pltpu.SMEM)] * len(scalars) + [pl.BlockSpec(memory_space=pltpu.VMEM)] * len(args),
         out_specs=[pl.BlockSpec(memory_space=pltpu.VMEM)] * len(shapes),
         compiler_params=pltpu.CompilerParams(vmem_limit_bytes=VMEM_BYTES),
         cost_estimate=pl.CostEstimate(flops=flops, bytes_accessed=moved, transcendentals=0),
-    )(*args)
-
-
-def call_at(body, where, args, shapes, flops=0):
-    def at(block, shifted):
-        zeros = (0,) * (len(block) - 1)
-        return pl.BlockSpec(block, lambda i, where: (*zeros, where[0] if shifted else 0))
-
-    moved = sum(functools.reduce(lambda p, q: p * q, b, 1) * 2 for _, b, _ in args)
-    moved += sum(functools.reduce(lambda p, q: p * q, s, 1) * jnp.dtype(d).itemsize for s, d in shapes)
-    return pl.pallas_call(
-        body,
-        grid_spec=pltpu.PrefetchScalarGridSpec(
-            num_scalar_prefetch=1,
-            grid=(1,),
-            in_specs=[at(block, shifted) for _, block, shifted in args],
-            out_specs=[at(shape, False) for shape, _ in shapes],
-        ),
-        out_shape=[jax.ShapeDtypeStruct(s, d) for s, d in shapes],
-        compiler_params=pltpu.CompilerParams(vmem_limit_bytes=VMEM_BYTES),
-        cost_estimate=pl.CostEstimate(flops=flops, bytes_accessed=moved, transcendentals=0),
-    )(where, *[a for a, _, _ in args])
+    )(*scalars, *args)
 
 
 def blocks_of(where, fb, sub):
@@ -134,36 +115,39 @@
             own[m, to_row : to_row + sub, to_lane : to_lane + fb] = source[pl.ds(row, sub), pl.ds(lanes(h), fb)]
 
 
-def place_body(where, own, both, layer_out, token_grad):
+def place_body(where, own, far, layer_out, token_grad):
     sub = own.shape[1] // 4
     fb = own.shape[2] // 8
     h = where[1]
     for m, out in enumerate((layer_out, token_grad)):
         for at_row, at_lane, row, lanes in blocks_of(where, fb, sub):
             out[pl.ds(row, sub), pl.ds(lanes(h), fb)] = own[m, at_row : at_row + sub, at_lane : at_lane + fb]
-            out[pl.ds(row, sub), pl.ds(lanes(1 - h), fb)] = both[1 - h, m, at_row : at_row + sub, at_lane : at_lane + fb]
-
-
-def forward_body(where, own, both, *refs):
-    columns, (gu, dn, tok, cot, keep, away) = refs[:8], refs[8:]
-    fb = columns[0].shape[-1]
+            out[pl.ds(row, sub), pl.ds(lanes(1 - h), fb)] = far[m, at_row : at_row + sub, at_lane : at_lane + fb]
+
+
+def join_body(own, far, tok, cot):
     tb = own.shape[1]
     half = tb // 2
-    h = where[1]
     for m, full in enumerate((tok, cot)):
         for oc in range(2):
             full[oc * tb : oc * tb + half, :] = own[m, oc * half : (oc + 1) * half, :]
-            full[oc * tb + half : (oc + 1) * tb, :] = both[1 - h, m, oc * half : (oc + 1) * half, :]
+            full[oc * tb + half : (oc + 1) * tb, :] = far[m, oc * half : (oc + 1) * half, :]
+
+
+def forward_body(tok, cot, *refs):
+    columns, (gu, dn, keep, away) = refs[:4], refs[4:]
+    tb = keep.shape[0]
+    fb = columns[0].shape[-1]
     for f in range(2):
         for j in range(NX):
-            column = columns[f * NX + j]
+            column = columns[j]
             at = (f * NX + j) * fb
             for g in range(2):
                 for e in range(2):
                     unit = (g * 2 + e) * fb
-                    gu[at : at + fb, unit : unit + fb] = column[g, e, 0]
-                    gu[at : at + fb, 4 * fb + unit : 4 * fb + unit + fb] = column[g, e, 1]
-                    dn[unit : unit + fb, at : at + fb] = column[g, e, 2]
+                    gu[at : at + fb, unit : unit + fb] = column[f * 2 + g, e, 0]
+                    gu[at : at + fb, 4 * fb + unit : 4 * fb + unit + fb] = column[f * 2 + g, e, 1]
+                    dn[unit : unit + fb, at : at + fb] = column[f * 2 + g, e, 2]
     wide = gu.shape[1]
     away[:, :wide] = nn(tok[tb:, :], gu[...]).astype(BF)
     away[:, wide:] = nt(cot[tb:, :], dn[...]).astype(BF)
@@ -208,36 +192,31 @@
     quarter = cotangent.shape[1]
     wide, hid = 8 * fb, 4 * fb
 
-    own, oth = call_at(
-        pick_body,
-        where,
-        [(tokens, (tb, quarter), True), (cotangent, (tb, quarter), False)],
-        [((2, tb, wide), BF)] * 2,
-    )
-    both = lax.all_gather(oth, "dp", axis_index_groups=PARTNERS)
-
-    block = jnp.stack([gate_weight, up_weight, down_weight])
-    pair = jnp.stack([block, send(block, swap_core)])
-
-    def column_of(f, value):
-        return [send(value, turn(f, g)) for g in range(2)]
-
-    def along(column):
-        return [column] + [send(column, along_x(-j)) for j in range(1, NX)]
-
-    near = column_of(0, pair)
-    pair, *near = lax.optimization_barrier((pair, *near))
-    near = along(jnp.stack(near))
-    far = along(jnp.stack(column_of(1, pair)))
+    with jax.named_scope("weights_core"):
+        block = jnp.stack([gate_weight, up_weight, down_weight])
+        pair = jnp.stack([block, send(block, swap_core)])
+
+    with jax.named_scope("weights_turn"):
+        column = jnp.stack([send(pair, turn(f, g)) for f in range(2) for g in range(2)])
+    where, tokens, cotangent, _ = lax.optimization_barrier((where, tokens, cotangent, pair))
+    with jax.named_scope("weights_x"):
+        columns = [column] + [send(column, along_x(-j)) for j in range(1, NX)]
+    with jax.named_scope("pick"):
+        picked = lax.dynamic_slice(tokens, (0, t * quarter), (tb, quarter))
+        own, oth = call(pick_body, [((2, tb, wide), BF)] * 2, [picked, cotangent], 0, where)
+    with jax.named_scope("input_swap"):
+        swapped = send(after(oth, column), swap_hi)
+    with jax.named_scope("join"):
+        tok, cot = call(join_body, [((2 * tb, wide), BF)] * 2, [own, swapped])
 
     product = 2 * 2 * tb * wide * hid
-    gu, dn, tok, cot, keep, away = call_at(
-        forward_body,
-        where,
-        [(a, a.shape, False) for a in (own, both, *near, *far)],
-        [((wide, 2 * hid), BF), ((hid, wide), BF), ((2 * tb, wide), BF), ((2 * tb, wide), BF), ((tb, 3 * hid), F32), ((tb, 3 * hid), BF)],
-        3 * product,
-    )
+    with jax.named_scope("forward"):
+        gu, dn, keep, away = call(
+            forward_body,
+            [((wide, 2 * hid), BF), ((hid, wide), BF), ((tb, 3 * hid), F32), ((tb, 3 * hid), BF)],
+            [tok, cot, *columns],
+            3 * product,
+        )
     part = keep + send(away, swap_core).astype(F32)
     pre = part[:sub]
     for k in range(1, 4):
@@ -264,28 +243,29 @@
         return total.astype(BF)
 
     def returned(f, total):
-        return [send_back(total[g], turn(f, g)) for g in range(2)]
-
-    p1, p3, p2, p0 = pieces_of(0)
-    q1, q3, q2, q0 = pieces_of(1)
-    p1, p3, p2 = send(p1, along_x(1)), send(p3, along_x(3)), send(p2, along_x(2))
-    p1, p3, q1, q3, q2 = lax.optimization_barrier((p1, p3, q1, q3, q2))
+        with jax.named_scope(f"grads_turn_{f}"):
+            return [send_back(total[g], turn(f, g)) for g in range(2)]
+
+    with jax.named_scope("grads"):
+        p1, p3, p2, p0 = pieces_of(0)
+        q1, q3, q2, q0 = pieces_of(1)
+    with jax.named_scope("grads_x_0"):
+        p1, p3, p2 = send(p1, along_x(1)), send(p3, along_x(3)), send(p2, along_x(2))
+    with jax.named_scope("outputs"):
+        own, oth = call(output_body, [((2, tb, wide), BF)] * 2, [*terms, gu, dn], 3 * product)
+    with jax.named_scope("output_swap"):
+        swapped = send(oth, swap_hi)
+    with jax.named_scope("place"):
+        layer_out, token_grad = call(place_body, [((tb, quarter), BF)] * 2, [own, swapped], 0, where)
+    p1, p3, q1, q3, q2, oth = lax.optimization_barrier((p1, p3, q1, q3, q2, oth))
+    with jax.named_scope("grads_x_1"):
+        q1, q3, q2 = send(q1, along_x(1)), send(q3, along_x(3)), send(q2, along_x(2))
     back = returned(0, summed((p1, p3, p2), p0))
-    q1, q3, q2 = send(q1, along_x(1)), send(q3, along_x(3)), send(q2, along_x(2))
-
-    own, oth = call(output_body, [((2, tb, wide), BF)] * 2, [*terms, gu, dn], 3 * product)
-    both = lax.all_gather(oth, "dp", axis_index_groups=PARTNERS)
-    layer_out, token_grad = call_at(
-        place_body,
-        where,
-        [(own, own.shape, False), (both, both.shape, False)],
-        [((tb, quarter), BF)] * 2,
-    )
-
-    back = back + returned(1, summed((q1, q3, q2), q0))
+    back = back + returned(1, after(summed((q1, q3, q2), q0), swapped))
     total = sum(piece.astype(F32) for piece in back)
     kept, moved, layer_out, token_grad = lax.optimization_barrier((total[0], total[1], layer_out, token_grad))
-    total = kept + send(moved, swap_core)
+    with jax.named_scope("grads_core"):
+        total = kept + send(moved, swap_core)
     return layer_out, token_grad, total[0], total[1], total[2]
 
 

time: 207 us -> 182 us (0.88)
  the two profiles are of different devices: /device:TPU:1 before, /device:TPU:9 now
where the time goes in v3:
time: 182 us
  waiting for transfers between devices  112 us (62%)
  starting transfers between devices  55.1 us (30%)
  Pallas kernels  9.89 us (5%)
  local copies, waits for them, and re-layouts  2.11 us (1%)
  other arithmetic  2.09 us (1%)
    ppermute x25, waiting for transfers between devices, send(): return lax.ppermute(value, AXES, pairs_of(move))  88.6 us
    ppermute x25, starting transfers between devices, send(): return lax.ppermute(value, AXES, pairs_of(move))  37.3 us
    ppermute x4, waiting for transfers between devices, send_back(): return lax.ppermute(value, AXES, [(b, a) for a, b in pairs_of(move)])  23.4 us
    ppermute x4, starting transfers between devices, send_back(): return lax.ppermute(value, AXES, [(b, a) for a, b in pairs_of(move)])  17.8 us
    pallas_call x7, Pallas kernels, call(): pl.pallas_call(body, out_shape=[jax.ShapeDtypeStruct(s, d) for s, d in sh...  9.89 us
  transfers between devices with their start and end apart: 29, of which 18 were waited for; matrix products, arithmetic and copies ran while one was open for 1% of the time, Pallas kernels for 4%

profile of v3, /device:TPU:9, one launch (start us, length us, event | category | flops | bytes accessed | tf_op | source)
XLA Modules:
  0.0 182.1 jit_solution(7147194679684647103)
XLA Ops:
  0.6 0.9 fusion.3
  1.5 0.8 collective-permute-start
  2.3 0.1 pad_add_fusion.where
  2.4 0.9 collective-permute-done
  3.3 8.5 %collective-permute-start.4 = (bf16[2,3,128,128]{3,2,1,0:T(8,128)(2,1)S(1)}, bf16[2,3,128,128]{3,2,1,0:T(8,128)(2,1)S(1)}, u32[]{:S(2)}, u32[]{:S(2)}) collective-permute-start(bf16[2,3,128,128]{3,2,1,0:T(8,128)(2,1)S(1)} %pad_maximum_fusion.2), channel_id=1, source_target_pairs={{0,192},{1,224},{2,128},{3,160},{4,196},{5,228},{6,132},{7,164},{8... | collective-permute-start | bytes 589832 | tf_op jit(solution)/shard_map/weights_turn/ppermute | solution.py:33
  11.8 0.1 collective-permute-start.3
  11.9 1.6 collective-permute-start.2
  13.4 3.9 %collective-permute-start.1 = (bf16[2,3,128,128]{3,2,1,0:T(8,128)(2,1)S(1)}, bf16[2,3,128,128]{3,2,1,0:T(8,128)(2,1)S(1)}, u32[]{:S(2)}, u32[]{:S(2)}) collective-permute-start(bf16[2,3,128,128]{3,2,1,0:T(8,128)(2,1)S(1)} %pad_maximum_fusion.2), channel_id=1, source_target_pairs={{0,0},{1,32},{2,64},{3,96},{4,4},{5,36},{6,68},{7,100},{8,8},{9,40... | collective-permute-start | bytes 589832 | tf_op jit(solution)/shard_map/weights_turn/ppermute | solution.py:33
  17.3 1.3 constant_dynamic-slice_fusion.tok
  18.6 1.1 pick.1
  19.8 9.4 %collective-permute-done.3 = bf16[2,3,128,128]{3,2,1,0:T(8,128)(2,1)S(1)} collective-permute-done((bf16[2,3,128,128]{3,2,1,0:T(8,128)(2,1)S(1)}, bf16[2,3,128,128]{3,2,1,0:T(8,128)(2,1)S(1)}, u32[]{:S(2)}, u32[]{:S(2)}) %collective-permute-start.3) | collective-permute-done | bytes 196640 | tf_op jit(solution)/shard_map/weights_turn/ppermute | solution.py:33
  29.2 3.1 %collective-permute-done.1 = bf16[2,3,128,128]{3,2,1,0:T(8,128)(2,1)S(1)} collective-permute-done((bf16[2,3,128,128]{3,2,1,0:T(8,128)(2,1)S(1)}, bf16[2,3,128,128]{3,2,1,0:T(8,128)(2,1)S(1)}, u32[]{:S(2)}, u32[]{:S(2)}) %collective-permute-start.1) | collective-permute-done | bytes 196640 | tf_op jit(solution)/shard_map/weights_turn/ppermute | solution.py:33
  32.3 0.1 pad_maximum_fusion.refs_0_
  32.4 2.2 %collective-permute-start.5 = (bf16[2,256,1024]{2,1,0:T(8,128)(2,1)S(1)}, bf16[2,256,1024]{2,1,0:T(8,128)(2,1)S(1)}, u32[]{:S(2)}, u32[]{:S(2)}) collective-permute-start(bf16[2,256,1024]{2,1,0:T(8,128)(2,1)S(1)} %get-tuple-element.44), channel_id=1, source_target_pairs={{0,16},{1,17},{2,18},{3,19},{4,20},{5,21},{6,22},{7,23},{8,24},{9,... | collective-permute-start | bytes 3145736 | tf_op jit(solution)/shard_map/input_swap/ppermute | solution.py:33
  34.7 2.5 %collective-permute-start.6 = (bf16[4,2,3,128,128]{4,3,2,1,0:T(8,128)(2,1)S(1)}, bf16[4,2,3,128,128]{4,3,2,1,0:T(8,128)(2,1)S(1)}, u32[]{:S(2)}, u32[]{:S(2)}) collective-permute-start(bf16[4,2,3,128,128]{4,3,2,1,0:T(8,128)(2,1)S(1)} %pad_maximum_fusion.refs_0_), channel_id=1, source_target_pairs={{0,12},{1,13},{2,14},{3,15},{4,0},{5,1},{6,2},{7,3},{8,4},{9,5},{1... | collective-permute-start | bytes 2359304 | tf_op jit(solution)/shard_map/weights_x/ppermute | solution.py:33
  37.1 0.5 collective-permute-start.7
  37.7 0.6 collective-permute-start.8
  38.3 20.5 %collective-permute-done.5.far = bf16[2,256,1024]{2,1,0:T(8,128)(2,1)S(1)} collective-permute-done((bf16[2,256,1024]{2,1,0:T(8,128)(2,1)S(1)}, bf16[2,256,1024]{2,1,0:T(8,128)(2,1)S(1)}, u32[]{:S(2)}, u32[]{:S(2)}) %collective-permute-start.5) | collective-permute-done | bytes 1048608 | tf_op jit(solution)/shard_map/input_swap/ppermute | solution.py:33
  58.7 0.1 join.1
  58.9 11.9 %collective-permute-done.6.refs_1_ = bf16[4,2,3,128,128]{4,3,2,1,0:T(8,128)(2,1)S(1)} collective-permute-done((bf16[4,2,3,128,128]{4,3,2,1,0:T(8,128)(2,1)S(1)}, bf16[4,2,3,128,128]{4,3,2,1,0:T(8,128)(2,1)S(1)}, u32[]{:S(2)}, u32[]{:S(2)}) %collective-permute-start.6) | collective-permute-done | bytes 786464 | tf_op jit(solution)/shard_map/weights_x/ppermute | solution.py:33
  70.8 4.2 %collective-permute-done.8.refs_3_ = bf16[4,2,3,128,128]{4,3,2,1,0:T(8,128)(2,1)S(1)} collective-permute-done((bf16[4,2,3,128,128]{4,3,2,1,0:T(8,128)(2,1)S(1)}, bf16[4,2,3,128,128]{4,3,2,1,0:T(8,128)(2,1)S(1)}, u32[]{:S(2)}, u32[]{:S(2)}) %collective-permute-start.8) | collective-permute-done | bytes 786464 | tf_op jit(solution)/shard_map/weights_x/ppermute | solution.py:33
  75.0 1.9 %forward.1 = (bf16[1024,1024]{1,0:T(8,128)(2,1)S(1)}, bf16[512,1024]{1,0:T(8,128)(2,1)S(1)}, f32[256,1536]{1,0:T(8,128)S(1)}, bf16[256,1536]{1,0:T(8,128)(2,1)S(1)}) custom-call(bf16[512,1024]{1,0:T(8,128)(2,1)S(1)} %get-tuple-element.45.tok, bf16[512,1024]{1,0:T(8,128)(2,1)S(1)} %get-tuple-element.46.cot, ...), custom_call_target="tpu_custom_call" | custom-call | flops 1610612736 | bytes 10747904 | tf_op jit(solution)/shard_map/forward/pallas_call | solution.py:83
  76.8 0.6 collective-permute-start.9
  77.4 1.9 %collective-permute-done.9 = bf16[256,1536]{1,0:T(8,128)(2,1)S(1)} collective-permute-done((bf16[256,1536]{1,0:T(8,128)(2,1)S(1)}, bf16[256,1536]{1,0:T(8,128)(2,1)S(1)}, u32[]{:S(2)}, u32[]{:S(2)}) %collective-permute-start.9) | collective-permute-done | bytes 786464 | tf_op jit(solution)/shard_map/ppermute | solution.py:33
  79.3 0.3 fusion.4
  79.7 0.1 collective-permute-start.12
  79.8 0.9 collective-permute-start.11
  80.7 2.3 %collective-permute-start.10 = (bf16[64,1536]{1,0:T(8,128)(2,1)S(1)}, bf16[64,1536]{1,0:T(8,128)(2,1)S(1)}, u32[]{:S(2)}, u32[]{:S(2)}) collective-permute-start(bf16[64,1536]{1,0:T(8,128)(2,1)S(1)} %get-tuple-element.75), channel_id=1, source_target_pairs={{0,2},{1,3},{2,0},{3,1},{4,6},{5,7},{6,4},{7,5},{8,10},{9,11},{10,... | collective-permute-start | bytes 589832 | tf_op jit(solution)/shard_map/ppermute | solution.py:33
  83.0 7.1 %collective-permute-done.12 = bf16[64,1536]{1,0:T(8,128)(2,1)S(1)} collective-permute-done((bf16[64,1536]{1,0:T(8,128)(2,1)S(1)}, bf16[64,1536]{1,0:T(8,128)(2,1)S(1)}, u32[]{:S(2)}, u32[]{:S(2)}) %collective-permute-start.12) | collective-permute-done | bytes 196640 | tf_op jit(solution)/shard_map/ppermute | solution.py:33
  90.1 1.6 collective-permute-done.10
  91.6 0.1 fusion.1
  91.7 0.1 multiply_convert_fusion.2
  91.8 0.5 collective-permute-start.15
  92.3 0.8 collective-permute-start.14
  93.1 2.1 %collective-permute-start.13 = (bf16[64,1536]{1,0:T(8,128)(2,1)S(1)}, bf16[64,1536]{1,0:T(8,128)(2,1)S(1)}, u32[]{:S(2)}, u32[]{:S(2)}) collective-permute-start(bf16[64,1536]{1,0:T(8,128)(2,1)S(1)} %pad_maximum_fusion.3), channel_id=1, source_target_pairs={{0,2},{1,3},{2,0},{3,1},{4,6},{5,7},{6,4},{7,5},{8,10},{9,11},{10,... | collective-permute-start | bytes 589832 | tf_op jit(solution)/shard_map/ppermute | solution.py:33
  95.2 4.2 %collective-permute-done.15 = bf16[64,1536]{1,0:T(8,128)(2,1)S(1)} collective-permute-done((bf16[64,1536]{1,0:T(8,128)(2,1)S(1)}, bf16[64,1536]{1,0:T(8,128)(2,1)S(1)}, u32[]{:S(2)}, u32[]{:S(2)}) %collective-permute-start.15) | collective-permute-done | bytes 196640 | tf_op jit(solution)/shard_map/ppermute | solution.py:33
  99.4 3.3 %collective-permute-done.13 = bf16[64,1536]{1,0:T(8,128)(2,1)S(1)} collective-permute-done((bf16[64,1536]{1,0:T(8,128)(2,1)S(1)}, bf16[64,1536]{1,0:T(8,128)(2,1)S(1)}, u32[]{:S(2)}, u32[]{:S(2)}) %collective-permute-start.13) | collective-permute-done | bytes 196640 | tf_op jit(solution)/shard_map/ppermute | solution.py:33
  102.7 0.1 pad_maximum_fusion.1.da
  102.7 2.7 %collective-permute-start.16 = (bf16[256,1536]{1,0:T(8,128)(2,1)S(1)}, bf16[256,1536]{1,0:T(8,128)(2,1)S(1)}, u32[]{:S(2)}, u32[]{:S(2)}) collective-permute-start(bf16[256,1536]{1,0:T(8,128)(2,1)S(1)} %pad_maximum_fusion.1.da), channel_id=1, source_target_pairs={{0,1},{1,0},{2,3},{3,2},{4,5},{5,4},{6,7},{7,6},{8,9},{9,8},{10,11... | collective-permute-start | bytes 2359304 | tf_op jit(solution)/shard_map/ppermute | solution.py:33
  105.4 1.9 %collective-permute-done.16.dc = bf16[256,1536]{1,0:T(8,128)(2,1)S(1)} collective-permute-done((bf16[256,1536]{1,0:T(8,128)(2,1)S(1)}, bf16[256,1536]{1,0:T(8,128)(2,1)S(1)}, u32[]{:S(2)}, u32[]{:S(2)}) %collective-permute-start.16) | collective-permute-done | bytes 786464 | tf_op jit(solution)/shard_map/ppermute | solution.py:33
  107.4 1.3 grads.2
  108.6 0.1 collective-permute-start.17
  108.7 2.7 %collective-permute-start.18 = (bf16[2,2,3,128,128]{4,3,2,1,0:T(8,128)(2,1)S(1)}, bf16[2,2,3,128,128]{4,3,2,1,0:T(8,128)(2,1)S(1)}, u32[]{:S(2)}, u32[]{:S(2)}) collective-permute-start(bf16[2,2,3,128,128]{4,3,2,1,0:T(8,128)(2,1)S(1)} %get-tuple-element.51), channel_id=1, source_target_pairs={{0,12},{1,13},{2,14},{3,15},{4,0},{5,1},{6,2},{7,3},{8,4},{9,5},{1... | collective-permute-start | bytes 1179656 | tf_op jit(solution)/shard_map/grads_x_0/ppermute | solution.py:33
  111.4 1.8 outputs.1
  113.2 0.9 collective-permute-start.25
  114.1 1.3 grads.3
  115.4 13.3 %collective-permute-done.17 = bf16[2,2,3,128,128]{4,3,2,1,0:T(8,128)(2,1)S(1)} collective-permute-done((bf16[2,2,3,128,128]{4,3,2,1,0:T(8,128)(2,1)S(1)}, bf16[2,2,3,128,128]{4,3,2,1,0:T(8,128)(2,1)S(1)}, u32[]{:S(2)}, u32[]{:S(2)}) %collective-permute-start.17) | collective-permute-done | bytes 393248 | tf_op jit(solution)/shard_map/grads_x_0/ppermute | solution.py:33
  128.7 2.4 %collective-permute-start.23 = (bf16[2,2,3,128,128]{4,3,2,1,0:T(8,128)(2,1)S(1)}, bf16[2,2,3,128,128]{4,3,2,1,0:T(8,128)(2,1)S(1)}, u32[]{:S(2)}, u32[]{:S(2)}) collective-permute-start(bf16[2,2,3,128,128]{4,3,2,1,0:T(8,128)(2,1)S(1)} %get-tuple-element.63), channel_id=1, source_target_pairs={{0,12},{1,13},{2,14},{3,15},{4,0},{5,1},{6,2},{7,3},{8,4},{9,5},{1... | collective-permute-start | bytes 1179656 | tf_op jit(solution)/shard_map/grads_x_1/ppermute | solution.py:33
  131.0 0.6 collective-permute-start.22
  131.6 0.2 add_convert_fusion.1
  131.9 4.2 %collective-permute-start.21 = (bf16[2,3,128,128]{3,2,1,0:T(8,128)(2,1)S(1)}, bf16[2,3,128,128]{3,2,1,0:T(8,128)(2,1)S(1)}, u32[]{:S(2)}, u32[]{:S(2)}) collective-permute-start(bf16[2,3,128,128]{3,2,1,0:T(8,128)(2,1)S(1)} %get-tuple-element.81), channel_id=1, source_target_pairs={{64,0},{96,1},{0,2},{32,3},{68,4},{100,5},{4,6},{36,7},{72,8},{104... | collective-permute-start | bytes 589832 | tf_op jit(solution)/shard_map/grads_turn_0/ppermute | solution.py:37
  136.0 3.6 %collective-permute-done.24 = bf16[2,2,3,128,128]{4,3,2,1,0:T(8,128)(2,1)S(1)} collective-permute-done((bf16[2,2,3,128,128]{4,3,2,1,0:T(8,128)(2,1)S(1)}, bf16[2,2,3,128,128]{4,3,2,1,0:T(8,128)(2,1)S(1)}, u32[]{:S(2)}, u32[]{:S(2)}) %collective-permute-start.24) | collective-permute-done | bytes 393248 | tf_op jit(solution)/shard_map/grads_x_1/ppermute | solution.py:33
  139.6 9.6 %collective-permute-start.20 = (bf16[2,3,128,128]{3,2,1,0:T(8,128)(2,1)S(1)}, bf16[2,3,128,128]{3,2,1,0:T(8,128)(2,1)S(1)}, u32[]{:S(2)}, u32[]{:S(2)}) collective-permute-start(bf16[2,3,128,128]{3,2,1,0:T(8,128)(2,1)S(1)} %get-tuple-element.80), channel_id=1, source_target_pairs={{0,0},{32,1},{64,2},{96,3},{4,4},{36,5},{68,6},{100,7},{8,8},{40,9... | collective-permute-start | bytes 589832 | tf_op jit(solution)/shard_map/grads_turn_0/ppermute | solution.py:37
  149.2 0.4 collective-permute-done.22
  149.7 0.2 add_convert_fusion
  149.9 1.9 %collective-permute-start.27 = (bf16[2,3,128,128]{3,2,1,0:T(8,128)(2,1)S(1)}, bf16[2,3,128,128]{3,2,1,0:T(8,128)(2,1)S(1)}, u32[]{:S(2)}, u32[]{:S(2)}) collective-permute-start(bf16[2,3,128,128]{3,2,1,0:T(8,128)(2,1)S(1)} %get-tuple-element.83), channel_id=1, source_target_pairs={{192,0},{224,1},{128,2},{160,3},{196,4},{228,5},{132,6},{164,7},{2... | collective-permute-start | bytes 589832 | tf_op jit(solution)/shard_map/grads_turn_1/ppermute | solution.py:37
  151.8 2.1 %collective-permute-start.26 = (bf16[2,3,128,128]{3,2,1,0:T(8,128)(2,1)S(1)}, bf16[2,3,128,128]{3,2,1,0:T(8,128)(2,1)S(1)}, u32[]{:S(2)}, u32[]{:S(2)}) collective-permute-start(bf16[2,3,128,128]{3,2,1,0:T(8,128)(2,1)S(1)} %get-tuple-element.82), channel_id=1, source_target_pairs={{128,0},{160,1},{192,2},{224,3},{132,4},{164,5},{196,6},{228,7},{1... | collective-permute-start | bytes 589832 | tf_op jit(solution)/shard_map/grads_turn_1/ppermute | solution.py:37
  154.0 2.4 %place.1 = (bf16[256,2048]{1,0:T(8,128)(2,1)}, bf16[256,2048]{1,0:T(8,128)(2,1)}) custom-call(s32[4]{0:T(128)S(1)} %pad_add_fusion.where, bf16[2,256,1024]{2,1,0:T(8,128)(2,1)S(1)} %get-tuple-element.66.own, bf16[2,256,1024]{2,1,0:T(8,128)(2,1)S(1)} %collective-permute-done.25.far), custom_call_target="tpu_custom_call" | custom-call | bytes 4194304 | tf_op jit(solution)/shard_map/place/pallas_call | solution.py:83
  156.3 15.8 %collective-permute-done.27 = bf16[2,3,128,128]{3,2,1,0:T(8,128)(2,1)S(1)} collective-permute-done((bf16[2,3,128,128]{3,2,1,0:T(8,128)(2,1)S(1)}, bf16[2,3,128,128]{3,2,1,0:T(8,128)(2,1)S(1)}, u32[]{:S(2)}, u32[]{:S(2)}) %collective-permute-start.27) | collective-permute-done | bytes 196640 | tf_op jit(solution)/shard_map/grads_turn_1/ppermute | solution.py:37
  172.1 7.6 %collective-permute-done.26 = bf16[2,3,128,128]{3,2,1,0:T(8,128)(2,1)S(1)} collective-permute-done((bf16[2,3,128,128]{3,2,1,0:T(8,128)(2,1)S(1)}, bf16[2,3,128,128]{3,2,1,0:T(8,128)(2,1)S(1)}, u32[]{:S(2)}, u32[]{:S(2)}) %collective-permute-start.26) | collective-permute-done | bytes 196640 | tf_op jit(solution)/shard_map/grads_turn_1/ppermute | solution.py:37
  179.7 0.1 convert_add_fusion.1
  179.9 0.1 collective-permute-start.28
  180.0 1.4 collective-permute-done.28
  181.4 0.7 slice_bitcast_fusion.6
  (22 shorter events, 0.2 us)
Async XLA Ops:
  0.6 18.0 %copy-start = (bf16[256,2048]{1,0:T(8,128)(2,1)S(1)}, bf16[256,2048]{1,0:T(8,128)(2,1)}, u32[]{:S(2)}) copy-start(bf16[256,2048]{1,0:T(8,128)(2,1)} %cot) | copy-start | bytes 3145732
  1.5 1.7 collective-permute-start
  3.3 16.5 %collective-permute-start.4 = (bf16[2,3,128,128]{3,2,1,0:T(8,128)(2,1)S(1)}, bf16[2,3,128,128]{3,2,1,0:T(8,128)(2,1)S(1)}, u32[]{:S(2)}, u32[]{:S(2)}) collective-permute-start(bf16[2,3,128,128]{3,2,1,0:T(8,128)(2,1)S(1)} %pad_maximum_fusion.2), channel_id=1, source_target_pairs={{0,192},{1,224},{2,128},{3,160},{4,196},{5,228},{6,132},{7,164},{8... | collective-permute-start | bytes 589832 | tf_op jit(solution)/shard_map/weights_turn/ppermute | solution.py:33
  11.8 17.4 %collective-permute-start.3 = (bf16[2,3,128,128]{3,2,1,0:T(8,128)(2,1)S(1)}, bf16[2,3,128,128]{3,2,1,0:T(8,128)(2,1)S(1)}, u32[]{:S(2)}, u32[]{:S(2)}) collective-permute-start(bf16[2,3,128,128]{3,2,1,0:T(8,128)(2,1)S(1)} %pad_maximum_fusion.2), channel_id=1, source_target_pairs={{0,128},{1,160},{2,192},{3,224},{4,132},{5,164},{6,196},{7,228},{8... | collective-permute-start | bytes 589832 | tf_op jit(solution)/shard_map/weights_turn/ppermute | solution.py:33
  11.9 17.3 %collective-permute-start.2 = (bf16[2,3,128,128]{3,2,1,0:T(8,128)(2,1)S(1)}, bf16[2,3,128,128]{3,2,1,0:T(8,128)(2,1)S(1)}, u32[]{:S(2)}, u32[]{:S(2)}) collective-permute-start(bf16[2,3,128,128]{3,2,1,0:T(8,128)(2,1)S(1)} %pad_maximum_fusion.2), channel_id=1, source_target_pairs={{0,64},{1,96},{2,0},{3,32},{4,68},{5,100},{6,4},{7,36},{8,72},{9,1... | collective-permute-start | bytes 589832 | tf_op jit(solution)/shard_map/weights_turn/ppermute | solution.py:33
  13.4 18.9 %collective-permute-start.1 = (bf16[2,3,128,128]{3,2,1,0:T(8,128)(2,1)S(1)}, bf16[2,3,128,128]{3,2,1,0:T(8,128)(2,1)S(1)}, u32[]{:S(2)}, u32[]{:S(2)}) collective-permute-start(bf16[2,3,128,128]{3,2,1,0:T(8,128)(2,1)S(1)} %pad_maximum_fusion.2), channel_id=1, source_target_pairs={{0,0},{1,32},{2,64},{3,96},{4,4},{5,36},{6,68},{7,100},{8,8},{9,40... | collective-permute-start | bytes 589832 | tf_op jit(solution)/shard_map/weights_turn/ppermute | solution.py:33
  32.4 26.3 %collective-permute-start.5 = (bf16[2,256,1024]{2,1,0:T(8,128)(2,1)S(1)}, bf16[2,256,1024]{2,1,0:T(8,128)(2,1)S(1)}, u32[]{:S(2)}, u32[]{:S(2)}) collective-permute-start(bf16[2,256,1024]{2,1,0:T(8,128)(2,1)S(1)} %get-tuple-element.44), channel_id=1, source_target_pairs={{0,16},{1,17},{2,18},{3,19},{4,20},{5,21},{6,22},{7,23},{8,24},{9,... | collective-permute-start | bytes 3145736 | tf_op jit(solution)/shard_map/input_swap/ppermute | solution.py:33
  34.7 36.1 %collective-permute-start.6 = (bf16[4,2,3,128,128]{4,3,2,1,0:T(8,128)(2,1)S(1)}, bf16[4,2,3,128,128]{4,3,2,1,0:T(8,128)(2,1)S(1)}, u32[]{:S(2)}, u32[]{:S(2)}) collective-permute-start(bf16[4,2,3,128,128]{4,3,2,1,0:T(8,128)(2,1)S(1)} %pad_maximum_fusion.refs_0_), channel_id=1, source_target_pairs={{0,12},{1,13},{2,14},{3,15},{4,0},{5,1},{6,2},{7,3},{8,4},{9,5},{1... | collective-permute-start | bytes 2359304 | tf_op jit(solution)/shard_map/weights_x/ppermute | solution.py:33
  37.1 33.6 %collective-permute-start.7 = (bf16[4,2,3,128,128]{4,3,2,1,0:T(8,128)(2,1)S(1)}, bf16[4,2,3,128,128]{4,3,2,1,0:T(8,128)(2,1)S(1)}, u32[]{:S(2)}, u32[]{:S(2)}) collective-permute-start(bf16[4,2,3,128,128]{4,3,2,1,0:T(8,128)(2,1)S(1)} %pad_maximum_fusion.refs_0_), channel_id=1, source_target_pairs={{0,8},{1,9},{2,10},{3,11},{4,12},{5,13},{6,14},{7,15},{8,0},{9,1},... | collective-permute-start | bytes 2359304 | tf_op jit(solution)/shard_map/weights_x/ppermute | solution.py:33
  37.7 37.3 %collective-permute-start.8 = (bf16[4,2,3,128,128]{4,3,2,1,0:T(8,128)(2,1)S(1)}, bf16[4,2,3,128,128]{4,3,2,1,0:T(8,128)(2,1)S(1)}, u32[]{:S(2)}, u32[]{:S(2)}) collective-permute-start(bf16[4,2,3,128,128]{4,3,2,1,0:T(8,128)(2,1)S(1)} %pad_maximum_fusion.refs_0_), channel_id=1, source_target_pairs={{0,4},{1,5},{2,6},{3,7},{4,8},{5,9},{6,10},{7,11},{8,12},{9,13},{1... | collective-permute-start | bytes 2359304 | tf_op jit(solution)/shard_map/weights_x/ppermute | solution.py:33
  76.8 2.5 %collective-permute-start.9 = (bf16[256,1536]{1,0:T(8,128)(2,1)S(1)}, bf16[256,1536]{1,0:T(8,128)(2,1)S(1)}, u32[]{:S(2)}, u32[]{:S(2)}) collective-permute-start(bf16[256,1536]{1,0:T(8,128)(2,1)S(1)} %get-tuple-element.48), channel_id=1, source_target_pairs={{0,1},{1,0},{2,3},{3,2},{4,5},{5,4},{6,7},{7,6},{8,9},{9,8},{10,11... | collective-permute-start | bytes 2359304 | tf_op jit(solution)/shard_map/ppermute | solution.py:33
  79.7 10.4 %collective-permute-start.12 = (bf16[64,1536]{1,0:T(8,128)(2,1)S(1)}, bf16[64,1536]{1,0:T(8,128)(2,1)S(1)}, u32[]{:S(2)}, u32[]{:S(2)}) collective-permute-start(bf16[64,1536]{1,0:T(8,128)(2,1)S(1)} %get-tuple-element.76), channel_id=1, source_target_pairs={{0,18},{1,19},{2,16},{3,17},{4,22},{5,23},{6,20},{7,21},{8,26},{9,... | collective-permute-start | bytes 589832 | tf_op jit(solution)/shard_map/ppermute | solution.py:33
  79.8 10.3 %collective-permute-start.11 = (bf16[64,1536]{1,0:T(8,128)(2,1)S(1)}, bf16[64,1536]{1,0:T(8,128)(2,1)S(1)}, u32[]{:S(2)}, u32[]{:S(2)}) collective-permute-start(bf16[64,1536]{1,0:T(8,128)(2,1)S(1)} %get-tuple-element.77), channel_id=1, source_target_pairs={{0,16},{1,17},{2,18},{3,19},{4,20},{5,21},{6,22},{7,23},{8,24},{9,... | collective-permute-start | bytes 589832 | tf_op jit(solution)/shard_map/ppermute | solution.py:33
  80.7 11.0 %collective-permute-start.10 = (bf16[64,1536]{1,0:T(8,128)(2,1)S(1)}, bf16[64,1536]{1,0:T(8,128)(2,1)S(1)}, u32[]{:S(2)}, u32[]{:S(2)}) collective-permute-start(bf16[64,1536]{1,0:T(8,128)(2,1)S(1)} %get-tuple-element.75), channel_id=1, source_target_pairs={{0,2},{1,3},{2,0},{3,1},{4,6},{5,7},{6,4},{7,5},{8,10},{9,11},{10,... | collective-permute-start | bytes 589832 | tf_op jit(solution)/shard_map/ppermute | solution.py:33
  91.8 7.6 %collective-permute-start.15 = (bf16[64,1536]{1,0:T(8,128)(2,1)S(1)}, bf16[64,1536]{1,0:T(8,128)(2,1)S(1)}, u32[]{:S(2)}, u32[]{:S(2)}) collective-permute-start(bf16[64,1536]{1,0:T(8,128)(2,1)S(1)} %pad_maximum_fusion.3), channel_id=1, source_target_pairs={{0,18},{1,19},{2,16},{3,17},{4,22},{5,23},{6,20},{7,21},{8,26},{9,... | collective-permute-start | bytes 589832 | tf_op jit(solution)/shard_map/ppermute | solution.py:33
  92.3 7.1 %collective-permute-start.14 = (bf16[64,1536]{1,0:T(8,128)(2,1)S(1)}, bf16[64,1536]{1,0:T(8,128)(2,1)S(1)}, u32[]{:S(2)}, u32[]{:S(2)}) collective-permute-start(bf16[64,1536]{1,0:T(8,128)(2,1)S(1)} %pad_maximum_fusion.3), channel_id=1, source_target_pairs={{0,16},{1,17},{2,18},{3,19},{4,20},{5,21},{6,22},{7,23},{8,24},{9,... | collective-permute-start | bytes 589832 | tf_op jit(solution)/shard_map/ppermute | solution.py:33
  93.1 9.5 %collective-permute-start.13 = (bf16[64,1536]{1,0:T(8,128)(2,1)S(1)}, bf16[64,1536]{1,0:T(8,128)(2,1)S(1)}, u32[]{:S(2)}, u32[]{:S(2)}) collective-permute-start(bf16[64,1536]{1,0:T(8,128)(2,1)S(1)} %pad_maximum_fusion.3), channel_id=1, source_target_pairs={{0,2},{1,3},{2,0},{3,1},{4,6},{5,7},{6,4},{7,5},{8,10},{9,11},{10,... | collective-permute-start | bytes 589832 | tf_op jit(solution)/shard_map/ppermute | solution.py:33
  102.7 4.6 %collective-permute-start.16 = (bf16[256,1536]{1,0:T(8,128)(2,1)S(1)}, bf16[256,1536]{1,0:T(8,128)(2,1)S(1)}, u32[]{:S(2)}, u32[]{:S(2)}) collective-permute-start(bf16[256,1536]{1,0:T(8,128)(2,1)S(1)} %pad_maximum_fusion.1.da), channel_id=1, source_target_pairs={{0,1},{1,0},{2,3},{3,2},{4,5},{5,4},{6,7},{7,6},{8,9},{9,8},{10,11... | collective-permute-start | bytes 2359304 | tf_op jit(solution)/shard_map/ppermute | solution.py:33
  108.6 20.0 %collective-permute-start.17 = (bf16[2,2,3,128,128]{4,3,2,1,0:T(8,128)(2,1)S(1)}, bf16[2,2,3,128,128]{4,3,2,1,0:T(8,128)(2,1)S(1)}, u32[]{:S(2)}, u32[]{:S(2)}) collective-permute-start(bf16[2,2,3,128,128]{4,3,2,1,0:T(8,128)(2,1)S(1)} %get-tuple-element.50), channel_id=1, source_target_pairs={{0,4},{1,5},{2,6},{3,7},{4,8},{5,9},{6,10},{7,11},{8,12},{9,13},{1... | collective-permute-start | bytes 1179656 | tf_op jit(solution)/shard_map/grads_x_0/ppermute | solution.py:33
  108.7 19.9 %collective-permute-start.18 = (bf16[2,2,3,128,128]{4,3,2,1,0:T(8,128)(2,1)S(1)}, bf16[2,2,3,128,128]{4,3,2,1,0:T(8,128)(2,1)S(1)}, u32[]{:S(2)}, u32[]{:S(2)}) collective-permute-start(bf16[2,2,3,128,128]{4,3,2,1,0:T(8,128)(2,1)S(1)} %get-tuple-element.51), channel_id=1, source_target_pairs={{0,12},{1,13},{2,14},{3,15},{4,0},{5,1},{6,2},{7,3},{8,4},{9,5},{1... | collective-permute-start | bytes 1179656 | tf_op jit(solution)/shard_map/grads_x_0/ppermute | solution.py:33
  111.4 20.2 %collective-permute-start.19 = (bf16[2,2,3,128,128]{4,3,2,1,0:T(8,128)(2,1)S(1)}, bf16[2,2,3,128,128]{4,3,2,1,0:T(8,128)(2,1)S(1)}, u32[]{:S(2)}, u32[]{:S(2)}) collective-permute-start(bf16[2,2,3,128,128]{4,3,2,1,0:T(8,128)(2,1)S(1)} %get-tuple-element.60), channel_id=1, source_target_pairs={{0,8},{1,9},{2,10},{3,11},{4,12},{5,13},{6,14},{7,15},{8,0},{9,1},... | collective-permute-start | bytes 1179656 | tf_op jit(solution)/shard_map/grads_x_0/ppermute | solution.py:33
  113.2 36.7 %collective-permute-start.25 = (bf16[2,256,1024]{2,1,0:T(8,128)(2,1)S(1)}, bf16[2,256,1024]{2,1,0:T(8,128)(2,1)S(1)}, u32[]{:S(2)}, u32[]{:S(2)}) collective-permute-start(bf16[2,256,1024]{2,1,0:T(8,128)(2,1)S(1)} %get-tuple-element.57), channel_id=1, source_target_pairs={{0,16},{1,17},{2,18},{3,19},{4,20},{5,21},{6,22},{7,23},{8,24},{9,... | collective-permute-start | bytes 3145736 | tf_op jit(solution)/shard_map/output_swap/ppermute | solution.py:33
  128.7 10.9 %collective-permute-start.24 = (bf16[2,2,3,128,128]{4,3,2,1,0:T(8,128)(2,1)S(1)}, bf16[2,2,3,128,128]{4,3,2,1,0:T(8,128)(2,1)S(1)}, u32[]{:S(2)}, u32[]{:S(2)}) collective-permute-start(bf16[2,2,3,128,128]{4,3,2,1,0:T(8,128)(2,1)S(1)} %get-tuple-element.64), channel_id=1, source_target_pairs={{0,8},{1,9},{2,10},{3,11},{4,12},{5,13},{6,14},{7,15},{8,0},{9,1},... | collective-permute-start | bytes 1179656 | tf_op jit(solution)/shard_map/grads_x_1/ppermute | solution.py:33
  128.7 20.6 %collective-permute-start.23 = (bf16[2,2,3,128,128]{4,3,2,1,0:T(8,128)(2,1)S(1)}, bf16[2,2,3,128,128]{4,3,2,1,0:T(8,128)(2,1)S(1)}, u32[]{:S(2)}, u32[]{:S(2)}) collective-permute-start(bf16[2,2,3,128,128]{4,3,2,1,0:T(8,128)(2,1)S(1)} %get-tuple-element.63), channel_id=1, source_target_pairs={{0,12},{1,13},{2,14},{3,15},{4,0},{5,1},{6,2},{7,3},{8,4},{9,5},{1... | collective-permute-start | bytes 1179656 | tf_op jit(solution)/shard_map/grads_x_1/ppermute | solution.py:33
  131.0 18.6 %collective-permute-start.22 = (bf16[2,2,3,128,128]{4,3,2,1,0:T(8,128)(2,1)S(1)}, bf16[2,2,3,128,128]{4,3,2,1,0:T(8,128)(2,1)S(1)}, u32[]{:S(2)}, u32[]{:S(2)}) collective-permute-start(bf16[2,2,3,128,128]{4,3,2,1,0:T(8,128)(2,1)S(1)} %get-tuple-element.62), channel_id=1, source_target_pairs={{0,4},{1,5},{2,6},{3,7},{4,8},{5,9},{6,10},{7,11},{8,12},{9,13},{1... | collective-permute-start | bytes 1179656 | tf_op jit(solution)/shard_map/grads_x_1/ppermute | solution.py:33
  131.9 24.5 %collective-permute-start.21 = (bf16[2,3,128,128]{3,2,1,0:T(8,128)(2,1)S(1)}, bf16[2,3,128,128]{3,2,1,0:T(8,128)(2,1)S(1)}, u32[]{:S(2)}, u32[]{:S(2)}) collective-permute-start(bf16[2,3,128,128]{3,2,1,0:T(8,128)(2,1)S(1)} %get-tuple-element.81), channel_id=1, source_target_pairs={{64,0},{96,1},{0,2},{32,3},{68,4},{100,5},{4,6},{36,7},{72,8},{104... | collective-permute-start | bytes 589832 | tf_op jit(solution)/shard_map/grads_turn_0/ppermute | solution.py:37
  139.6 16.7 %collective-permute-start.20 = (bf16[2,3,128,128]{3,2,1,0:T(8,128)(2,1)S(1)}, bf16[2,3,128,128]{3,2,1,0:T(8,128)(2,1)S(1)}, u32[]{:S(2)}, u32[]{:S(2)}) collective-permute-start(bf16[2,3,128,128]{3,2,1,0:T(8,128)(2,1)S(1)} %get-tuple-element.80), channel_id=1, source_target_pairs={{0,0},{32,1},{64,2},{96,3},{4,4},{36,5},{68,6},{100,7},{8,8},{40,9... | collective-permute-start | bytes 589832 | tf_op jit(solution)/shard_map/grads_turn_0/ppermute | solution.py:37
  149.9 22.2 %collective-permute-start.27 = (bf16[2,3,128,128]{3,2,1,0:T(8,128)(2,1)S(1)}, bf16[2,3,128,128]{3,2,1,0:T(8,128)(2,1)S(1)}, u32[]{:S(2)}, u32[]{:S(2)}) collective-permute-start(bf16[2,3,128,128]{3,2,1,0:T(8,128)(2,1)S(1)} %get-tuple-element.83), channel_id=1, source_target_pairs={{192,0},{224,1},{128,2},{160,3},{196,4},{228,5},{132,6},{164,7},{2... | collective-permute-start | bytes 589832 | tf_op jit(solution)/shard_map/grads_turn_1/ppermute | solution.py:37
  151.8 27.9 %collective-permute-start.26 = (bf16[2,3,128,128]{3,2,1,0:T(8,128)(2,1)S(1)}, bf16[2,3,128,128]{3,2,1,0:T(8,128)(2,1)S(1)}, u32[]{:S(2)}, u32[]{:S(2)}) collective-permute-start(bf16[2,3,128,128]{3,2,1,0:T(8,128)(2,1)S(1)} %get-tuple-element.82), channel_id=1, source_target_pairs={{128,0},{160,1},{192,2},{224,3},{132,4},{164,5},{196,6},{228,7},{1... | collective-permute-start | bytes 589832 | tf_op jit(solution)/shard_map/grads_turn_1/ppermute | solution.py:37
  179.9 1.5 collective-permute-start.28

commit v4 on v3

--- a/solution.py
+++ b/solution.py
@@ -134,20 +134,16 @@
             full[oc * tb + half : (oc + 1) * tb, :] = far[m, oc * half : (oc + 1) * half, :]
 
 
-def forward_body(tok, cot, *refs):
-    columns, (gu, dn, keep, away) = refs[:4], refs[4:]
+def forward_body(tok, cot, c0, c1, c2, c3, gu, dn, keep, away):
+    fb = c0.shape[-1]
     tb = keep.shape[0]
-    fb = columns[0].shape[-1]
     for f in range(2):
-        for j in range(NX):
-            column = columns[j]
+        for j, column in enumerate((c0, c1, c2, c3)):
             at = (f * NX + j) * fb
-            for g in range(2):
-                for e in range(2):
-                    unit = (g * 2 + e) * fb
-                    gu[at : at + fb, unit : unit + fb] = column[f * 2 + g, e, 0]
-                    gu[at : at + fb, 4 * fb + unit : 4 * fb + unit + fb] = column[f * 2 + g, e, 1]
-                    dn[unit : unit + fb, at : at + fb] = column[f * 2 + g, e, 2]
+            for e in range(2):
+                gu[at : at + fb, e * fb : e * fb + fb] = column[f, e, 0]
+                gu[at : at + fb, (2 + e) * fb : (2 + e) * fb + fb] = column[f, e, 1]
+                dn[e * fb : e * fb + fb, at : at + fb] = column[f, e, 2]
     wide = gu.shape[1]
     away[:, :wide] = nn(tok[tb:, :], gu[...]).astype(BF)
     away[:, wide:] = nt(cot[tb:, :], dn[...]).astype(BF)
@@ -155,28 +151,27 @@
     keep[:, wide:] = nt(cot[:tb, :], dn[...])
 
 
-def grad_body(f, da, dc, tok, cot, p1, p3, p2, p0):
+def grad_body(da, dc, tok, cot, p1, p3, p2, p0):
     tb = da.shape[0]
     fb = p0.shape[-1]
-    hid = 4 * fb
+    wide = 4 * fb
     for j, piece in ((1, p1), (3, p3), (2, p2), (0, p0)):
-        at = (f * NX + j) * fb
-        gu = tn(tok[:tb, at : at + fb], da[:, : 2 * hid]) + tn(tok[tb:, at : at + fb], dc[:, : 2 * hid])
-        dn = tn(da[:, 2 * hid :], cot[:tb, at : at + fb]) + tn(dc[:, 2 * hid :], cot[tb:, at : at + fb])
-        for g in range(2):
+        for f in range(2):
+            at = (f * NX + j) * fb
+            gu = tn(tok[:tb, at : at + fb], da[:, :wide]) + tn(tok[tb:, at : at + fb], dc[:, :wide])
+            dn = tn(da[:, wide:], cot[:tb, at : at + fb]) + tn(dc[:, wide:], cot[tb:, at : at + fb])
             for e in range(2):
-                unit = (g * 2 + e) * fb
-                piece[g, e, 0] = gu[:, unit : unit + fb].astype(piece.dtype)
-                piece[g, e, 1] = gu[:, hid + unit : hid + unit + fb].astype(piece.dtype)
-                piece[g, e, 2] = dn[unit : unit + fb].astype(piece.dtype)
-
-
-def output_body(da, dc, gu, dn, own, oth):
-    tb, wide = da.shape[0], gu.shape[1]
-    half = tb // 2
-    for oc, part in ((0, da), (1, dc)):
-        out = nn(part[:, wide:], dn[...]).astype(BF)
-        grad = nt(part[:, :wide], gu[...]).astype(BF)
+                piece[f, e, 0] = gu[:, e * fb : e * fb + fb].astype(piece.dtype)
+                piece[f, e, 1] = gu[:, (2 + e) * fb : (2 + e) * fb + fb].astype(piece.dtype)
+                piece[f, e, 2] = dn[e * fb : e * fb + fb].astype(piece.dtype)
+
+
+def output_body(da, dc, ea, ec, gu_d, dn_d, gu_e, dn_e, own, oth):
+    wide = gu_d.shape[1]
+    half = da.shape[0] // 2
+    for oc, d, e in ((0, da, ea), (1, dc, ec)):
+        out = (nn(d[:, wide:], dn_d[...]) + nn(e[:, wide:], dn_e[...])).astype(BF)
+        grad = (nt(d[:, :wide], gu_d[...]) + nt(e[:, :wide], gu_e[...])).astype(BF)
         for m, rows in ((0, out), (1, grad)):
             own[m, oc * half : (oc + 1) * half, :] = rows[:half]
             oth[m, oc * half : (oc + 1) * half, :] = rows[half:]
@@ -190,51 +185,76 @@
     tb = tokens.shape[0]
     sub = tb // 4
     quarter = cotangent.shape[1]
-    wide, hid = 8 * fb, 4 * fb
+    wide, unit = 8 * fb, 2 * fb
 
     with jax.named_scope("weights_core"):
         block = jnp.stack([gate_weight, up_weight, down_weight])
         pair = jnp.stack([block, send(block, swap_core)])
 
-    with jax.named_scope("weights_turn"):
-        column = jnp.stack([send(pair, turn(f, g)) for f in range(2) for g in range(2)])
+    def turned(g, value):
+        with jax.named_scope(f"weights_turn_{g}"):
+            return [send(value, turn(f, g)) for f in range(2)]
+
+    def along(g, column):
+        with jax.named_scope(f"weights_x_{g}"):
+            return [column] + [send(column, along_x(-j)) for j in range(1, NX)]
+
+    first = jnp.stack(turned(0, pair))
     where, tokens, cotangent, _ = lax.optimization_barrier((where, tokens, cotangent, pair))
-    with jax.named_scope("weights_x"):
-        columns = [column] + [send(column, along_x(-j)) for j in range(1, NX)]
+    second = jnp.stack(turned(1, after(pair, first)))
     with jax.named_scope("pick"):
         picked = lax.dynamic_slice(tokens, (0, t * quarter), (tb, quarter))
         own, oth = call(pick_body, [((2, tb, wide), BF)] * 2, [picked, cotangent], 0, where)
     with jax.named_scope("input_swap"):
-        swapped = send(after(oth, column), swap_hi)
+        swapped = send(after(oth, first), swap_hi)
     with jax.named_scope("join"):
         tok, cot = call(join_body, [((2 * tb, wide), BF)] * 2, [own, swapped])
-
-    product = 2 * 2 * tb * wide * hid
-    with jax.named_scope("forward"):
-        gu, dn, keep, away = call(
-            forward_body,
-            [((wide, 2 * hid), BF), ((hid, wide), BF), ((tb, 3 * hid), F32), ((tb, 3 * hid), BF)],
-            [tok, cot, *columns],
-            3 * product,
-        )
-    part = keep + send(away, swap_core).astype(F32)
-    pre = part[:sub]
-    for k in range(1, 4):
-        pre = pre + send(part[k * sub : (k + 1) * sub].astype(BF), along_y(k)).astype(F32)
-    gate_pre, up_pre, d_hidden = pre[:, :hid], pre[:, hid : 2 * hid], pre[:, 2 * hid :]
-    sig = jax.nn.sigmoid(gate_pre)
-    act = gate_pre * sig
-    hidden = (act * up_pre).astype(BF)
-    d_gate = (d_hidden * up_pre * sig * (1.0 + gate_pre * (1.0 - sig))).astype(BF)
-    d_up = (d_hidden * act).astype(BF)
-    mine = jnp.concatenate([d_gate, d_up, hidden], axis=1)
-    four = jnp.concatenate([mine] + [send(mine, along_y(k)) for k in range(1, 4)], axis=0)
-    terms = (four, send(four, swap_core))
+    first = along(0, first)
+    first[0] = after(first[0], second)
+    second = along(1, after(second, *first[1:]))
+
+    product = 2 * 2 * tb * wide * unit
+
+    def forward(g, columns, rows):
+        with jax.named_scope(f"forward_{g}"):
+            return call(
+                forward_body,
+                [((wide, 2 * unit), BF), ((unit, wide), BF), ((tb, 3 * unit), F32), ((tb, 3 * unit), BF)],
+                [rows, cot, *columns],
+                3 * product,
+            )
+
+    def core_reduced(g, keep, away):
+        with jax.named_scope(f"reduce_core_{g}"):
+            return keep + send(away, swap_core).astype(F32)
+
+    def ring_reduced(g, part, *others):
+        with jax.named_scope(f"reduce_ring_{g}"):
+            total = after(part[:sub], *others)
+            for k in range(1, 4):
+                total = total + send(part[k * sub : (k + 1) * sub].astype(BF), along_y(k)).astype(F32)
+            return total
+
+    def activations(pre):
+        gate_pre, up_pre, d_hidden = pre[:, :unit], pre[:, unit : 2 * unit], pre[:, 2 * unit :]
+        sig = jax.nn.sigmoid(gate_pre)
+        act = gate_pre * sig
+        hidden = (act * up_pre).astype(BF)
+        d_gate = (d_hidden * up_pre * sig * (1.0 + gate_pre * (1.0 - sig))).astype(BF)
+        d_up = (d_hidden * act).astype(BF)
+        return jnp.concatenate([d_gate, d_up, hidden], axis=1)
+
+    def gathered(g, mine, *others):
+        with jax.named_scope(f"gather_ring_{g}"):
+            four = jnp.concatenate([mine] + [send(mine, along_y(k)) for k in range(1, 4)], axis=0)
+        with jax.named_scope(f"gather_core_{g}"):
+            return four, send(after(four, *others), swap_core)
 
     shape = (2, 2, 3, fb, fb)
 
-    def pieces_of(f):
-        return call(functools.partial(grad_body, f), [(shape, BF)] * 3 + [(shape, F32)], [*terms, tok, cot], 3 * product // 2)
+    def pieces_of(g, terms):
+        with jax.named_scope(f"grads_{g}"):
+            return call(grad_body, [(shape, BF)] * 3 + [(shape, F32)], [*terms, tok, cot], 3 * product)
 
     def summed(moved, kept):
         total = kept
@@ -242,25 +262,31 @@
             total = total + piece.astype(F32)
         return total.astype(BF)
 
-    def returned(f, total):
-        with jax.named_scope(f"grads_turn_{f}"):
-            return [send_back(total[g], turn(f, g)) for g in range(2)]
-
-    with jax.named_scope("grads"):
-        p1, p3, p2, p0 = pieces_of(0)
-        q1, q3, q2, q0 = pieces_of(1)
+    def returned(g, total):
+        with jax.named_scope(f"grads_turn_{g}"):
+            return [send_back(total[f], turn(f, g)) for f in range(2)]
+
+    gu_0, dn_0, keep_0, away_0 = forward(0, first, tok)
+    part_0 = core_reduced(0, keep_0, away_0)
+    gu_1, dn_1, keep_1, away_1 = forward(1, second, after(tok, part_0))
+    mine_0 = activations(ring_reduced(0, part_0, keep_1))
+    mine_1 = activations(ring_reduced(1, core_reduced(1, keep_1, away_1)))
+    terms_0 = gathered(0, mine_0, mine_1)
+    p1, p3, p2, p0 = pieces_of(0, terms_0)
     with jax.named_scope("grads_x_0"):
         p1, p3, p2 = send(p1, along_x(1)), send(p3, along_x(3)), send(p2, along_x(2))
+
+    terms_1 = gathered(1, mine_1, p1, p3, p2)
+    q1, q3, q2, q0 = pieces_of(1, terms_1)
     with jax.named_scope("outputs"):
-        own, oth = call(output_body, [((2, tb, wide), BF)] * 2, [*terms, gu, dn], 3 * product)
+        own, oth = call(output_body, [((2, tb, wide), BF)] * 2, [*terms_0, *terms_1, after(gu_0, q0), dn_0, gu_1, dn_1], 6 * product)
     with jax.named_scope("output_swap"):
         swapped = send(oth, swap_hi)
     with jax.named_scope("place"):
         layer_out, token_grad = call(place_body, [((tb, quarter), BF)] * 2, [own, swapped], 0, where)
-    p1, p3, q1, q3, q2, oth = lax.optimization_barrier((p1, p3, q1, q3, q2, oth))
+    back = returned(0, summed((p1, p3, p2), p0))
     with jax.named_scope("grads_x_1"):
         q1, q3, q2 = send(q1, along_x(1)), send(q3, along_x(3)), send(q2, along_x(2))
-    back = returned(0, summed((p1, p3, p2), p0))
     back = back + returned(1, after(summed((q1, q3, q2), q0), swapped))
     total = sum(piece.astype(F32) for piece in back)
     kept, moved, layer_out, token_grad = lax.optimization_barrier((total[0], total[1], layer_out, token_grad))

time: 182 us -> 189 us (1.038)
  starting transfers between devices: 55.1 us -> 102 us
  waiting for transfers between devices: 112 us -> 69.5 us
    ppermute x25 -> x36, starting transfers between devices: 37.3 us -> 68.7 us  [send(): return lax.ppermute(value, AXES, pairs_of(move))]
    ppermute x25 -> x36, waiting for transfers between devices: 88.6 us -> 59.8 us  [send(): return lax.ppermute(value, AXES, pairs_of(move))]
    ppermute x4, starting transfers between devices: 17.8 us -> 33.5 us  [send_back(): return lax.ppermute(value, AXES, [(b, a) for a, b in pairs_of(move)])]
    ppermute x4, waiting for transfers between devices: 23.4 us -> 9.69 us  [send_back(): return lax.ppermute(value, AXES, [(b, a) for a, b in pairs_of(move)])]
    pallas_call x7 -> x8, Pallas kernels: 9.89 us -> 10.2 us  [call(): pl.pallas_call(body, out_shape=[jax.ShapeDtypeStruct(s, d) for s, d in sh...]
  transfers between devices with their start and end apart: 29 -> 40, of which waited for: 18 -> 19; matrix products, arithmetic and copies ran while one was open for 1% -> 1% of each run, Pallas kernels for 4% -> 3%
where the time goes in v4:
time: 189 us; the launch traced here: 188 us
  starting transfers between devices  102 us (54%)
  waiting for transfers between devices  69.5 us (37%)
  Pallas kernels  10.2 us (5%)
  local copies, waits for them, and re-layouts  3.38 us (2%)
  other arithmetic  1.91 us (1%)
    ppermute x36, starting transfers between devices, send(): return lax.ppermute(value, AXES, pairs_of(move))  68.7 us
    ppermute x36, waiting for transfers between devices, send(): return lax.ppermute(value, AXES, pairs_of(move))  59.8 us
    ppermute x4, starting transfers between devices, send_back(): return lax.ppermute(value, AXES, [(b, a) for a, b in pairs_of(move)])  33.5 us
    pallas_call x8, Pallas kernels, call(): pl.pallas_call(body, out_shape=[jax.ShapeDtypeStruct(s, d) for s, d in sh...  10.2 us
    ppermute x4, waiting for transfers between devices, send_back(): return lax.ppermute(value, AXES, [(b, a) for a, b in pairs_of(move)])  9.69 us
  transfers between devices with their start and end apart: 40, of which 19 were waited for; matrix products, arithmetic and copies ran while one was open for 1% of the time, Pallas kernels for 3%

profile of v4, /device:TPU:9, one launch (start us, length us, event | category | flops | bytes accessed | tf_op | source)
XLA Modules:
  0.0 188.1 jit_solution(13567263668372754748)
XLA Ops:
  0.6 0.8 fusion.2
  1.4 0.8 collective-permute-start
  2.3 0.9 collective-permute-done
  3.2 5.8 %collective-permute-start.2 = (bf16[2,3,128,128]{3,2,1,0:T(8,128)(2,1)S(1)}, bf16[2,3,128,128]{3,2,1,0:T(8,128)(2,1)S(1)}, u32[]{:S(2)}, u32[]{:S(2)}) collective-permute-start(bf16[2,3,128,128]{3,2,1,0:T(8,128)(2,1)S(1)} %pad_maximum_fusion.4), channel_id=1, source_target_pairs={{0,128},{1,160},{2,192},{3,224},{4,132},{5,164},{6,196},{7,228},{8... | collective-permute-start | bytes 589832 | tf_op jit(solution)/shard_map/weights_turn_0/ppermute | solution.py:33
  9.0 1.9 %collective-permute-start.1 = (bf16[2,3,128,128]{3,2,1,0:T(8,128)(2,1)S(1)}, bf16[2,3,128,128]{3,2,1,0:T(8,128)(2,1)S(1)}, u32[]{:S(2)}, u32[]{:S(2)}) collective-permute-start(bf16[2,3,128,128]{3,2,1,0:T(8,128)(2,1)S(1)} %pad_maximum_fusion.4), channel_id=1, source_target_pairs={{0,0},{1,32},{2,64},{3,96},{4,4},{5,36},{6,68},{7,100},{8,8},{9,40... | collective-permute-start | bytes 589832 | tf_op jit(solution)/shard_map/weights_turn_0/ppermute | solution.py:33
  10.9 1.3 constant_dynamic-slice_fusion.tok
  12.2 1.2 copy-done
  13.4 1.1 pick.1
  14.6 7.7 %collective-permute-done.2 = bf16[2,3,128,128]{3,2,1,0:T(8,128)(2,1)S(1)} collective-permute-done((bf16[2,3,128,128]{3,2,1,0:T(8,128)(2,1)S(1)}, bf16[2,3,128,128]{3,2,1,0:T(8,128)(2,1)S(1)}, u32[]{:S(2)}, u32[]{:S(2)}) %collective-permute-start.2) | collective-permute-done | bytes 196640 | tf_op jit(solution)/shard_map/weights_turn_0/ppermute | solution.py:33
  22.4 2.4 %collective-permute-start.3 = (bf16[2,256,1024]{2,1,0:T(8,128)(2,1)S(1)}, bf16[2,256,1024]{2,1,0:T(8,128)(2,1)S(1)}, u32[]{:S(2)}, u32[]{:S(2)}) collective-permute-start(bf16[2,256,1024]{2,1,0:T(8,128)(2,1)S(1)} %get-tuple-element.51), channel_id=1, source_target_pairs={{0,16},{1,17},{2,18},{3,19},{4,20},{5,21},{6,22},{7,23},{8,24},{9,... | collective-permute-start | bytes 3145736 | tf_op jit(solution)/shard_map/input_swap/ppermute | solution.py:33
  24.7 2.0 %collective-permute-start.5 = (bf16[2,3,128,128]{3,2,1,0:T(8,128)(2,1)S(1)}, bf16[2,3,128,128]{3,2,1,0:T(8,128)(2,1)S(1)}, u32[]{:S(2)}, u32[]{:S(2)}) collective-permute-start(bf16[2,3,128,128]{3,2,1,0:T(8,128)(2,1)S(1)} %pad_maximum_fusion.4), channel_id=1, source_target_pairs={{0,192},{1,224},{2,128},{3,160},{4,196},{5,228},{6,132},{7,164},{8... | collective-permute-start | bytes 589832 | tf_op jit(solution)/shard_map/weights_turn_1/ppermute | solution.py:33
  26.8 1.3 collective-permute-start.8
  28.1 2.5 %collective-permute-start.7 = (bf16[2,2,3,128,128]{4,3,2,1,0:T(8,128)(2,1)S(1)}, bf16[2,2,3,128,128]{4,3,2,1,0:T(8,128)(2,1)S(1)}, u32[]{:S(2)}, u32[]{:S(2)}) collective-permute-start(bf16[2,2,3,128,128]{4,3,2,1,0:T(8,128)(2,1)S(1)} %pad_maximum_fusion.c0), channel_id=1, source_target_pairs={{0,8},{1,9},{2,10},{3,11},{4,12},{5,13},{6,14},{7,15},{8,0},{9,1},... | collective-permute-start | bytes 1179656 | tf_op jit(solution)/shard_map/weights_x_0/ppermute | solution.py:33
  30.5 1.2 collective-permute-start.6
  31.7 5.6 %collective-permute-done.5 = bf16[2,3,128,128]{3,2,1,0:T(8,128)(2,1)S(1)} collective-permute-done((bf16[2,3,128,128]{3,2,1,0:T(8,128)(2,1)S(1)}, bf16[2,3,128,128]{3,2,1,0:T(8,128)(2,1)S(1)}, u32[]{:S(2)}, u32[]{:S(2)}) %collective-permute-start.5) | collective-permute-done | bytes 196640 | tf_op jit(solution)/shard_map/weights_turn_1/ppermute | solution.py:33
  37.3 17.3 %collective-permute-start.4 = (bf16[2,3,128,128]{3,2,1,0:T(8,128)(2,1)S(1)}, bf16[2,3,128,128]{3,2,1,0:T(8,128)(2,1)S(1)}, u32[]{:S(2)}, u32[]{:S(2)}) collective-permute-start(bf16[2,3,128,128]{3,2,1,0:T(8,128)(2,1)S(1)} %pad_maximum_fusion.4), channel_id=1, source_target_pairs={{0,64},{1,96},{2,0},{3,32},{4,68},{5,100},{6,4},{7,36},{8,72},{9,1... | collective-permute-start | bytes 589832 | tf_op jit(solution)/shard_map/weights_turn_1/ppermute | solution.py:33
  54.6 4.7 %collective-permute-done.4 = bf16[2,3,128,128]{3,2,1,0:T(8,128)(2,1)S(1)} collective-permute-done((bf16[2,3,128,128]{3,2,1,0:T(8,128)(2,1)S(1)}, bf16[2,3,128,128]{3,2,1,0:T(8,128)(2,1)S(1)}, u32[]{:S(2)}, u32[]{:S(2)}) %collective-permute-start.4) | collective-permute-done | bytes 196640 | tf_op jit(solution)/shard_map/weights_turn_1/ppermute | solution.py:33
  59.5 1.1 forward_0.1
  60.7 1.3 collective-permute-start.12
  62.0 2.4 %collective-permute-start.11 = (bf16[2,2,3,128,128]{4,3,2,1,0:T(8,128)(2,1)S(1)}, bf16[2,2,3,128,128]{4,3,2,1,0:T(8,128)(2,1)S(1)}, u32[]{:S(2)}, u32[]{:S(2)}) collective-permute-start(bf16[2,2,3,128,128]{4,3,2,1,0:T(8,128)(2,1)S(1)} %pad_maximum_fusion.1.c0), channel_id=1, source_target_pairs={{0,8},{1,9},{2,10},{3,11},{4,12},{5,13},{6,14},{7,15},{8,0},{9,1},... | collective-permute-start | bytes 1179656 | tf_op jit(solution)/shard_map/weights_x_1/ppermute | solution.py:33
  64.4 1.2 collective-permute-start.10
  65.8 0.9 collective-permute-start.15
  66.7 5.5 %collective-permute-done.12.c3 = bf16[2,2,3,128,128]{4,3,2,1,0:T(8,128)(2,1)S(1)} collective-permute-done((bf16[2,2,3,128,128]{4,3,2,1,0:T(8,128)(2,1)S(1)}, bf16[2,2,3,128,128]{4,3,2,1,0:T(8,128)(2,1)S(1)}, u32[]{:S(2)}, u32[]{:S(2)}) %collective-permute-start.12) | collective-permute-done | bytes 393248 | tf_op jit(solution)/shard_map/weights_x_1/ppermute | solution.py:33
  72.2 0.6 collective-permute-start.14
  72.9 8.7 %collective-permute-done.11.c2 = bf16[2,2,3,128,128]{4,3,2,1,0:T(8,128)(2,1)S(1)} collective-permute-done((bf16[2,2,3,128,128]{4,3,2,1,0:T(8,128)(2,1)S(1)}, bf16[2,2,3,128,128]{4,3,2,1,0:T(8,128)(2,1)S(1)}, u32[]{:S(2)}, u32[]{:S(2)}) %collective-permute-start.11) | collective-permute-done | bytes 393248 | tf_op jit(solution)/shard_map/weights_x_1/ppermute | solution.py:33
  81.7 1.1 forward_1.1
  82.7 1.3 collective-permute-start.19
  84.3 1.1 collective-permute-start.17
  85.4 2.1 %collective-permute-start.16 = (bf16[64,768]{1,0:T(8,128)(2,1)S(1)}, bf16[64,768]{1,0:T(8,128)(2,1)S(1)}, u32[]{:S(2)}, u32[]{:S(2)}) collective-permute-start(bf16[64,768]{1,0:T(8,128)(2,1)S(1)} %pad_maximum_fusion.6), channel_id=1, source_target_pairs={{0,2},{1,3},{2,0},{3,1},{4,6},{5,7},{6,4},{7,5},{8,10},{9,11},{10,... | collective-permute-start | bytes 294920 | tf_op jit(solution)/shard_map/gather_ring_0/ppermute | solution.py:33
  87.8 0.9 collective-permute-start.22
  88.7 4.0 %collective-permute-start.21 = (bf16[64,768]{1,0:T(8,128)(2,1)S(1)}, bf16[64,768]{1,0:T(8,128)(2,1)S(1)}, u32[]{:S(2)}, u32[]{:S(2)}) collective-permute-start(bf16[64,768]{1,0:T(8,128)(2,1)S(1)} %get-tuple-element.102), channel_id=1, source_target_pairs={{0,16},{1,17},{2,18},{3,19},{4,20},{5,21},{6,22},{7,23},{8,24},{9,... | collective-permute-start | bytes 294920 | tf_op jit(solution)/shard_map/reduce_ring_1/ppermute | solution.py:33
  92.7 1.7 collective-permute-done.20
  94.4 1.4 collective-permute-done.21
  95.8 2.4 %collective-permute-start.23 = (bf16[256,768]{1,0:T(8,128)(2,1)S(1)}, bf16[256,768]{1,0:T(8,128)(2,1)S(1)}, u32[]{:S(2)}, u32[]{:S(2)}) collective-permute-start(bf16[256,768]{1,0:T(8,128)(2,1)S(1)} %pad_maximum_fusion.2.da), channel_id=1, source_target_pairs={{0,1},{1,0},{2,3},{3,2},{4,5},{5,4},{6,7},{7,6},{8,9},{9,8},{10,11... | collective-permute-start | bytes 1179656 | tf_op jit(solution)/shard_map/gather_core_0/ppermute | solution.py:33
  98.2 1.3 collective-permute-done.23.dc
  99.6 1.3 grads_0.1
  100.9 1.1 collective-permute-start.24
  102.0 1.6 collective-permute-start.25
  103.6 1.2 collective-permute-start.26
  104.8 0.8 collective-permute-start.31
  105.6 1.9 collective-permute-start.30
  107.4 1.1 collective-permute-done.31
  108.6 2.1 %collective-permute-start.29 = (bf16[64,768]{1,0:T(8,128)(2,1)S(1)}, bf16[64,768]{1,0:T(8,128)(2,1)S(1)}, u32[]{:S(2)}, u32[]{:S(2)}) collective-permute-start(bf16[64,768]{1,0:T(8,128)(2,1)S(1)} %pad_maximum_fusion.7), channel_id=1, source_target_pairs={{0,2},{1,3},{2,0},{3,1},{4,6},{5,7},{6,4},{7,5},{8,10},{9,11},{10,... | collective-permute-start | bytes 294920 | tf_op jit(solution)/shard_map/gather_ring_1/ppermute | solution.py:33
  110.9 2.5 %collective-permute-done.29 = bf16[64,768]{1,0:T(8,128)(2,1)S(1)} collective-permute-done((bf16[64,768]{1,0:T(8,128)(2,1)S(1)}, bf16[64,768]{1,0:T(8,128)(2,1)S(1)}, u32[]{:S(2)}, u32[]{:S(2)}) %collective-permute-start.29) | collective-permute-done | bytes 98336 | tf_op jit(solution)/shard_map/gather_ring_1/ppermute | solution.py:33
  113.4 8.0 %collective-permute-done.26 = bf16[2,2,3,128,128]{4,3,2,1,0:T(8,128)(2,1)S(1)} collective-permute-done((bf16[2,2,3,128,128]{4,3,2,1,0:T(8,128)(2,1)S(1)}, bf16[2,2,3,128,128]{4,3,2,1,0:T(8,128)(2,1)S(1)}, u32[]{:S(2)}, u32[]{:S(2)}) %collective-permute-start.26) | collective-permute-done | bytes 393248 | tf_op jit(solution)/shard_map/grads_x_0/ppermute | solution.py:33
  121.4 1.2 collective-permute-start.32
  122.6 1.3 collective-permute-done.32.dc.ec
  123.9 1.3 grads_1.1
  125.3 1.8 outputs.1
  127.1 1.7 collective-permute-start.36
  128.8 0.9 collective-permute-start.33
  129.6 1.8 collective-permute-start.34
  131.4 0.7 collective-permute-start.35
  132.4 8.9 %collective-permute-start.27 = (bf16[2,3,128,128]{3,2,1,0:T(8,128)(2,1)S(1)}, bf16[2,3,128,128]{3,2,1,0:T(8,128)(2,1)S(1)}, u32[]{:S(2)}, u32[]{:S(2)}) collective-permute-start(bf16[2,3,128,128]{3,2,1,0:T(8,128)(2,1)S(1)} %get-tuple-element.93), channel_id=1, source_target_pairs={{0,0},{32,1},{64,2},{96,3},{4,4},{36,5},{68,6},{100,7},{8,8},{40,9... | collective-permute-start | bytes 589832 | tf_op jit(solution)/shard_map/grads_turn_0/ppermute | solution.py:37
  141.3 3.9 %collective-permute-start.28 = (bf16[2,3,128,128]{3,2,1,0:T(8,128)(2,1)S(1)}, bf16[2,3,128,128]{3,2,1,0:T(8,128)(2,1)S(1)}, u32[]{:S(2)}, u32[]{:S(2)}) collective-permute-start(bf16[2,3,128,128]{3,2,1,0:T(8,128)(2,1)S(1)} %get-tuple-element.94), channel_id=1, source_target_pairs={{128,0},{160,1},{192,2},{224,3},{132,4},{164,5},{196,6},{228,7},{1... | collective-permute-start | bytes 589832 | tf_op jit(solution)/shard_map/grads_turn_0/ppermute | solution.py:37
  145.3 3.8 %collective-permute-done.35 = bf16[2,2,3,128,128]{4,3,2,1,0:T(8,128)(2,1)S(1)} collective-permute-done((bf16[2,2,3,128,128]{4,3,2,1,0:T(8,128)(2,1)S(1)}, bf16[2,2,3,128,128]{4,3,2,1,0:T(8,128)(2,1)S(1)}, u32[]{:S(2)}, u32[]{:S(2)}) %collective-permute-start.35) | collective-permute-done | bytes 393248 | tf_op jit(solution)/shard_map/grads_x_1/ppermute | solution.py:33
  149.3 3.7 %collective-permute-done.36.far = bf16[2,256,1024]{2,1,0:T(8,128)(2,1)S(1)} collective-permute-done((bf16[2,256,1024]{2,1,0:T(8,128)(2,1)S(1)}, bf16[2,256,1024]{2,1,0:T(8,128)(2,1)S(1)}, u32[]{:S(2)}, u32[]{:S(2)}) %collective-permute-start.36) | collective-permute-done | bytes 1048608 | tf_op jit(solution)/shard_map/output_swap/ppermute | solution.py:33
  153.1 18.7 %collective-permute-start.37 = (bf16[2,3,128,128]{3,2,1,0:T(8,128)(2,1)S(1)}, bf16[2,3,128,128]{3,2,1,0:T(8,128)(2,1)S(1)}, u32[]{:S(2)}, u32[]{:S(2)}) collective-permute-start(bf16[2,3,128,128]{3,2,1,0:T(8,128)(2,1)S(1)} %get-tuple-element.95), channel_id=1, source_target_pairs={{64,0},{96,1},{0,2},{32,3},{68,4},{100,5},{4,6},{36,7},{72,8},{104... | collective-permute-start | bytes 589832 | tf_op jit(solution)/shard_map/grads_turn_1/ppermute | solution.py:37
  171.7 1.9 %collective-permute-start.38 = (bf16[2,3,128,128]{3,2,1,0:T(8,128)(2,1)S(1)}, bf16[2,3,128,128]{3,2,1,0:T(8,128)(2,1)S(1)}, u32[]{:S(2)}, u32[]{:S(2)}) collective-permute-start(bf16[2,3,128,128]{3,2,1,0:T(8,128)(2,1)S(1)} %get-tuple-element.96), channel_id=1, source_target_pairs={{192,0},{224,1},{128,2},{160,3},{196,4},{228,5},{132,6},{164,7},{2... | collective-permute-start | bytes 589832 | tf_op jit(solution)/shard_map/grads_turn_1/ppermute | solution.py:37
  173.6 2.4 %place.1 = (bf16[256,2048]{1,0:T(8,128)(2,1)}, bf16[256,2048]{1,0:T(8,128)(2,1)}) custom-call(s32[4]{0:T(128)S(1)} %pad_add_fusion.where, bf16[2,256,1024]{2,1,0:T(8,128)(2,1)S(1)} %get-tuple-element.80.own, bf16[2,256,1024]{2,1,0:T(8,128)(2,1)S(1)} %collective-permute-done.36.far), custom_call_target="tpu_custom_call" | custom-call | bytes 4194304 | tf_op jit(solution)/shard_map/place/pallas_call | solution.py:83
  176.0 7.7 %collective-permute-done.37 = bf16[2,3,128,128]{3,2,1,0:T(8,128)(2,1)S(1)} collective-permute-done((bf16[2,3,128,128]{3,2,1,0:T(8,128)(2,1)S(1)}, bf16[2,3,128,128]{3,2,1,0:T(8,128)(2,1)S(1)}, u32[]{:S(2)}, u32[]{:S(2)}) %collective-permute-start.37) | collective-permute-done | bytes 196640 | tf_op jit(solution)/shard_map/grads_turn_1/ppermute | solution.py:37
  183.7 2.0 %collective-permute-done.38 = bf16[2,3,128,128]{3,2,1,0:T(8,128)(2,1)S(1)} collective-permute-done((bf16[2,3,128,128]{3,2,1,0:T(8,128)(2,1)S(1)}, bf16[2,3,128,128]{3,2,1,0:T(8,128)(2,1)S(1)}, u32[]{:S(2)}, u32[]{:S(2)}) %collective-permute-start.38) | collective-permute-done | bytes 196640 | tf_op jit(solution)/shard_map/grads_turn_1/ppermute | solution.py:37
  185.9 1.4 collective-permute-done.39
  187.4 0.7 slice_bitcast_fusion.6
  (54 shorter events, 2.2 us)
Async XLA Ops:
  1.4 1.7 collective-permute-start
  3.2 19.2 %collective-permute-start.2 = (bf16[2,3,128,128]{3,2,1,0:T(8,128)(2,1)S(1)}, bf16[2,3,128,128]{3,2,1,0:T(8,128)(2,1)S(1)}, u32[]{:S(2)}, u32[]{:S(2)}) collective-permute-start(bf16[2,3,128,128]{3,2,1,0:T(8,128)(2,1)S(1)} %pad_maximum_fusion.4), channel_id=1, source_target_pairs={{0,128},{1,160},{2,192},{3,224},{4,132},{5,164},{6,196},{7,228},{8... | collective-permute-start | bytes 589832 | tf_op jit(solution)/shard_map/weights_turn_0/ppermute | solution.py:33
  9.0 13.4 %collective-permute-start.1 = (bf16[2,3,128,128]{3,2,1,0:T(8,128)(2,1)S(1)}, bf16[2,3,128,128]{3,2,1,0:T(8,128)(2,1)S(1)}, u32[]{:S(2)}, u32[]{:S(2)}) collective-permute-start(bf16[2,3,128,128]{3,2,1,0:T(8,128)(2,1)S(1)} %pad_maximum_fusion.4), channel_id=1, source_target_pairs={{0,0},{1,32},{2,64},{3,96},{4,4},{5,36},{6,68},{7,100},{8,8},{9,40... | collective-permute-start | bytes 589832 | tf_op jit(solution)/shard_map/weights_turn_0/ppermute | solution.py:33
  12.2 1.2 copy-start
  22.4 37.0 %collective-permute-start.3 = (bf16[2,256,1024]{2,1,0:T(8,128)(2,1)S(1)}, bf16[2,256,1024]{2,1,0:T(8,128)(2,1)S(1)}, u32[]{:S(2)}, u32[]{:S(2)}) collective-permute-start(bf16[2,256,1024]{2,1,0:T(8,128)(2,1)S(1)} %get-tuple-element.51), channel_id=1, source_target_pairs={{0,16},{1,17},{2,18},{3,19},{4,20},{5,21},{6,22},{7,23},{8,24},{9,... | collective-permute-start | bytes 3145736 | tf_op jit(solution)/shard_map/input_swap/ppermute | solution.py:33
  24.7 12.6 %collective-permute-start.5 = (bf16[2,3,128,128]{3,2,1,0:T(8,128)(2,1)S(1)}, bf16[2,3,128,128]{3,2,1,0:T(8,128)(2,1)S(1)}, u32[]{:S(2)}, u32[]{:S(2)}) collective-permute-start(bf16[2,3,128,128]{3,2,1,0:T(8,128)(2,1)S(1)} %pad_maximum_fusion.4), channel_id=1, source_target_pairs={{0,192},{1,224},{2,128},{3,160},{4,196},{5,228},{6,132},{7,164},{8... | collective-permute-start | bytes 589832 | tf_op jit(solution)/shard_map/weights_turn_1/ppermute | solution.py:33
  26.8 32.7 %collective-permute-start.8 = (bf16[2,2,3,128,128]{4,3,2,1,0:T(8,128)(2,1)S(1)}, bf16[2,2,3,128,128]{4,3,2,1,0:T(8,128)(2,1)S(1)}, u32[]{:S(2)}, u32[]{:S(2)}) collective-permute-start(bf16[2,2,3,128,128]{4,3,2,1,0:T(8,128)(2,1)S(1)} %pad_maximum_fusion.c0), channel_id=1, source_target_pairs={{0,4},{1,5},{2,6},{3,7},{4,8},{5,9},{6,10},{7,11},{8,12},{9,13},{1... | collective-permute-start | bytes 1179656 | tf_op jit(solution)/shard_map/weights_x_0/ppermute | solution.py:33
  28.1 31.4 %collective-permute-start.7 = (bf16[2,2,3,128,128]{4,3,2,1,0:T(8,128)(2,1)S(1)}, bf16[2,2,3,128,128]{4,3,2,1,0:T(8,128)(2,1)S(1)}, u32[]{:S(2)}, u32[]{:S(2)}) collective-permute-start(bf16[2,2,3,128,128]{4,3,2,1,0:T(8,128)(2,1)S(1)} %pad_maximum_fusion.c0), channel_id=1, source_target_pairs={{0,8},{1,9},{2,10},{3,11},{4,12},{5,13},{6,14},{7,15},{8,0},{9,1},... | collective-permute-start | bytes 1179656 | tf_op jit(solution)/shard_map/weights_x_0/ppermute | solution.py:33
  30.5 29.0 %collective-permute-start.6 = (bf16[2,2,3,128,128]{4,3,2,1,0:T(8,128)(2,1)S(1)}, bf16[2,2,3,128,128]{4,3,2,1,0:T(8,128)(2,1)S(1)}, u32[]{:S(2)}, u32[]{:S(2)}) collective-permute-start(bf16[2,2,3,128,128]{4,3,2,1,0:T(8,128)(2,1)S(1)} %pad_maximum_fusion.c0), channel_id=1, source_target_pairs={{0,12},{1,13},{2,14},{3,15},{4,0},{5,1},{6,2},{7,3},{8,4},{9,5},{1... | collective-permute-start | bytes 1179656 | tf_op jit(solution)/shard_map/weights_x_0/ppermute | solution.py:33
  37.3 22.0 %collective-permute-start.4 = (bf16[2,3,128,128]{3,2,1,0:T(8,128)(2,1)S(1)}, bf16[2,3,128,128]{3,2,1,0:T(8,128)(2,1)S(1)}, u32[]{:S(2)}, u32[]{:S(2)}) collective-permute-start(bf16[2,3,128,128]{3,2,1,0:T(8,128)(2,1)S(1)} %pad_maximum_fusion.4), channel_id=1, source_target_pairs={{0,64},{1,96},{2,0},{3,32},{4,68},{5,100},{6,4},{7,36},{8,72},{9,1... | collective-permute-start | bytes 589832 | tf_op jit(solution)/shard_map/weights_turn_1/ppermute | solution.py:33
  60.6 5.0 %collective-permute-start.9 = (bf16[256,768]{1,0:T(8,128)(2,1)S(1)}, bf16[256,768]{1,0:T(8,128)(2,1)S(1)}, u32[]{:S(2)}, u32[]{:S(2)}) collective-permute-start(bf16[256,768]{1,0:T(8,128)(2,1)S(1)} %get-tuple-element.57), channel_id=1, source_target_pairs={{0,1},{1,0},{2,3},{3,2},{4,5},{5,4},{6,7},{7,6},{8,9},{9,8},{10,11... | collective-permute-start | bytes 1179656 | tf_op jit(solution)/shard_map/reduce_core_0/ppermute | solution.py:33
  60.7 11.6 %collective-permute-start.12 = (bf16[2,2,3,128,128]{4,3,2,1,0:T(8,128)(2,1)S(1)}, bf16[2,2,3,128,128]{4,3,2,1,0:T(8,128)(2,1)S(1)}, u32[]{:S(2)}, u32[]{:S(2)}) collective-permute-start(bf16[2,2,3,128,128]{4,3,2,1,0:T(8,128)(2,1)S(1)} %pad_maximum_fusion.1.c0), channel_id=1, source_target_pairs={{0,4},{1,5},{2,6},{3,7},{4,8},{5,9},{6,10},{7,11},{8,12},{9,13},{1... | collective-permute-start | bytes 1179656 | tf_op jit(solution)/shard_map/weights_x_1/ppermute | solution.py:33
  62.0 19.7 %collective-permute-start.11 = (bf16[2,2,3,128,128]{4,3,2,1,0:T(8,128)(2,1)S(1)}, bf16[2,2,3,128,128]{4,3,2,1,0:T(8,128)(2,1)S(1)}, u32[]{:S(2)}, u32[]{:S(2)}) collective-permute-start(bf16[2,2,3,128,128]{4,3,2,1,0:T(8,128)(2,1)S(1)} %pad_maximum_fusion.1.c0), channel_id=1, source_target_pairs={{0,8},{1,9},{2,10},{3,11},{4,12},{5,13},{6,14},{7,15},{8,0},{9,1},... | collective-permute-start | bytes 1179656 | tf_op jit(solution)/shard_map/weights_x_1/ppermute | solution.py:33
  64.4 17.2 %collective-permute-start.10 = (bf16[2,2,3,128,128]{4,3,2,1,0:T(8,128)(2,1)S(1)}, bf16[2,2,3,128,128]{4,3,2,1,0:T(8,128)(2,1)S(1)}, u32[]{:S(2)}, u32[]{:S(2)}) collective-permute-start(bf16[2,2,3,128,128]{4,3,2,1,0:T(8,128)(2,1)S(1)} %pad_maximum_fusion.1.c0), channel_id=1, source_target_pairs={{0,12},{1,13},{2,14},{3,15},{4,0},{5,1},{6,2},{7,3},{8,4},{9,5},{1... | collective-permute-start | bytes 1179656 | tf_op jit(solution)/shard_map/weights_x_1/ppermute | solution.py:33
  65.7 18.4 %collective-permute-start.13 = (bf16[64,768]{1,0:T(8,128)(2,1)S(1)}, bf16[64,768]{1,0:T(8,128)(2,1)S(1)}, u32[]{:S(2)}, u32[]{:S(2)}) collective-permute-start(bf16[64,768]{1,0:T(8,128)(2,1)S(1)} %get-tuple-element.97), channel_id=1, source_target_pairs={{0,2},{1,3},{2,0},{3,1},{4,6},{5,7},{6,4},{7,5},{8,10},{9,11},{10,... | collective-permute-start | bytes 294920 | tf_op jit(solution)/shard_map/reduce_ring_0/ppermute | solution.py:33
  65.8 18.3 %collective-permute-start.15 = (bf16[64,768]{1,0:T(8,128)(2,1)S(1)}, bf16[64,768]{1,0:T(8,128)(2,1)S(1)}, u32[]{:S(2)}, u32[]{:S(2)}) collective-permute-start(bf16[64,768]{1,0:T(8,128)(2,1)S(1)} %get-tuple-element.98), channel_id=1, source_target_pairs={{0,18},{1,19},{2,16},{3,17},{4,22},{5,23},{6,20},{7,21},{8,26},{9,... | collective-permute-start | bytes 294920 | tf_op jit(solution)/shard_map/reduce_ring_0/ppermute | solution.py:33
  72.2 11.8 %collective-permute-start.14 = (bf16[64,768]{1,0:T(8,128)(2,1)S(1)}, bf16[64,768]{1,0:T(8,128)(2,1)S(1)}, u32[]{:S(2)}, u32[]{:S(2)}) collective-permute-start(bf16[64,768]{1,0:T(8,128)(2,1)S(1)} %get-tuple-element.99), channel_id=1, source_target_pairs={{0,16},{1,17},{2,18},{3,19},{4,20},{5,21},{6,22},{7,23},{8,24},{9,... | collective-permute-start | bytes 294920 | tf_op jit(solution)/shard_map/reduce_ring_0/ppermute | solution.py:33
  82.7 4.8 %collective-permute-start.19 = (bf16[256,768]{1,0:T(8,128)(2,1)S(1)}, bf16[256,768]{1,0:T(8,128)(2,1)S(1)}, u32[]{:S(2)}, u32[]{:S(2)}) collective-permute-start(bf16[256,768]{1,0:T(8,128)(2,1)S(1)} %get-tuple-element.62), channel_id=1, source_target_pairs={{0,1},{1,0},{2,3},{3,2},{4,5},{5,4},{6,7},{7,6},{8,9},{9,8},{10,11... | collective-permute-start | bytes 1179656 | tf_op jit(solution)/shard_map/reduce_core_1/ppermute | solution.py:33
  84.2 4.5 %collective-permute-start.18 = (bf16[64,768]{1,0:T(8,128)(2,1)S(1)}, bf16[64,768]{1,0:T(8,128)(2,1)S(1)}, u32[]{:S(2)}, u32[]{:S(2)}) collective-permute-start(bf16[64,768]{1,0:T(8,128)(2,1)S(1)} %pad_maximum_fusion.6), channel_id=1, source_target_pairs={{0,18},{1,19},{2,16},{3,17},{4,22},{5,23},{6,20},{7,21},{8,26},{9,... | collective-permute-start | bytes 294920 | tf_op jit(solution)/shard_map/gather_ring_0/ppermute | solution.py:33
  84.3 8.3 %collective-permute-start.17 = (bf16[64,768]{1,0:T(8,128)(2,1)S(1)}, bf16[64,768]{1,0:T(8,128)(2,1)S(1)}, u32[]{:S(2)}, u32[]{:S(2)}) collective-permute-start(bf16[64,768]{1,0:T(8,128)(2,1)S(1)} %pad_maximum_fusion.6), channel_id=1, source_target_pairs={{0,16},{1,17},{2,18},{3,19},{4,20},{5,21},{6,22},{7,23},{8,24},{9,... | collective-permute-start | bytes 294920 | tf_op jit(solution)/shard_map/gather_ring_0/ppermute | solution.py:33
  85.4 7.3 %collective-permute-start.16 = (bf16[64,768]{1,0:T(8,128)(2,1)S(1)}, bf16[64,768]{1,0:T(8,128)(2,1)S(1)}, u32[]{:S(2)}, u32[]{:S(2)}) collective-permute-start(bf16[64,768]{1,0:T(8,128)(2,1)S(1)} %pad_maximum_fusion.6), channel_id=1, source_target_pairs={{0,2},{1,3},{2,0},{3,1},{4,6},{5,7},{6,4},{7,5},{8,10},{9,11},{10,... | collective-permute-start | bytes 294920 | tf_op jit(solution)/shard_map/gather_ring_0/ppermute | solution.py:33
  87.7 6.7 %collective-permute-start.20 = (bf16[64,768]{1,0:T(8,128)(2,1)S(1)}, bf16[64,768]{1,0:T(8,128)(2,1)S(1)}, u32[]{:S(2)}, u32[]{:S(2)}) collective-permute-start(bf16[64,768]{1,0:T(8,128)(2,1)S(1)} %get-tuple-element.100), channel_id=1, source_target_pairs={{0,2},{1,3},{2,0},{3,1},{4,6},{5,7},{6,4},{7,5},{8,10},{9,11},{10,... | collective-permute-start | bytes 294920 | tf_op jit(solution)/shard_map/reduce_ring_1/ppermute | solution.py:33
  87.8 6.6 %collective-permute-start.22 = (bf16[64,768]{1,0:T(8,128)(2,1)S(1)}, bf16[64,768]{1,0:T(8,128)(2,1)S(1)}, u32[]{:S(2)}, u32[]{:S(2)}) collective-permute-start(bf16[64,768]{1,0:T(8,128)(2,1)S(1)} %get-tuple-element.101), channel_id=1, source_target_pairs={{0,18},{1,19},{2,16},{3,17},{4,22},{5,23},{6,20},{7,21},{8,26},{9,... | collective-permute-start | bytes 294920 | tf_op jit(solution)/shard_map/reduce_ring_1/ppermute | solution.py:33
  88.7 7.0 %collective-permute-start.21 = (bf16[64,768]{1,0:T(8,128)(2,1)S(1)}, bf16[64,768]{1,0:T(8,128)(2,1)S(1)}, u32[]{:S(2)}, u32[]{:S(2)}) collective-permute-start(bf16[64,768]{1,0:T(8,128)(2,1)S(1)} %get-tuple-element.102), channel_id=1, source_target_pairs={{0,16},{1,17},{2,18},{3,19},{4,20},{5,21},{6,22},{7,23},{8,24},{9,... | collective-permute-start | bytes 294920 | tf_op jit(solution)/shard_map/reduce_ring_1/ppermute | solution.py:33
  95.8 3.7 %collective-permute-start.23 = (bf16[256,768]{1,0:T(8,128)(2,1)S(1)}, bf16[256,768]{1,0:T(8,128)(2,1)S(1)}, u32[]{:S(2)}, u32[]{:S(2)}) collective-permute-start(bf16[256,768]{1,0:T(8,128)(2,1)S(1)} %pad_maximum_fusion.2.da), channel_id=1, source_target_pairs={{0,1},{1,0},{2,3},{3,2},{4,5},{5,4},{6,7},{7,6},{8,9},{9,8},{10,11... | collective-permute-start | bytes 1179656 | tf_op jit(solution)/shard_map/gather_core_0/ppermute | solution.py:33
  100.9 12.5 %collective-permute-start.24 = (bf16[2,2,3,128,128]{4,3,2,1,0:T(8,128)(2,1)S(1)}, bf16[2,2,3,128,128]{4,3,2,1,0:T(8,128)(2,1)S(1)}, u32[]{:S(2)}, u32[]{:S(2)}) collective-permute-start(bf16[2,2,3,128,128]{4,3,2,1,0:T(8,128)(2,1)S(1)} %get-tuple-element.65), channel_id=1, source_target_pairs={{0,4},{1,5},{2,6},{3,7},{4,8},{5,9},{6,10},{7,11},{8,12},{9,13},{1... | collective-permute-start | bytes 1179656 | tf_op jit(solution)/shard_map/grads_x_0/ppermute | solution.py:33
  102.0 11.4 %collective-permute-start.25 = (bf16[2,2,3,128,128]{4,3,2,1,0:T(8,128)(2,1)S(1)}, bf16[2,2,3,128,128]{4,3,2,1,0:T(8,128)(2,1)S(1)}, u32[]{:S(2)}, u32[]{:S(2)}) collective-permute-start(bf16[2,2,3,128,128]{4,3,2,1,0:T(8,128)(2,1)S(1)} %get-tuple-element.66), channel_id=1, source_target_pairs={{0,12},{1,13},{2,14},{3,15},{4,0},{5,1},{6,2},{7,3},{8,4},{9,5},{1... | collective-permute-start | bytes 1179656 | tf_op jit(solution)/shard_map/grads_x_0/ppermute | solution.py:33
  103.6 17.8 %collective-permute-start.26 = (bf16[2,2,3,128,128]{4,3,2,1,0:T(8,128)(2,1)S(1)}, bf16[2,2,3,128,128]{4,3,2,1,0:T(8,128)(2,1)S(1)}, u32[]{:S(2)}, u32[]{:S(2)}) collective-permute-start(bf16[2,2,3,128,128]{4,3,2,1,0:T(8,128)(2,1)S(1)} %get-tuple-element.67), channel_id=1, source_target_pairs={{0,8},{1,9},{2,10},{3,11},{4,12},{5,13},{6,14},{7,15},{8,0},{9,1},... | collective-permute-start | bytes 1179656 | tf_op jit(solution)/shard_map/grads_x_0/ppermute | solution.py:33
  104.8 3.8 %collective-permute-start.31 = (bf16[64,768]{1,0:T(8,128)(2,1)S(1)}, bf16[64,768]{1,0:T(8,128)(2,1)S(1)}, u32[]{:S(2)}, u32[]{:S(2)}) collective-permute-start(bf16[64,768]{1,0:T(8,128)(2,1)S(1)} %pad_maximum_fusion.7), channel_id=1, source_target_pairs={{0,18},{1,19},{2,16},{3,17},{4,22},{5,23},{6,20},{7,21},{8,26},{9,... | collective-permute-start | bytes 294920 | tf_op jit(solution)/shard_map/gather_ring_1/ppermute | solution.py:33
  105.6 5.3 %collective-permute-start.30 = (bf16[64,768]{1,0:T(8,128)(2,1)S(1)}, bf16[64,768]{1,0:T(8,128)(2,1)S(1)}, u32[]{:S(2)}, u32[]{:S(2)}) collective-permute-start(bf16[64,768]{1,0:T(8,128)(2,1)S(1)} %pad_maximum_fusion.7), channel_id=1, source_target_pairs={{0,16},{1,17},{2,18},{3,19},{4,20},{5,21},{6,22},{7,23},{8,24},{9,... | collective-permute-start | bytes 294920 | tf_op jit(solution)/shard_map/gather_ring_1/ppermute | solution.py:33
  108.6 4.8 %collective-permute-start.29 = (bf16[64,768]{1,0:T(8,128)(2,1)S(1)}, bf16[64,768]{1,0:T(8,128)(2,1)S(1)}, u32[]{:S(2)}, u32[]{:S(2)}) collective-permute-start(bf16[64,768]{1,0:T(8,128)(2,1)S(1)} %pad_maximum_fusion.7), channel_id=1, source_target_pairs={{0,2},{1,3},{2,0},{3,1},{4,6},{5,7},{6,4},{7,5},{8,10},{9,11},{10,... | collective-permute-start | bytes 294920 | tf_op jit(solution)/shard_map/gather_ring_1/ppermute | solution.py:33
  121.4 2.6 %collective-permute-start.32 = (bf16[256,768]{1,0:T(8,128)(2,1)S(1)}, bf16[256,768]{1,0:T(8,128)(2,1)S(1)}, u32[]{:S(2)}, u32[]{:S(2)}) collective-permute-start(bf16[256,768]{1,0:T(8,128)(2,1)S(1)} %pad_maximum_fusion.3.da.ea), channel_id=1, source_target_pairs={{0,1},{1,0},{2,3},{3,2},{4,5},{5,4},{6,7},{7,6},{8,9},{9,8},{10,11... | collective-permute-start | bytes 1179656 | tf_op jit(solution)/shard_map/gather_core_1/ppermute | solution.py:33
  127.1 26.0 %collective-permute-start.36 = (bf16[2,256,1024]{2,1,0:T(8,128)(2,1)S(1)}, bf16[2,256,1024]{2,1,0:T(8,128)(2,1)S(1)}, u32[]{:S(2)}, u32[]{:S(2)}) collective-permute-start(bf16[2,256,1024]{2,1,0:T(8,128)(2,1)S(1)} %get-tuple-element.78), channel_id=1, source_target_pairs={{0,16},{1,17},{2,18},{3,19},{4,20},{5,21},{6,22},{7,23},{8,24},{9,... | collective-permute-start | bytes 3145736 | tf_op jit(solution)/shard_map/output_swap/ppermute | solution.py:33
  128.8 12.6 %collective-permute-start.33 = (bf16[2,2,3,128,128]{4,3,2,1,0:T(8,128)(2,1)S(1)}, bf16[2,2,3,128,128]{4,3,2,1,0:T(8,128)(2,1)S(1)}, u32[]{:S(2)}, u32[]{:S(2)}) collective-permute-start(bf16[2,2,3,128,128]{4,3,2,1,0:T(8,128)(2,1)S(1)} %get-tuple-element.70), channel_id=1, source_target_pairs={{0,4},{1,5},{2,6},{3,7},{4,8},{5,9},{6,10},{7,11},{8,12},{9,13},{1... | collective-permute-start | bytes 1179656 | tf_op jit(solution)/shard_map/grads_x_1/ppermute | solution.py:33
  129.6 15.7 %collective-permute-start.34 = (bf16[2,2,3,128,128]{4,3,2,1,0:T(8,128)(2,1)S(1)}, bf16[2,2,3,128,128]{4,3,2,1,0:T(8,128)(2,1)S(1)}, u32[]{:S(2)}, u32[]{:S(2)}) collective-permute-start(bf16[2,2,3,128,128]{4,3,2,1,0:T(8,128)(2,1)S(1)} %get-tuple-element.71), channel_id=1, source_target_pairs={{0,12},{1,13},{2,14},{3,15},{4,0},{5,1},{6,2},{7,3},{8,4},{9,5},{1... | collective-permute-start | bytes 1179656 | tf_op jit(solution)/shard_map/grads_x_1/ppermute | solution.py:33
  131.4 17.7 %collective-permute-start.35 = (bf16[2,2,3,128,128]{4,3,2,1,0:T(8,128)(2,1)S(1)}, bf16[2,2,3,128,128]{4,3,2,1,0:T(8,128)(2,1)S(1)}, u32[]{:S(2)}, u32[]{:S(2)}) collective-permute-start(bf16[2,2,3,128,128]{4,3,2,1,0:T(8,128)(2,1)S(1)} %get-tuple-element.72), channel_id=1, source_target_pairs={{0,8},{1,9},{2,10},{3,11},{4,12},{5,13},{6,14},{7,15},{8,0},{9,1},... | collective-permute-start | bytes 1179656 | tf_op jit(solution)/shard_map/grads_x_1/ppermute | solution.py:33
  132.4 43.6 %collective-permute-start.27 = (bf16[2,3,128,128]{3,2,1,0:T(8,128)(2,1)S(1)}, bf16[2,3,128,128]{3,2,1,0:T(8,128)(2,1)S(1)}, u32[]{:S(2)}, u32[]{:S(2)}) collective-permute-start(bf16[2,3,128,128]{3,2,1,0:T(8,128)(2,1)S(1)} %get-tuple-element.93), channel_id=1, source_target_pairs={{0,0},{32,1},{64,2},{96,3},{4,4},{36,5},{68,6},{100,7},{8,8},{40,9... | collective-permute-start | bytes 589832 | tf_op jit(solution)/shard_map/grads_turn_0/ppermute | solution.py:37
  141.3 34.7 %collective-permute-start.28 = (bf16[2,3,128,128]{3,2,1,0:T(8,128)(2,1)S(1)}, bf16[2,3,128,128]{3,2,1,0:T(8,128)(2,1)S(1)}, u32[]{:S(2)}, u32[]{:S(2)}) collective-permute-start(bf16[2,3,128,128]{3,2,1,0:T(8,128)(2,1)S(1)} %get-tuple-element.94), channel_id=1, source_target_pairs={{128,0},{160,1},{192,2},{224,3},{132,4},{164,5},{196,6},{228,7},{1... | collective-permute-start | bytes 589832 | tf_op jit(solution)/shard_map/grads_turn_0/ppermute | solution.py:37
  153.1 30.6 %collective-permute-start.37 = (bf16[2,3,128,128]{3,2,1,0:T(8,128)(2,1)S(1)}, bf16[2,3,128,128]{3,2,1,0:T(8,128)(2,1)S(1)}, u32[]{:S(2)}, u32[]{:S(2)}) collective-permute-start(bf16[2,3,128,128]{3,2,1,0:T(8,128)(2,1)S(1)} %get-tuple-element.95), channel_id=1, source_target_pairs={{64,0},{96,1},{0,2},{32,3},{68,4},{100,5},{4,6},{36,7},{72,8},{104... | collective-permute-start | bytes 589832 | tf_op jit(solution)/shard_map/grads_turn_1/ppermute | solution.py:37
  171.7 14.0 %collective-permute-start.38 = (bf16[2,3,128,128]{3,2,1,0:T(8,128)(2,1)S(1)}, bf16[2,3,128,128]{3,2,1,0:T(8,128)(2,1)S(1)}, u32[]{:S(2)}, u32[]{:S(2)}) collective-permute-start(bf16[2,3,128,128]{3,2,1,0:T(8,128)(2,1)S(1)} %get-tuple-element.96), channel_id=1, source_target_pairs={{192,0},{224,1},{128,2},{160,3},{196,4},{228,5},{132,6},{164,7},{2... | collective-permute-start | bytes 589832 | tf_op jit(solution)/shard_map/grads_turn_1/ppermute | solution.py:37
  185.8 1.5 collective-permute-start.39

commit v5 on v3

--- a/solution.py
+++ b/solution.py
@@ -46,7 +46,7 @@
 
 
 def along_x(step):
-    return lambda z, h, x, l, c: (z, h, (x + step) % NX, l, c)
+    return lambda z, h, x, l, c: (z, h, x ^ step, l, c)
 
 
 def along_y(k):
@@ -55,7 +55,7 @@
 
 def turn(f, g):
     def move(z, h, x, l, c):
-        return 4 * ((z % 2) ^ f) + 2 * (l ^ g) + c, h, x, z // 4, (z // 2) % 2
+        return 4 * (l ^ g) + 2 * c + ((z % 2) ^ f), h, x, z // 4, (z // 2) % 2
 
     return move
 
@@ -97,7 +97,7 @@
             rows = pl.multiple_of((t ^ (2 * ol + oc)) * sub, sub)
             for r in range(2):
                 for j in range(NX):
-                    s = lax.rem(x + j, NX)
+                    s = x ^ j
 
                     def lanes(half, r=r, s=s):
                         return pl.multiple_of((((r ^ b) * NH + half) * NX + s) * fb, fb)
@@ -185,7 +185,7 @@
 def shards(tokens, gate_weight, up_weight, down_weight, cotangent):
     dp, t = lax.axis_index("dp"), lax.axis_index("tensor")
     z, h, x = dp // (NH * NX), (dp // NX) % NH, dp % NX
-    where = jnp.stack([t, h, x, z // 4]).astype(jnp.int32)
+    where = jnp.stack([t, h, x, z % 2]).astype(jnp.int32)
     fb = gate_weight.shape[0]
     tb = tokens.shape[0]
     sub = tb // 4
@@ -197,15 +197,16 @@
         pair = jnp.stack([block, send(block, swap_core)])
 
     with jax.named_scope("weights_turn"):
-        column = jnp.stack([send(pair, turn(f, g)) for f in range(2) for g in range(2)])
+        turned = [send(pair, turn(f, g)) for f in range(2) for g in range(2)]
+        column = jnp.stack(turned)
     where, tokens, cotangent, _ = lax.optimization_barrier((where, tokens, cotangent, pair))
     with jax.named_scope("weights_x"):
-        columns = [column] + [send(column, along_x(-j)) for j in range(1, NX)]
+        columns = [column] + [send(column, along_x(j)) for j in range(1, NX)]
     with jax.named_scope("pick"):
         picked = lax.dynamic_slice(tokens, (0, t * quarter), (tb, quarter))
         own, oth = call(pick_body, [((2, tb, wide), BF)] * 2, [picked, cotangent], 0, where)
     with jax.named_scope("input_swap"):
-        swapped = send(after(oth, column), swap_hi)
+        swapped = send(after(oth, turned[0], turned[2]), swap_hi)
     with jax.named_scope("join"):
         tok, cot = call(join_body, [((2 * tb, wide), BF)] * 2, [own, swapped])
 
@@ -257,7 +258,6 @@
         swapped = send(oth, swap_hi)
     with jax.named_scope("place"):
         layer_out, token_grad = call(place_body, [((tb, quarter), BF)] * 2, [own, swapped], 0, where)
-    p1, p3, q1, q3, q2, oth = lax.optimization_barrier((p1, p3, q1, q3, q2, oth))
     with jax.named_scope("grads_x_1"):
         q1, q3, q2 = send(q1, along_x(1)), send(q3, along_x(3)), send(q2, along_x(2))
     back = returned(0, summed((p1, p3, p2), p0))

time: 182 us -> 171 us (0.940)
  waiting for transfers between devices: 112 us -> 97.7 us
  starting transfers between devices: 55.1 us -> 57.2 us
    ppermute x25, waiting for transfers between devices: 88.6 us -> 79.4 us  [send(): return lax.ppermute(value, AXES, pairs_of(move))]
    ppermute x4, waiting for transfers between devices: 23.4 us -> 18.2 us  [send_back(): return lax.ppermute(value, AXES, [(b, a) for a, b in pairs_of(move)])]
    ppermute x25, starting transfers between devices: 37.3 us -> 41.5 us  [send(): return lax.ppermute(value, AXES, pairs_of(move))]
    ppermute x4, starting transfers between devices: 17.8 us -> 15.7 us  [send_back(): return lax.ppermute(value, AXES, [(b, a) for a, b in pairs_of(move)])]
  transfers between devices with their start and end apart: 29 -> 29, of which waited for: 18 -> 22; matrix products, arithmetic and copies ran while one was open for 1% -> 1% of each run, Pallas kernels for 4% -> 4%
where the time goes in v5:
time: 171 us; the launch traced here: 170 us
  waiting for transfers between devices  97.7 us (57%)
  starting transfers between devices  57.2 us (33%)
  Pallas kernels  9.87 us (6%)
  local copies, waits for them, and re-layouts  2.11 us (1%)
  other arithmetic  2.09 us (1%)
    ppermute x25, waiting for transfers between devices, send(): return lax.ppermute(value, AXES, pairs_of(move))  79.4 us
    ppermute x25, starting transfers between devices, send(): return lax.ppermute(value, AXES, pairs_of(move))  41.5 us
    ppermute x4, waiting for transfers between devices, send_back(): return lax.ppermute(value, AXES, [(b, a) for a, b in pairs_of(move)])  18.2 us
    ppermute x4, starting transfers between devices, send_back(): return lax.ppermute(value, AXES, [(b, a) for a, b in pairs_of(move)])  15.7 us
    pallas_call x7, Pallas kernels, call(): pl.pallas_call(body, out_shape=[jax.ShapeDtypeStruct(s, d) for s, d in sh...  9.87 us
  transfers between devices with their start and end apart: 29, of which 22 were waited for; matrix products, arithmetic and copies ran while one was open for 1% of the time, Pallas kernels for 4%

profile of v5, /device:TPU:9, one launch (start us, length us, event | category | flops | bytes accessed | tf_op | source)
XLA Modules:
  0.0 169.9 jit_solution(13383054075630227498)
XLA Ops:
  0.6 0.9 fusion.3
  1.5 0.8 collective-permute-start
  2.4 0.9 collective-permute-done
  3.3 4.5 %collective-permute-start.5 = (bf16[2,3,128,128]{3,2,1,0:T(8,128)(2,1)S(1)}, bf16[2,3,128,128]{3,2,1,0:T(8,128)(2,1)S(1)}, u32[]{:S(2)}, u32[]{:S(2)}) collective-permute-start(bf16[2,3,128,128]{3,2,1,0:T(8,128)(2,1)S(1)} %pad_maximum_fusion.2), channel_id=1, source_target_pairs={{0,160},{1,224},{2,32},{3,96},{4,164},{5,228},{6,36},{7,100},{8,16... | collective-permute-start | bytes 589832 | tf_op jit(solution)/shard_map/weights_turn/ppermute | solution.py:33
  7.8 3.3 %collective-permute-start.4 = (bf16[2,3,128,128]{3,2,1,0:T(8,128)(2,1)S(1)}, bf16[2,3,128,128]{3,2,1,0:T(8,128)(2,1)S(1)}, u32[]{:S(2)}, u32[]{:S(2)}) collective-permute-start(bf16[2,3,128,128]{3,2,1,0:T(8,128)(2,1)S(1)} %pad_maximum_fusion.2), channel_id=1, source_target_pairs={{0,128},{1,192},{2,0},{3,64},{4,132},{5,196},{6,4},{7,68},{8,136},... | collective-permute-start | bytes 589832 | tf_op jit(solution)/shard_map/weights_turn/ppermute | solution.py:33
  11.2 0.6 collective-permute-start.2
  11.7 5.6 %collective-permute-start.1 = (bf16[2,3,128,128]{3,2,1,0:T(8,128)(2,1)S(1)}, bf16[2,3,128,128]{3,2,1,0:T(8,128)(2,1)S(1)}, u32[]{:S(2)}, u32[]{:S(2)}) collective-permute-start(bf16[2,3,128,128]{3,2,1,0:T(8,128)(2,1)S(1)} %pad_maximum_fusion.2), channel_id=1, source_target_pairs={{0,0},{1,64},{2,128},{3,192},{4,4},{5,68},{6,132},{7,196},{8,8},{9... | collective-permute-start | bytes 589832 | tf_op jit(solution)/shard_map/weights_turn/ppermute | solution.py:33
  17.4 1.3 constant_dynamic-slice_fusion.tok
  18.7 1.1 pick.1
  19.8 8.4 %collective-permute-done.2 = bf16[2,3,128,128]{3,2,1,0:T(8,128)(2,1)S(1)} collective-permute-done((bf16[2,3,128,128]{3,2,1,0:T(8,128)(2,1)S(1)}, bf16[2,3,128,128]{3,2,1,0:T(8,128)(2,1)S(1)}, u32[]{:S(2)}, u32[]{:S(2)}) %collective-permute-start.2) | collective-permute-done | bytes 196640 | tf_op jit(solution)/shard_map/weights_turn/ppermute | solution.py:33
  28.2 2.1 %collective-permute-done.1 = bf16[2,3,128,128]{3,2,1,0:T(8,128)(2,1)S(1)} collective-permute-done((bf16[2,3,128,128]{3,2,1,0:T(8,128)(2,1)S(1)}, bf16[2,3,128,128]{3,2,1,0:T(8,128)(2,1)S(1)}, u32[]{:S(2)}, u32[]{:S(2)}) %collective-permute-start.1) | collective-permute-done | bytes 196640 | tf_op jit(solution)/shard_map/weights_turn/ppermute | solution.py:33
  30.3 2.2 %collective-permute-start.3 = (bf16[2,256,1024]{2,1,0:T(8,128)(2,1)S(1)}, bf16[2,256,1024]{2,1,0:T(8,128)(2,1)S(1)}, u32[]{:S(2)}, u32[]{:S(2)}) collective-permute-start(bf16[2,256,1024]{2,1,0:T(8,128)(2,1)S(1)} %get-tuple-element.39), channel_id=1, source_target_pairs={{0,16},{1,17},{2,18},{3,19},{4,20},{5,21},{6,22},{7,23},{8,24},{9,... | collective-permute-start | bytes 3145736 | tf_op jit(solution)/shard_map/input_swap/ppermute | solution.py:33
  32.5 0.1 pad_maximum_fusion.refs_0_
  32.6 2.6 %collective-permute-start.8 = (bf16[4,2,3,128,128]{4,3,2,1,0:T(8,128)(2,1)S(1)}, bf16[4,2,3,128,128]{4,3,2,1,0:T(8,128)(2,1)S(1)}, u32[]{:S(2)}, u32[]{:S(2)}) collective-permute-start(bf16[4,2,3,128,128]{4,3,2,1,0:T(8,128)(2,1)S(1)} %pad_maximum_fusion.refs_0_), channel_id=1, source_target_pairs={{0,12},{1,13},{2,14},{3,15},{4,8},{5,9},{6,10},{7,11},{8,4},{9,5},... | collective-permute-start | bytes 2359304 | tf_op jit(solution)/shard_map/weights_x/ppermute | solution.py:33
  35.2 0.5 collective-permute-start.7
  35.7 0.3 collective-permute-start.6
  36.0 20.4 %collective-permute-done.3.far = bf16[2,256,1024]{2,1,0:T(8,128)(2,1)S(1)} collective-permute-done((bf16[2,256,1024]{2,1,0:T(8,128)(2,1)S(1)}, bf16[2,256,1024]{2,1,0:T(8,128)(2,1)S(1)}, u32[]{:S(2)}, u32[]{:S(2)}) %collective-permute-start.3) | collective-permute-done | bytes 1048608 | tf_op jit(solution)/shard_map/input_swap/ppermute | solution.py:33
  56.4 0.1 join.1
  56.5 13.2 %collective-permute-done.8.refs_3_ = bf16[4,2,3,128,128]{4,3,2,1,0:T(8,128)(2,1)S(1)} collective-permute-done((bf16[4,2,3,128,128]{4,3,2,1,0:T(8,128)(2,1)S(1)}, bf16[4,2,3,128,128]{4,3,2,1,0:T(8,128)(2,1)S(1)}, u32[]{:S(2)}, u32[]{:S(2)}) %collective-permute-start.8) | collective-permute-done | bytes 786464 | tf_op jit(solution)/shard_map/weights_x/ppermute | solution.py:33
  69.7 0.3 collective-permute-done.6.refs_1_
  70.0 1.9 %forward.1 = (bf16[1024,1024]{1,0:T(8,128)(2,1)S(1)}, bf16[512,1024]{1,0:T(8,128)(2,1)S(1)}, f32[256,1536]{1,0:T(8,128)S(1)}, bf16[256,1536]{1,0:T(8,128)(2,1)S(1)}) custom-call(bf16[512,1024]{1,0:T(8,128)(2,1)S(1)} %get-tuple-element.40.tok, bf16[512,1024]{1,0:T(8,128)(2,1)S(1)} %get-tuple-element.41.cot, ...), custom_call_target="tpu_custom_call" | custom-call | flops 1610612736 | bytes 10747904 | tf_op jit(solution)/shard_map/forward/pallas_call | solution.py:83
  71.9 1.4 collective-permute-start.9
  73.3 1.9 %collective-permute-done.9 = bf16[256,1536]{1,0:T(8,128)(2,1)S(1)} collective-permute-done((bf16[256,1536]{1,0:T(8,128)(2,1)S(1)}, bf16[256,1536]{1,0:T(8,128)(2,1)S(1)}, u32[]{:S(2)}, u32[]{:S(2)}) %collective-permute-start.9) | collective-permute-done | bytes 786464 | tf_op jit(solution)/shard_map/ppermute | solution.py:33
  75.3 0.3 fusion.4
  75.6 0.1 collective-permute-start.10
  75.7 1.0 collective-permute-start.12
  76.7 2.2 %collective-permute-start.11 = (bf16[64,1536]{1,0:T(8,128)(2,1)S(1)}, bf16[64,1536]{1,0:T(8,128)(2,1)S(1)}, u32[]{:S(2)}, u32[]{:S(2)}) collective-permute-start(bf16[64,1536]{1,0:T(8,128)(2,1)S(1)} %get-tuple-element.67), channel_id=1, source_target_pairs={{0,16},{1,17},{2,18},{3,19},{4,20},{5,21},{6,22},{7,23},{8,24},{9,... | collective-permute-start | bytes 589832 | tf_op jit(solution)/shard_map/ppermute | solution.py:33
  78.9 2.9 %collective-permute-done.10 = bf16[64,1536]{1,0:T(8,128)(2,1)S(1)} collective-permute-done((bf16[64,1536]{1,0:T(8,128)(2,1)S(1)}, bf16[64,1536]{1,0:T(8,128)(2,1)S(1)}, u32[]{:S(2)}, u32[]{:S(2)}) %collective-permute-start.10) | collective-permute-done | bytes 196640 | tf_op jit(solution)/shard_map/ppermute | solution.py:33
  81.8 0.6 collective-permute-done.12
  82.4 3.3 %collective-permute-done.11 = bf16[64,1536]{1,0:T(8,128)(2,1)S(1)} collective-permute-done((bf16[64,1536]{1,0:T(8,128)(2,1)S(1)}, bf16[64,1536]{1,0:T(8,128)(2,1)S(1)}, u32[]{:S(2)}, u32[]{:S(2)}) %collective-permute-start.11) | collective-permute-done | bytes 196640 | tf_op jit(solution)/shard_map/ppermute | solution.py:33
  85.6 0.1 fusion.1
  85.8 1.6 collective-permute-start.15
  87.5 3.0 %collective-permute-start.14 = (bf16[64,1536]{1,0:T(8,128)(2,1)S(1)}, bf16[64,1536]{1,0:T(8,128)(2,1)S(1)}, u32[]{:S(2)}, u32[]{:S(2)}) collective-permute-start(bf16[64,1536]{1,0:T(8,128)(2,1)S(1)} %pad_maximum_fusion.3), channel_id=1, source_target_pairs={{0,16},{1,17},{2,18},{3,19},{4,20},{5,21},{6,22},{7,23},{8,24},{9,... | collective-permute-start | bytes 589832 | tf_op jit(solution)/shard_map/ppermute | solution.py:33
  90.4 2.7 %collective-permute-done.15 = bf16[64,1536]{1,0:T(8,128)(2,1)S(1)} collective-permute-done((bf16[64,1536]{1,0:T(8,128)(2,1)S(1)}, bf16[64,1536]{1,0:T(8,128)(2,1)S(1)}, u32[]{:S(2)}, u32[]{:S(2)}) %collective-permute-start.15) | collective-permute-done | bytes 196640 | tf_op jit(solution)/shard_map/ppermute | solution.py:33
  93.2 0.8 collective-permute-done.14
  93.9 3.4 %collective-permute-done.13 = bf16[64,1536]{1,0:T(8,128)(2,1)S(1)} collective-permute-done((bf16[64,1536]{1,0:T(8,128)(2,1)S(1)}, bf16[64,1536]{1,0:T(8,128)(2,1)S(1)}, u32[]{:S(2)}, u32[]{:S(2)}) %collective-permute-start.13) | collective-permute-done | bytes 196640 | tf_op jit(solution)/shard_map/ppermute | solution.py:33
  97.4 2.7 %collective-permute-start.16 = (bf16[256,1536]{1,0:T(8,128)(2,1)S(1)}, bf16[256,1536]{1,0:T(8,128)(2,1)S(1)}, u32[]{:S(2)}, u32[]{:S(2)}) collective-permute-start(bf16[256,1536]{1,0:T(8,128)(2,1)S(1)} %pad_maximum_fusion.1.da), channel_id=1, source_target_pairs={{0,1},{1,0},{2,3},{3,2},{4,5},{5,4},{6,7},{7,6},{8,9},{9,8},{10,11... | collective-permute-start | bytes 2359304 | tf_op jit(solution)/shard_map/ppermute | solution.py:33
  100.1 1.9 %collective-permute-done.16.dc = bf16[256,1536]{1,0:T(8,128)(2,1)S(1)} collective-permute-done((bf16[256,1536]{1,0:T(8,128)(2,1)S(1)}, bf16[256,1536]{1,0:T(8,128)(2,1)S(1)}, u32[]{:S(2)}, u32[]{:S(2)}) %collective-permute-start.16) | collective-permute-done | bytes 786464 | tf_op jit(solution)/shard_map/ppermute | solution.py:33
  102.0 1.3 grads.2
  103.3 1.3 collective-permute-start.17
  104.6 1.8 %collective-permute-start.18 = (bf16[2,2,3,128,128]{4,3,2,1,0:T(8,128)(2,1)S(1)}, bf16[2,2,3,128,128]{4,3,2,1,0:T(8,128)(2,1)S(1)}, u32[]{:S(2)}, u32[]{:S(2)}) collective-permute-start(bf16[2,2,3,128,128]{4,3,2,1,0:T(8,128)(2,1)S(1)} %get-tuple-element.46), channel_id=1, source_target_pairs={{0,12},{1,13},{2,14},{3,15},{4,8},{5,9},{6,10},{7,11},{8,4},{9,5},... | collective-permute-start | bytes 1179656 | tf_op jit(solution)/shard_map/grads_x_0/ppermute | solution.py:33
  106.4 0.6 collective-permute-start.19
  107.1 1.8 %outputs.1 = (bf16[2,256,1024]{2,1,0:T(8,128)(2,1)S(1)}, bf16[2,256,1024]{2,1,0:T(8,128)(2,1)S(1)}) custom-call(bf16[256,1536]{1,0:T(8,128)(2,1)S(1)} %pad_maximum_fusion.1.da, bf16[256,1536]{1,0:T(8,128)(2,1)S(1)} %collective-permute-done.16.dc, bf16[1024,1024]{1,0:T(8,128)(2,1)S(1)} %get-tuple-element.52.gu, bf16[512,1024]{1,0:T(8,128)(2,1)S(1)} %get-tuple-element.53.dn), custom_call_target="tpu_custom_call" | custom-call | flops 1610612736 | bytes 6815744 | tf_op jit(solution)/shard_map/outputs/pallas_call | solution.py:83
  108.9 1.8 %collective-permute-start.25 = (bf16[2,256,1024]{2,1,0:T(8,128)(2,1)S(1)}, bf16[2,256,1024]{2,1,0:T(8,128)(2,1)S(1)}, u32[]{:S(2)}, u32[]{:S(2)}) collective-permute-start(bf16[2,256,1024]{2,1,0:T(8,128)(2,1)S(1)} %get-tuple-element.54), channel_id=1, source_target_pairs={{0,16},{1,17},{2,18},{3,19},{4,20},{5,21},{6,22},{7,23},{8,24},{9,... | collective-permute-start | bytes 3145736 | tf_op jit(solution)/shard_map/output_swap/ppermute | solution.py:33
  110.7 1.3 grads.3
  112.0 0.9 collective-permute-start.22
  112.9 0.9 collective-permute-done.17
  113.7 2.5 %collective-permute-start.23 = (bf16[2,2,3,128,128]{4,3,2,1,0:T(8,128)(2,1)S(1)}, bf16[2,2,3,128,128]{4,3,2,1,0:T(8,128)(2,1)S(1)}, u32[]{:S(2)}, u32[]{:S(2)}) collective-permute-start(bf16[2,2,3,128,128]{4,3,2,1,0:T(8,128)(2,1)S(1)} %get-tuple-element.50), channel_id=1, source_target_pairs={{0,12},{1,13},{2,14},{3,15},{4,8},{5,9},{6,10},{7,11},{8,4},{9,5},... | collective-permute-start | bytes 1179656 | tf_op jit(solution)/shard_map/grads_x_1/ppermute | solution.py:33
  116.2 5.8 %collective-permute-done.18 = bf16[2,2,3,128,128]{4,3,2,1,0:T(8,128)(2,1)S(1)} collective-permute-done((bf16[2,2,3,128,128]{4,3,2,1,0:T(8,128)(2,1)S(1)}, bf16[2,2,3,128,128]{4,3,2,1,0:T(8,128)(2,1)S(1)}, u32[]{:S(2)}, u32[]{:S(2)}) %collective-permute-start.18) | collective-permute-done | bytes 393248 | tf_op jit(solution)/shard_map/grads_x_0/ppermute | solution.py:33
  122.0 2.4 %collective-permute-done.19 = bf16[2,2,3,128,128]{4,3,2,1,0:T(8,128)(2,1)S(1)} collective-permute-done((bf16[2,2,3,128,128]{4,3,2,1,0:T(8,128)(2,1)S(1)}, bf16[2,2,3,128,128]{4,3,2,1,0:T(8,128)(2,1)S(1)}, u32[]{:S(2)}, u32[]{:S(2)}) %collective-permute-start.19) | collective-permute-done | bytes 393248 | tf_op jit(solution)/shard_map/grads_x_0/ppermute | solution.py:33
  124.4 0.2 add_convert_fusion.1
  124.6 10.2 %collective-permute-start.20 = (bf16[2,3,128,128]{3,2,1,0:T(8,128)(2,1)S(1)}, bf16[2,3,128,128]{3,2,1,0:T(8,128)(2,1)S(1)}, u32[]{:S(2)}, u32[]{:S(2)}) collective-permute-start(bf16[2,3,128,128]{3,2,1,0:T(8,128)(2,1)S(1)} %get-tuple-element.70), channel_id=1, source_target_pairs={{0,0},{64,1},{128,2},{192,3},{4,4},{68,5},{132,6},{196,7},{8,8},{7... | collective-permute-start | bytes 589832 | tf_op jit(solution)/shard_map/grads_turn_0/ppermute | solution.py:37
  134.9 1.0 collective-permute-start.21
  135.9 6.3 %collective-permute-done.23 = bf16[2,2,3,128,128]{4,3,2,1,0:T(8,128)(2,1)S(1)} collective-permute-done((bf16[2,2,3,128,128]{4,3,2,1,0:T(8,128)(2,1)S(1)}, bf16[2,2,3,128,128]{4,3,2,1,0:T(8,128)(2,1)S(1)}, u32[]{:S(2)}, u32[]{:S(2)}) %collective-permute-start.23) | collective-permute-done | bytes 393248 | tf_op jit(solution)/shard_map/grads_x_1/ppermute | solution.py:33
  142.2 0.2 add_convert_fusion
  142.4 1.1 collective-permute-start.26
  143.6 3.3 %collective-permute-start.27 = (bf16[2,3,128,128]{3,2,1,0:T(8,128)(2,1)S(1)}, bf16[2,3,128,128]{3,2,1,0:T(8,128)(2,1)S(1)}, u32[]{:S(2)}, u32[]{:S(2)}) collective-permute-start(bf16[2,3,128,128]{3,2,1,0:T(8,128)(2,1)S(1)} %get-tuple-element.73), channel_id=1, source_target_pairs={{160,0},{224,1},{32,2},{96,3},{164,4},{228,5},{36,6},{100,7},{168,... | collective-permute-start | bytes 589832 | tf_op jit(solution)/shard_map/grads_turn_1/ppermute | solution.py:37
  146.9 2.4 %place.1 = (bf16[256,2048]{1,0:T(8,128)(2,1)}, bf16[256,2048]{1,0:T(8,128)(2,1)}) custom-call(s32[4]{0:T(128)S(1)} %pad_add_fusion.where, bf16[2,256,1024]{2,1,0:T(8,128)(2,1)S(1)} %get-tuple-element.56.own, bf16[2,256,1024]{2,1,0:T(8,128)(2,1)S(1)} %collective-permute-done.25.far), custom_call_target="tpu_custom_call" | custom-call | bytes 4194304 | tf_op jit(solution)/shard_map/place/pallas_call | solution.py:83
  149.3 7.9 %collective-permute-done.21 = bf16[2,3,128,128]{3,2,1,0:T(8,128)(2,1)S(1)} collective-permute-done((bf16[2,3,128,128]{3,2,1,0:T(8,128)(2,1)S(1)}, bf16[2,3,128,128]{3,2,1,0:T(8,128)(2,1)S(1)}, u32[]{:S(2)}, u32[]{:S(2)}) %collective-permute-start.21) | collective-permute-done | bytes 196640 | tf_op jit(solution)/shard_map/grads_turn_0/ppermute | solution.py:37
  157.2 8.0 %collective-permute-done.26 = bf16[2,3,128,128]{3,2,1,0:T(8,128)(2,1)S(1)} collective-permute-done((bf16[2,3,128,128]{3,2,1,0:T(8,128)(2,1)S(1)}, bf16[2,3,128,128]{3,2,1,0:T(8,128)(2,1)S(1)}, u32[]{:S(2)}, u32[]{:S(2)}) %collective-permute-start.26) | collective-permute-done | bytes 196640 | tf_op jit(solution)/shard_map/grads_turn_1/ppermute | solution.py:37
  165.2 2.3 %collective-permute-done.27 = bf16[2,3,128,128]{3,2,1,0:T(8,128)(2,1)S(1)} collective-permute-done((bf16[2,3,128,128]{3,2,1,0:T(8,128)(2,1)S(1)}, bf16[2,3,128,128]{3,2,1,0:T(8,128)(2,1)S(1)}, u32[]{:S(2)}, u32[]{:S(2)}) %collective-permute-start.27) | collective-permute-done | bytes 196640 | tf_op jit(solution)/shard_map/grads_turn_1/ppermute | solution.py:37
  167.5 0.1 convert_add_fusion.1
  167.7 1.4 collective-permute-done.28
  169.2 0.7 slice_bitcast_fusion.6
  (22 shorter events, 0.5 us)
Async XLA Ops:
  0.6 18.0 %copy-start = (bf16[256,2048]{1,0:T(8,128)(2,1)S(1)}, bf16[256,2048]{1,0:T(8,128)(2,1)}, u32[]{:S(2)}) copy-start(bf16[256,2048]{1,0:T(8,128)(2,1)} %cot) | copy-start | bytes 3145732
  1.5 1.7 %collective-permute-start = (bf16[3,128,128]{2,1,0:T(8,128)(2,1)S(1)}, bf16[3,128,128]{2,1,0:T(8,128)(2,1)S(1)}, u32[]{:S(2)}, u32[]{:S(2)}) collective-permute-start(bf16[3,128,128]{2,1,0:T(8,128)(2,1)S(1)} %get-tuple-element.81), channel_id=1, source_target_pairs={{0,1},{1,0},{2,3},{3,2},{4,5},{5,4},{6,7},{7,6},{8,9},{9,8},{10,11... | collective-permute-start | bytes 294920 | tf_op jit(solution)/shard_map/weights_core/ppermute | solution.py:33
  3.3 29.3 %collective-permute-start.5 = (bf16[2,3,128,128]{3,2,1,0:T(8,128)(2,1)S(1)}, bf16[2,3,128,128]{3,2,1,0:T(8,128)(2,1)S(1)}, u32[]{:S(2)}, u32[]{:S(2)}) collective-permute-start(bf16[2,3,128,128]{3,2,1,0:T(8,128)(2,1)S(1)} %pad_maximum_fusion.2), channel_id=1, source_target_pairs={{0,160},{1,224},{2,32},{3,96},{4,164},{5,228},{6,36},{7,100},{8,16... | collective-permute-start | bytes 589832 | tf_op jit(solution)/shard_map/weights_turn/ppermute | solution.py:33
  7.8 24.7 %collective-permute-start.4 = (bf16[2,3,128,128]{3,2,1,0:T(8,128)(2,1)S(1)}, bf16[2,3,128,128]{3,2,1,0:T(8,128)(2,1)S(1)}, u32[]{:S(2)}, u32[]{:S(2)}) collective-permute-start(bf16[2,3,128,128]{3,2,1,0:T(8,128)(2,1)S(1)} %pad_maximum_fusion.2), channel_id=1, source_target_pairs={{0,128},{1,192},{2,0},{3,64},{4,132},{5,196},{6,4},{7,68},{8,136},... | collective-permute-start | bytes 589832 | tf_op jit(solution)/shard_map/weights_turn/ppermute | solution.py:33
  11.2 17.0 %collective-permute-start.2 = (bf16[2,3,128,128]{3,2,1,0:T(8,128)(2,1)S(1)}, bf16[2,3,128,128]{3,2,1,0:T(8,128)(2,1)S(1)}, u32[]{:S(2)}, u32[]{:S(2)}) collective-permute-start(bf16[2,3,128,128]{3,2,1,0:T(8,128)(2,1)S(1)} %pad_maximum_fusion.2), channel_id=1, source_target_pairs={{0,32},{1,96},{2,160},{3,224},{4,36},{5,100},{6,164},{7,228},{8,40... | collective-permute-start | bytes 589832 | tf_op jit(solution)/shard_map/weights_turn/ppermute | solution.py:33
  11.7 18.6 %collective-permute-start.1 = (bf16[2,3,128,128]{3,2,1,0:T(8,128)(2,1)S(1)}, bf16[2,3,128,128]{3,2,1,0:T(8,128)(2,1)S(1)}, u32[]{:S(2)}, u32[]{:S(2)}) collective-permute-start(bf16[2,3,128,128]{3,2,1,0:T(8,128)(2,1)S(1)} %pad_maximum_fusion.2), channel_id=1, source_target_pairs={{0,0},{1,64},{2,128},{3,192},{4,4},{5,68},{6,132},{7,196},{8,8},{9... | collective-permute-start | bytes 589832 | tf_op jit(solution)/shard_map/weights_turn/ppermute | solution.py:33
  30.3 26.1 %collective-permute-start.3 = (bf16[2,256,1024]{2,1,0:T(8,128)(2,1)S(1)}, bf16[2,256,1024]{2,1,0:T(8,128)(2,1)S(1)}, u32[]{:S(2)}, u32[]{:S(2)}) collective-permute-start(bf16[2,256,1024]{2,1,0:T(8,128)(2,1)S(1)} %get-tuple-element.39), channel_id=1, source_target_pairs={{0,16},{1,17},{2,18},{3,19},{4,20},{5,21},{6,22},{7,23},{8,24},{9,... | collective-permute-start | bytes 3145736 | tf_op jit(solution)/shard_map/input_swap/ppermute | solution.py:33
  32.6 37.1 %collective-permute-start.8 = (bf16[4,2,3,128,128]{4,3,2,1,0:T(8,128)(2,1)S(1)}, bf16[4,2,3,128,128]{4,3,2,1,0:T(8,128)(2,1)S(1)}, u32[]{:S(2)}, u32[]{:S(2)}) collective-permute-start(bf16[4,2,3,128,128]{4,3,2,1,0:T(8,128)(2,1)S(1)} %pad_maximum_fusion.refs_0_), channel_id=1, source_target_pairs={{0,12},{1,13},{2,14},{3,15},{4,8},{5,9},{6,10},{7,11},{8,4},{9,5},... | collective-permute-start | bytes 2359304 | tf_op jit(solution)/shard_map/weights_x/ppermute | solution.py:33
  35.2 34.5 %collective-permute-start.7 = (bf16[4,2,3,128,128]{4,3,2,1,0:T(8,128)(2,1)S(1)}, bf16[4,2,3,128,128]{4,3,2,1,0:T(8,128)(2,1)S(1)}, u32[]{:S(2)}, u32[]{:S(2)}) collective-permute-start(bf16[4,2,3,128,128]{4,3,2,1,0:T(8,128)(2,1)S(1)} %pad_maximum_fusion.refs_0_), channel_id=1, source_target_pairs={{0,8},{1,9},{2,10},{3,11},{4,12},{5,13},{6,14},{7,15},{8,0},{9,1},... | collective-permute-start | bytes 2359304 | tf_op jit(solution)/shard_map/weights_x/ppermute | solution.py:33
  35.7 34.3 %collective-permute-start.6 = (bf16[4,2,3,128,128]{4,3,2,1,0:T(8,128)(2,1)S(1)}, bf16[4,2,3,128,128]{4,3,2,1,0:T(8,128)(2,1)S(1)}, u32[]{:S(2)}, u32[]{:S(2)}) collective-permute-start(bf16[4,2,3,128,128]{4,3,2,1,0:T(8,128)(2,1)S(1)} %pad_maximum_fusion.refs_0_), channel_id=1, source_target_pairs={{0,4},{1,5},{2,6},{3,7},{4,0},{5,1},{6,2},{7,3},{8,12},{9,13},{10,... | collective-permute-start | bytes 2359304 | tf_op jit(solution)/shard_map/weights_x/ppermute | solution.py:33
  71.9 3.4 %collective-permute-start.9 = (bf16[256,1536]{1,0:T(8,128)(2,1)S(1)}, bf16[256,1536]{1,0:T(8,128)(2,1)S(1)}, u32[]{:S(2)}, u32[]{:S(2)}) collective-permute-start(bf16[256,1536]{1,0:T(8,128)(2,1)S(1)} %get-tuple-element.43), channel_id=1, source_target_pairs={{0,1},{1,0},{2,3},{3,2},{4,5},{5,4},{6,7},{7,6},{8,9},{9,8},{10,11... | collective-permute-start | bytes 2359304 | tf_op jit(solution)/shard_map/ppermute | solution.py:33
  75.6 6.2 %collective-permute-start.10 = (bf16[64,1536]{1,0:T(8,128)(2,1)S(1)}, bf16[64,1536]{1,0:T(8,128)(2,1)S(1)}, u32[]{:S(2)}, u32[]{:S(2)}) collective-permute-start(bf16[64,1536]{1,0:T(8,128)(2,1)S(1)} %get-tuple-element.65), channel_id=1, source_target_pairs={{0,2},{1,3},{2,0},{3,1},{4,6},{5,7},{6,4},{7,5},{8,10},{9,11},{10,... | collective-permute-start | bytes 589832 | tf_op jit(solution)/shard_map/ppermute | solution.py:33
  75.7 6.7 %collective-permute-start.12 = (bf16[64,1536]{1,0:T(8,128)(2,1)S(1)}, bf16[64,1536]{1,0:T(8,128)(2,1)S(1)}, u32[]{:S(2)}, u32[]{:S(2)}) collective-permute-start(bf16[64,1536]{1,0:T(8,128)(2,1)S(1)} %get-tuple-element.66), channel_id=1, source_target_pairs={{0,18},{1,19},{2,16},{3,17},{4,22},{5,23},{6,20},{7,21},{8,26},{9,... | collective-permute-start | bytes 589832 | tf_op jit(solution)/shard_map/ppermute | solution.py:33
  76.7 8.9 %collective-permute-start.11 = (bf16[64,1536]{1,0:T(8,128)(2,1)S(1)}, bf16[64,1536]{1,0:T(8,128)(2,1)S(1)}, u32[]{:S(2)}, u32[]{:S(2)}) collective-permute-start(bf16[64,1536]{1,0:T(8,128)(2,1)S(1)} %get-tuple-element.67), channel_id=1, source_target_pairs={{0,16},{1,17},{2,18},{3,19},{4,20},{5,21},{6,22},{7,23},{8,24},{9,... | collective-permute-start | bytes 589832 | tf_op jit(solution)/shard_map/ppermute | solution.py:33
  85.8 7.3 %collective-permute-start.15 = (bf16[64,1536]{1,0:T(8,128)(2,1)S(1)}, bf16[64,1536]{1,0:T(8,128)(2,1)S(1)}, u32[]{:S(2)}, u32[]{:S(2)}) collective-permute-start(bf16[64,1536]{1,0:T(8,128)(2,1)S(1)} %pad_maximum_fusion.3), channel_id=1, source_target_pairs={{0,18},{1,19},{2,16},{3,17},{4,22},{5,23},{6,20},{7,21},{8,26},{9,... | collective-permute-start | bytes 589832 | tf_op jit(solution)/shard_map/ppermute | solution.py:33
  87.5 6.5 %collective-permute-start.14 = (bf16[64,1536]{1,0:T(8,128)(2,1)S(1)}, bf16[64,1536]{1,0:T(8,128)(2,1)S(1)}, u32[]{:S(2)}, u32[]{:S(2)}) collective-permute-start(bf16[64,1536]{1,0:T(8,128)(2,1)S(1)} %pad_maximum_fusion.3), channel_id=1, source_target_pairs={{0,16},{1,17},{2,18},{3,19},{4,20},{5,21},{6,22},{7,23},{8,24},{9,... | collective-permute-start | bytes 589832 | tf_op jit(solution)/shard_map/ppermute | solution.py:33
  90.4 6.9 %collective-permute-start.13 = (bf16[64,1536]{1,0:T(8,128)(2,1)S(1)}, bf16[64,1536]{1,0:T(8,128)(2,1)S(1)}, u32[]{:S(2)}, u32[]{:S(2)}) collective-permute-start(bf16[64,1536]{1,0:T(8,128)(2,1)S(1)} %pad_maximum_fusion.3), channel_id=1, source_target_pairs={{0,2},{1,3},{2,0},{3,1},{4,6},{5,7},{6,4},{7,5},{8,10},{9,11},{10,... | collective-permute-start | bytes 589832 | tf_op jit(solution)/shard_map/ppermute | solution.py:33
  97.4 4.6 %collective-permute-start.16 = (bf16[256,1536]{1,0:T(8,128)(2,1)S(1)}, bf16[256,1536]{1,0:T(8,128)(2,1)S(1)}, u32[]{:S(2)}, u32[]{:S(2)}) collective-permute-start(bf16[256,1536]{1,0:T(8,128)(2,1)S(1)} %pad_maximum_fusion.1.da), channel_id=1, source_target_pairs={{0,1},{1,0},{2,3},{3,2},{4,5},{5,4},{6,7},{7,6},{8,9},{9,8},{10,11... | collective-permute-start | bytes 2359304 | tf_op jit(solution)/shard_map/ppermute | solution.py:33
  103.3 10.4 %collective-permute-start.17 = (bf16[2,2,3,128,128]{4,3,2,1,0:T(8,128)(2,1)S(1)}, bf16[2,2,3,128,128]{4,3,2,1,0:T(8,128)(2,1)S(1)}, u32[]{:S(2)}, u32[]{:S(2)}) collective-permute-start(bf16[2,2,3,128,128]{4,3,2,1,0:T(8,128)(2,1)S(1)} %get-tuple-element.45), channel_id=1, source_target_pairs={{0,4},{1,5},{2,6},{3,7},{4,0},{5,1},{6,2},{7,3},{8,12},{9,13},{10,... | collective-permute-start | bytes 1179656 | tf_op jit(solution)/shard_map/grads_x_0/ppermute | solution.py:33
  104.6 17.4 %collective-permute-start.18 = (bf16[2,2,3,128,128]{4,3,2,1,0:T(8,128)(2,1)S(1)}, bf16[2,2,3,128,128]{4,3,2,1,0:T(8,128)(2,1)S(1)}, u32[]{:S(2)}, u32[]{:S(2)}) collective-permute-start(bf16[2,2,3,128,128]{4,3,2,1,0:T(8,128)(2,1)S(1)} %get-tuple-element.46), channel_id=1, source_target_pairs={{0,12},{1,13},{2,14},{3,15},{4,8},{5,9},{6,10},{7,11},{8,4},{9,5},... | collective-permute-start | bytes 1179656 | tf_op jit(solution)/shard_map/grads_x_0/ppermute | solution.py:33
  106.4 18.0 %collective-permute-start.19 = (bf16[2,2,3,128,128]{4,3,2,1,0:T(8,128)(2,1)S(1)}, bf16[2,2,3,128,128]{4,3,2,1,0:T(8,128)(2,1)S(1)}, u32[]{:S(2)}, u32[]{:S(2)}) collective-permute-start(bf16[2,2,3,128,128]{4,3,2,1,0:T(8,128)(2,1)S(1)} %get-tuple-element.47), channel_id=1, source_target_pairs={{0,8},{1,9},{2,10},{3,11},{4,12},{5,13},{6,14},{7,15},{8,0},{9,1},... | collective-permute-start | bytes 1179656 | tf_op jit(solution)/shard_map/grads_x_0/ppermute | solution.py:33
  108.9 33.5 %collective-permute-start.25 = (bf16[2,256,1024]{2,1,0:T(8,128)(2,1)S(1)}, bf16[2,256,1024]{2,1,0:T(8,128)(2,1)S(1)}, u32[]{:S(2)}, u32[]{:S(2)}) collective-permute-start(bf16[2,256,1024]{2,1,0:T(8,128)(2,1)S(1)} %get-tuple-element.54), channel_id=1, source_target_pairs={{0,16},{1,17},{2,18},{3,19},{4,20},{5,21},{6,22},{7,23},{8,24},{9,... | collective-permute-start | bytes 3145736 | tf_op jit(solution)/shard_map/output_swap/ppermute | solution.py:33
  112.0 22.9 %collective-permute-start.22 = (bf16[2,2,3,128,128]{4,3,2,1,0:T(8,128)(2,1)S(1)}, bf16[2,2,3,128,128]{4,3,2,1,0:T(8,128)(2,1)S(1)}, u32[]{:S(2)}, u32[]{:S(2)}) collective-permute-start(bf16[2,2,3,128,128]{4,3,2,1,0:T(8,128)(2,1)S(1)} %get-tuple-element.49), channel_id=1, source_target_pairs={{0,4},{1,5},{2,6},{3,7},{4,0},{5,1},{6,2},{7,3},{8,12},{9,13},{10,... | collective-permute-start | bytes 1179656 | tf_op jit(solution)/shard_map/grads_x_1/ppermute | solution.py:33
  113.7 28.4 %collective-permute-start.23 = (bf16[2,2,3,128,128]{4,3,2,1,0:T(8,128)(2,1)S(1)}, bf16[2,2,3,128,128]{4,3,2,1,0:T(8,128)(2,1)S(1)}, u32[]{:S(2)}, u32[]{:S(2)}) collective-permute-start(bf16[2,2,3,128,128]{4,3,2,1,0:T(8,128)(2,1)S(1)} %get-tuple-element.50), channel_id=1, source_target_pairs={{0,12},{1,13},{2,14},{3,15},{4,8},{5,9},{6,10},{7,11},{8,4},{9,5},... | collective-permute-start | bytes 1179656 | tf_op jit(solution)/shard_map/grads_x_1/ppermute | solution.py:33
  122.0 20.1 %collective-permute-start.24 = (bf16[2,2,3,128,128]{4,3,2,1,0:T(8,128)(2,1)S(1)}, bf16[2,2,3,128,128]{4,3,2,1,0:T(8,128)(2,1)S(1)}, u32[]{:S(2)}, u32[]{:S(2)}) collective-permute-start(bf16[2,2,3,128,128]{4,3,2,1,0:T(8,128)(2,1)S(1)} %get-tuple-element.51), channel_id=1, source_target_pairs={{0,8},{1,9},{2,10},{3,11},{4,12},{5,13},{6,14},{7,15},{8,0},{9,1},... | collective-permute-start | bytes 1179656 | tf_op jit(solution)/shard_map/grads_x_1/ppermute | solution.py:33
  124.6 24.6 %collective-permute-start.20 = (bf16[2,3,128,128]{3,2,1,0:T(8,128)(2,1)S(1)}, bf16[2,3,128,128]{3,2,1,0:T(8,128)(2,1)S(1)}, u32[]{:S(2)}, u32[]{:S(2)}) collective-permute-start(bf16[2,3,128,128]{3,2,1,0:T(8,128)(2,1)S(1)} %get-tuple-element.70), channel_id=1, source_target_pairs={{0,0},{64,1},{128,2},{192,3},{4,4},{68,5},{132,6},{196,7},{8,8},{7... | collective-permute-start | bytes 589832 | tf_op jit(solution)/shard_map/grads_turn_0/ppermute | solution.py:37
  134.9 22.3 %collective-permute-start.21 = (bf16[2,3,128,128]{3,2,1,0:T(8,128)(2,1)S(1)}, bf16[2,3,128,128]{3,2,1,0:T(8,128)(2,1)S(1)}, u32[]{:S(2)}, u32[]{:S(2)}) collective-permute-start(bf16[2,3,128,128]{3,2,1,0:T(8,128)(2,1)S(1)} %get-tuple-element.71), channel_id=1, source_target_pairs={{128,0},{192,1},{0,2},{64,3},{132,4},{196,5},{4,6},{68,7},{136,8},... | collective-permute-start | bytes 589832 | tf_op jit(solution)/shard_map/grads_turn_0/ppermute | solution.py:37
  142.4 22.7 %collective-permute-start.26 = (bf16[2,3,128,128]{3,2,1,0:T(8,128)(2,1)S(1)}, bf16[2,3,128,128]{3,2,1,0:T(8,128)(2,1)S(1)}, u32[]{:S(2)}, u32[]{:S(2)}) collective-permute-start(bf16[2,3,128,128]{3,2,1,0:T(8,128)(2,1)S(1)} %get-tuple-element.72), channel_id=1, source_target_pairs={{32,0},{96,1},{160,2},{224,3},{36,4},{100,5},{164,6},{228,7},{40,8... | collective-permute-start | bytes 589832 | tf_op jit(solution)/shard_map/grads_turn_1/ppermute | solution.py:37
  143.6 23.9 %collective-permute-start.27 = (bf16[2,3,128,128]{3,2,1,0:T(8,128)(2,1)S(1)}, bf16[2,3,128,128]{3,2,1,0:T(8,128)(2,1)S(1)}, u32[]{:S(2)}, u32[]{:S(2)}) collective-permute-start(bf16[2,3,128,128]{3,2,1,0:T(8,128)(2,1)S(1)} %get-tuple-element.73), channel_id=1, source_target_pairs={{160,0},{224,1},{32,2},{96,3},{164,4},{228,5},{36,6},{100,7},{168,... | collective-permute-start | bytes 589832 | tf_op jit(solution)/shard_map/grads_turn_1/ppermute | solution.py:37
  167.6 1.5 collective-permute-start.28

commit v6 on v5

--- a/solution.py
+++ b/solution.py
@@ -45,6 +45,10 @@
     return z, h, x, l, 1 - c
 
 
+def swap_plane(z, h, x, l, c):
+    return z ^ 1, h, x, l, c
+
+
 def along_x(step):
     return lambda z, h, x, l, c: (z, h, x ^ step, l, c)
 
@@ -53,9 +57,9 @@
     return lambda z, h, x, l, c: (z, h ^ (k // 2), x, l ^ (k % 2), c)
 
 
-def turn(f, g):
+def turn(g):
     def move(z, h, x, l, c):
-        return 4 * (l ^ g) + 2 * c + ((z % 2) ^ f), h, x, z // 4, (z // 2) % 2
+        return 4 * (l ^ g) + 2 * c + z % 2, h, x, z // 4, (z // 2) % 2
 
     return move
 
@@ -135,19 +139,19 @@
 
 
 def forward_body(tok, cot, *refs):
-    columns, (gu, dn, keep, away) = refs[:4], refs[4:]
+    columns, (gu, dn, keep, away) = refs[:8], refs[8:]
     tb = keep.shape[0]
     fb = columns[0].shape[-1]
     for f in range(2):
         for j in range(NX):
-            column = columns[j]
+            column = columns[f * NX + j]
             at = (f * NX + j) * fb
             for g in range(2):
                 for e in range(2):
                     unit = (g * 2 + e) * fb
-                    gu[at : at + fb, unit : unit + fb] = column[f * 2 + g, e, 0]
-                    gu[at : at + fb, 4 * fb + unit : 4 * fb + unit + fb] = column[f * 2 + g, e, 1]
-                    dn[unit : unit + fb, at : at + fb] = column[f * 2 + g, e, 2]
+                    gu[at : at + fb, unit : unit + fb] = column[g, e, 0]
+                    gu[at : at + fb, 4 * fb + unit : 4 * fb + unit + fb] = column[g, e, 1]
+                    dn[unit : unit + fb, at : at + fb] = column[g, e, 2]
     wide = gu.shape[1]
     away[:, :wide] = nn(tok[tb:, :], gu[...]).astype(BF)
     away[:, wide:] = nt(cot[tb:, :], dn[...]).astype(BF)
@@ -197,16 +201,22 @@
         pair = jnp.stack([block, send(block, swap_core)])
 
     with jax.named_scope("weights_turn"):
-        turned = [send(pair, turn(f, g)) for f in range(2) for g in range(2)]
-        column = jnp.stack(turned)
+        near = jnp.stack([send(pair, turn(g)) for g in range(2)])
+    with jax.named_scope("weights_plane"):
+        far = send(near, swap_plane)
     where, tokens, cotangent, _ = lax.optimization_barrier((where, tokens, cotangent, pair))
-    with jax.named_scope("weights_x"):
-        columns = [column] + [send(column, along_x(j)) for j in range(1, NX)]
     with jax.named_scope("pick"):
         picked = lax.dynamic_slice(tokens, (0, t * quarter), (tb, quarter))
         own, oth = call(pick_body, [((2, tb, wide), BF)] * 2, [picked, cotangent], 0, where)
     with jax.named_scope("input_swap"):
-        swapped = send(after(oth, turned[0], turned[2]), swap_hi)
+        swapped = send(after(oth, near), swap_hi)
+
+    def along(f, column):
+        with jax.named_scope(f"weights_x_{f}"):
+            return [column] + [send(column, along_x(j)) for j in range(1, NX)]
+
+    near = along(0, near)
+    far = along(1, after(far, near[1], near[3]))
     with jax.named_scope("join"):
         tok, cot = call(join_body, [((2 * tb, wide), BF)] * 2, [own, swapped])
 
@@ -215,7 +225,7 @@
         gu, dn, keep, away = call(
             forward_body,
             [((wide, 2 * hid), BF), ((hid, wide), BF), ((tb, 3 * hid), F32), ((tb, 3 * hid), BF)],
-            [tok, cot, *columns],
+            [tok, cot, *near, *far],
             3 * product,
         )
     part = keep + send(away, swap_core).astype(F32)
@@ -243,26 +253,24 @@
             total = total + piece.astype(F32)
         return total.astype(BF)
 
-    def returned(f, total):
-        with jax.named_scope(f"grads_turn_{f}"):
-            return [send_back(total[g], turn(f, g)) for g in range(2)]
-
     with jax.named_scope("grads"):
+        q1, q3, q2, q0 = pieces_of(1)
         p1, p3, p2, p0 = pieces_of(0)
-        q1, q3, q2, q0 = pieces_of(1)
-    with jax.named_scope("grads_x_0"):
-        p1, p3, p2 = send(p1, along_x(1)), send(p3, along_x(3)), send(p2, along_x(2))
+    with jax.named_scope("grads_x_1"):
+        q1, q3, q2 = send(q1, along_x(1)), send(q3, along_x(3)), send(q2, along_x(2))
     with jax.named_scope("outputs"):
         own, oth = call(output_body, [((2, tb, wide), BF)] * 2, [*terms, gu, dn], 3 * product)
     with jax.named_scope("output_swap"):
         swapped = send(oth, swap_hi)
     with jax.named_scope("place"):
         layer_out, token_grad = call(place_body, [((tb, quarter), BF)] * 2, [own, swapped], 0, where)
-    with jax.named_scope("grads_x_1"):
-        q1, q3, q2 = send(q1, along_x(1)), send(q3, along_x(3)), send(q2, along_x(2))
-    back = returned(0, summed((p1, p3, p2), p0))
-    back = back + returned(1, after(summed((q1, q3, q2), q0), swapped))
-    total = sum(piece.astype(F32) for piece in back)
+    with jax.named_scope("grads_x_0"):
+        p1, p3, p2 = send(p1, along_x(1)), send(p3, along_x(3)), send(p2, along_x(2))
+    with jax.named_scope("grads_plane"):
+        q0 = send(summed((q1, q3, q2), q0), swap_plane)
+    total = after(summed((p1, p3, p2, q0), p0), swapped)
+    with jax.named_scope("grads_turn"):
+        total = sum(send_back(total[g], turn(g)).astype(F32) for g in range(2))
     kept, moved, layer_out, token_grad = lax.optimization_barrier((total[0], total[1], layer_out, token_grad))
     with jax.named_scope("grads_core"):
         total = kept + send(moved, swap_core)

time: 171 us -> 163 us (0.953)
  waiting for transfers between devices: 97.7 us -> 89 us
  starting transfers between devices: 57.2 us -> 59 us
    ppermute x25 -> x28, starting transfers between devices: 41.5 us -> 49.3 us  [send(): return lax.ppermute(value, AXES, pairs_of(move))]
    ppermute x4 -> x2, starting transfers between devices: 15.7 us -> 9.71 us  [send_back(): return lax.ppermute(value, AXES, [(b, a) for a, b in pairs_of(move)])]
    ppermute x4 -> x2, waiting for transfers between devices: 18.2 us -> 13.8 us  [send_back(): return lax.ppermute(value, AXES, [(b, a) for a, b in pairs_of(move)])]
    ppermute x25 -> x28, waiting for transfers between devices: 79.4 us -> 75.2 us  [send(): return lax.ppermute(value, AXES, pairs_of(move))]
  transfers between devices with their start and end apart: 29 -> 30, of which waited for: 22 -> 23; matrix products, arithmetic and copies ran while one was open for 1% -> 1% of each run, Pallas kernels for 4% -> 4%
where the time goes in v6:
time: 163 us
  waiting for transfers between devices  89 us (55%)
  starting transfers between devices  59 us (36%)
  Pallas kernels  9.91 us (6%)
  local copies, waits for them, and re-layouts  2.11 us (1%)
  other arithmetic  2.04 us (1%)
    ppermute x28, waiting for transfers between devices, send(): return lax.ppermute(value, AXES, pairs_of(move))  75.2 us
    ppermute x28, starting transfers between devices, send(): return lax.ppermute(value, AXES, pairs_of(move))  49.3 us
    ppermute x2, waiting for transfers between devices, send_back(): return lax.ppermute(value, AXES, [(b, a) for a, b in pairs_of(move)])  13.8 us
    pallas_call x7, Pallas kernels, call(): pl.pallas_call(body, out_shape=[jax.ShapeDtypeStruct(s, d) for s, d in sh...  9.91 us
    ppermute x2, starting transfers between devices, send_back(): return lax.ppermute(value, AXES, [(b, a) for a, b in pairs_of(move)])  9.71 us
  transfers between devices with their start and end apart: 30, of which 23 were waited for; matrix products, arithmetic and copies ran while one was open for 1% of the time, Pallas kernels for 4%

profile of v6, /device:TPU:9, one launch (start us, length us, event | category | flops | bytes accessed | tf_op | source)
XLA Modules:
  0.0 162.9 jit_solution(6361939043713207466)
XLA Ops:
  0.6 0.9 fusion.3
  1.5 0.8 collective-permute-start
  2.4 0.9 collective-permute-done
  3.3 3.2 %collective-permute-start.2 = (bf16[2,3,128,128]{3,2,1,0:T(8,128)(2,1)S(1)}, bf16[2,3,128,128]{3,2,1,0:T(8,128)(2,1)S(1)}, u32[]{:S(2)}, u32[]{:S(2)}) collective-permute-start(bf16[2,3,128,128]{3,2,1,0:T(8,128)(2,1)S(1)} %pad_maximum_fusion.2), channel_id=1, source_target_pairs={{0,128},{1,192},{2,0},{3,64},{4,132},{5,196},{6,4},{7,68},{8,136},... | collective-permute-start | bytes 589832 | tf_op jit(solution)/shard_map/weights_turn/ppermute | solution.py:33
  6.5 7.1 %collective-permute-start.1 = (bf16[2,3,128,128]{3,2,1,0:T(8,128)(2,1)S(1)}, bf16[2,3,128,128]{3,2,1,0:T(8,128)(2,1)S(1)}, u32[]{:S(2)}, u32[]{:S(2)}) collective-permute-start(bf16[2,3,128,128]{3,2,1,0:T(8,128)(2,1)S(1)} %pad_maximum_fusion.2), channel_id=1, source_target_pairs={{0,0},{1,64},{2,128},{3,192},{4,4},{5,68},{6,132},{7,196},{8,8},{9... | collective-permute-start | bytes 589832 | tf_op jit(solution)/shard_map/weights_turn/ppermute | solution.py:33
  13.6 1.3 constant_dynamic-slice_fusion.tok
  15.0 1.1 pick.1
  16.1 3.2 %collective-permute-done.2 = bf16[2,3,128,128]{3,2,1,0:T(8,128)(2,1)S(1)} collective-permute-done((bf16[2,3,128,128]{3,2,1,0:T(8,128)(2,1)S(1)}, bf16[2,3,128,128]{3,2,1,0:T(8,128)(2,1)S(1)}, u32[]{:S(2)}, u32[]{:S(2)}) %collective-permute-start.2) | collective-permute-done | bytes 196640 | tf_op jit(solution)/shard_map/weights_turn/ppermute | solution.py:33
  19.3 3.2 %collective-permute-done.1 = bf16[2,3,128,128]{3,2,1,0:T(8,128)(2,1)S(1)} collective-permute-done((bf16[2,3,128,128]{3,2,1,0:T(8,128)(2,1)S(1)}, bf16[2,3,128,128]{3,2,1,0:T(8,128)(2,1)S(1)}, u32[]{:S(2)}, u32[]{:S(2)}) %collective-permute-start.1) | collective-permute-done | bytes 196640 | tf_op jit(solution)/shard_map/weights_turn/ppermute | solution.py:33
  22.6 2.1 %collective-permute-start.3 = (bf16[2,256,1024]{2,1,0:T(8,128)(2,1)S(1)}, bf16[2,256,1024]{2,1,0:T(8,128)(2,1)S(1)}, u32[]{:S(2)}, u32[]{:S(2)}) collective-permute-start(bf16[2,256,1024]{2,1,0:T(8,128)(2,1)S(1)} %get-tuple-element.40), channel_id=1, source_target_pairs={{0,16},{1,17},{2,18},{3,19},{4,20},{5,21},{6,22},{7,23},{8,24},{9,... | collective-permute-start | bytes 3145736 | tf_op jit(solution)/shard_map/input_swap/ppermute | solution.py:33
  24.7 1.2 collective-permute-start.7
  25.9 2.5 %collective-permute-start.6 = (bf16[2,2,3,128,128]{4,3,2,1,0:T(8,128)(2,1)S(1)}, bf16[2,2,3,128,128]{4,3,2,1,0:T(8,128)(2,1)S(1)}, u32[]{:S(2)}, u32[]{:S(2)}) collective-permute-start(bf16[2,2,3,128,128]{4,3,2,1,0:T(8,128)(2,1)S(1)} %pad_maximum_fusion.1.refs_0_), channel_id=1, source_target_pairs={{0,12},{1,13},{2,14},{3,15},{4,8},{5,9},{6,10},{7,11},{8,4},{9,5},... | collective-permute-start | bytes 1179656 | tf_op jit(solution)/shard_map/weights_x_0/ppermute | solution.py:33
  28.4 1.4 collective-permute-start.5
  29.7 5.4 %collective-permute-done.7.refs_4_ = bf16[2,2,3,128,128]{4,3,2,1,0:T(8,128)(2,1)S(1)} collective-permute-done((bf16[2,2,3,128,128]{4,3,2,1,0:T(8,128)(2,1)S(1)}, bf16[2,2,3,128,128]{4,3,2,1,0:T(8,128)(2,1)S(1)}, u32[]{:S(2)}, u32[]{:S(2)}) %collective-permute-start.7) | collective-permute-done | bytes 393248 | tf_op jit(solution)/shard_map/weights_plane/ppermute | solution.py:33
  35.1 1.5 collective-permute-done.6.refs_3_
  36.6 1.0 collective-permute-done.4.refs_1_
  37.6 1.5 collective-permute-start.10
  39.1 0.4 collective-permute-start.9
  39.4 1.4 collective-permute-start.8
  40.8 7.5 %collective-permute-done.3.far = bf16[2,256,1024]{2,1,0:T(8,128)(2,1)S(1)} collective-permute-done((bf16[2,256,1024]{2,1,0:T(8,128)(2,1)S(1)}, bf16[2,256,1024]{2,1,0:T(8,128)(2,1)S(1)}, u32[]{:S(2)}, u32[]{:S(2)}) %collective-permute-start.3) | collective-permute-done | bytes 1048608 | tf_op jit(solution)/shard_map/input_swap/ppermute | solution.py:33
  48.3 0.1 join.1
  48.4 16.1 %collective-permute-done.10.refs_7_ = bf16[2,2,3,128,128]{4,3,2,1,0:T(8,128)(2,1)S(1)} collective-permute-done((bf16[2,2,3,128,128]{4,3,2,1,0:T(8,128)(2,1)S(1)}, bf16[2,2,3,128,128]{4,3,2,1,0:T(8,128)(2,1)S(1)}, u32[]{:S(2)}, u32[]{:S(2)}) %collective-permute-start.10) | collective-permute-done | bytes 393248 | tf_op jit(solution)/shard_map/weights_x_1/ppermute | solution.py:33
  64.6 1.9 %forward.1 = (bf16[1024,1024]{1,0:T(8,128)(2,1)S(1)}, bf16[512,1024]{1,0:T(8,128)(2,1)S(1)}, f32[256,1536]{1,0:T(8,128)S(1)}, bf16[256,1536]{1,0:T(8,128)(2,1)S(1)}) custom-call(bf16[512,1024]{1,0:T(8,128)(2,1)S(1)} %get-tuple-element.41.tok, bf16[512,1024]{1,0:T(8,128)(2,1)S(1)} %get-tuple-element.42.cot, ...), custom_call_target="tpu_custom_call" | custom-call | flops 1610612736 | bytes 10747904 | tf_op jit(solution)/shard_map/forward/pallas_call | solution.py:87
  66.5 0.7 collective-permute-start.11
  67.2 1.9 %collective-permute-done.11 = bf16[256,1536]{1,0:T(8,128)(2,1)S(1)} collective-permute-done((bf16[256,1536]{1,0:T(8,128)(2,1)S(1)}, bf16[256,1536]{1,0:T(8,128)(2,1)S(1)}, u32[]{:S(2)}, u32[]{:S(2)}) %collective-permute-start.11) | collective-permute-done | bytes 786464 | tf_op jit(solution)/shard_map/ppermute | solution.py:33
  69.1 0.3 fusion.4
  69.4 0.1 collective-permute-start.12
  69.5 1.1 collective-permute-start.14
  70.7 2.1 %collective-permute-start.13 = (bf16[64,1536]{1,0:T(8,128)(2,1)S(1)}, bf16[64,1536]{1,0:T(8,128)(2,1)S(1)}, u32[]{:S(2)}, u32[]{:S(2)}) collective-permute-start(bf16[64,1536]{1,0:T(8,128)(2,1)S(1)} %get-tuple-element.69), channel_id=1, source_target_pairs={{0,16},{1,17},{2,18},{3,19},{4,20},{5,21},{6,22},{7,23},{8,24},{9,... | collective-permute-start | bytes 589832 | tf_op jit(solution)/shard_map/ppermute | solution.py:33
  72.8 2.9 %collective-permute-done.12 = bf16[64,1536]{1,0:T(8,128)(2,1)S(1)} collective-permute-done((bf16[64,1536]{1,0:T(8,128)(2,1)S(1)}, bf16[64,1536]{1,0:T(8,128)(2,1)S(1)}, u32[]{:S(2)}, u32[]{:S(2)}) %collective-permute-start.12) | collective-permute-done | bytes 196640 | tf_op jit(solution)/shard_map/ppermute | solution.py:33
  75.6 0.5 collective-permute-done.14
  76.1 3.5 %collective-permute-done.13 = bf16[64,1536]{1,0:T(8,128)(2,1)S(1)} collective-permute-done((bf16[64,1536]{1,0:T(8,128)(2,1)S(1)}, bf16[64,1536]{1,0:T(8,128)(2,1)S(1)}, u32[]{:S(2)}, u32[]{:S(2)}) %collective-permute-start.13) | collective-permute-done | bytes 196640 | tf_op jit(solution)/shard_map/ppermute | solution.py:33
  79.8 1.5 collective-permute-start.17
  81.3 2.1 %collective-permute-start.16 = (bf16[64,1536]{1,0:T(8,128)(2,1)S(1)}, bf16[64,1536]{1,0:T(8,128)(2,1)S(1)}, u32[]{:S(2)}, u32[]{:S(2)}) collective-permute-start(bf16[64,1536]{1,0:T(8,128)(2,1)S(1)} %pad_maximum_fusion.3), channel_id=1, source_target_pairs={{0,16},{1,17},{2,18},{3,19},{4,20},{5,21},{6,22},{7,23},{8,24},{9,... | collective-permute-start | bytes 589832 | tf_op jit(solution)/shard_map/ppermute | solution.py:33
  83.4 3.2 %collective-permute-done.17 = bf16[64,1536]{1,0:T(8,128)(2,1)S(1)} collective-permute-done((bf16[64,1536]{1,0:T(8,128)(2,1)S(1)}, bf16[64,1536]{1,0:T(8,128)(2,1)S(1)}, u32[]{:S(2)}, u32[]{:S(2)}) %collective-permute-start.17) | collective-permute-done | bytes 196640 | tf_op jit(solution)/shard_map/ppermute | solution.py:33
  86.6 1.2 collective-permute-done.16
  87.8 3.2 %collective-permute-done.15 = bf16[64,1536]{1,0:T(8,128)(2,1)S(1)} collective-permute-done((bf16[64,1536]{1,0:T(8,128)(2,1)S(1)}, bf16[64,1536]{1,0:T(8,128)(2,1)S(1)}, u32[]{:S(2)}, u32[]{:S(2)}) %collective-permute-start.15) | collective-permute-done | bytes 196640 | tf_op jit(solution)/shard_map/ppermute | solution.py:33
  91.1 2.6 %collective-permute-start.18 = (bf16[256,1536]{1,0:T(8,128)(2,1)S(1)}, bf16[256,1536]{1,0:T(8,128)(2,1)S(1)}, u32[]{:S(2)}, u32[]{:S(2)}) collective-permute-start(bf16[256,1536]{1,0:T(8,128)(2,1)S(1)} %pad_maximum_fusion.da), channel_id=1, source_target_pairs={{0,1},{1,0},{2,3},{3,2},{4,5},{5,4},{6,7},{7,6},{8,9},{9,8},{10,11... | collective-permute-start | bytes 2359304 | tf_op jit(solution)/shard_map/ppermute | solution.py:33
  93.6 1.9 %collective-permute-done.18.dc = bf16[256,1536]{1,0:T(8,128)(2,1)S(1)} collective-permute-done((bf16[256,1536]{1,0:T(8,128)(2,1)S(1)}, bf16[256,1536]{1,0:T(8,128)(2,1)S(1)}, u32[]{:S(2)}, u32[]{:S(2)}) %collective-permute-start.18) | collective-permute-done | bytes 786464 | tf_op jit(solution)/shard_map/ppermute | solution.py:33
  95.5 1.3 grads.3
  96.8 0.1 collective-permute-start.22
  96.9 2.2 %collective-permute-start.23 = (bf16[2,2,3,128,128]{4,3,2,1,0:T(8,128)(2,1)S(1)}, bf16[2,2,3,128,128]{4,3,2,1,0:T(8,128)(2,1)S(1)}, u32[]{:S(2)}, u32[]{:S(2)}) collective-permute-start(bf16[2,2,3,128,128]{4,3,2,1,0:T(8,128)(2,1)S(1)} %get-tuple-element.52), channel_id=1, source_target_pairs={{0,12},{1,13},{2,14},{3,15},{4,8},{5,9},{6,10},{7,11},{8,4},{9,5},... | collective-permute-start | bytes 1179656 | tf_op jit(solution)/shard_map/grads_x_1/ppermute | solution.py:33
  99.2 1.1 collective-permute-start.24
  100.2 1.8 %outputs.1 = (bf16[2,256,1024]{2,1,0:T(8,128)(2,1)S(1)}, bf16[2,256,1024]{2,1,0:T(8,128)(2,1)S(1)}) custom-call(bf16[256,1536]{1,0:T(8,128)(2,1)S(1)} %pad_maximum_fusion.da, bf16[256,1536]{1,0:T(8,128)(2,1)S(1)} %collective-permute-done.18.dc, bf16[1024,1024]{1,0:T(8,128)(2,1)S(1)} %get-tuple-element.54.gu, bf16[512,1024]{1,0:T(8,128)(2,1)S(1)} %get-tuple-element.55.dn), custom_call_target="tpu_custom_call" | custom-call | flops 1610612736 | bytes 6815744 | tf_op jit(solution)/shard_map/outputs/pallas_call | solution.py:87
  102.0 1.9 %collective-permute-start.26 = (bf16[2,256,1024]{2,1,0:T(8,128)(2,1)S(1)}, bf16[2,256,1024]{2,1,0:T(8,128)(2,1)S(1)}, u32[]{:S(2)}, u32[]{:S(2)}) collective-permute-start(bf16[2,256,1024]{2,1,0:T(8,128)(2,1)S(1)} %get-tuple-element.56), channel_id=1, source_target_pairs={{0,16},{1,17},{2,18},{3,19},{4,20},{5,21},{6,22},{7,23},{8,24},{9,... | collective-permute-start | bytes 3145736 | tf_op jit(solution)/shard_map/output_swap/ppermute | solution.py:33
  103.9 1.3 grads.2
  105.2 0.2 collective-permute-start.19
  105.4 1.8 %collective-permute-done.22 = bf16[2,2,3,128,128]{4,3,2,1,0:T(8,128)(2,1)S(1)} collective-permute-done((bf16[2,2,3,128,128]{4,3,2,1,0:T(8,128)(2,1)S(1)}, bf16[2,2,3,128,128]{4,3,2,1,0:T(8,128)(2,1)S(1)}, u32[]{:S(2)}, u32[]{:S(2)}) %collective-permute-start.22) | collective-permute-done | bytes 393248 | tf_op jit(solution)/shard_map/grads_x_1/ppermute | solution.py:33
  107.3 2.1 %collective-permute-start.20 = (bf16[2,2,3,128,128]{4,3,2,1,0:T(8,128)(2,1)S(1)}, bf16[2,2,3,128,128]{4,3,2,1,0:T(8,128)(2,1)S(1)}, u32[]{:S(2)}, u32[]{:S(2)}) collective-permute-start(bf16[2,2,3,128,128]{4,3,2,1,0:T(8,128)(2,1)S(1)} %get-tuple-element.48), channel_id=1, source_target_pairs={{0,12},{1,13},{2,14},{3,15},{4,8},{5,9},{6,10},{7,11},{8,4},{9,5},... | collective-permute-start | bytes 1179656 | tf_op jit(solution)/shard_map/grads_x_0/ppermute | solution.py:33
  109.4 9.1 %collective-permute-start.21 = (bf16[2,2,3,128,128]{4,3,2,1,0:T(8,128)(2,1)S(1)}, bf16[2,2,3,128,128]{4,3,2,1,0:T(8,128)(2,1)S(1)}, u32[]{:S(2)}, u32[]{:S(2)}) collective-permute-start(bf16[2,2,3,128,128]{4,3,2,1,0:T(8,128)(2,1)S(1)} %get-tuple-element.49), channel_id=1, source_target_pairs={{0,8},{1,9},{2,10},{3,11},{4,12},{5,13},{6,14},{7,15},{8,0},{9,1},... | collective-permute-start | bytes 1179656 | tf_op jit(solution)/shard_map/grads_x_0/ppermute | solution.py:33
  118.5 0.2 add_convert_fusion.1
  118.7 0.8 collective-permute-start.25
  119.5 4.7 %collective-permute-done.19 = bf16[2,2,3,128,128]{4,3,2,1,0:T(8,128)(2,1)S(1)} collective-permute-done((bf16[2,2,3,128,128]{4,3,2,1,0:T(8,128)(2,1)S(1)}, bf16[2,2,3,128,128]{4,3,2,1,0:T(8,128)(2,1)S(1)}, u32[]{:S(2)}, u32[]{:S(2)}) %collective-permute-start.19) | collective-permute-done | bytes 393248 | tf_op jit(solution)/shard_map/grads_x_0/ppermute | solution.py:33
  124.2 3.2 %collective-permute-done.20 = bf16[2,2,3,128,128]{4,3,2,1,0:T(8,128)(2,1)S(1)} collective-permute-done((bf16[2,2,3,128,128]{4,3,2,1,0:T(8,128)(2,1)S(1)}, bf16[2,2,3,128,128]{4,3,2,1,0:T(8,128)(2,1)S(1)}, u32[]{:S(2)}, u32[]{:S(2)}) %collective-permute-start.20) | collective-permute-done | bytes 393248 | tf_op jit(solution)/shard_map/grads_x_0/ppermute | solution.py:33
  127.3 7.1 %collective-permute-done.21 = bf16[2,2,3,128,128]{4,3,2,1,0:T(8,128)(2,1)S(1)} collective-permute-done((bf16[2,2,3,128,128]{4,3,2,1,0:T(8,128)(2,1)S(1)}, bf16[2,2,3,128,128]{4,3,2,1,0:T(8,128)(2,1)S(1)}, u32[]{:S(2)}, u32[]{:S(2)}) %collective-permute-start.21) | collective-permute-done | bytes 393248 | tf_op jit(solution)/shard_map/grads_x_0/ppermute | solution.py:33
  134.4 0.3 add_convert_fusion
  134.7 8.5 %collective-permute-start.27 = (bf16[2,3,128,128]{3,2,1,0:T(8,128)(2,1)S(1)}, bf16[2,3,128,128]{3,2,1,0:T(8,128)(2,1)S(1)}, u32[]{:S(2)}, u32[]{:S(2)}) collective-permute-start(bf16[2,3,128,128]{3,2,1,0:T(8,128)(2,1)S(1)} %get-tuple-element.72), channel_id=1, source_target_pairs={{0,0},{64,1},{128,2},{192,3},{4,4},{68,5},{132,6},{196,7},{8,8},{7... | collective-permute-start | bytes 589832 | tf_op jit(solution)/shard_map/grads_turn/ppermute | solution.py:37
  143.2 1.2 collective-permute-start.28
  144.5 2.4 %place.1 = (bf16[256,2048]{1,0:T(8,128)(2,1)}, bf16[256,2048]{1,0:T(8,128)(2,1)}) custom-call(s32[4]{0:T(128)S(1)} %pad_add_fusion.where, bf16[2,256,1024]{2,1,0:T(8,128)(2,1)S(1)} %get-tuple-element.58.own, bf16[2,256,1024]{2,1,0:T(8,128)(2,1)S(1)} %collective-permute-done.26.far), custom_call_target="tpu_custom_call" | custom-call | bytes 4194304 | tf_op jit(solution)/shard_map/place/pallas_call | solution.py:87
  146.8 6.2 %collective-permute-done.27 = bf16[2,3,128,128]{3,2,1,0:T(8,128)(2,1)S(1)} collective-permute-done((bf16[2,3,128,128]{3,2,1,0:T(8,128)(2,1)S(1)}, bf16[2,3,128,128]{3,2,1,0:T(8,128)(2,1)S(1)}, u32[]{:S(2)}, u32[]{:S(2)}) %collective-permute-start.27) | collective-permute-done | bytes 196640 | tf_op jit(solution)/shard_map/grads_turn/ppermute | solution.py:37
  153.0 7.6 %collective-permute-done.28 = bf16[2,3,128,128]{3,2,1,0:T(8,128)(2,1)S(1)} collective-permute-done((bf16[2,3,128,128]{3,2,1,0:T(8,128)(2,1)S(1)}, bf16[2,3,128,128]{3,2,1,0:T(8,128)(2,1)S(1)}, u32[]{:S(2)}, u32[]{:S(2)}) %collective-permute-start.28) | collective-permute-done | bytes 196640 | tf_op jit(solution)/shard_map/grads_turn/ppermute | solution.py:37
  160.7 0.1 collective-permute-start.29
  160.8 1.4 collective-permute-done.29
  162.3 0.7 slice_bitcast_fusion.4
  (23 shorter events, 0.5 us)
Async XLA Ops:
  0.6 14.3 %copy-start = (bf16[256,2048]{1,0:T(8,128)(2,1)S(1)}, bf16[256,2048]{1,0:T(8,128)(2,1)}, u32[]{:S(2)}) copy-start(bf16[256,2048]{1,0:T(8,128)(2,1)} %cot) | copy-start | bytes 3145732
  1.5 1.7 %collective-permute-start = (bf16[3,128,128]{2,1,0:T(8,128)(2,1)S(1)}, bf16[3,128,128]{2,1,0:T(8,128)(2,1)S(1)}, u32[]{:S(2)}, u32[]{:S(2)}) collective-permute-start(bf16[3,128,128]{2,1,0:T(8,128)(2,1)S(1)} %get-tuple-element.81), channel_id=1, source_target_pairs={{0,1},{1,0},{2,3},{3,2},{4,5},{5,4},{6,7},{7,6},{8,9},{9,8},{10,11... | collective-permute-start | bytes 294920 | tf_op jit(solution)/shard_map/weights_core/ppermute | solution.py:33
  3.3 16.1 %collective-permute-start.2 = (bf16[2,3,128,128]{3,2,1,0:T(8,128)(2,1)S(1)}, bf16[2,3,128,128]{3,2,1,0:T(8,128)(2,1)S(1)}, u32[]{:S(2)}, u32[]{:S(2)}) collective-permute-start(bf16[2,3,128,128]{3,2,1,0:T(8,128)(2,1)S(1)} %pad_maximum_fusion.2), channel_id=1, source_target_pairs={{0,128},{1,192},{2,0},{3,64},{4,132},{5,196},{6,4},{7,68},{8,136},... | collective-permute-start | bytes 589832 | tf_op jit(solution)/shard_map/weights_turn/ppermute | solution.py:33
  6.5 16.1 %collective-permute-start.1 = (bf16[2,3,128,128]{3,2,1,0:T(8,128)(2,1)S(1)}, bf16[2,3,128,128]{3,2,1,0:T(8,128)(2,1)S(1)}, u32[]{:S(2)}, u32[]{:S(2)}) collective-permute-start(bf16[2,3,128,128]{3,2,1,0:T(8,128)(2,1)S(1)} %pad_maximum_fusion.2), channel_id=1, source_target_pairs={{0,0},{1,64},{2,128},{3,192},{4,4},{5,68},{6,132},{7,196},{8,8},{9... | collective-permute-start | bytes 589832 | tf_op jit(solution)/shard_map/weights_turn/ppermute | solution.py:33
  22.6 25.7 %collective-permute-start.3 = (bf16[2,256,1024]{2,1,0:T(8,128)(2,1)S(1)}, bf16[2,256,1024]{2,1,0:T(8,128)(2,1)S(1)}, u32[]{:S(2)}, u32[]{:S(2)}) collective-permute-start(bf16[2,256,1024]{2,1,0:T(8,128)(2,1)S(1)} %get-tuple-element.40), channel_id=1, source_target_pairs={{0,16},{1,17},{2,18},{3,19},{4,20},{5,21},{6,22},{7,23},{8,24},{9,... | collective-permute-start | bytes 3145736 | tf_op jit(solution)/shard_map/input_swap/ppermute | solution.py:33
  24.7 10.4 %collective-permute-start.7 = (bf16[2,2,3,128,128]{4,3,2,1,0:T(8,128)(2,1)S(1)}, bf16[2,2,3,128,128]{4,3,2,1,0:T(8,128)(2,1)S(1)}, u32[]{:S(2)}, u32[]{:S(2)}) collective-permute-start(bf16[2,2,3,128,128]{4,3,2,1,0:T(8,128)(2,1)S(1)} %pad_maximum_fusion.1.refs_0_), channel_id=1, source_target_pairs={{0,32},{1,33},{2,34},{3,35},{4,36},{5,37},{6,38},{7,39},{8,40},{9,... | collective-permute-start | bytes 1179656 | tf_op jit(solution)/shard_map/weights_plane/ppermute | solution.py:33
  25.9 10.7 %collective-permute-start.6 = (bf16[2,2,3,128,128]{4,3,2,1,0:T(8,128)(2,1)S(1)}, bf16[2,2,3,128,128]{4,3,2,1,0:T(8,128)(2,1)S(1)}, u32[]{:S(2)}, u32[]{:S(2)}) collective-permute-start(bf16[2,2,3,128,128]{4,3,2,1,0:T(8,128)(2,1)S(1)} %pad_maximum_fusion.1.refs_0_), channel_id=1, source_target_pairs={{0,12},{1,13},{2,14},{3,15},{4,8},{5,9},{6,10},{7,11},{8,4},{9,5},... | collective-permute-start | bytes 1179656 | tf_op jit(solution)/shard_map/weights_x_0/ppermute | solution.py:33
  28.3 9.2 %collective-permute-start.4 = (bf16[2,2,3,128,128]{4,3,2,1,0:T(8,128)(2,1)S(1)}, bf16[2,2,3,128,128]{4,3,2,1,0:T(8,128)(2,1)S(1)}, u32[]{:S(2)}, u32[]{:S(2)}) collective-permute-start(bf16[2,2,3,128,128]{4,3,2,1,0:T(8,128)(2,1)S(1)} %pad_maximum_fusion.1.refs_0_), channel_id=1, source_target_pairs={{0,4},{1,5},{2,6},{3,7},{4,0},{5,1},{6,2},{7,3},{8,12},{9,13},{10,... | collective-permute-start | bytes 1179656 | tf_op jit(solution)/shard_map/weights_x_0/ppermute | solution.py:33
  28.4 20.1 %collective-permute-start.5 = (bf16[2,2,3,128,128]{4,3,2,1,0:T(8,128)(2,1)S(1)}, bf16[2,2,3,128,128]{4,3,2,1,0:T(8,128)(2,1)S(1)}, u32[]{:S(2)}, u32[]{:S(2)}) collective-permute-start(bf16[2,2,3,128,128]{4,3,2,1,0:T(8,128)(2,1)S(1)} %pad_maximum_fusion.1.refs_0_), channel_id=1, source_target_pairs={{0,8},{1,9},{2,10},{3,11},{4,12},{5,13},{6,14},{7,15},{8,0},{9,1},... | collective-permute-start | bytes 1179656 | tf_op jit(solution)/shard_map/weights_x_0/ppermute | solution.py:33
  37.6 27.0 %collective-permute-start.10 = (bf16[2,2,3,128,128]{4,3,2,1,0:T(8,128)(2,1)S(1)}, bf16[2,2,3,128,128]{4,3,2,1,0:T(8,128)(2,1)S(1)}, u32[]{:S(2)}, u32[]{:S(2)}) collective-permute-start(bf16[2,2,3,128,128]{4,3,2,1,0:T(8,128)(2,1)S(1)} %collective-permute-done.7.refs_4_), channel_id=1, source_target_pairs={{0,12},{1,13},{2,14},{3,15},{4,8},{5,9},{6,10},{7,11},{8,4},{9,5},... | collective-permute-start | bytes 1179656 | tf_op jit(solution)/shard_map/weights_x_1/ppermute | solution.py:33
  39.1 25.5 %collective-permute-start.9 = (bf16[2,2,3,128,128]{4,3,2,1,0:T(8,128)(2,1)S(1)}, bf16[2,2,3,128,128]{4,3,2,1,0:T(8,128)(2,1)S(1)}, u32[]{:S(2)}, u32[]{:S(2)}) collective-permute-start(bf16[2,2,3,128,128]{4,3,2,1,0:T(8,128)(2,1)S(1)} %collective-permute-done.7.refs_4_), channel_id=1, source_target_pairs={{0,8},{1,9},{2,10},{3,11},{4,12},{5,13},{6,14},{7,15},{8,0},{9,1},... | collective-permute-start | bytes 1179656 | tf_op jit(solution)/shard_map/weights_x_1/ppermute | solution.py:33
  39.4 25.2 %collective-permute-start.8 = (bf16[2,2,3,128,128]{4,3,2,1,0:T(8,128)(2,1)S(1)}, bf16[2,2,3,128,128]{4,3,2,1,0:T(8,128)(2,1)S(1)}, u32[]{:S(2)}, u32[]{:S(2)}) collective-permute-start(bf16[2,2,3,128,128]{4,3,2,1,0:T(8,128)(2,1)S(1)} %collective-permute-done.7.refs_4_), channel_id=1, source_target_pairs={{0,4},{1,5},{2,6},{3,7},{4,0},{5,1},{6,2},{7,3},{8,12},{9,13},{10,... | collective-permute-start | bytes 1179656 | tf_op jit(solution)/shard_map/weights_x_1/ppermute | solution.py:33
  66.5 2.6 %collective-permute-start.11 = (bf16[256,1536]{1,0:T(8,128)(2,1)S(1)}, bf16[256,1536]{1,0:T(8,128)(2,1)S(1)}, u32[]{:S(2)}, u32[]{:S(2)}) collective-permute-start(bf16[256,1536]{1,0:T(8,128)(2,1)S(1)} %get-tuple-element.45), channel_id=1, source_target_pairs={{0,1},{1,0},{2,3},{3,2},{4,5},{5,4},{6,7},{7,6},{8,9},{9,8},{10,11... | collective-permute-start | bytes 2359304 | tf_op jit(solution)/shard_map/ppermute | solution.py:33
  69.4 6.2 %collective-permute-start.12 = (bf16[64,1536]{1,0:T(8,128)(2,1)S(1)}, bf16[64,1536]{1,0:T(8,128)(2,1)S(1)}, u32[]{:S(2)}, u32[]{:S(2)}) collective-permute-start(bf16[64,1536]{1,0:T(8,128)(2,1)S(1)} %get-tuple-element.67), channel_id=1, source_target_pairs={{0,2},{1,3},{2,0},{3,1},{4,6},{5,7},{6,4},{7,5},{8,10},{9,11},{10,... | collective-permute-start | bytes 589832 | tf_op jit(solution)/shard_map/ppermute | solution.py:33
  69.5 6.6 %collective-permute-start.14 = (bf16[64,1536]{1,0:T(8,128)(2,1)S(1)}, bf16[64,1536]{1,0:T(8,128)(2,1)S(1)}, u32[]{:S(2)}, u32[]{:S(2)}) collective-permute-start(bf16[64,1536]{1,0:T(8,128)(2,1)S(1)} %get-tuple-element.68), channel_id=1, source_target_pairs={{0,18},{1,19},{2,16},{3,17},{4,22},{5,23},{6,20},{7,21},{8,26},{9,... | collective-permute-start | bytes 589832 | tf_op jit(solution)/shard_map/ppermute | solution.py:33
  70.7 8.9 %collective-permute-start.13 = (bf16[64,1536]{1,0:T(8,128)(2,1)S(1)}, bf16[64,1536]{1,0:T(8,128)(2,1)S(1)}, u32[]{:S(2)}, u32[]{:S(2)}) collective-permute-start(bf16[64,1536]{1,0:T(8,128)(2,1)S(1)} %get-tuple-element.69), channel_id=1, source_target_pairs={{0,16},{1,17},{2,18},{3,19},{4,20},{5,21},{6,22},{7,23},{8,24},{9,... | collective-permute-start | bytes 589832 | tf_op jit(solution)/shard_map/ppermute | solution.py:33
  79.8 6.8 %collective-permute-start.17 = (bf16[64,1536]{1,0:T(8,128)(2,1)S(1)}, bf16[64,1536]{1,0:T(8,128)(2,1)S(1)}, u32[]{:S(2)}, u32[]{:S(2)}) collective-permute-start(bf16[64,1536]{1,0:T(8,128)(2,1)S(1)} %pad_maximum_fusion.3), channel_id=1, source_target_pairs={{0,18},{1,19},{2,16},{3,17},{4,22},{5,23},{6,20},{7,21},{8,26},{9,... | collective-permute-start | bytes 589832 | tf_op jit(solution)/shard_map/ppermute | solution.py:33
  81.3 6.5 %collective-permute-start.16 = (bf16[64,1536]{1,0:T(8,128)(2,1)S(1)}, bf16[64,1536]{1,0:T(8,128)(2,1)S(1)}, u32[]{:S(2)}, u32[]{:S(2)}) collective-permute-start(bf16[64,1536]{1,0:T(8,128)(2,1)S(1)} %pad_maximum_fusion.3), channel_id=1, source_target_pairs={{0,16},{1,17},{2,18},{3,19},{4,20},{5,21},{6,22},{7,23},{8,24},{9,... | collective-permute-start | bytes 589832 | tf_op jit(solution)/shard_map/ppermute | solution.py:33
  83.4 7.6 %collective-permute-start.15 = (bf16[64,1536]{1,0:T(8,128)(2,1)S(1)}, bf16[64,1536]{1,0:T(8,128)(2,1)S(1)}, u32[]{:S(2)}, u32[]{:S(2)}) collective-permute-start(bf16[64,1536]{1,0:T(8,128)(2,1)S(1)} %pad_maximum_fusion.3), channel_id=1, source_target_pairs={{0,2},{1,3},{2,0},{3,1},{4,6},{5,7},{6,4},{7,5},{8,10},{9,11},{10,... | collective-permute-start | bytes 589832 | tf_op jit(solution)/shard_map/ppermute | solution.py:33
  91.1 4.5 %collective-permute-start.18 = (bf16[256,1536]{1,0:T(8,128)(2,1)S(1)}, bf16[256,1536]{1,0:T(8,128)(2,1)S(1)}, u32[]{:S(2)}, u32[]{:S(2)}) collective-permute-start(bf16[256,1536]{1,0:T(8,128)(2,1)S(1)} %pad_maximum_fusion.da), channel_id=1, source_target_pairs={{0,1},{1,0},{2,3},{3,2},{4,5},{5,4},{6,7},{7,6},{8,9},{9,8},{10,11... | collective-permute-start | bytes 2359304 | tf_op jit(solution)/shard_map/ppermute | solution.py:33
  96.8 10.4 %collective-permute-start.22 = (bf16[2,2,3,128,128]{4,3,2,1,0:T(8,128)(2,1)S(1)}, bf16[2,2,3,128,128]{4,3,2,1,0:T(8,128)(2,1)S(1)}, u32[]{:S(2)}, u32[]{:S(2)}) collective-permute-start(bf16[2,2,3,128,128]{4,3,2,1,0:T(8,128)(2,1)S(1)} %get-tuple-element.51), channel_id=1, source_target_pairs={{0,4},{1,5},{2,6},{3,7},{4,0},{5,1},{6,2},{7,3},{8,12},{9,13},{10,... | collective-permute-start | bytes 1179656 | tf_op jit(solution)/shard_map/grads_x_1/ppermute | solution.py:33
  96.9 12.4 %collective-permute-start.23 = (bf16[2,2,3,128,128]{4,3,2,1,0:T(8,128)(2,1)S(1)}, bf16[2,2,3,128,128]{4,3,2,1,0:T(8,128)(2,1)S(1)}, u32[]{:S(2)}, u32[]{:S(2)}) collective-permute-start(bf16[2,2,3,128,128]{4,3,2,1,0:T(8,128)(2,1)S(1)} %get-tuple-element.52), channel_id=1, source_target_pairs={{0,12},{1,13},{2,14},{3,15},{4,8},{5,9},{6,10},{7,11},{8,4},{9,5},... | collective-permute-start | bytes 1179656 | tf_op jit(solution)/shard_map/grads_x_1/ppermute | solution.py:33
  99.2 19.3 %collective-permute-start.24 = (bf16[2,2,3,128,128]{4,3,2,1,0:T(8,128)(2,1)S(1)}, bf16[2,2,3,128,128]{4,3,2,1,0:T(8,128)(2,1)S(1)}, u32[]{:S(2)}, u32[]{:S(2)}) collective-permute-start(bf16[2,2,3,128,128]{4,3,2,1,0:T(8,128)(2,1)S(1)} %get-tuple-element.53), channel_id=1, source_target_pairs={{0,8},{1,9},{2,10},{3,11},{4,12},{5,13},{6,14},{7,15},{8,0},{9,1},... | collective-permute-start | bytes 1179656 | tf_op jit(solution)/shard_map/grads_x_1/ppermute | solution.py:33
  102.0 32.7 %collective-permute-start.26 = (bf16[2,256,1024]{2,1,0:T(8,128)(2,1)S(1)}, bf16[2,256,1024]{2,1,0:T(8,128)(2,1)S(1)}, u32[]{:S(2)}, u32[]{:S(2)}) collective-permute-start(bf16[2,256,1024]{2,1,0:T(8,128)(2,1)S(1)} %get-tuple-element.56), channel_id=1, source_target_pairs={{0,16},{1,17},{2,18},{3,19},{4,20},{5,21},{6,22},{7,23},{8,24},{9,... | collective-permute-start | bytes 3145736 | tf_op jit(solution)/shard_map/output_swap/ppermute | solution.py:33
  105.2 18.9 %collective-permute-start.19 = (bf16[2,2,3,128,128]{4,3,2,1,0:T(8,128)(2,1)S(1)}, bf16[2,2,3,128,128]{4,3,2,1,0:T(8,128)(2,1)S(1)}, u32[]{:S(2)}, u32[]{:S(2)}) collective-permute-start(bf16[2,2,3,128,128]{4,3,2,1,0:T(8,128)(2,1)S(1)} %get-tuple-element.47), channel_id=1, source_target_pairs={{0,4},{1,5},{2,6},{3,7},{4,0},{5,1},{6,2},{7,3},{8,12},{9,13},{10,... | collective-permute-start | bytes 1179656 | tf_op jit(solution)/shard_map/grads_x_0/ppermute | solution.py:33
  107.3 20.1 %collective-permute-start.20 = (bf16[2,2,3,128,128]{4,3,2,1,0:T(8,128)(2,1)S(1)}, bf16[2,2,3,128,128]{4,3,2,1,0:T(8,128)(2,1)S(1)}, u32[]{:S(2)}, u32[]{:S(2)}) collective-permute-start(bf16[2,2,3,128,128]{4,3,2,1,0:T(8,128)(2,1)S(1)} %get-tuple-element.48), channel_id=1, source_target_pairs={{0,12},{1,13},{2,14},{3,15},{4,8},{5,9},{6,10},{7,11},{8,4},{9,5},... | collective-permute-start | bytes 1179656 | tf_op jit(solution)/shard_map/grads_x_0/ppermute | solution.py:33
  109.4 25.0 %collective-permute-start.21 = (bf16[2,2,3,128,128]{4,3,2,1,0:T(8,128)(2,1)S(1)}, bf16[2,2,3,128,128]{4,3,2,1,0:T(8,128)(2,1)S(1)}, u32[]{:S(2)}, u32[]{:S(2)}) collective-permute-start(bf16[2,2,3,128,128]{4,3,2,1,0:T(8,128)(2,1)S(1)} %get-tuple-element.49), channel_id=1, source_target_pairs={{0,8},{1,9},{2,10},{3,11},{4,12},{5,13},{6,14},{7,15},{8,0},{9,1},... | collective-permute-start | bytes 1179656 | tf_op jit(solution)/shard_map/grads_x_0/ppermute | solution.py:33
  118.7 15.7 %collective-permute-start.25 = (bf16[2,2,3,128,128]{4,3,2,1,0:T(8,128)(2,1)S(1)}, bf16[2,2,3,128,128]{4,3,2,1,0:T(8,128)(2,1)S(1)}, u32[]{:S(2)}, u32[]{:S(2)}) collective-permute-start(bf16[2,2,3,128,128]{4,3,2,1,0:T(8,128)(2,1)S(1)} %add_convert_fusion.1), channel_id=1, source_target_pairs={{0,32},{1,33},{2,34},{3,35},{4,36},{5,37},{6,38},{7,39},{8,40},{9,... | collective-permute-start | bytes 1179656 | tf_op jit(solution)/shard_map/grads_plane/ppermute | solution.py:33
  134.7 18.3 %collective-permute-start.27 = (bf16[2,3,128,128]{3,2,1,0:T(8,128)(2,1)S(1)}, bf16[2,3,128,128]{3,2,1,0:T(8,128)(2,1)S(1)}, u32[]{:S(2)}, u32[]{:S(2)}) collective-permute-start(bf16[2,3,128,128]{3,2,1,0:T(8,128)(2,1)S(1)} %get-tuple-element.72), channel_id=1, source_target_pairs={{0,0},{64,1},{128,2},{192,3},{4,4},{68,5},{132,6},{196,7},{8,8},{7... | collective-permute-start | bytes 589832 | tf_op jit(solution)/shard_map/grads_turn/ppermute | solution.py:37
  143.2 17.4 %collective-permute-start.28 = (bf16[2,3,128,128]{3,2,1,0:T(8,128)(2,1)S(1)}, bf16[2,3,128,128]{3,2,1,0:T(8,128)(2,1)S(1)}, u32[]{:S(2)}, u32[]{:S(2)}) collective-permute-start(bf16[2,3,128,128]{3,2,1,0:T(8,128)(2,1)S(1)} %get-tuple-element.73), channel_id=1, source_target_pairs={{128,0},{192,1},{0,2},{64,3},{132,4},{196,5},{4,6},{68,7},{136,8},... | collective-permute-start | bytes 589832 | tf_op jit(solution)/shard_map/grads_turn/ppermute | solution.py:37
  160.7 1.5 collective-permute-start.29

commit v7 on v6

--- a/solution.py
+++ b/solution.py
@@ -57,9 +57,9 @@
     return lambda z, h, x, l, c: (z, h ^ (k // 2), x, l ^ (k % 2), c)
 
 
-def turn(g):
+def turn(g, e=0):
     def move(z, h, x, l, c):
-        return 4 * (l ^ g) + 2 * c + z % 2, h, x, z // 4, (z // 2) % 2
+        return 4 * (l ^ g) + 2 * (c ^ e) + z % 2, h, x, z // 4, (z // 2) % 2
 
     return move
 
@@ -270,10 +270,9 @@
         q0 = send(summed((q1, q3, q2), q0), swap_plane)
     total = after(summed((p1, p3, p2, q0), p0), swapped)
     with jax.named_scope("grads_turn"):
-        total = sum(send_back(total[g], turn(g)).astype(F32) for g in range(2))
-    kept, moved, layer_out, token_grad = lax.optimization_barrier((total[0], total[1], layer_out, token_grad))
-    with jax.named_scope("grads_core"):
-        total = kept + send(moved, swap_core)
+        pieces = [send_back(total[g, e], turn(g, e)) for g in range(2) for e in range(2)]
+    *pieces, layer_out, token_grad = lax.optimization_barrier((*pieces, layer_out, token_grad))
+    total = sum(piece.astype(F32) for piece in pieces)
     return layer_out, token_grad, total[0], total[1], total[2]
 
 

time: 163 us -> 160 us (0.982)
  waiting for transfers between devices: 89 us -> 79 us
  starting transfers between devices: 59 us -> 65.3 us
    ppermute x2 -> x4, waiting for transfers between devices: 13.8 us -> 5.2 us  [send_back(): return lax.ppermute(value, AXES, [(b, a) for a, b in pairs_of(move)])]
    ppermute x2 -> x4, starting transfers between devices: 9.71 us -> 16.1 us  [send_back(): return lax.ppermute(value, AXES, [(b, a) for a, b in pairs_of(move)])]
    ppermute x28 -> x27, waiting for transfers between devices: 75.2 us -> 73.8 us  [send(): return lax.ppermute(value, AXES, pairs_of(move))]
    ppermute x28 -> x27, starting transfers between devices: 49.3 us -> 49.2 us  [send(): return lax.ppermute(value, AXES, pairs_of(move))]
  transfers between devices with their start and end apart: 30 -> 31, of which waited for: 23 -> 23; matrix products, arithmetic and copies ran while one was open for 1% -> 1% of each run, Pallas kernels for 4% -> 4%
where the time goes in v7:
time: 160 us; the launch traced here: 159 us
  waiting for transfers between devices  79 us (49%)
  starting transfers between devices  65.3 us (41%)
  Pallas kernels  9.92 us (6%)
  local copies, waits for them, and re-layouts  2.09 us (1%)
  other arithmetic  2.02 us (1%)
    ppermute x27, waiting for transfers between devices, send(): return lax.ppermute(value, AXES, pairs_of(move))  73.8 us
    ppermute x27, starting transfers between devices, send(): return lax.ppermute(value, AXES, pairs_of(move))  49.2 us
    ppermute x4, starting transfers between devices, send_back(): return lax.ppermute(value, AXES, [(b, a) for a, b in pairs_of(move)])  16.1 us
    pallas_call x7, Pallas kernels, call(): pl.pallas_call(body, out_shape=[jax.ShapeDtypeStruct(s, d) for s, d in sh...  9.92 us
    ppermute x4, waiting for transfers between devices, send_back(): return lax.ppermute(value, AXES, [(b, a) for a, b in pairs_of(move)])  5.2 us
  transfers between devices with their start and end apart: 31, of which 23 were waited for; matrix products, arithmetic and copies ran while one was open for 1% of the time, Pallas kernels for 4%

profile of v7, /device:TPU:9, one launch (start us, length us, event | category | flops | bytes accessed | tf_op | source)
XLA Modules:
  0.0 159.1 jit_solution(11021044697560758644)
XLA Ops:
  0.6 0.9 fusion.3
  1.5 0.8 collective-permute-start
  2.4 0.9 collective-permute-done
  3.3 3.2 %collective-permute-start.2 = (bf16[2,3,128,128]{3,2,1,0:T(8,128)(2,1)S(1)}, bf16[2,3,128,128]{3,2,1,0:T(8,128)(2,1)S(1)}, u32[]{:S(2)}, u32[]{:S(2)}) collective-permute-start(bf16[2,3,128,128]{3,2,1,0:T(8,128)(2,1)S(1)} %pad_maximum_fusion.2), channel_id=1, source_target_pairs={{0,128},{1,192},{2,0},{3,64},{4,132},{5,196},{6,4},{7,68},{8,136},... | collective-permute-start | bytes 589832 | tf_op jit(solution)/shard_map/weights_turn/ppermute | solution.py:33
  6.5 7.1 %collective-permute-start.1 = (bf16[2,3,128,128]{3,2,1,0:T(8,128)(2,1)S(1)}, bf16[2,3,128,128]{3,2,1,0:T(8,128)(2,1)S(1)}, u32[]{:S(2)}, u32[]{:S(2)}) collective-permute-start(bf16[2,3,128,128]{3,2,1,0:T(8,128)(2,1)S(1)} %pad_maximum_fusion.2), channel_id=1, source_target_pairs={{0,0},{1,64},{2,128},{3,192},{4,4},{5,68},{6,132},{7,196},{8,8},{9... | collective-permute-start | bytes 589832 | tf_op jit(solution)/shard_map/weights_turn/ppermute | solution.py:33
  13.6 1.3 constant_dynamic-slice_fusion.tok
  15.0 1.1 pick.1
  16.1 3.2 %collective-permute-done.2 = bf16[2,3,128,128]{3,2,1,0:T(8,128)(2,1)S(1)} collective-permute-done((bf16[2,3,128,128]{3,2,1,0:T(8,128)(2,1)S(1)}, bf16[2,3,128,128]{3,2,1,0:T(8,128)(2,1)S(1)}, u32[]{:S(2)}, u32[]{:S(2)}) %collective-permute-start.2) | collective-permute-done | bytes 196640 | tf_op jit(solution)/shard_map/weights_turn/ppermute | solution.py:33
  19.3 3.2 %collective-permute-done.1 = bf16[2,3,128,128]{3,2,1,0:T(8,128)(2,1)S(1)} collective-permute-done((bf16[2,3,128,128]{3,2,1,0:T(8,128)(2,1)S(1)}, bf16[2,3,128,128]{3,2,1,0:T(8,128)(2,1)S(1)}, u32[]{:S(2)}, u32[]{:S(2)}) %collective-permute-start.1) | collective-permute-done | bytes 196640 | tf_op jit(solution)/shard_map/weights_turn/ppermute | solution.py:33
  22.6 2.1 %collective-permute-start.3 = (bf16[2,256,1024]{2,1,0:T(8,128)(2,1)S(1)}, bf16[2,256,1024]{2,1,0:T(8,128)(2,1)S(1)}, u32[]{:S(2)}, u32[]{:S(2)}) collective-permute-start(bf16[2,256,1024]{2,1,0:T(8,128)(2,1)S(1)} %get-tuple-element.42), channel_id=1, source_target_pairs={{0,16},{1,17},{2,18},{3,19},{4,20},{5,21},{6,22},{7,23},{8,24},{9,... | collective-permute-start | bytes 3145736 | tf_op jit(solution)/shard_map/input_swap/ppermute | solution.py:33
  24.7 1.2 collective-permute-start.7
  25.9 2.5 %collective-permute-start.6 = (bf16[2,2,3,128,128]{4,3,2,1,0:T(8,128)(2,1)S(1)}, bf16[2,2,3,128,128]{4,3,2,1,0:T(8,128)(2,1)S(1)}, u32[]{:S(2)}, u32[]{:S(2)}) collective-permute-start(bf16[2,2,3,128,128]{4,3,2,1,0:T(8,128)(2,1)S(1)} %pad_maximum_fusion.1.refs_0_), channel_id=1, source_target_pairs={{0,12},{1,13},{2,14},{3,15},{4,8},{5,9},{6,10},{7,11},{8,4},{9,5},... | collective-permute-start | bytes 1179656 | tf_op jit(solution)/shard_map/weights_x_0/ppermute | solution.py:33
  28.4 1.4 collective-permute-start.5
  29.7 5.4 %collective-permute-done.7.refs_4_ = bf16[2,2,3,128,128]{4,3,2,1,0:T(8,128)(2,1)S(1)} collective-permute-done((bf16[2,2,3,128,128]{4,3,2,1,0:T(8,128)(2,1)S(1)}, bf16[2,2,3,128,128]{4,3,2,1,0:T(8,128)(2,1)S(1)}, u32[]{:S(2)}, u32[]{:S(2)}) %collective-permute-start.7) | collective-permute-done | bytes 393248 | tf_op jit(solution)/shard_map/weights_plane/ppermute | solution.py:33
  35.1 1.5 collective-permute-done.6.refs_3_
  36.6 1.0 collective-permute-done.4.refs_1_
  37.6 1.5 collective-permute-start.10
  39.1 0.4 collective-permute-start.9
  39.4 1.4 collective-permute-start.8
  40.8 7.5 %collective-permute-done.3.far = bf16[2,256,1024]{2,1,0:T(8,128)(2,1)S(1)} collective-permute-done((bf16[2,256,1024]{2,1,0:T(8,128)(2,1)S(1)}, bf16[2,256,1024]{2,1,0:T(8,128)(2,1)S(1)}, u32[]{:S(2)}, u32[]{:S(2)}) %collective-permute-start.3) | collective-permute-done | bytes 1048608 | tf_op jit(solution)/shard_map/input_swap/ppermute | solution.py:33
  48.3 0.1 join.1
  48.4 16.1 %collective-permute-done.10.refs_7_ = bf16[2,2,3,128,128]{4,3,2,1,0:T(8,128)(2,1)S(1)} collective-permute-done((bf16[2,2,3,128,128]{4,3,2,1,0:T(8,128)(2,1)S(1)}, bf16[2,2,3,128,128]{4,3,2,1,0:T(8,128)(2,1)S(1)}, u32[]{:S(2)}, u32[]{:S(2)}) %collective-permute-start.10) | collective-permute-done | bytes 393248 | tf_op jit(solution)/shard_map/weights_x_1/ppermute | solution.py:33
  64.6 1.9 %forward.1 = (bf16[1024,1024]{1,0:T(8,128)(2,1)S(1)}, bf16[512,1024]{1,0:T(8,128)(2,1)S(1)}, f32[256,1536]{1,0:T(8,128)S(1)}, bf16[256,1536]{1,0:T(8,128)(2,1)S(1)}) custom-call(bf16[512,1024]{1,0:T(8,128)(2,1)S(1)} %get-tuple-element.43.tok, bf16[512,1024]{1,0:T(8,128)(2,1)S(1)} %get-tuple-element.44.cot, ...), custom_call_target="tpu_custom_call" | custom-call | flops 1610612736 | bytes 10747904 | tf_op jit(solution)/shard_map/forward/pallas_call | solution.py:87
  66.5 0.7 collective-permute-start.11
  67.2 1.9 %collective-permute-done.11 = bf16[256,1536]{1,0:T(8,128)(2,1)S(1)} collective-permute-done((bf16[256,1536]{1,0:T(8,128)(2,1)S(1)}, bf16[256,1536]{1,0:T(8,128)(2,1)S(1)}, u32[]{:S(2)}, u32[]{:S(2)}) %collective-permute-start.11) | collective-permute-done | bytes 786464 | tf_op jit(solution)/shard_map/ppermute | solution.py:33
  69.1 0.3 fusion.4
  69.4 0.1 collective-permute-start.12
  69.5 1.1 collective-permute-start.14
  70.7 2.1 %collective-permute-start.13 = (bf16[64,1536]{1,0:T(8,128)(2,1)S(1)}, bf16[64,1536]{1,0:T(8,128)(2,1)S(1)}, u32[]{:S(2)}, u32[]{:S(2)}) collective-permute-start(bf16[64,1536]{1,0:T(8,128)(2,1)S(1)} %get-tuple-element.73), channel_id=1, source_target_pairs={{0,16},{1,17},{2,18},{3,19},{4,20},{5,21},{6,22},{7,23},{8,24},{9,... | collective-permute-start | bytes 589832 | tf_op jit(solution)/shard_map/ppermute | solution.py:33
  72.8 2.9 %collective-permute-done.12 = bf16[64,1536]{1,0:T(8,128)(2,1)S(1)} collective-permute-done((bf16[64,1536]{1,0:T(8,128)(2,1)S(1)}, bf16[64,1536]{1,0:T(8,128)(2,1)S(1)}, u32[]{:S(2)}, u32[]{:S(2)}) %collective-permute-start.12) | collective-permute-done | bytes 196640 | tf_op jit(solution)/shard_map/ppermute | solution.py:33
  75.6 0.5 collective-permute-done.14
  76.1 3.5 %collective-permute-done.13 = bf16[64,1536]{1,0:T(8,128)(2,1)S(1)} collective-permute-done((bf16[64,1536]{1,0:T(8,128)(2,1)S(1)}, bf16[64,1536]{1,0:T(8,128)(2,1)S(1)}, u32[]{:S(2)}, u32[]{:S(2)}) %collective-permute-start.13) | collective-permute-done | bytes 196640 | tf_op jit(solution)/shard_map/ppermute | solution.py:33
  79.8 1.5 collective-permute-start.17
  81.3 2.1 %collective-permute-start.16 = (bf16[64,1536]{1,0:T(8,128)(2,1)S(1)}, bf16[64,1536]{1,0:T(8,128)(2,1)S(1)}, u32[]{:S(2)}, u32[]{:S(2)}) collective-permute-start(bf16[64,1536]{1,0:T(8,128)(2,1)S(1)} %pad_maximum_fusion.3), channel_id=1, source_target_pairs={{0,16},{1,17},{2,18},{3,19},{4,20},{5,21},{6,22},{7,23},{8,24},{9,... | collective-permute-start | bytes 589832 | tf_op jit(solution)/shard_map/ppermute | solution.py:33
  83.4 3.2 %collective-permute-done.17 = bf16[64,1536]{1,0:T(8,128)(2,1)S(1)} collective-permute-done((bf16[64,1536]{1,0:T(8,128)(2,1)S(1)}, bf16[64,1536]{1,0:T(8,128)(2,1)S(1)}, u32[]{:S(2)}, u32[]{:S(2)}) %collective-permute-start.17) | collective-permute-done | bytes 196640 | tf_op jit(solution)/shard_map/ppermute | solution.py:33
  86.6 1.2 collective-permute-done.16
  87.8 3.2 %collective-permute-done.15 = bf16[64,1536]{1,0:T(8,128)(2,1)S(1)} collective-permute-done((bf16[64,1536]{1,0:T(8,128)(2,1)S(1)}, bf16[64,1536]{1,0:T(8,128)(2,1)S(1)}, u32[]{:S(2)}, u32[]{:S(2)}) %collective-permute-start.15) | collective-permute-done | bytes 196640 | tf_op jit(solution)/shard_map/ppermute | solution.py:33
  91.1 2.6 %collective-permute-start.18 = (bf16[256,1536]{1,0:T(8,128)(2,1)S(1)}, bf16[256,1536]{1,0:T(8,128)(2,1)S(1)}, u32[]{:S(2)}, u32[]{:S(2)}) collective-permute-start(bf16[256,1536]{1,0:T(8,128)(2,1)S(1)} %pad_maximum_fusion.da), channel_id=1, source_target_pairs={{0,1},{1,0},{2,3},{3,2},{4,5},{5,4},{6,7},{7,6},{8,9},{9,8},{10,11... | collective-permute-start | bytes 2359304 | tf_op jit(solution)/shard_map/ppermute | solution.py:33
  93.6 1.9 %collective-permute-done.18.dc = bf16[256,1536]{1,0:T(8,128)(2,1)S(1)} collective-permute-done((bf16[256,1536]{1,0:T(8,128)(2,1)S(1)}, bf16[256,1536]{1,0:T(8,128)(2,1)S(1)}, u32[]{:S(2)}, u32[]{:S(2)}) %collective-permute-start.18) | collective-permute-done | bytes 786464 | tf_op jit(solution)/shard_map/ppermute | solution.py:33
  95.5 1.3 grads.3
  96.8 0.1 collective-permute-start.22
  96.9 2.2 %collective-permute-start.23 = (bf16[2,2,3,128,128]{4,3,2,1,0:T(8,128)(2,1)S(1)}, bf16[2,2,3,128,128]{4,3,2,1,0:T(8,128)(2,1)S(1)}, u32[]{:S(2)}, u32[]{:S(2)}) collective-permute-start(bf16[2,2,3,128,128]{4,3,2,1,0:T(8,128)(2,1)S(1)} %get-tuple-element.54), channel_id=1, source_target_pairs={{0,12},{1,13},{2,14},{3,15},{4,8},{5,9},{6,10},{7,11},{8,4},{9,5},... | collective-permute-start | bytes 1179656 | tf_op jit(solution)/shard_map/grads_x_1/ppermute | solution.py:33
  99.2 1.1 collective-permute-start.24
  100.2 1.8 %outputs.1 = (bf16[2,256,1024]{2,1,0:T(8,128)(2,1)S(1)}, bf16[2,256,1024]{2,1,0:T(8,128)(2,1)S(1)}) custom-call(bf16[256,1536]{1,0:T(8,128)(2,1)S(1)} %pad_maximum_fusion.da, bf16[256,1536]{1,0:T(8,128)(2,1)S(1)} %collective-permute-done.18.dc, bf16[1024,1024]{1,0:T(8,128)(2,1)S(1)} %get-tuple-element.56.gu, bf16[512,1024]{1,0:T(8,128)(2,1)S(1)} %get-tuple-element.57.dn), custom_call_target="tpu_custom_call" | custom-call | flops 1610612736 | bytes 6815744 | tf_op jit(solution)/shard_map/outputs/pallas_call | solution.py:87
  102.0 1.9 %collective-permute-start.26 = (bf16[2,256,1024]{2,1,0:T(8,128)(2,1)S(1)}, bf16[2,256,1024]{2,1,0:T(8,128)(2,1)S(1)}, u32[]{:S(2)}, u32[]{:S(2)}) collective-permute-start(bf16[2,256,1024]{2,1,0:T(8,128)(2,1)S(1)} %get-tuple-element.58), channel_id=1, source_target_pairs={{0,16},{1,17},{2,18},{3,19},{4,20},{5,21},{6,22},{7,23},{8,24},{9,... | collective-permute-start | bytes 3145736 | tf_op jit(solution)/shard_map/output_swap/ppermute | solution.py:33
  103.9 1.3 grads.2
  105.2 0.2 collective-permute-start.19
  105.4 1.8 %collective-permute-done.22 = bf16[2,2,3,128,128]{4,3,2,1,0:T(8,128)(2,1)S(1)} collective-permute-done((bf16[2,2,3,128,128]{4,3,2,1,0:T(8,128)(2,1)S(1)}, bf16[2,2,3,128,128]{4,3,2,1,0:T(8,128)(2,1)S(1)}, u32[]{:S(2)}, u32[]{:S(2)}) %collective-permute-start.22) | collective-permute-done | bytes 393248 | tf_op jit(solution)/shard_map/grads_x_1/ppermute | solution.py:33
  107.3 2.1 %collective-permute-start.20 = (bf16[2,2,3,128,128]{4,3,2,1,0:T(8,128)(2,1)S(1)}, bf16[2,2,3,128,128]{4,3,2,1,0:T(8,128)(2,1)S(1)}, u32[]{:S(2)}, u32[]{:S(2)}) collective-permute-start(bf16[2,2,3,128,128]{4,3,2,1,0:T(8,128)(2,1)S(1)} %get-tuple-element.50), channel_id=1, source_target_pairs={{0,12},{1,13},{2,14},{3,15},{4,8},{5,9},{6,10},{7,11},{8,4},{9,5},... | collective-permute-start | bytes 1179656 | tf_op jit(solution)/shard_map/grads_x_0/ppermute | solution.py:33
  109.4 9.1 %collective-permute-start.21 = (bf16[2,2,3,128,128]{4,3,2,1,0:T(8,128)(2,1)S(1)}, bf16[2,2,3,128,128]{4,3,2,1,0:T(8,128)(2,1)S(1)}, u32[]{:S(2)}, u32[]{:S(2)}) collective-permute-start(bf16[2,2,3,128,128]{4,3,2,1,0:T(8,128)(2,1)S(1)} %get-tuple-element.51), channel_id=1, source_target_pairs={{0,8},{1,9},{2,10},{3,11},{4,12},{5,13},{6,14},{7,15},{8,0},{9,1},... | collective-permute-start | bytes 1179656 | tf_op jit(solution)/shard_map/grads_x_0/ppermute | solution.py:33
  118.5 0.2 add_convert_fusion.1
  118.7 0.8 collective-permute-start.25
  119.5 4.7 %collective-permute-done.19 = bf16[2,2,3,128,128]{4,3,2,1,0:T(8,128)(2,1)S(1)} collective-permute-done((bf16[2,2,3,128,128]{4,3,2,1,0:T(8,128)(2,1)S(1)}, bf16[2,2,3,128,128]{4,3,2,1,0:T(8,128)(2,1)S(1)}, u32[]{:S(2)}, u32[]{:S(2)}) %collective-permute-start.19) | collective-permute-done | bytes 393248 | tf_op jit(solution)/shard_map/grads_x_0/ppermute | solution.py:33
  124.2 3.2 %collective-permute-done.20 = bf16[2,2,3,128,128]{4,3,2,1,0:T(8,128)(2,1)S(1)} collective-permute-done((bf16[2,2,3,128,128]{4,3,2,1,0:T(8,128)(2,1)S(1)}, bf16[2,2,3,128,128]{4,3,2,1,0:T(8,128)(2,1)S(1)}, u32[]{:S(2)}, u32[]{:S(2)}) %collective-permute-start.20) | collective-permute-done | bytes 393248 | tf_op jit(solution)/shard_map/grads_x_0/ppermute | solution.py:33
  127.3 7.1 %collective-permute-done.21 = bf16[2,2,3,128,128]{4,3,2,1,0:T(8,128)(2,1)S(1)} collective-permute-done((bf16[2,2,3,128,128]{4,3,2,1,0:T(8,128)(2,1)S(1)}, bf16[2,2,3,128,128]{4,3,2,1,0:T(8,128)(2,1)S(1)}, u32[]{:S(2)}, u32[]{:S(2)}) %collective-permute-start.21) | collective-permute-done | bytes 393248 | tf_op jit(solution)/shard_map/grads_x_0/ppermute | solution.py:33
  134.4 0.3 add_convert_fusion
  134.7 4.2 %collective-permute-start.30 = (bf16[3,128,128]{2,1,0:T(8,128)(2,1)S(1)}, bf16[3,128,128]{2,1,0:T(8,128)(2,1)S(1)}, u32[]{:S(2)}, u32[]{:S(2)}) collective-permute-start(bf16[3,128,128]{2,1,0:T(8,128)(2,1)S(1)} %get-tuple-element.74), channel_id=1, source_target_pairs={{192,0},{128,1},{64,2},{0,3},{196,4},{132,5},{68,6},{4,7},{200,8},... | collective-permute-start | bytes 294920 | tf_op jit(solution)/shard_map/grads_turn/ppermute | solution.py:37
  139.0 6.0 %collective-permute-start.29 = (bf16[3,128,128]{2,1,0:T(8,128)(2,1)S(1)}, bf16[3,128,128]{2,1,0:T(8,128)(2,1)S(1)}, u32[]{:S(2)}, u32[]{:S(2)}) collective-permute-start(bf16[3,128,128]{2,1,0:T(8,128)(2,1)S(1)} %get-tuple-element.75), channel_id=1, source_target_pairs={{128,0},{192,1},{0,2},{64,3},{132,4},{196,5},{4,6},{68,7},{136,8},... | collective-permute-start | bytes 294920 | tf_op jit(solution)/shard_map/grads_turn/ppermute | solution.py:37
  145.0 5.8 %collective-permute-start.27 = (bf16[3,128,128]{2,1,0:T(8,128)(2,1)S(1)}, bf16[3,128,128]{2,1,0:T(8,128)(2,1)S(1)}, u32[]{:S(2)}, u32[]{:S(2)}) collective-permute-start(bf16[3,128,128]{2,1,0:T(8,128)(2,1)S(1)} %get-tuple-element.77), channel_id=1, source_target_pairs={{0,0},{64,1},{128,2},{192,3},{4,4},{68,5},{132,6},{196,7},{8,8},{7... | collective-permute-start | bytes 294920 | tf_op jit(solution)/shard_map/grads_turn/ppermute | solution.py:37
  150.8 2.4 %place.1 = (bf16[256,2048]{1,0:T(8,128)(2,1)}, bf16[256,2048]{1,0:T(8,128)(2,1)}) custom-call(s32[4]{0:T(128)S(1)} %pad_add_fusion.where, bf16[2,256,1024]{2,1,0:T(8,128)(2,1)S(1)} %get-tuple-element.60.own, bf16[2,256,1024]{2,1,0:T(8,128)(2,1)S(1)} %collective-permute-done.26.far), custom_call_target="tpu_custom_call" | custom-call | bytes 4194304 | tf_op jit(solution)/shard_map/place/pallas_call | solution.py:87
  153.2 1.0 collective-permute-done.29
  154.2 3.2 %collective-permute-done.28 = bf16[3,128,128]{2,1,0:T(8,128)(2,1)S(1)} collective-permute-done((bf16[3,128,128]{2,1,0:T(8,128)(2,1)S(1)}, bf16[3,128,128]{2,1,0:T(8,128)(2,1)S(1)}, u32[]{:S(2)}, u32[]{:S(2)}) %collective-permute-start.28) | collective-permute-done | bytes 98336 | tf_op jit(solution)/shard_map/grads_turn/ppermute | solution.py:37
  157.4 1.1 collective-permute-done.27
  158.5 0.7 slice_bitcast_fusion.4
  (23 shorter events, 0.5 us)
Async XLA Ops:
  0.6 14.3 %copy-start = (bf16[256,2048]{1,0:T(8,128)(2,1)S(1)}, bf16[256,2048]{1,0:T(8,128)(2,1)}, u32[]{:S(2)}) copy-start(bf16[256,2048]{1,0:T(8,128)(2,1)} %cot) | copy-start | bytes 3145732
  1.5 1.7 %collective-permute-start = (bf16[3,128,128]{2,1,0:T(8,128)(2,1)S(1)}, bf16[3,128,128]{2,1,0:T(8,128)(2,1)S(1)}, u32[]{:S(2)}, u32[]{:S(2)}) collective-permute-start(bf16[3,128,128]{2,1,0:T(8,128)(2,1)S(1)} %get-tuple-element.85), channel_id=1, source_target_pairs={{0,1},{1,0},{2,3},{3,2},{4,5},{5,4},{6,7},{7,6},{8,9},{9,8},{10,11... | collective-permute-start | bytes 294920 | tf_op jit(solution)/shard_map/weights_core/ppermute | solution.py:33
  3.3 16.1 %collective-permute-start.2 = (bf16[2,3,128,128]{3,2,1,0:T(8,128)(2,1)S(1)}, bf16[2,3,128,128]{3,2,1,0:T(8,128)(2,1)S(1)}, u32[]{:S(2)}, u32[]{:S(2)}) collective-permute-start(bf16[2,3,128,128]{3,2,1,0:T(8,128)(2,1)S(1)} %pad_maximum_fusion.2), channel_id=1, source_target_pairs={{0,128},{1,192},{2,0},{3,64},{4,132},{5,196},{6,4},{7,68},{8,136},... | collective-permute-start | bytes 589832 | tf_op jit(solution)/shard_map/weights_turn/ppermute | solution.py:33
  6.5 16.1 %collective-permute-start.1 = (bf16[2,3,128,128]{3,2,1,0:T(8,128)(2,1)S(1)}, bf16[2,3,128,128]{3,2,1,0:T(8,128)(2,1)S(1)}, u32[]{:S(2)}, u32[]{:S(2)}) collective-permute-start(bf16[2,3,128,128]{3,2,1,0:T(8,128)(2,1)S(1)} %pad_maximum_fusion.2), channel_id=1, source_target_pairs={{0,0},{1,64},{2,128},{3,192},{4,4},{5,68},{6,132},{7,196},{8,8},{9... | collective-permute-start | bytes 589832 | tf_op jit(solution)/shard_map/weights_turn/ppermute | solution.py:33
  22.6 25.7 %collective-permute-start.3 = (bf16[2,256,1024]{2,1,0:T(8,128)(2,1)S(1)}, bf16[2,256,1024]{2,1,0:T(8,128)(2,1)S(1)}, u32[]{:S(2)}, u32[]{:S(2)}) collective-permute-start(bf16[2,256,1024]{2,1,0:T(8,128)(2,1)S(1)} %get-tuple-element.42), channel_id=1, source_target_pairs={{0,16},{1,17},{2,18},{3,19},{4,20},{5,21},{6,22},{7,23},{8,24},{9,... | collective-permute-start | bytes 3145736 | tf_op jit(solution)/shard_map/input_swap/ppermute | solution.py:33
  24.7 10.4 %collective-permute-start.7 = (bf16[2,2,3,128,128]{4,3,2,1,0:T(8,128)(2,1)S(1)}, bf16[2,2,3,128,128]{4,3,2,1,0:T(8,128)(2,1)S(1)}, u32[]{:S(2)}, u32[]{:S(2)}) collective-permute-start(bf16[2,2,3,128,128]{4,3,2,1,0:T(8,128)(2,1)S(1)} %pad_maximum_fusion.1.refs_0_), channel_id=1, source_target_pairs={{0,32},{1,33},{2,34},{3,35},{4,36},{5,37},{6,38},{7,39},{8,40},{9,... | collective-permute-start | bytes 1179656 | tf_op jit(solution)/shard_map/weights_plane/ppermute | solution.py:33
  25.9 10.7 %collective-permute-start.6 = (bf16[2,2,3,128,128]{4,3,2,1,0:T(8,128)(2,1)S(1)}, bf16[2,2,3,128,128]{4,3,2,1,0:T(8,128)(2,1)S(1)}, u32[]{:S(2)}, u32[]{:S(2)}) collective-permute-start(bf16[2,2,3,128,128]{4,3,2,1,0:T(8,128)(2,1)S(1)} %pad_maximum_fusion.1.refs_0_), channel_id=1, source_target_pairs={{0,12},{1,13},{2,14},{3,15},{4,8},{5,9},{6,10},{7,11},{8,4},{9,5},... | collective-permute-start | bytes 1179656 | tf_op jit(solution)/shard_map/weights_x_0/ppermute | solution.py:33
  28.3 9.2 %collective-permute-start.4 = (bf16[2,2,3,128,128]{4,3,2,1,0:T(8,128)(2,1)S(1)}, bf16[2,2,3,128,128]{4,3,2,1,0:T(8,128)(2,1)S(1)}, u32[]{:S(2)}, u32[]{:S(2)}) collective-permute-start(bf16[2,2,3,128,128]{4,3,2,1,0:T(8,128)(2,1)S(1)} %pad_maximum_fusion.1.refs_0_), channel_id=1, source_target_pairs={{0,4},{1,5},{2,6},{3,7},{4,0},{5,1},{6,2},{7,3},{8,12},{9,13},{10,... | collective-permute-start | bytes 1179656 | tf_op jit(solution)/shard_map/weights_x_0/ppermute | solution.py:33
  28.4 20.1 %collective-permute-start.5 = (bf16[2,2,3,128,128]{4,3,2,1,0:T(8,128)(2,1)S(1)}, bf16[2,2,3,128,128]{4,3,2,1,0:T(8,128)(2,1)S(1)}, u32[]{:S(2)}, u32[]{:S(2)}) collective-permute-start(bf16[2,2,3,128,128]{4,3,2,1,0:T(8,128)(2,1)S(1)} %pad_maximum_fusion.1.refs_0_), channel_id=1, source_target_pairs={{0,8},{1,9},{2,10},{3,11},{4,12},{5,13},{6,14},{7,15},{8,0},{9,1},... | collective-permute-start | bytes 1179656 | tf_op jit(solution)/shard_map/weights_x_0/ppermute | solution.py:33
  37.6 27.0 %collective-permute-start.10 = (bf16[2,2,3,128,128]{4,3,2,1,0:T(8,128)(2,1)S(1)}, bf16[2,2,3,128,128]{4,3,2,1,0:T(8,128)(2,1)S(1)}, u32[]{:S(2)}, u32[]{:S(2)}) collective-permute-start(bf16[2,2,3,128,128]{4,3,2,1,0:T(8,128)(2,1)S(1)} %collective-permute-done.7.refs_4_), channel_id=1, source_target_pairs={{0,12},{1,13},{2,14},{3,15},{4,8},{5,9},{6,10},{7,11},{8,4},{9,5},... | collective-permute-start | bytes 1179656 | tf_op jit(solution)/shard_map/weights_x_1/ppermute | solution.py:33
  39.1 25.5 %collective-permute-start.9 = (bf16[2,2,3,128,128]{4,3,2,1,0:T(8,128)(2,1)S(1)}, bf16[2,2,3,128,128]{4,3,2,1,0:T(8,128)(2,1)S(1)}, u32[]{:S(2)}, u32[]{:S(2)}) collective-permute-start(bf16[2,2,3,128,128]{4,3,2,1,0:T(8,128)(2,1)S(1)} %collective-permute-done.7.refs_4_), channel_id=1, source_target_pairs={{0,8},{1,9},{2,10},{3,11},{4,12},{5,13},{6,14},{7,15},{8,0},{9,1},... | collective-permute-start | bytes 1179656 | tf_op jit(solution)/shard_map/weights_x_1/ppermute | solution.py:33
  39.4 25.2 %collective-permute-start.8 = (bf16[2,2,3,128,128]{4,3,2,1,0:T(8,128)(2,1)S(1)}, bf16[2,2,3,128,128]{4,3,2,1,0:T(8,128)(2,1)S(1)}, u32[]{:S(2)}, u32[]{:S(2)}) collective-permute-start(bf16[2,2,3,128,128]{4,3,2,1,0:T(8,128)(2,1)S(1)} %collective-permute-done.7.refs_4_), channel_id=1, source_target_pairs={{0,4},{1,5},{2,6},{3,7},{4,0},{5,1},{6,2},{7,3},{8,12},{9,13},{10,... | collective-permute-start | bytes 1179656 | tf_op jit(solution)/shard_map/weights_x_1/ppermute | solution.py:33
  66.5 2.6 %collective-permute-start.11 = (bf16[256,1536]{1,0:T(8,128)(2,1)S(1)}, bf16[256,1536]{1,0:T(8,128)(2,1)S(1)}, u32[]{:S(2)}, u32[]{:S(2)}) collective-permute-start(bf16[256,1536]{1,0:T(8,128)(2,1)S(1)} %get-tuple-element.47), channel_id=1, source_target_pairs={{0,1},{1,0},{2,3},{3,2},{4,5},{5,4},{6,7},{7,6},{8,9},{9,8},{10,11... | collective-permute-start | bytes 2359304 | tf_op jit(solution)/shard_map/ppermute | solution.py:33
  69.4 6.2 %collective-permute-start.12 = (bf16[64,1536]{1,0:T(8,128)(2,1)S(1)}, bf16[64,1536]{1,0:T(8,128)(2,1)S(1)}, u32[]{:S(2)}, u32[]{:S(2)}) collective-permute-start(bf16[64,1536]{1,0:T(8,128)(2,1)S(1)} %get-tuple-element.71), channel_id=1, source_target_pairs={{0,2},{1,3},{2,0},{3,1},{4,6},{5,7},{6,4},{7,5},{8,10},{9,11},{10,... | collective-permute-start | bytes 589832 | tf_op jit(solution)/shard_map/ppermute | solution.py:33
  69.5 6.6 %collective-permute-start.14 = (bf16[64,1536]{1,0:T(8,128)(2,1)S(1)}, bf16[64,1536]{1,0:T(8,128)(2,1)S(1)}, u32[]{:S(2)}, u32[]{:S(2)}) collective-permute-start(bf16[64,1536]{1,0:T(8,128)(2,1)S(1)} %get-tuple-element.72), channel_id=1, source_target_pairs={{0,18},{1,19},{2,16},{3,17},{4,22},{5,23},{6,20},{7,21},{8,26},{9,... | collective-permute-start | bytes 589832 | tf_op jit(solution)/shard_map/ppermute | solution.py:33
  70.7 8.9 %collective-permute-start.13 = (bf16[64,1536]{1,0:T(8,128)(2,1)S(1)}, bf16[64,1536]{1,0:T(8,128)(2,1)S(1)}, u32[]{:S(2)}, u32[]{:S(2)}) collective-permute-start(bf16[64,1536]{1,0:T(8,128)(2,1)S(1)} %get-tuple-element.73), channel_id=1, source_target_pairs={{0,16},{1,17},{2,18},{3,19},{4,20},{5,21},{6,22},{7,23},{8,24},{9,... | collective-permute-start | bytes 589832 | tf_op jit(solution)/shard_map/ppermute | solution.py:33
  79.8 6.8 %collective-permute-start.17 = (bf16[64,1536]{1,0:T(8,128)(2,1)S(1)}, bf16[64,1536]{1,0:T(8,128)(2,1)S(1)}, u32[]{:S(2)}, u32[]{:S(2)}) collective-permute-start(bf16[64,1536]{1,0:T(8,128)(2,1)S(1)} %pad_maximum_fusion.3), channel_id=1, source_target_pairs={{0,18},{1,19},{2,16},{3,17},{4,22},{5,23},{6,20},{7,21},{8,26},{9,... | collective-permute-start | bytes 589832 | tf_op jit(solution)/shard_map/ppermute | solution.py:33
  81.3 6.5 %collective-permute-start.16 = (bf16[64,1536]{1,0:T(8,128)(2,1)S(1)}, bf16[64,1536]{1,0:T(8,128)(2,1)S(1)}, u32[]{:S(2)}, u32[]{:S(2)}) collective-permute-start(bf16[64,1536]{1,0:T(8,128)(2,1)S(1)} %pad_maximum_fusion.3), channel_id=1, source_target_pairs={{0,16},{1,17},{2,18},{3,19},{4,20},{5,21},{6,22},{7,23},{8,24},{9,... | collective-permute-start | bytes 589832 | tf_op jit(solution)/shard_map/ppermute | solution.py:33
  83.4 7.6 %collective-permute-start.15 = (bf16[64,1536]{1,0:T(8,128)(2,1)S(1)}, bf16[64,1536]{1,0:T(8,128)(2,1)S(1)}, u32[]{:S(2)}, u32[]{:S(2)}) collective-permute-start(bf16[64,1536]{1,0:T(8,128)(2,1)S(1)} %pad_maximum_fusion.3), channel_id=1, source_target_pairs={{0,2},{1,3},{2,0},{3,1},{4,6},{5,7},{6,4},{7,5},{8,10},{9,11},{10,... | collective-permute-start | bytes 589832 | tf_op jit(solution)/shard_map/ppermute | solution.py:33
  91.1 4.5 %collective-permute-start.18 = (bf16[256,1536]{1,0:T(8,128)(2,1)S(1)}, bf16[256,1536]{1,0:T(8,128)(2,1)S(1)}, u32[]{:S(2)}, u32[]{:S(2)}) collective-permute-start(bf16[256,1536]{1,0:T(8,128)(2,1)S(1)} %pad_maximum_fusion.da), channel_id=1, source_target_pairs={{0,1},{1,0},{2,3},{3,2},{4,5},{5,4},{6,7},{7,6},{8,9},{9,8},{10,11... | collective-permute-start | bytes 2359304 | tf_op jit(solution)/shard_map/ppermute | solution.py:33
  96.8 10.4 %collective-permute-start.22 = (bf16[2,2,3,128,128]{4,3,2,1,0:T(8,128)(2,1)S(1)}, bf16[2,2,3,128,128]{4,3,2,1,0:T(8,128)(2,1)S(1)}, u32[]{:S(2)}, u32[]{:S(2)}) collective-permute-start(bf16[2,2,3,128,128]{4,3,2,1,0:T(8,128)(2,1)S(1)} %get-tuple-element.53), channel_id=1, source_target_pairs={{0,4},{1,5},{2,6},{3,7},{4,0},{5,1},{6,2},{7,3},{8,12},{9,13},{10,... | collective-permute-start | bytes 1179656 | tf_op jit(solution)/shard_map/grads_x_1/ppermute | solution.py:33
  96.9 12.4 %collective-permute-start.23 = (bf16[2,2,3,128,128]{4,3,2,1,0:T(8,128)(2,1)S(1)}, bf16[2,2,3,128,128]{4,3,2,1,0:T(8,128)(2,1)S(1)}, u32[]{:S(2)}, u32[]{:S(2)}) collective-permute-start(bf16[2,2,3,128,128]{4,3,2,1,0:T(8,128)(2,1)S(1)} %get-tuple-element.54), channel_id=1, source_target_pairs={{0,12},{1,13},{2,14},{3,15},{4,8},{5,9},{6,10},{7,11},{8,4},{9,5},... | collective-permute-start | bytes 1179656 | tf_op jit(solution)/shard_map/grads_x_1/ppermute | solution.py:33
  99.2 19.3 %collective-permute-start.24 = (bf16[2,2,3,128,128]{4,3,2,1,0:T(8,128)(2,1)S(1)}, bf16[2,2,3,128,128]{4,3,2,1,0:T(8,128)(2,1)S(1)}, u32[]{:S(2)}, u32[]{:S(2)}) collective-permute-start(bf16[2,2,3,128,128]{4,3,2,1,0:T(8,128)(2,1)S(1)} %get-tuple-element.55), channel_id=1, source_target_pairs={{0,8},{1,9},{2,10},{3,11},{4,12},{5,13},{6,14},{7,15},{8,0},{9,1},... | collective-permute-start | bytes 1179656 | tf_op jit(solution)/shard_map/grads_x_1/ppermute | solution.py:33
  102.0 32.7 %collective-permute-start.26 = (bf16[2,256,1024]{2,1,0:T(8,128)(2,1)S(1)}, bf16[2,256,1024]{2,1,0:T(8,128)(2,1)S(1)}, u32[]{:S(2)}, u32[]{:S(2)}) collective-permute-start(bf16[2,256,1024]{2,1,0:T(8,128)(2,1)S(1)} %get-tuple-element.58), channel_id=1, source_target_pairs={{0,16},{1,17},{2,18},{3,19},{4,20},{5,21},{6,22},{7,23},{8,24},{9,... | collective-permute-start | bytes 3145736 | tf_op jit(solution)/shard_map/output_swap/ppermute | solution.py:33
  105.2 18.9 %collective-permute-start.19 = (bf16[2,2,3,128,128]{4,3,2,1,0:T(8,128)(2,1)S(1)}, bf16[2,2,3,128,128]{4,3,2,1,0:T(8,128)(2,1)S(1)}, u32[]{:S(2)}, u32[]{:S(2)}) collective-permute-start(bf16[2,2,3,128,128]{4,3,2,1,0:T(8,128)(2,1)S(1)} %get-tuple-element.49), channel_id=1, source_target_pairs={{0,4},{1,5},{2,6},{3,7},{4,0},{5,1},{6,2},{7,3},{8,12},{9,13},{10,... | collective-permute-start | bytes 1179656 | tf_op jit(solution)/shard_map/grads_x_0/ppermute | solution.py:33
  107.3 20.1 %collective-permute-start.20 = (bf16[2,2,3,128,128]{4,3,2,1,0:T(8,128)(2,1)S(1)}, bf16[2,2,3,128,128]{4,3,2,1,0:T(8,128)(2,1)S(1)}, u32[]{:S(2)}, u32[]{:S(2)}) collective-permute-start(bf16[2,2,3,128,128]{4,3,2,1,0:T(8,128)(2,1)S(1)} %get-tuple-element.50), channel_id=1, source_target_pairs={{0,12},{1,13},{2,14},{3,15},{4,8},{5,9},{6,10},{7,11},{8,4},{9,5},... | collective-permute-start | bytes 1179656 | tf_op jit(solution)/shard_map/grads_x_0/ppermute | solution.py:33
  109.4 25.0 %collective-permute-start.21 = (bf16[2,2,3,128,128]{4,3,2,1,0:T(8,128)(2,1)S(1)}, bf16[2,2,3,128,128]{4,3,2,1,0:T(8,128)(2,1)S(1)}, u32[]{:S(2)}, u32[]{:S(2)}) collective-permute-start(bf16[2,2,3,128,128]{4,3,2,1,0:T(8,128)(2,1)S(1)} %get-tuple-element.51), channel_id=1, source_target_pairs={{0,8},{1,9},{2,10},{3,11},{4,12},{5,13},{6,14},{7,15},{8,0},{9,1},... | collective-permute-start | bytes 1179656 | tf_op jit(solution)/shard_map/grads_x_0/ppermute | solution.py:33
  118.7 15.7 %collective-permute-start.25 = (bf16[2,2,3,128,128]{4,3,2,1,0:T(8,128)(2,1)S(1)}, bf16[2,2,3,128,128]{4,3,2,1,0:T(8,128)(2,1)S(1)}, u32[]{:S(2)}, u32[]{:S(2)}) collective-permute-start(bf16[2,2,3,128,128]{4,3,2,1,0:T(8,128)(2,1)S(1)} %add_convert_fusion.1), channel_id=1, source_target_pairs={{0,32},{1,33},{2,34},{3,35},{4,36},{5,37},{6,38},{7,39},{8,40},{9,... | collective-permute-start | bytes 1179656 | tf_op jit(solution)/shard_map/grads_plane/ppermute | solution.py:33
  134.7 18.5 %collective-permute-start.30 = (bf16[3,128,128]{2,1,0:T(8,128)(2,1)S(1)}, bf16[3,128,128]{2,1,0:T(8,128)(2,1)S(1)}, u32[]{:S(2)}, u32[]{:S(2)}) collective-permute-start(bf16[3,128,128]{2,1,0:T(8,128)(2,1)S(1)} %get-tuple-element.74), channel_id=1, source_target_pairs={{192,0},{128,1},{64,2},{0,3},{196,4},{132,5},{68,6},{4,7},{200,8},... | collective-permute-start | bytes 294920 | tf_op jit(solution)/shard_map/grads_turn/ppermute | solution.py:37
  139.0 15.2 %collective-permute-start.29 = (bf16[3,128,128]{2,1,0:T(8,128)(2,1)S(1)}, bf16[3,128,128]{2,1,0:T(8,128)(2,1)S(1)}, u32[]{:S(2)}, u32[]{:S(2)}) collective-permute-start(bf16[3,128,128]{2,1,0:T(8,128)(2,1)S(1)} %get-tuple-element.75), channel_id=1, source_target_pairs={{128,0},{192,1},{0,2},{64,3},{132,4},{196,5},{4,6},{68,7},{136,8},... | collective-permute-start | bytes 294920 | tf_op jit(solution)/shard_map/grads_turn/ppermute | solution.py:37
  145.0 12.4 %collective-permute-start.28 = (bf16[3,128,128]{2,1,0:T(8,128)(2,1)S(1)}, bf16[3,128,128]{2,1,0:T(8,128)(2,1)S(1)}, u32[]{:S(2)}, u32[]{:S(2)}) collective-permute-start(bf16[3,128,128]{2,1,0:T(8,128)(2,1)S(1)} %get-tuple-element.76), channel_id=1, source_target_pairs={{64,0},{0,1},{192,2},{128,3},{68,4},{4,5},{196,6},{132,7},{72,8},{... | collective-permute-start | bytes 294920 | tf_op jit(solution)/shard_map/grads_turn/ppermute | solution.py:37
  145.0 13.4 %collective-permute-start.27 = (bf16[3,128,128]{2,1,0:T(8,128)(2,1)S(1)}, bf16[3,128,128]{2,1,0:T(8,128)(2,1)S(1)}, u32[]{:S(2)}, u32[]{:S(2)}) collective-permute-start(bf16[3,128,128]{2,1,0:T(8,128)(2,1)S(1)} %get-tuple-element.77), channel_id=1, source_target_pairs={{0,0},{64,1},{128,2},{192,3},{4,4},{68,5},{132,6},{196,7},{8,8},{7... | collective-permute-start | bytes 294920 | tf_op jit(solution)/shard_map/grads_turn/ppermute | solution.py:37

commit v8 on v7

--- a/solution.py
+++ b/solution.py
@@ -196,15 +196,14 @@
     quarter = cotangent.shape[1]
     wide, hid = 8 * fb, 4 * fb
 
-    with jax.named_scope("weights_core"):
+    with jax.named_scope("weights"):
         block = jnp.stack([gate_weight, up_weight, down_weight])
-        pair = jnp.stack([block, send(block, swap_core)])
-
     with jax.named_scope("weights_turn"):
-        near = jnp.stack([send(pair, turn(g)) for g in range(2)])
+        turned = [send(block, turn(g, e)) for g in range(2) for e in range(2)]
+        near = jnp.stack(turned).reshape(2, 2, *block.shape)
     with jax.named_scope("weights_plane"):
         far = send(near, swap_plane)
-    where, tokens, cotangent, _ = lax.optimization_barrier((where, tokens, cotangent, pair))
+    where, tokens, cotangent, _ = lax.optimization_barrier((where, tokens, cotangent, block))
     with jax.named_scope("pick"):
         picked = lax.dynamic_slice(tokens, (0, t * quarter), (tb, quarter))
         own, oth = call(pick_body, [((2, tb, wide), BF)] * 2, [picked, cotangent], 0, where)

time: 160 us -> 159 us (level); the launches traced: 159 us -> 156 us
  starting transfers between devices: 65.3 us -> 61.2 us
    ppermute x4, starting transfers between devices: 16.1 us -> 12.8 us  [send_back(): return lax.ppermute(value, AXES, [(b, a) for a, b in pairs_of(move)])]
    ppermute x27 -> x28, waiting for transfers between devices: 73.8 us -> 75.9 us  [send(): return lax.ppermute(value, AXES, pairs_of(move))]
    ppermute x27 -> x28, starting transfers between devices: 49.2 us -> 48.4 us  [send(): return lax.ppermute(value, AXES, pairs_of(move))]
  transfers between devices with their start and end apart: 31 -> 32, of which waited for: 23 -> 22; matrix products, arithmetic and copies ran while one was open for 1% -> 1% of each run, Pallas kernels for 4% -> 4%
where the time goes in v8:
time: 159 us; the launch traced here: 156 us
  waiting for transfers between devices  80.1 us (50%)
  starting transfers between devices  61.2 us (38%)
  Pallas kernels  9.89 us (6%)
  local copies, waits for them, and re-layouts  2.08 us (1%)
  other arithmetic  2.01 us (1%)
    ppermute x28, waiting for transfers between devices, send(): return lax.ppermute(value, AXES, pairs_of(move))  75.9 us
    ppermute x28, starting transfers between devices, send(): return lax.ppermute(value, AXES, pairs_of(move))  48.4 us
    ppermute x4, starting transfers between devices, send_back(): return lax.ppermute(value, AXES, [(b, a) for a, b in pairs_of(move)])  12.8 us
    pallas_call x7, Pallas kernels, call(): pl.pallas_call(body, out_shape=[jax.ShapeDtypeStruct(s, d) for s, d in sh...  9.89 us
    ppermute x4, waiting for transfers between devices, send_back(): return lax.ppermute(value, AXES, [(b, a) for a, b in pairs_of(move)])  4.19 us
  transfers between devices with their start and end apart: 32, of which 22 were waited for; matrix products, arithmetic and copies ran while one was open for 1% of the time, Pallas kernels for 4%

profile of v8, /device:TPU:9, one launch (start us, length us, event | category | flops | bytes accessed | tf_op | source)
XLA Modules:
  0.0 156.2 jit_solution(17136652486382008137)
XLA Ops:
  0.6 0.9 pad_maximum_fusion.3
  1.5 2.6 %collective-permute-start.3 = (bf16[3,128,128]{2,1,0:T(8,128)(2,1)S(1)}, bf16[3,128,128]{2,1,0:T(8,128)(2,1)S(1)}, u32[]{:S(2)}, u32[]{:S(2)}) collective-permute-start(bf16[3,128,128]{2,1,0:T(8,128)(2,1)S(1)} %pad_maximum_fusion.3), channel_id=1, source_target_pairs={{0,192},{1,128},{2,64},{3,0},{4,196},{5,132},{6,68},{7,4},{8,200},... | collective-permute-start | bytes 294920 | tf_op jit(solution)/shard_map/weights_turn/ppermute | solution.py:33
  4.1 5.8 %collective-permute-start.2 = (bf16[3,128,128]{2,1,0:T(8,128)(2,1)S(1)}, bf16[3,128,128]{2,1,0:T(8,128)(2,1)S(1)}, u32[]{:S(2)}, u32[]{:S(2)}) collective-permute-start(bf16[3,128,128]{2,1,0:T(8,128)(2,1)S(1)} %pad_maximum_fusion.3), channel_id=1, source_target_pairs={{0,128},{1,192},{2,0},{3,64},{4,132},{5,196},{6,4},{7,68},{8,136},... | collective-permute-start | bytes 294920 | tf_op jit(solution)/shard_map/weights_turn/ppermute | solution.py:33
  9.9 1.6 %collective-permute-start.1 = (bf16[3,128,128]{2,1,0:T(8,128)(2,1)S(1)}, bf16[3,128,128]{2,1,0:T(8,128)(2,1)S(1)}, u32[]{:S(2)}, u32[]{:S(2)}) collective-permute-start(bf16[3,128,128]{2,1,0:T(8,128)(2,1)S(1)} %pad_maximum_fusion.3), channel_id=1, source_target_pairs={{0,64},{1,0},{2,192},{3,128},{4,68},{5,4},{6,196},{7,132},{8,72},{... | collective-permute-start | bytes 294920 | tf_op jit(solution)/shard_map/weights_turn/ppermute | solution.py:33
  11.5 3.9 %collective-permute-start = (bf16[3,128,128]{2,1,0:T(8,128)(2,1)S(1)}, bf16[3,128,128]{2,1,0:T(8,128)(2,1)S(1)}, u32[]{:S(2)}, u32[]{:S(2)}) collective-permute-start(bf16[3,128,128]{2,1,0:T(8,128)(2,1)S(1)} %pad_maximum_fusion.3), channel_id=1, source_target_pairs={{0,0},{1,64},{2,128},{3,192},{4,4},{5,68},{6,132},{7,196},{8,8},{9... | collective-permute-start | bytes 294920 | tf_op jit(solution)/shard_map/weights_turn/ppermute | solution.py:33
  15.5 1.3 constant_dynamic-slice_fusion.tok
  16.8 1.1 pick.1
  18.0 4.5 %collective-permute-done = bf16[3,128,128]{2,1,0:T(8,128)(2,1)S(1)} collective-permute-done((bf16[3,128,128]{2,1,0:T(8,128)(2,1)S(1)}, bf16[3,128,128]{2,1,0:T(8,128)(2,1)S(1)}, u32[]{:S(2)}, u32[]{:S(2)}) %collective-permute-start) | collective-permute-done | bytes 98336 | tf_op jit(solution)/shard_map/weights_turn/ppermute | solution.py:33
  22.6 2.2 %collective-permute-start.4 = (bf16[2,256,1024]{2,1,0:T(8,128)(2,1)S(1)}, bf16[2,256,1024]{2,1,0:T(8,128)(2,1)S(1)}, u32[]{:S(2)}, u32[]{:S(2)}) collective-permute-start(bf16[2,256,1024]{2,1,0:T(8,128)(2,1)S(1)} %get-tuple-element.42), channel_id=1, source_target_pairs={{0,16},{1,17},{2,18},{3,19},{4,20},{5,21},{6,22},{7,23},{8,24},{9,... | collective-permute-start | bytes 3145736 | tf_op jit(solution)/shard_map/input_swap/ppermute | solution.py:33
  24.7 2.1 %collective-permute-start.8 = (bf16[2,2,3,128,128]{4,3,2,1,0:T(8,128)(2,1)S(1)}, bf16[2,2,3,128,128]{4,3,2,1,0:T(8,128)(2,1)S(1)}, u32[]{:S(2)}, u32[]{:S(2)}) collective-permute-start(bf16[2,2,3,128,128]{4,3,2,1,0:T(8,128)(2,1)S(1)} %bitcast.26), channel_id=1, source_target_pairs={{0,32},{1,33},{2,34},{3,35},{4,36},{5,37},{6,38},{7,39},{8,40},{9,... | collective-permute-start | bytes 1179656 | tf_op jit(solution)/shard_map/weights_plane/ppermute | solution.py:33
  26.9 2.5 %collective-permute-start.7 = (bf16[2,2,3,128,128]{4,3,2,1,0:T(8,128)(2,1)S(1)}, bf16[2,2,3,128,128]{4,3,2,1,0:T(8,128)(2,1)S(1)}, u32[]{:S(2)}, u32[]{:S(2)}) collective-permute-start(bf16[2,2,3,128,128]{4,3,2,1,0:T(8,128)(2,1)S(1)} %bitcast.27), channel_id=1, source_target_pairs={{0,12},{1,13},{2,14},{3,15},{4,8},{5,9},{6,10},{7,11},{8,4},{9,5},... | collective-permute-start | bytes 1179656 | tf_op jit(solution)/shard_map/weights_x_0/ppermute | solution.py:33
  29.4 1.4 collective-permute-start.6
  30.7 5.7 %collective-permute-done.8.refs_4_ = bf16[2,2,3,128,128]{4,3,2,1,0:T(8,128)(2,1)S(1)} collective-permute-done((bf16[2,2,3,128,128]{4,3,2,1,0:T(8,128)(2,1)S(1)}, bf16[2,2,3,128,128]{4,3,2,1,0:T(8,128)(2,1)S(1)}, u32[]{:S(2)}, u32[]{:S(2)}) %collective-permute-start.8) | collective-permute-done | bytes 393248 | tf_op jit(solution)/shard_map/weights_plane/ppermute | solution.py:33
  36.4 2.5 %collective-permute-done.7.refs_3_ = bf16[2,2,3,128,128]{4,3,2,1,0:T(8,128)(2,1)S(1)} collective-permute-done((bf16[2,2,3,128,128]{4,3,2,1,0:T(8,128)(2,1)S(1)}, bf16[2,2,3,128,128]{4,3,2,1,0:T(8,128)(2,1)S(1)}, u32[]{:S(2)}, u32[]{:S(2)}) %collective-permute-start.7) | collective-permute-done | bytes 393248 | tf_op jit(solution)/shard_map/weights_x_0/ppermute | solution.py:33
  38.9 0.9 collective-permute-done.5.refs_1_
  39.8 1.5 collective-permute-start.11
  41.4 0.3 collective-permute-start.10
  41.7 1.4 collective-permute-start.9
  43.1 5.8 %collective-permute-done.4.far = bf16[2,256,1024]{2,1,0:T(8,128)(2,1)S(1)} collective-permute-done((bf16[2,256,1024]{2,1,0:T(8,128)(2,1)S(1)}, bf16[2,256,1024]{2,1,0:T(8,128)(2,1)S(1)}, u32[]{:S(2)}, u32[]{:S(2)}) %collective-permute-start.4) | collective-permute-done | bytes 1048608 | tf_op jit(solution)/shard_map/input_swap/ppermute | solution.py:33
  48.9 0.1 join.1
  49.0 16.5 %collective-permute-done.11.refs_7_ = bf16[2,2,3,128,128]{4,3,2,1,0:T(8,128)(2,1)S(1)} collective-permute-done((bf16[2,2,3,128,128]{4,3,2,1,0:T(8,128)(2,1)S(1)}, bf16[2,2,3,128,128]{4,3,2,1,0:T(8,128)(2,1)S(1)}, u32[]{:S(2)}, u32[]{:S(2)}) %collective-permute-start.11) | collective-permute-done | bytes 393248 | tf_op jit(solution)/shard_map/weights_x_1/ppermute | solution.py:33
  65.6 1.9 %forward.1 = (bf16[1024,1024]{1,0:T(8,128)(2,1)S(1)}, bf16[512,1024]{1,0:T(8,128)(2,1)S(1)}, f32[256,1536]{1,0:T(8,128)S(1)}, bf16[256,1536]{1,0:T(8,128)(2,1)S(1)}) custom-call(bf16[512,1024]{1,0:T(8,128)(2,1)S(1)} %get-tuple-element.43.tok, bf16[512,1024]{1,0:T(8,128)(2,1)S(1)} %get-tuple-element.44.cot, bf16[2,2,3,128,128]{4,3,2,1,0:T(8,128)(2,1)S(1)} %bitcast.30, ...), custom_call_target="tpu_custom_call" | custom-call | flops 1610612736 | bytes 10747904 | tf_op jit(solution)/shard_map/forward/pallas_call | solution.py:87
  67.5 0.7 collective-permute-start.12
  68.2 1.9 %collective-permute-done.12 = bf16[256,1536]{1,0:T(8,128)(2,1)S(1)} collective-permute-done((bf16[256,1536]{1,0:T(8,128)(2,1)S(1)}, bf16[256,1536]{1,0:T(8,128)(2,1)S(1)}, u32[]{:S(2)}, u32[]{:S(2)}) %collective-permute-start.12) | collective-permute-done | bytes 786464 | tf_op jit(solution)/shard_map/ppermute | solution.py:33
  70.1 0.3 fusion.3
  70.4 0.1 collective-permute-start.13
  70.5 0.9 collective-permute-start.15
  71.4 2.3 %collective-permute-start.14 = (bf16[64,1536]{1,0:T(8,128)(2,1)S(1)}, bf16[64,1536]{1,0:T(8,128)(2,1)S(1)}, u32[]{:S(2)}, u32[]{:S(2)}) collective-permute-start(bf16[64,1536]{1,0:T(8,128)(2,1)S(1)} %get-tuple-element.73), channel_id=1, source_target_pairs={{0,16},{1,17},{2,18},{3,19},{4,20},{5,21},{6,22},{7,23},{8,24},{9,... | collective-permute-start | bytes 589832 | tf_op jit(solution)/shard_map/ppermute | solution.py:33
  73.8 2.9 %collective-permute-done.13 = bf16[64,1536]{1,0:T(8,128)(2,1)S(1)} collective-permute-done((bf16[64,1536]{1,0:T(8,128)(2,1)S(1)}, bf16[64,1536]{1,0:T(8,128)(2,1)S(1)}, u32[]{:S(2)}, u32[]{:S(2)}) %collective-permute-start.13) | collective-permute-done | bytes 196640 | tf_op jit(solution)/shard_map/ppermute | solution.py:33
  76.6 0.6 collective-permute-done.15
  77.2 3.2 %collective-permute-done.14 = bf16[64,1536]{1,0:T(8,128)(2,1)S(1)} collective-permute-done((bf16[64,1536]{1,0:T(8,128)(2,1)S(1)}, bf16[64,1536]{1,0:T(8,128)(2,1)S(1)}, u32[]{:S(2)}, u32[]{:S(2)}) %collective-permute-start.14) | collective-permute-done | bytes 196640 | tf_op jit(solution)/shard_map/ppermute | solution.py:33
  80.6 1.7 %collective-permute-start.18 = (bf16[64,1536]{1,0:T(8,128)(2,1)S(1)}, bf16[64,1536]{1,0:T(8,128)(2,1)S(1)}, u32[]{:S(2)}, u32[]{:S(2)}) collective-permute-start(bf16[64,1536]{1,0:T(8,128)(2,1)S(1)} %pad_maximum_fusion.2), channel_id=1, source_target_pairs={{0,18},{1,19},{2,16},{3,17},{4,22},{5,23},{6,20},{7,21},{8,26},{9,... | collective-permute-start | bytes 589832 | tf_op jit(solution)/shard_map/ppermute | solution.py:33
  82.3 3.0 %collective-permute-start.17 = (bf16[64,1536]{1,0:T(8,128)(2,1)S(1)}, bf16[64,1536]{1,0:T(8,128)(2,1)S(1)}, u32[]{:S(2)}, u32[]{:S(2)}) collective-permute-start(bf16[64,1536]{1,0:T(8,128)(2,1)S(1)} %pad_maximum_fusion.2), channel_id=1, source_target_pairs={{0,16},{1,17},{2,18},{3,19},{4,20},{5,21},{6,22},{7,23},{8,24},{9,... | collective-permute-start | bytes 589832 | tf_op jit(solution)/shard_map/ppermute | solution.py:33
  85.3 2.7 %collective-permute-done.18 = bf16[64,1536]{1,0:T(8,128)(2,1)S(1)} collective-permute-done((bf16[64,1536]{1,0:T(8,128)(2,1)S(1)}, bf16[64,1536]{1,0:T(8,128)(2,1)S(1)}, u32[]{:S(2)}, u32[]{:S(2)}) %collective-permute-start.18) | collective-permute-done | bytes 196640 | tf_op jit(solution)/shard_map/ppermute | solution.py:33
  88.0 0.8 collective-permute-done.17
  88.8 3.4 %collective-permute-done.16 = bf16[64,1536]{1,0:T(8,128)(2,1)S(1)} collective-permute-done((bf16[64,1536]{1,0:T(8,128)(2,1)S(1)}, bf16[64,1536]{1,0:T(8,128)(2,1)S(1)}, u32[]{:S(2)}, u32[]{:S(2)}) %collective-permute-start.16) | collective-permute-done | bytes 196640 | tf_op jit(solution)/shard_map/ppermute | solution.py:33
  92.2 2.5 %collective-permute-start.19 = (bf16[256,1536]{1,0:T(8,128)(2,1)S(1)}, bf16[256,1536]{1,0:T(8,128)(2,1)S(1)}, u32[]{:S(2)}, u32[]{:S(2)}) collective-permute-start(bf16[256,1536]{1,0:T(8,128)(2,1)S(1)} %pad_maximum_fusion.da), channel_id=1, source_target_pairs={{0,1},{1,0},{2,3},{3,2},{4,5},{5,4},{6,7},{7,6},{8,9},{9,8},{10,11... | collective-permute-start | bytes 2359304 | tf_op jit(solution)/shard_map/ppermute | solution.py:33
  94.8 1.9 %collective-permute-done.19.dc = bf16[256,1536]{1,0:T(8,128)(2,1)S(1)} collective-permute-done((bf16[256,1536]{1,0:T(8,128)(2,1)S(1)}, bf16[256,1536]{1,0:T(8,128)(2,1)S(1)}, u32[]{:S(2)}, u32[]{:S(2)}) %collective-permute-start.19) | collective-permute-done | bytes 786464 | tf_op jit(solution)/shard_map/ppermute | solution.py:33
  96.7 1.3 grads.3
  98.0 0.1 collective-permute-start.23
  98.1 2.4 %collective-permute-start.24 = (bf16[2,2,3,128,128]{4,3,2,1,0:T(8,128)(2,1)S(1)}, bf16[2,2,3,128,128]{4,3,2,1,0:T(8,128)(2,1)S(1)}, u32[]{:S(2)}, u32[]{:S(2)}) collective-permute-start(bf16[2,2,3,128,128]{4,3,2,1,0:T(8,128)(2,1)S(1)} %get-tuple-element.54), channel_id=1, source_target_pairs={{0,12},{1,13},{2,14},{3,15},{4,8},{5,9},{6,10},{7,11},{8,4},{9,5},... | collective-permute-start | bytes 1179656 | tf_op jit(solution)/shard_map/grads_x_1/ppermute | solution.py:33
  100.5 1.1 collective-permute-start.25
  101.6 1.8 %outputs.1 = (bf16[2,256,1024]{2,1,0:T(8,128)(2,1)S(1)}, bf16[2,256,1024]{2,1,0:T(8,128)(2,1)S(1)}) custom-call(bf16[256,1536]{1,0:T(8,128)(2,1)S(1)} %pad_maximum_fusion.da, bf16[256,1536]{1,0:T(8,128)(2,1)S(1)} %collective-permute-done.19.dc, bf16[1024,1024]{1,0:T(8,128)(2,1)S(1)} %get-tuple-element.56.gu, bf16[512,1024]{1,0:T(8,128)(2,1)S(1)} %get-tuple-element.57.dn), custom_call_target="tpu_custom_call" | custom-call | flops 1610612736 | bytes 6815744 | tf_op jit(solution)/shard_map/outputs/pallas_call | solution.py:87
  103.4 1.8 %collective-permute-start.27 = (bf16[2,256,1024]{2,1,0:T(8,128)(2,1)S(1)}, bf16[2,256,1024]{2,1,0:T(8,128)(2,1)S(1)}, u32[]{:S(2)}, u32[]{:S(2)}) collective-permute-start(bf16[2,256,1024]{2,1,0:T(8,128)(2,1)S(1)} %get-tuple-element.58), channel_id=1, source_target_pairs={{0,16},{1,17},{2,18},{3,19},{4,20},{5,21},{6,22},{7,23},{8,24},{9,... | collective-permute-start | bytes 3145736 | tf_op jit(solution)/shard_map/output_swap/ppermute | solution.py:33
  105.2 1.3 grads.2
  106.5 0.1 collective-permute-start.20
  106.6 1.8 %collective-permute-done.23 = bf16[2,2,3,128,128]{4,3,2,1,0:T(8,128)(2,1)S(1)} collective-permute-done((bf16[2,2,3,128,128]{4,3,2,1,0:T(8,128)(2,1)S(1)}, bf16[2,2,3,128,128]{4,3,2,1,0:T(8,128)(2,1)S(1)}, u32[]{:S(2)}, u32[]{:S(2)}) %collective-permute-start.23) | collective-permute-done | bytes 393248 | tf_op jit(solution)/shard_map/grads_x_1/ppermute | solution.py:33
  108.4 2.3 %collective-permute-start.21 = (bf16[2,2,3,128,128]{4,3,2,1,0:T(8,128)(2,1)S(1)}, bf16[2,2,3,128,128]{4,3,2,1,0:T(8,128)(2,1)S(1)}, u32[]{:S(2)}, u32[]{:S(2)}) collective-permute-start(bf16[2,2,3,128,128]{4,3,2,1,0:T(8,128)(2,1)S(1)} %get-tuple-element.50), channel_id=1, source_target_pairs={{0,12},{1,13},{2,14},{3,15},{4,8},{5,9},{6,10},{7,11},{8,4},{9,5},... | collective-permute-start | bytes 1179656 | tf_op jit(solution)/shard_map/grads_x_0/ppermute | solution.py:33
  110.7 5.4 %collective-permute-done.24 = bf16[2,2,3,128,128]{4,3,2,1,0:T(8,128)(2,1)S(1)} collective-permute-done((bf16[2,2,3,128,128]{4,3,2,1,0:T(8,128)(2,1)S(1)}, bf16[2,2,3,128,128]{4,3,2,1,0:T(8,128)(2,1)S(1)}, u32[]{:S(2)}, u32[]{:S(2)}) %collective-permute-start.24) | collective-permute-done | bytes 393248 | tf_op jit(solution)/shard_map/grads_x_1/ppermute | solution.py:33
  116.1 3.9 %collective-permute-start.22 = (bf16[2,2,3,128,128]{4,3,2,1,0:T(8,128)(2,1)S(1)}, bf16[2,2,3,128,128]{4,3,2,1,0:T(8,128)(2,1)S(1)}, u32[]{:S(2)}, u32[]{:S(2)}) collective-permute-start(bf16[2,2,3,128,128]{4,3,2,1,0:T(8,128)(2,1)S(1)} %get-tuple-element.51), channel_id=1, source_target_pairs={{0,8},{1,9},{2,10},{3,11},{4,12},{5,13},{6,14},{7,15},{8,0},{9,1},... | collective-permute-start | bytes 1179656 | tf_op jit(solution)/shard_map/grads_x_0/ppermute | solution.py:33
  120.0 0.2 add_convert_fusion.1
  120.2 0.1 collective-permute-start.26
  120.3 5.0 %collective-permute-done.20 = bf16[2,2,3,128,128]{4,3,2,1,0:T(8,128)(2,1)S(1)} collective-permute-done((bf16[2,2,3,128,128]{4,3,2,1,0:T(8,128)(2,1)S(1)}, bf16[2,2,3,128,128]{4,3,2,1,0:T(8,128)(2,1)S(1)}, u32[]{:S(2)}, u32[]{:S(2)}) %collective-permute-start.20) | collective-permute-done | bytes 393248 | tf_op jit(solution)/shard_map/grads_x_0/ppermute | solution.py:33
  125.3 3.4 %collective-permute-done.21 = bf16[2,2,3,128,128]{4,3,2,1,0:T(8,128)(2,1)S(1)} collective-permute-done((bf16[2,2,3,128,128]{4,3,2,1,0:T(8,128)(2,1)S(1)}, bf16[2,2,3,128,128]{4,3,2,1,0:T(8,128)(2,1)S(1)}, u32[]{:S(2)}, u32[]{:S(2)}) %collective-permute-start.21) | collective-permute-done | bytes 393248 | tf_op jit(solution)/shard_map/grads_x_0/ppermute | solution.py:33
  128.7 7.1 %collective-permute-done.22 = bf16[2,2,3,128,128]{4,3,2,1,0:T(8,128)(2,1)S(1)} collective-permute-done((bf16[2,2,3,128,128]{4,3,2,1,0:T(8,128)(2,1)S(1)}, bf16[2,2,3,128,128]{4,3,2,1,0:T(8,128)(2,1)S(1)}, u32[]{:S(2)}, u32[]{:S(2)}) %collective-permute-start.22) | collective-permute-done | bytes 393248 | tf_op jit(solution)/shard_map/grads_x_0/ppermute | solution.py:33
  135.8 0.3 add_convert_fusion
  136.1 1.4 collective-permute-start.31
  137.6 5.5 %collective-permute-start.30 = (bf16[3,128,128]{2,1,0:T(8,128)(2,1)S(1)}, bf16[3,128,128]{2,1,0:T(8,128)(2,1)S(1)}, u32[]{:S(2)}, u32[]{:S(2)}) collective-permute-start(bf16[3,128,128]{2,1,0:T(8,128)(2,1)S(1)} %get-tuple-element.75), channel_id=1, source_target_pairs={{128,0},{192,1},{0,2},{64,3},{132,4},{196,5},{4,6},{68,7},{136,8},... | collective-permute-start | bytes 294920 | tf_op jit(solution)/shard_map/grads_turn/ppermute | solution.py:37
  143.1 5.8 %collective-permute-start.28 = (bf16[3,128,128]{2,1,0:T(8,128)(2,1)S(1)}, bf16[3,128,128]{2,1,0:T(8,128)(2,1)S(1)}, u32[]{:S(2)}, u32[]{:S(2)}) collective-permute-start(bf16[3,128,128]{2,1,0:T(8,128)(2,1)S(1)} %get-tuple-element.77), channel_id=1, source_target_pairs={{0,0},{64,1},{128,2},{192,3},{4,4},{68,5},{132,6},{196,7},{8,8},{7... | collective-permute-start | bytes 294920 | tf_op jit(solution)/shard_map/grads_turn/ppermute | solution.py:37
  148.9 2.4 %place.1 = (bf16[256,2048]{1,0:T(8,128)(2,1)}, bf16[256,2048]{1,0:T(8,128)(2,1)}) custom-call(s32[4]{0:T(128)S(1)} %pad_add_fusion.where, bf16[2,256,1024]{2,1,0:T(8,128)(2,1)S(1)} %get-tuple-element.60.own, bf16[2,256,1024]{2,1,0:T(8,128)(2,1)S(1)} %collective-permute-done.27.far), custom_call_target="tpu_custom_call" | custom-call | bytes 4194304 | tf_op jit(solution)/shard_map/place/pallas_call | solution.py:87
  151.3 1.0 collective-permute-done.30
  152.3 2.1 %collective-permute-done.29 = bf16[3,128,128]{2,1,0:T(8,128)(2,1)S(1)} collective-permute-done((bf16[3,128,128]{2,1,0:T(8,128)(2,1)S(1)}, bf16[3,128,128]{2,1,0:T(8,128)(2,1)S(1)}, u32[]{:S(2)}, u32[]{:S(2)}) %collective-permute-start.29) | collective-permute-done | bytes 98336 | tf_op jit(solution)/shard_map/grads_turn/ppermute | solution.py:37
  154.4 1.1 collective-permute-done.28
  155.6 0.7 slice_bitcast_fusion.4
  (24 shorter events, 0.5 us)
Async XLA Ops:
  0.6 16.2 %copy-start = (bf16[256,2048]{1,0:T(8,128)(2,1)S(1)}, bf16[256,2048]{1,0:T(8,128)(2,1)}, u32[]{:S(2)}) copy-start(bf16[256,2048]{1,0:T(8,128)(2,1)} %cot) | copy-start | bytes 3145732
  1.5 16.5 %collective-permute-start.3 = (bf16[3,128,128]{2,1,0:T(8,128)(2,1)S(1)}, bf16[3,128,128]{2,1,0:T(8,128)(2,1)S(1)}, u32[]{:S(2)}, u32[]{:S(2)}) collective-permute-start(bf16[3,128,128]{2,1,0:T(8,128)(2,1)S(1)} %pad_maximum_fusion.3), channel_id=1, source_target_pairs={{0,192},{1,128},{2,64},{3,0},{4,196},{5,132},{6,68},{7,4},{8,200},... | collective-permute-start | bytes 294920 | tf_op jit(solution)/shard_map/weights_turn/ppermute | solution.py:33
  4.1 13.9 %collective-permute-start.2 = (bf16[3,128,128]{2,1,0:T(8,128)(2,1)S(1)}, bf16[3,128,128]{2,1,0:T(8,128)(2,1)S(1)}, u32[]{:S(2)}, u32[]{:S(2)}) collective-permute-start(bf16[3,128,128]{2,1,0:T(8,128)(2,1)S(1)} %pad_maximum_fusion.3), channel_id=1, source_target_pairs={{0,128},{1,192},{2,0},{3,64},{4,132},{5,196},{6,4},{7,68},{8,136},... | collective-permute-start | bytes 294920 | tf_op jit(solution)/shard_map/weights_turn/ppermute | solution.py:33
  9.9 8.1 %collective-permute-start.1 = (bf16[3,128,128]{2,1,0:T(8,128)(2,1)S(1)}, bf16[3,128,128]{2,1,0:T(8,128)(2,1)S(1)}, u32[]{:S(2)}, u32[]{:S(2)}) collective-permute-start(bf16[3,128,128]{2,1,0:T(8,128)(2,1)S(1)} %pad_maximum_fusion.3), channel_id=1, source_target_pairs={{0,64},{1,0},{2,192},{3,128},{4,68},{5,4},{6,196},{7,132},{8,72},{... | collective-permute-start | bytes 294920 | tf_op jit(solution)/shard_map/weights_turn/ppermute | solution.py:33
  11.5 11.0 %collective-permute-start = (bf16[3,128,128]{2,1,0:T(8,128)(2,1)S(1)}, bf16[3,128,128]{2,1,0:T(8,128)(2,1)S(1)}, u32[]{:S(2)}, u32[]{:S(2)}) collective-permute-start(bf16[3,128,128]{2,1,0:T(8,128)(2,1)S(1)} %pad_maximum_fusion.3), channel_id=1, source_target_pairs={{0,0},{1,64},{2,128},{3,192},{4,4},{5,68},{6,132},{7,196},{8,8},{9... | collective-permute-start | bytes 294920 | tf_op jit(solution)/shard_map/weights_turn/ppermute | solution.py:33
  22.6 26.3 %collective-permute-start.4 = (bf16[2,256,1024]{2,1,0:T(8,128)(2,1)S(1)}, bf16[2,256,1024]{2,1,0:T(8,128)(2,1)S(1)}, u32[]{:S(2)}, u32[]{:S(2)}) collective-permute-start(bf16[2,256,1024]{2,1,0:T(8,128)(2,1)S(1)} %get-tuple-element.42), channel_id=1, source_target_pairs={{0,16},{1,17},{2,18},{3,19},{4,20},{5,21},{6,22},{7,23},{8,24},{9,... | collective-permute-start | bytes 3145736 | tf_op jit(solution)/shard_map/input_swap/ppermute | solution.py:33
  24.7 11.7 %collective-permute-start.8 = (bf16[2,2,3,128,128]{4,3,2,1,0:T(8,128)(2,1)S(1)}, bf16[2,2,3,128,128]{4,3,2,1,0:T(8,128)(2,1)S(1)}, u32[]{:S(2)}, u32[]{:S(2)}) collective-permute-start(bf16[2,2,3,128,128]{4,3,2,1,0:T(8,128)(2,1)S(1)} %bitcast.26), channel_id=1, source_target_pairs={{0,32},{1,33},{2,34},{3,35},{4,36},{5,37},{6,38},{7,39},{8,40},{9,... | collective-permute-start | bytes 1179656 | tf_op jit(solution)/shard_map/weights_plane/ppermute | solution.py:33
  26.9 12.0 %collective-permute-start.7 = (bf16[2,2,3,128,128]{4,3,2,1,0:T(8,128)(2,1)S(1)}, bf16[2,2,3,128,128]{4,3,2,1,0:T(8,128)(2,1)S(1)}, u32[]{:S(2)}, u32[]{:S(2)}) collective-permute-start(bf16[2,2,3,128,128]{4,3,2,1,0:T(8,128)(2,1)S(1)} %bitcast.27), channel_id=1, source_target_pairs={{0,12},{1,13},{2,14},{3,15},{4,8},{5,9},{6,10},{7,11},{8,4},{9,5},... | collective-permute-start | bytes 1179656 | tf_op jit(solution)/shard_map/weights_x_0/ppermute | solution.py:33
  29.3 10.5 %collective-permute-start.5 = (bf16[2,2,3,128,128]{4,3,2,1,0:T(8,128)(2,1)S(1)}, bf16[2,2,3,128,128]{4,3,2,1,0:T(8,128)(2,1)S(1)}, u32[]{:S(2)}, u32[]{:S(2)}) collective-permute-start(bf16[2,2,3,128,128]{4,3,2,1,0:T(8,128)(2,1)S(1)} %bitcast.28), channel_id=1, source_target_pairs={{0,4},{1,5},{2,6},{3,7},{4,0},{5,1},{6,2},{7,3},{8,12},{9,13},{10,... | collective-permute-start | bytes 1179656 | tf_op jit(solution)/shard_map/weights_x_0/ppermute | solution.py:33
  29.4 19.7 %collective-permute-start.6 = (bf16[2,2,3,128,128]{4,3,2,1,0:T(8,128)(2,1)S(1)}, bf16[2,2,3,128,128]{4,3,2,1,0:T(8,128)(2,1)S(1)}, u32[]{:S(2)}, u32[]{:S(2)}) collective-permute-start(bf16[2,2,3,128,128]{4,3,2,1,0:T(8,128)(2,1)S(1)} %bitcast.29), channel_id=1, source_target_pairs={{0,8},{1,9},{2,10},{3,11},{4,12},{5,13},{6,14},{7,15},{8,0},{9,1},... | collective-permute-start | bytes 1179656 | tf_op jit(solution)/shard_map/weights_x_0/ppermute | solution.py:33
  39.8 25.8 %collective-permute-start.11 = (bf16[2,2,3,128,128]{4,3,2,1,0:T(8,128)(2,1)S(1)}, bf16[2,2,3,128,128]{4,3,2,1,0:T(8,128)(2,1)S(1)}, u32[]{:S(2)}, u32[]{:S(2)}) collective-permute-start(bf16[2,2,3,128,128]{4,3,2,1,0:T(8,128)(2,1)S(1)} %collective-permute-done.8.refs_4_), channel_id=1, source_target_pairs={{0,12},{1,13},{2,14},{3,15},{4,8},{5,9},{6,10},{7,11},{8,4},{9,5},... | collective-permute-start | bytes 1179656 | tf_op jit(solution)/shard_map/weights_x_1/ppermute | solution.py:33
  41.4 24.2 %collective-permute-start.10 = (bf16[2,2,3,128,128]{4,3,2,1,0:T(8,128)(2,1)S(1)}, bf16[2,2,3,128,128]{4,3,2,1,0:T(8,128)(2,1)S(1)}, u32[]{:S(2)}, u32[]{:S(2)}) collective-permute-start(bf16[2,2,3,128,128]{4,3,2,1,0:T(8,128)(2,1)S(1)} %collective-permute-done.8.refs_4_), channel_id=1, source_target_pairs={{0,8},{1,9},{2,10},{3,11},{4,12},{5,13},{6,14},{7,15},{8,0},{9,1},... | collective-permute-start | bytes 1179656 | tf_op jit(solution)/shard_map/weights_x_1/ppermute | solution.py:33
  41.7 23.9 %collective-permute-start.9 = (bf16[2,2,3,128,128]{4,3,2,1,0:T(8,128)(2,1)S(1)}, bf16[2,2,3,128,128]{4,3,2,1,0:T(8,128)(2,1)S(1)}, u32[]{:S(2)}, u32[]{:S(2)}) collective-permute-start(bf16[2,2,3,128,128]{4,3,2,1,0:T(8,128)(2,1)S(1)} %collective-permute-done.8.refs_4_), channel_id=1, source_target_pairs={{0,4},{1,5},{2,6},{3,7},{4,0},{5,1},{6,2},{7,3},{8,12},{9,13},{10,... | collective-permute-start | bytes 1179656 | tf_op jit(solution)/shard_map/weights_x_1/ppermute | solution.py:33
  67.5 2.6 %collective-permute-start.12 = (bf16[256,1536]{1,0:T(8,128)(2,1)S(1)}, bf16[256,1536]{1,0:T(8,128)(2,1)S(1)}, u32[]{:S(2)}, u32[]{:S(2)}) collective-permute-start(bf16[256,1536]{1,0:T(8,128)(2,1)S(1)} %get-tuple-element.47), channel_id=1, source_target_pairs={{0,1},{1,0},{2,3},{3,2},{4,5},{5,4},{6,7},{7,6},{8,9},{9,8},{10,11... | collective-permute-start | bytes 2359304 | tf_op jit(solution)/shard_map/ppermute | solution.py:33
  70.4 6.2 %collective-permute-start.13 = (bf16[64,1536]{1,0:T(8,128)(2,1)S(1)}, bf16[64,1536]{1,0:T(8,128)(2,1)S(1)}, u32[]{:S(2)}, u32[]{:S(2)}) collective-permute-start(bf16[64,1536]{1,0:T(8,128)(2,1)S(1)} %get-tuple-element.71), channel_id=1, source_target_pairs={{0,2},{1,3},{2,0},{3,1},{4,6},{5,7},{6,4},{7,5},{8,10},{9,11},{10,... | collective-permute-start | bytes 589832 | tf_op jit(solution)/shard_map/ppermute | solution.py:33
  70.5 6.7 %collective-permute-start.15 = (bf16[64,1536]{1,0:T(8,128)(2,1)S(1)}, bf16[64,1536]{1,0:T(8,128)(2,1)S(1)}, u32[]{:S(2)}, u32[]{:S(2)}) collective-permute-start(bf16[64,1536]{1,0:T(8,128)(2,1)S(1)} %get-tuple-element.72), channel_id=1, source_target_pairs={{0,18},{1,19},{2,16},{3,17},{4,22},{5,23},{6,20},{7,21},{8,26},{9,... | collective-permute-start | bytes 589832 | tf_op jit(solution)/shard_map/ppermute | solution.py:33
  71.4 8.9 %collective-permute-start.14 = (bf16[64,1536]{1,0:T(8,128)(2,1)S(1)}, bf16[64,1536]{1,0:T(8,128)(2,1)S(1)}, u32[]{:S(2)}, u32[]{:S(2)}) collective-permute-start(bf16[64,1536]{1,0:T(8,128)(2,1)S(1)} %get-tuple-element.73), channel_id=1, source_target_pairs={{0,16},{1,17},{2,18},{3,19},{4,20},{5,21},{6,22},{7,23},{8,24},{9,... | collective-permute-start | bytes 589832 | tf_op jit(solution)/shard_map/ppermute | solution.py:33
  80.6 7.4 %collective-permute-start.18 = (bf16[64,1536]{1,0:T(8,128)(2,1)S(1)}, bf16[64,1536]{1,0:T(8,128)(2,1)S(1)}, u32[]{:S(2)}, u32[]{:S(2)}) collective-permute-start(bf16[64,1536]{1,0:T(8,128)(2,1)S(1)} %pad_maximum_fusion.2), channel_id=1, source_target_pairs={{0,18},{1,19},{2,16},{3,17},{4,22},{5,23},{6,20},{7,21},{8,26},{9,... | collective-permute-start | bytes 589832 | tf_op jit(solution)/shard_map/ppermute | solution.py:33
  82.3 6.5 %collective-permute-start.17 = (bf16[64,1536]{1,0:T(8,128)(2,1)S(1)}, bf16[64,1536]{1,0:T(8,128)(2,1)S(1)}, u32[]{:S(2)}, u32[]{:S(2)}) collective-permute-start(bf16[64,1536]{1,0:T(8,128)(2,1)S(1)} %pad_maximum_fusion.2), channel_id=1, source_target_pairs={{0,16},{1,17},{2,18},{3,19},{4,20},{5,21},{6,22},{7,23},{8,24},{9,... | collective-permute-start | bytes 589832 | tf_op jit(solution)/shard_map/ppermute | solution.py:33
  85.3 6.9 %collective-permute-start.16 = (bf16[64,1536]{1,0:T(8,128)(2,1)S(1)}, bf16[64,1536]{1,0:T(8,128)(2,1)S(1)}, u32[]{:S(2)}, u32[]{:S(2)}) collective-permute-start(bf16[64,1536]{1,0:T(8,128)(2,1)S(1)} %pad_maximum_fusion.2), channel_id=1, source_target_pairs={{0,2},{1,3},{2,0},{3,1},{4,6},{5,7},{6,4},{7,5},{8,10},{9,11},{10,... | collective-permute-start | bytes 589832 | tf_op jit(solution)/shard_map/ppermute | solution.py:33
  92.2 4.5 %collective-permute-start.19 = (bf16[256,1536]{1,0:T(8,128)(2,1)S(1)}, bf16[256,1536]{1,0:T(8,128)(2,1)S(1)}, u32[]{:S(2)}, u32[]{:S(2)}) collective-permute-start(bf16[256,1536]{1,0:T(8,128)(2,1)S(1)} %pad_maximum_fusion.da), channel_id=1, source_target_pairs={{0,1},{1,0},{2,3},{3,2},{4,5},{5,4},{6,7},{7,6},{8,9},{9,8},{10,11... | collective-permute-start | bytes 2359304 | tf_op jit(solution)/shard_map/ppermute | solution.py:33
  98.0 10.4 %collective-permute-start.23 = (bf16[2,2,3,128,128]{4,3,2,1,0:T(8,128)(2,1)S(1)}, bf16[2,2,3,128,128]{4,3,2,1,0:T(8,128)(2,1)S(1)}, u32[]{:S(2)}, u32[]{:S(2)}) collective-permute-start(bf16[2,2,3,128,128]{4,3,2,1,0:T(8,128)(2,1)S(1)} %get-tuple-element.53), channel_id=1, source_target_pairs={{0,4},{1,5},{2,6},{3,7},{4,0},{5,1},{6,2},{7,3},{8,12},{9,13},{10,... | collective-permute-start | bytes 1179656 | tf_op jit(solution)/shard_map/grads_x_1/ppermute | solution.py:33
  98.1 18.0 %collective-permute-start.24 = (bf16[2,2,3,128,128]{4,3,2,1,0:T(8,128)(2,1)S(1)}, bf16[2,2,3,128,128]{4,3,2,1,0:T(8,128)(2,1)S(1)}, u32[]{:S(2)}, u32[]{:S(2)}) collective-permute-start(bf16[2,2,3,128,128]{4,3,2,1,0:T(8,128)(2,1)S(1)} %get-tuple-element.54), channel_id=1, source_target_pairs={{0,12},{1,13},{2,14},{3,15},{4,8},{5,9},{6,10},{7,11},{8,4},{9,5},... | collective-permute-start | bytes 1179656 | tf_op jit(solution)/shard_map/grads_x_1/ppermute | solution.py:33
  100.5 19.5 %collective-permute-start.25 = (bf16[2,2,3,128,128]{4,3,2,1,0:T(8,128)(2,1)S(1)}, bf16[2,2,3,128,128]{4,3,2,1,0:T(8,128)(2,1)S(1)}, u32[]{:S(2)}, u32[]{:S(2)}) collective-permute-start(bf16[2,2,3,128,128]{4,3,2,1,0:T(8,128)(2,1)S(1)} %get-tuple-element.55), channel_id=1, source_target_pairs={{0,8},{1,9},{2,10},{3,11},{4,12},{5,13},{6,14},{7,15},{8,0},{9,1},... | collective-permute-start | bytes 1179656 | tf_op jit(solution)/shard_map/grads_x_1/ppermute | solution.py:33
  103.4 32.7 %collective-permute-start.27 = (bf16[2,256,1024]{2,1,0:T(8,128)(2,1)S(1)}, bf16[2,256,1024]{2,1,0:T(8,128)(2,1)S(1)}, u32[]{:S(2)}, u32[]{:S(2)}) collective-permute-start(bf16[2,256,1024]{2,1,0:T(8,128)(2,1)S(1)} %get-tuple-element.58), channel_id=1, source_target_pairs={{0,16},{1,17},{2,18},{3,19},{4,20},{5,21},{6,22},{7,23},{8,24},{9,... | collective-permute-start | bytes 3145736 | tf_op jit(solution)/shard_map/output_swap/ppermute | solution.py:33
  106.5 18.8 %collective-permute-start.20 = (bf16[2,2,3,128,128]{4,3,2,1,0:T(8,128)(2,1)S(1)}, bf16[2,2,3,128,128]{4,3,2,1,0:T(8,128)(2,1)S(1)}, u32[]{:S(2)}, u32[]{:S(2)}) collective-permute-start(bf16[2,2,3,128,128]{4,3,2,1,0:T(8,128)(2,1)S(1)} %get-tuple-element.49), channel_id=1, source_target_pairs={{0,4},{1,5},{2,6},{3,7},{4,0},{5,1},{6,2},{7,3},{8,12},{9,13},{10,... | collective-permute-start | bytes 1179656 | tf_op jit(solution)/shard_map/grads_x_0/ppermute | solution.py:33
  108.4 20.3 %collective-permute-start.21 = (bf16[2,2,3,128,128]{4,3,2,1,0:T(8,128)(2,1)S(1)}, bf16[2,2,3,128,128]{4,3,2,1,0:T(8,128)(2,1)S(1)}, u32[]{:S(2)}, u32[]{:S(2)}) collective-permute-start(bf16[2,2,3,128,128]{4,3,2,1,0:T(8,128)(2,1)S(1)} %get-tuple-element.50), channel_id=1, source_target_pairs={{0,12},{1,13},{2,14},{3,15},{4,8},{5,9},{6,10},{7,11},{8,4},{9,5},... | collective-permute-start | bytes 1179656 | tf_op jit(solution)/shard_map/grads_x_0/ppermute | solution.py:33
  116.1 19.7 %collective-permute-start.22 = (bf16[2,2,3,128,128]{4,3,2,1,0:T(8,128)(2,1)S(1)}, bf16[2,2,3,128,128]{4,3,2,1,0:T(8,128)(2,1)S(1)}, u32[]{:S(2)}, u32[]{:S(2)}) collective-permute-start(bf16[2,2,3,128,128]{4,3,2,1,0:T(8,128)(2,1)S(1)} %get-tuple-element.51), channel_id=1, source_target_pairs={{0,8},{1,9},{2,10},{3,11},{4,12},{5,13},{6,14},{7,15},{8,0},{9,1},... | collective-permute-start | bytes 1179656 | tf_op jit(solution)/shard_map/grads_x_0/ppermute | solution.py:33
  120.2 15.6 %collective-permute-start.26 = (bf16[2,2,3,128,128]{4,3,2,1,0:T(8,128)(2,1)S(1)}, bf16[2,2,3,128,128]{4,3,2,1,0:T(8,128)(2,1)S(1)}, u32[]{:S(2)}, u32[]{:S(2)}) collective-permute-start(bf16[2,2,3,128,128]{4,3,2,1,0:T(8,128)(2,1)S(1)} %add_convert_fusion.1), channel_id=1, source_target_pairs={{0,32},{1,33},{2,34},{3,35},{4,36},{5,37},{6,38},{7,39},{8,40},{9,... | collective-permute-start | bytes 1179656 | tf_op jit(solution)/shard_map/grads_plane/ppermute | solution.py:33
  136.1 15.2 %collective-permute-start.31 = (bf16[3,128,128]{2,1,0:T(8,128)(2,1)S(1)}, bf16[3,128,128]{2,1,0:T(8,128)(2,1)S(1)}, u32[]{:S(2)}, u32[]{:S(2)}) collective-permute-start(bf16[3,128,128]{2,1,0:T(8,128)(2,1)S(1)} %get-tuple-element.74), channel_id=1, source_target_pairs={{192,0},{128,1},{64,2},{0,3},{196,4},{132,5},{68,6},{4,7},{200,8},... | collective-permute-start | bytes 294920 | tf_op jit(solution)/shard_map/grads_turn/ppermute | solution.py:37
  137.6 14.8 %collective-permute-start.30 = (bf16[3,128,128]{2,1,0:T(8,128)(2,1)S(1)}, bf16[3,128,128]{2,1,0:T(8,128)(2,1)S(1)}, u32[]{:S(2)}, u32[]{:S(2)}) collective-permute-start(bf16[3,128,128]{2,1,0:T(8,128)(2,1)S(1)} %get-tuple-element.75), channel_id=1, source_target_pairs={{128,0},{192,1},{0,2},{64,3},{132,4},{196,5},{4,6},{68,7},{136,8},... | collective-permute-start | bytes 294920 | tf_op jit(solution)/shard_map/grads_turn/ppermute | solution.py:37
  143.1 11.4 %collective-permute-start.29 = (bf16[3,128,128]{2,1,0:T(8,128)(2,1)S(1)}, bf16[3,128,128]{2,1,0:T(8,128)(2,1)S(1)}, u32[]{:S(2)}, u32[]{:S(2)}) collective-permute-start(bf16[3,128,128]{2,1,0:T(8,128)(2,1)S(1)} %get-tuple-element.76), channel_id=1, source_target_pairs={{64,0},{0,1},{192,2},{128,3},{68,4},{4,5},{196,6},{132,7},{72,8},{... | collective-permute-start | bytes 294920 | tf_op jit(solution)/shard_map/grads_turn/ppermute | solution.py:37
  143.1 12.4 %collective-permute-start.28 = (bf16[3,128,128]{2,1,0:T(8,128)(2,1)S(1)}, bf16[3,128,128]{2,1,0:T(8,128)(2,1)S(1)}, u32[]{:S(2)}, u32[]{:S(2)}) collective-permute-start(bf16[3,128,128]{2,1,0:T(8,128)(2,1)S(1)} %get-tuple-element.77), channel_id=1, source_target_pairs={{0,0},{64,1},{128,2},{192,3},{4,4},{68,5},{132,6},{196,7},{8,8},{7... | collective-permute-start | bytes 294920 | tf_op jit(solution)/shard_map/grads_turn/ppermute | solution.py:37

commit v9 on v8

--- a/solution.py
+++ b/solution.py
@@ -139,8 +139,8 @@
 
 
 def forward_body(tok, cot, *refs):
-    columns, (gu, dn, keep, away) = refs[:8], refs[8:]
-    tb = keep.shape[0]
+    columns, (gu, dn, away) = refs[:8], refs[8:]
+    tb = away.shape[0]
     fb = columns[0].shape[-1]
     for f in range(2):
         for j in range(NX):
@@ -155,6 +155,10 @@
     wide = gu.shape[1]
     away[:, :wide] = nn(tok[tb:, :], gu[...]).astype(BF)
     away[:, wide:] = nt(cot[tb:, :], dn[...]).astype(BF)
+
+
+def keep_body(tok, cot, gu, dn, keep):
+    tb, wide = keep.shape[0], gu.shape[1]
     keep[:, :wide] = nn(tok[:tb, :], gu[...])
     keep[:, wide:] = nt(cot[:tb, :], dn[...])
 
@@ -221,12 +225,13 @@
 
     product = 2 * 2 * tb * wide * hid
     with jax.named_scope("forward"):
-        gu, dn, keep, away = call(
+        gu, dn, away = call(
             forward_body,
-            [((wide, 2 * hid), BF), ((hid, wide), BF), ((tb, 3 * hid), F32), ((tb, 3 * hid), BF)],
+            [((wide, 2 * hid), BF), ((hid, wide), BF), ((tb, 3 * hid), BF)],
             [tok, cot, *near, *far],
-            3 * product,
+            3 * product // 2,
         )
+        (keep,) = call(keep_body, [((tb, 3 * hid), F32)], [tok, cot, gu, dn], 3 * product // 2)
     part = keep + send(away, swap_core).astype(F32)
     pre = part[:sub]
     for k in range(1, 4):

time: 159 us -> 165 us (1.038); the launches traced: 156 us -> 165 us
  waiting for transfers between devices: 80.1 us -> 93.8 us
  starting transfers between devices: 61.2 us -> 55.9 us
    ppermute x4, waiting for transfers between devices: 4.19 us -> 14.7 us  [send_back(): return lax.ppermute(value, AXES, [(b, a) for a, b in pairs_of(move)])]
    ppermute x4, starting transfers between devices: 12.8 us -> 6.95 us  [send_back(): return lax.ppermute(value, AXES, [(b, a) for a, b in pairs_of(move)])]
    ppermute x28, waiting for transfers between devices: 75.9 us -> 79.1 us  [send(): return lax.ppermute(value, AXES, pairs_of(move))]
    pallas_call x7 -> x8, Pallas kernels: 9.89 us -> 10.1 us  [call(): pl.pallas_call(body, out_shape=[jax.ShapeDtypeStruct(s, d) for s, d in sh...]
  transfers between devices with their start and end apart: 32 -> 32, of which waited for: 22 -> 20; matrix products, arithmetic and copies ran while one was open for 1% -> 1% of each run, Pallas kernels for 4% -> 5%
where the time goes in v9:
time: 165 us
  waiting for transfers between devices  93.8 us (57%)
  starting transfers between devices  55.9 us (34%)
  Pallas kernels  10.1 us (6%)
  local copies, waits for them, and re-layouts  2.08 us (1%)
  other arithmetic  2.01 us (1%)
    ppermute x28, waiting for transfers between devices, send(): return lax.ppermute(value, AXES, pairs_of(move))  79.1 us
    ppermute x28, starting transfers between devices, send(): return lax.ppermute(value, AXES, pairs_of(move))  48.9 us
    ppermute x4, waiting for transfers between devices, send_back(): return lax.ppermute(value, AXES, [(b, a) for a, b in pairs_of(move)])  14.7 us
    pallas_call x8, Pallas kernels, call(): pl.pallas_call(body, out_shape=[jax.ShapeDtypeStruct(s, d) for s, d in sh...  10.1 us
    ppermute x4, starting transfers between devices, send_back(): return lax.ppermute(value, AXES, [(b, a) for a, b in pairs_of(move)])  6.95 us
  transfers between devices with their start and end apart: 32, of which 20 were waited for; matrix products, arithmetic and copies ran while one was open for 1% of the time, Pallas kernels for 5%

profile of v9, /device:TPU:9, one launch (start us, length us, event | category | flops | bytes accessed | tf_op | source)
XLA Modules:
  0.0 164.8 jit_solution(6622253415306957599)
XLA Ops:
  0.6 0.9 pad_maximum_fusion.3
  1.5 2.6 %collective-permute-start.3 = (bf16[3,128,128]{2,1,0:T(8,128)(2,1)S(1)}, bf16[3,128,128]{2,1,0:T(8,128)(2,1)S(1)}, u32[]{:S(2)}, u32[]{:S(2)}) collective-permute-start(bf16[3,128,128]{2,1,0:T(8,128)(2,1)S(1)} %pad_maximum_fusion.3), channel_id=1, source_target_pairs={{0,192},{1,128},{2,64},{3,0},{4,196},{5,132},{6,68},{7,4},{8,200},... | collective-permute-start | bytes 294920 | tf_op jit(solution)/shard_map/weights_turn/ppermute | solution.py:33
  4.1 5.8 %collective-permute-start.2 = (bf16[3,128,128]{2,1,0:T(8,128)(2,1)S(1)}, bf16[3,128,128]{2,1,0:T(8,128)(2,1)S(1)}, u32[]{:S(2)}, u32[]{:S(2)}) collective-permute-start(bf16[3,128,128]{2,1,0:T(8,128)(2,1)S(1)} %pad_maximum_fusion.3), channel_id=1, source_target_pairs={{0,128},{1,192},{2,0},{3,64},{4,132},{5,196},{6,4},{7,68},{8,136},... | collective-permute-start | bytes 294920 | tf_op jit(solution)/shard_map/weights_turn/ppermute | solution.py:33
  9.9 1.6 collective-permute-start.1
  11.5 3.9 %collective-permute-start = (bf16[3,128,128]{2,1,0:T(8,128)(2,1)S(1)}, bf16[3,128,128]{2,1,0:T(8,128)(2,1)S(1)}, u32[]{:S(2)}, u32[]{:S(2)}) collective-permute-start(bf16[3,128,128]{2,1,0:T(8,128)(2,1)S(1)} %pad_maximum_fusion.3), channel_id=1, source_target_pairs={{0,0},{1,64},{2,128},{3,192},{4,4},{5,68},{6,132},{7,196},{8,8},{9... | collective-permute-start | bytes 294920 | tf_op jit(solution)/shard_map/weights_turn/ppermute | solution.py:33
  15.4 0.1 pad_add_fusion.where
  15.5 1.3 constant_dynamic-slice_fusion.tok
  16.8 1.1 pick.1
  18.0 4.5 %collective-permute-done = bf16[3,128,128]{2,1,0:T(8,128)(2,1)S(1)} collective-permute-done((bf16[3,128,128]{2,1,0:T(8,128)(2,1)S(1)}, bf16[3,128,128]{2,1,0:T(8,128)(2,1)S(1)}, u32[]{:S(2)}, u32[]{:S(2)}) %collective-permute-start) | collective-permute-done | bytes 98336 | tf_op jit(solution)/shard_map/weights_turn/ppermute | solution.py:33
  22.6 2.2 %collective-permute-start.4 = (bf16[2,256,1024]{2,1,0:T(8,128)(2,1)S(1)}, bf16[2,256,1024]{2,1,0:T(8,128)(2,1)S(1)}, u32[]{:S(2)}, u32[]{:S(2)}) collective-permute-start(bf16[2,256,1024]{2,1,0:T(8,128)(2,1)S(1)} %get-tuple-element.41), channel_id=1, source_target_pairs={{0,16},{1,17},{2,18},{3,19},{4,20},{5,21},{6,22},{7,23},{8,24},{9,... | collective-permute-start | bytes 3145736 | tf_op jit(solution)/shard_map/input_swap/ppermute | solution.py:33
  24.7 1.2 collective-permute-start.5
  25.9 1.8 %collective-permute-start.7 = (bf16[2,2,3,128,128]{4,3,2,1,0:T(8,128)(2,1)S(1)}, bf16[2,2,3,128,128]{4,3,2,1,0:T(8,128)(2,1)S(1)}, u32[]{:S(2)}, u32[]{:S(2)}) collective-permute-start(bf16[2,2,3,128,128]{4,3,2,1,0:T(8,128)(2,1)S(1)} %bitcast.27), channel_id=1, source_target_pairs={{0,12},{1,13},{2,14},{3,15},{4,8},{5,9},{6,10},{7,11},{8,4},{9,5},... | collective-permute-start | bytes 1179656 | tf_op jit(solution)/shard_map/weights_x_0/ppermute | solution.py:33
  27.8 2.1 %collective-permute-start.8 = (bf16[2,2,3,128,128]{4,3,2,1,0:T(8,128)(2,1)S(1)}, bf16[2,2,3,128,128]{4,3,2,1,0:T(8,128)(2,1)S(1)}, u32[]{:S(2)}, u32[]{:S(2)}) collective-permute-start(bf16[2,2,3,128,128]{4,3,2,1,0:T(8,128)(2,1)S(1)} %bitcast.28), channel_id=1, source_target_pairs={{0,32},{1,33},{2,34},{3,35},{4,36},{5,37},{6,38},{7,39},{8,40},{9,... | collective-permute-start | bytes 1179656 | tf_op jit(solution)/shard_map/weights_plane/ppermute | solution.py:33
  29.8 0.6 collective-permute-start.6
  30.4 4.6 %collective-permute-done.5.refs_1_ = bf16[2,2,3,128,128]{4,3,2,1,0:T(8,128)(2,1)S(1)} collective-permute-done((bf16[2,2,3,128,128]{4,3,2,1,0:T(8,128)(2,1)S(1)}, bf16[2,2,3,128,128]{4,3,2,1,0:T(8,128)(2,1)S(1)}, u32[]{:S(2)}, u32[]{:S(2)}) %collective-permute-start.5) | collective-permute-done | bytes 393248 | tf_op jit(solution)/shard_map/weights_x_0/ppermute | solution.py:33
  35.1 8.8 %collective-permute-done.7.refs_3_ = bf16[2,2,3,128,128]{4,3,2,1,0:T(8,128)(2,1)S(1)} collective-permute-done((bf16[2,2,3,128,128]{4,3,2,1,0:T(8,128)(2,1)S(1)}, bf16[2,2,3,128,128]{4,3,2,1,0:T(8,128)(2,1)S(1)}, u32[]{:S(2)}, u32[]{:S(2)}) %collective-permute-start.7) | collective-permute-done | bytes 393248 | tf_op jit(solution)/shard_map/weights_x_0/ppermute | solution.py:33
  43.9 4.7 %collective-permute-start.10 = (bf16[2,2,3,128,128]{4,3,2,1,0:T(8,128)(2,1)S(1)}, bf16[2,2,3,128,128]{4,3,2,1,0:T(8,128)(2,1)S(1)}, u32[]{:S(2)}, u32[]{:S(2)}) collective-permute-start(bf16[2,2,3,128,128]{4,3,2,1,0:T(8,128)(2,1)S(1)} %collective-permute-done.8.refs_4_), channel_id=1, source_target_pairs={{0,8},{1,9},{2,10},{3,11},{4,12},{5,13},{6,14},{7,15},{8,0},{9,1},... | collective-permute-start | bytes 1179656 | tf_op jit(solution)/shard_map/weights_x_1/ppermute | solution.py:33
  48.6 0.3 collective-permute-done.4.far
  48.9 0.1 join.1
  49.0 2.2 %collective-permute-done.9.refs_5_ = bf16[2,2,3,128,128]{4,3,2,1,0:T(8,128)(2,1)S(1)} collective-permute-done((bf16[2,2,3,128,128]{4,3,2,1,0:T(8,128)(2,1)S(1)}, bf16[2,2,3,128,128]{4,3,2,1,0:T(8,128)(2,1)S(1)}, u32[]{:S(2)}, u32[]{:S(2)}) %collective-permute-start.9) | collective-permute-done | bytes 393248 | tf_op jit(solution)/shard_map/weights_x_1/ppermute | solution.py:33
  51.2 13.5 %collective-permute-done.10.refs_6_ = bf16[2,2,3,128,128]{4,3,2,1,0:T(8,128)(2,1)S(1)} collective-permute-done((bf16[2,2,3,128,128]{4,3,2,1,0:T(8,128)(2,1)S(1)}, bf16[2,2,3,128,128]{4,3,2,1,0:T(8,128)(2,1)S(1)}, u32[]{:S(2)}, u32[]{:S(2)}) %collective-permute-start.10) | collective-permute-done | bytes 393248 | tf_op jit(solution)/shard_map/weights_x_1/ppermute | solution.py:33
  64.7 1.1 forward.2
  65.8 5.1 %collective-permute-start.12 = (bf16[256,1536]{1,0:T(8,128)(2,1)S(1)}, bf16[256,1536]{1,0:T(8,128)(2,1)S(1)}, u32[]{:S(2)}, u32[]{:S(2)}) collective-permute-start(bf16[256,1536]{1,0:T(8,128)(2,1)S(1)} %get-tuple-element.47), channel_id=1, source_target_pairs={{0,1},{1,0},{2,3},{3,2},{4,5},{5,4},{6,7},{7,6},{8,9},{9,8},{10,11... | collective-permute-start | bytes 2359304 | tf_op jit(solution)/shard_map/ppermute | solution.py:33
  70.9 1.0 forward.3
  71.9 0.9 collective-permute-done.12
  72.9 0.3 fusion.3
  73.2 0.1 collective-permute-start.15
  73.3 1.0 collective-permute-start.14
  74.3 2.3 %collective-permute-start.13 = (bf16[64,1536]{1,0:T(8,128)(2,1)S(1)}, bf16[64,1536]{1,0:T(8,128)(2,1)S(1)}, u32[]{:S(2)}, u32[]{:S(2)}) collective-permute-start(bf16[64,1536]{1,0:T(8,128)(2,1)S(1)} %get-tuple-element.69), channel_id=1, source_target_pairs={{0,2},{1,3},{2,0},{3,1},{4,6},{5,7},{6,4},{7,5},{8,10},{9,11},{10,... | collective-permute-start | bytes 589832 | tf_op jit(solution)/shard_map/ppermute | solution.py:33
  76.5 7.1 %collective-permute-done.15 = bf16[64,1536]{1,0:T(8,128)(2,1)S(1)} collective-permute-done((bf16[64,1536]{1,0:T(8,128)(2,1)S(1)}, bf16[64,1536]{1,0:T(8,128)(2,1)S(1)}, u32[]{:S(2)}, u32[]{:S(2)}) %collective-permute-start.15) | collective-permute-done | bytes 196640 | tf_op jit(solution)/shard_map/ppermute | solution.py:33
  83.6 1.6 collective-permute-done.13
  85.2 0.1 fusion.1
  85.3 0.5 collective-permute-start.18
  85.8 0.9 collective-permute-start.17
  86.7 2.0 %collective-permute-start.16 = (bf16[64,1536]{1,0:T(8,128)(2,1)S(1)}, bf16[64,1536]{1,0:T(8,128)(2,1)S(1)}, u32[]{:S(2)}, u32[]{:S(2)}) collective-permute-start(bf16[64,1536]{1,0:T(8,128)(2,1)S(1)} %pad_maximum_fusion.2), channel_id=1, source_target_pairs={{0,2},{1,3},{2,0},{3,1},{4,6},{5,7},{6,4},{7,5},{8,10},{9,11},{10,... | collective-permute-start | bytes 589832 | tf_op jit(solution)/shard_map/ppermute | solution.py:33
  88.7 4.2 %collective-permute-done.18 = bf16[64,1536]{1,0:T(8,128)(2,1)S(1)} collective-permute-done((bf16[64,1536]{1,0:T(8,128)(2,1)S(1)}, bf16[64,1536]{1,0:T(8,128)(2,1)S(1)}, u32[]{:S(2)}, u32[]{:S(2)}) %collective-permute-start.18) | collective-permute-done | bytes 196640 | tf_op jit(solution)/shard_map/ppermute | solution.py:33
  92.9 3.3 %collective-permute-done.16 = bf16[64,1536]{1,0:T(8,128)(2,1)S(1)} collective-permute-done((bf16[64,1536]{1,0:T(8,128)(2,1)S(1)}, bf16[64,1536]{1,0:T(8,128)(2,1)S(1)}, u32[]{:S(2)}, u32[]{:S(2)}) %collective-permute-start.16) | collective-permute-done | bytes 196640 | tf_op jit(solution)/shard_map/ppermute | solution.py:33
  96.2 2.7 %collective-permute-start.19 = (bf16[256,1536]{1,0:T(8,128)(2,1)S(1)}, bf16[256,1536]{1,0:T(8,128)(2,1)S(1)}, u32[]{:S(2)}, u32[]{:S(2)}) collective-permute-start(bf16[256,1536]{1,0:T(8,128)(2,1)S(1)} %pad_maximum_fusion.da), channel_id=1, source_target_pairs={{0,1},{1,0},{2,3},{3,2},{4,5},{5,4},{6,7},{7,6},{8,9},{9,8},{10,11... | collective-permute-start | bytes 2359304 | tf_op jit(solution)/shard_map/ppermute | solution.py:33
  98.9 1.9 %collective-permute-done.19.dc = bf16[256,1536]{1,0:T(8,128)(2,1)S(1)} collective-permute-done((bf16[256,1536]{1,0:T(8,128)(2,1)S(1)}, bf16[256,1536]{1,0:T(8,128)(2,1)S(1)}, u32[]{:S(2)}, u32[]{:S(2)}) %collective-permute-start.19) | collective-permute-done | bytes 786464 | tf_op jit(solution)/shard_map/ppermute | solution.py:33
  100.9 1.3 grads.3
  102.2 0.1 collective-permute-start.25
  102.3 0.6 collective-permute-start.24
  102.8 2.1 %collective-permute-start.23 = (bf16[2,2,3,128,128]{4,3,2,1,0:T(8,128)(2,1)S(1)}, bf16[2,2,3,128,128]{4,3,2,1,0:T(8,128)(2,1)S(1)}, u32[]{:S(2)}, u32[]{:S(2)}) collective-permute-start(bf16[2,2,3,128,128]{4,3,2,1,0:T(8,128)(2,1)S(1)} %get-tuple-element.53), channel_id=1, source_target_pairs={{0,4},{1,5},{2,6},{3,7},{4,0},{5,1},{6,2},{7,3},{8,12},{9,13},{10,... | collective-permute-start | bytes 1179656 | tf_op jit(solution)/shard_map/grads_x_1/ppermute | solution.py:33
  104.9 1.8 %outputs.1 = (bf16[2,256,1024]{2,1,0:T(8,128)(2,1)S(1)}, bf16[2,256,1024]{2,1,0:T(8,128)(2,1)S(1)}) custom-call(bf16[256,1536]{1,0:T(8,128)(2,1)S(1)} %pad_maximum_fusion.da, bf16[256,1536]{1,0:T(8,128)(2,1)S(1)} %collective-permute-done.19.dc, bf16[1024,1024]{1,0:T(8,128)(2,1)S(1)} %get-tuple-element.45.gu, bf16[512,1024]{1,0:T(8,128)(2,1)S(1)} %get-tuple-element.46.dn), custom_call_target="tpu_custom_call" | custom-call | flops 1610612736 | bytes 6815744 | tf_op jit(solution)/shard_map/outputs/pallas_call | solution.py:87
  106.7 1.0 collective-permute-start.27
  107.7 1.3 grads.2
  109.0 1.4 collective-permute-start.22
  110.4 3.8 %collective-permute-done.25 = bf16[2,2,3,128,128]{4,3,2,1,0:T(8,128)(2,1)S(1)} collective-permute-done((bf16[2,2,3,128,128]{4,3,2,1,0:T(8,128)(2,1)S(1)}, bf16[2,2,3,128,128]{4,3,2,1,0:T(8,128)(2,1)S(1)}, u32[]{:S(2)}, u32[]{:S(2)}) %collective-permute-start.25) | collective-permute-done | bytes 393248 | tf_op jit(solution)/shard_map/grads_x_1/ppermute | solution.py:33
  114.1 9.0 %collective-permute-done.24 = bf16[2,2,3,128,128]{4,3,2,1,0:T(8,128)(2,1)S(1)} collective-permute-done((bf16[2,2,3,128,128]{4,3,2,1,0:T(8,128)(2,1)S(1)}, bf16[2,2,3,128,128]{4,3,2,1,0:T(8,128)(2,1)S(1)}, u32[]{:S(2)}, u32[]{:S(2)}) %collective-permute-start.24) | collective-permute-done | bytes 393248 | tf_op jit(solution)/shard_map/grads_x_1/ppermute | solution.py:33
  123.1 0.2 add_convert_fusion.1
  123.3 2.8 %collective-permute-start.26 = (bf16[2,2,3,128,128]{4,3,2,1,0:T(8,128)(2,1)S(1)}, bf16[2,2,3,128,128]{4,3,2,1,0:T(8,128)(2,1)S(1)}, u32[]{:S(2)}, u32[]{:S(2)}) collective-permute-start(bf16[2,2,3,128,128]{4,3,2,1,0:T(8,128)(2,1)S(1)} %add_convert_fusion.1), channel_id=1, source_target_pairs={{0,32},{1,33},{2,34},{3,35},{4,36},{5,37},{6,38},{7,39},{8,40},{9,... | collective-permute-start | bytes 1179656 | tf_op jit(solution)/shard_map/grads_plane/ppermute | solution.py:33
  126.1 4.9 %collective-permute-done.22 = bf16[2,2,3,128,128]{4,3,2,1,0:T(8,128)(2,1)S(1)} collective-permute-done((bf16[2,2,3,128,128]{4,3,2,1,0:T(8,128)(2,1)S(1)}, bf16[2,2,3,128,128]{4,3,2,1,0:T(8,128)(2,1)S(1)}, u32[]{:S(2)}, u32[]{:S(2)}) %collective-permute-start.22) | collective-permute-done | bytes 393248 | tf_op jit(solution)/shard_map/grads_x_0/ppermute | solution.py:33
  131.0 8.7 %collective-permute-done.21 = bf16[2,2,3,128,128]{4,3,2,1,0:T(8,128)(2,1)S(1)} collective-permute-done((bf16[2,2,3,128,128]{4,3,2,1,0:T(8,128)(2,1)S(1)}, bf16[2,2,3,128,128]{4,3,2,1,0:T(8,128)(2,1)S(1)}, u32[]{:S(2)}, u32[]{:S(2)}) %collective-permute-start.21) | collective-permute-done | bytes 393248 | tf_op jit(solution)/shard_map/grads_x_0/ppermute | solution.py:33
  139.7 0.3 add_convert_fusion
  140.0 6.7 %collective-permute-start.28 = (bf16[3,128,128]{2,1,0:T(8,128)(2,1)S(1)}, bf16[3,128,128]{2,1,0:T(8,128)(2,1)S(1)}, u32[]{:S(2)}, u32[]{:S(2)}) collective-permute-start(bf16[3,128,128]{2,1,0:T(8,128)(2,1)S(1)} %get-tuple-element.75), channel_id=1, source_target_pairs={{0,0},{64,1},{128,2},{192,3},{4,4},{68,5},{132,6},{196,7},{8,8},{7... | collective-permute-start | bytes 294920 | tf_op jit(solution)/shard_map/grads_turn/ppermute | solution.py:37
  146.7 0.1 collective-permute-start.29
  146.8 0.1 collective-permute-start.30
  146.9 0.1 collective-permute-start.31
  147.0 2.4 %place.1 = (bf16[256,2048]{1,0:T(8,128)(2,1)}, bf16[256,2048]{1,0:T(8,128)(2,1)}) custom-call(s32[4]{0:T(128)S(1)} %pad_add_fusion.where, bf16[2,256,1024]{2,1,0:T(8,128)(2,1)S(1)} %get-tuple-element.58.own, bf16[2,256,1024]{2,1,0:T(8,128)(2,1)S(1)} %collective-permute-done.27.far), custom_call_target="tpu_custom_call" | custom-call | bytes 4194304 | tf_op jit(solution)/shard_map/place/pallas_call | solution.py:87
  149.3 11.5 %collective-permute-done.28 = bf16[3,128,128]{2,1,0:T(8,128)(2,1)S(1)} collective-permute-done((bf16[3,128,128]{2,1,0:T(8,128)(2,1)S(1)}, bf16[3,128,128]{2,1,0:T(8,128)(2,1)S(1)}, u32[]{:S(2)}, u32[]{:S(2)}) %collective-permute-start.28) | collective-permute-done | bytes 98336 | tf_op jit(solution)/shard_map/grads_turn/ppermute | solution.py:37
  160.9 1.1 collective-permute-done.29
  161.9 1.1 collective-permute-done.30
  163.0 1.1 collective-permute-done.31
  164.1 0.7 slice_bitcast_fusion.4
  (25 shorter events, 0.4 us)
Async XLA Ops:
  0.6 16.2 %copy-start = (bf16[256,2048]{1,0:T(8,128)(2,1)S(1)}, bf16[256,2048]{1,0:T(8,128)(2,1)}, u32[]{:S(2)}) copy-start(bf16[256,2048]{1,0:T(8,128)(2,1)} %cot) | copy-start | bytes 3145732
  1.5 16.5 %collective-permute-start.3 = (bf16[3,128,128]{2,1,0:T(8,128)(2,1)S(1)}, bf16[3,128,128]{2,1,0:T(8,128)(2,1)S(1)}, u32[]{:S(2)}, u32[]{:S(2)}) collective-permute-start(bf16[3,128,128]{2,1,0:T(8,128)(2,1)S(1)} %pad_maximum_fusion.3), channel_id=1, source_target_pairs={{0,192},{1,128},{2,64},{3,0},{4,196},{5,132},{6,68},{7,4},{8,200},... | collective-permute-start | bytes 294920 | tf_op jit(solution)/shard_map/weights_turn/ppermute | solution.py:33
  4.1 13.9 %collective-permute-start.2 = (bf16[3,128,128]{2,1,0:T(8,128)(2,1)S(1)}, bf16[3,128,128]{2,1,0:T(8,128)(2,1)S(1)}, u32[]{:S(2)}, u32[]{:S(2)}) collective-permute-start(bf16[3,128,128]{2,1,0:T(8,128)(2,1)S(1)} %pad_maximum_fusion.3), channel_id=1, source_target_pairs={{0,128},{1,192},{2,0},{3,64},{4,132},{5,196},{6,4},{7,68},{8,136},... | collective-permute-start | bytes 294920 | tf_op jit(solution)/shard_map/weights_turn/ppermute | solution.py:33
  9.9 8.1 %collective-permute-start.1 = (bf16[3,128,128]{2,1,0:T(8,128)(2,1)S(1)}, bf16[3,128,128]{2,1,0:T(8,128)(2,1)S(1)}, u32[]{:S(2)}, u32[]{:S(2)}) collective-permute-start(bf16[3,128,128]{2,1,0:T(8,128)(2,1)S(1)} %pad_maximum_fusion.3), channel_id=1, source_target_pairs={{0,64},{1,0},{2,192},{3,128},{4,68},{5,4},{6,196},{7,132},{8,72},{... | collective-permute-start | bytes 294920 | tf_op jit(solution)/shard_map/weights_turn/ppermute | solution.py:33
  11.5 11.0 %collective-permute-start = (bf16[3,128,128]{2,1,0:T(8,128)(2,1)S(1)}, bf16[3,128,128]{2,1,0:T(8,128)(2,1)S(1)}, u32[]{:S(2)}, u32[]{:S(2)}) collective-permute-start(bf16[3,128,128]{2,1,0:T(8,128)(2,1)S(1)} %pad_maximum_fusion.3), channel_id=1, source_target_pairs={{0,0},{1,64},{2,128},{3,192},{4,4},{5,68},{6,132},{7,196},{8,8},{9... | collective-permute-start | bytes 294920 | tf_op jit(solution)/shard_map/weights_turn/ppermute | solution.py:33
  22.6 26.3 %collective-permute-start.4 = (bf16[2,256,1024]{2,1,0:T(8,128)(2,1)S(1)}, bf16[2,256,1024]{2,1,0:T(8,128)(2,1)S(1)}, u32[]{:S(2)}, u32[]{:S(2)}) collective-permute-start(bf16[2,256,1024]{2,1,0:T(8,128)(2,1)S(1)} %get-tuple-element.41), channel_id=1, source_target_pairs={{0,16},{1,17},{2,18},{3,19},{4,20},{5,21},{6,22},{7,23},{8,24},{9,... | collective-permute-start | bytes 3145736 | tf_op jit(solution)/shard_map/input_swap/ppermute | solution.py:33
  24.7 10.3 %collective-permute-start.5 = (bf16[2,2,3,128,128]{4,3,2,1,0:T(8,128)(2,1)S(1)}, bf16[2,2,3,128,128]{4,3,2,1,0:T(8,128)(2,1)S(1)}, u32[]{:S(2)}, u32[]{:S(2)}) collective-permute-start(bf16[2,2,3,128,128]{4,3,2,1,0:T(8,128)(2,1)S(1)} %bitcast.26), channel_id=1, source_target_pairs={{0,4},{1,5},{2,6},{3,7},{4,0},{5,1},{6,2},{7,3},{8,12},{9,13},{10,... | collective-permute-start | bytes 1179656 | tf_op jit(solution)/shard_map/weights_x_0/ppermute | solution.py:33
  25.9 17.9 %collective-permute-start.7 = (bf16[2,2,3,128,128]{4,3,2,1,0:T(8,128)(2,1)S(1)}, bf16[2,2,3,128,128]{4,3,2,1,0:T(8,128)(2,1)S(1)}, u32[]{:S(2)}, u32[]{:S(2)}) collective-permute-start(bf16[2,2,3,128,128]{4,3,2,1,0:T(8,128)(2,1)S(1)} %bitcast.27), channel_id=1, source_target_pairs={{0,12},{1,13},{2,14},{3,15},{4,8},{5,9},{6,10},{7,11},{8,4},{9,5},... | collective-permute-start | bytes 1179656 | tf_op jit(solution)/shard_map/weights_x_0/ppermute | solution.py:33
  27.8 16.1 %collective-permute-start.8 = (bf16[2,2,3,128,128]{4,3,2,1,0:T(8,128)(2,1)S(1)}, bf16[2,2,3,128,128]{4,3,2,1,0:T(8,128)(2,1)S(1)}, u32[]{:S(2)}, u32[]{:S(2)}) collective-permute-start(bf16[2,2,3,128,128]{4,3,2,1,0:T(8,128)(2,1)S(1)} %bitcast.28), channel_id=1, source_target_pairs={{0,32},{1,33},{2,34},{3,35},{4,36},{5,37},{6,38},{7,39},{8,40},{9,... | collective-permute-start | bytes 1179656 | tf_op jit(solution)/shard_map/weights_plane/ppermute | solution.py:33
  29.8 19.2 %collective-permute-start.6 = (bf16[2,2,3,128,128]{4,3,2,1,0:T(8,128)(2,1)S(1)}, bf16[2,2,3,128,128]{4,3,2,1,0:T(8,128)(2,1)S(1)}, u32[]{:S(2)}, u32[]{:S(2)}) collective-permute-start(bf16[2,2,3,128,128]{4,3,2,1,0:T(8,128)(2,1)S(1)} %bitcast.29), channel_id=1, source_target_pairs={{0,8},{1,9},{2,10},{3,11},{4,12},{5,13},{6,14},{7,15},{8,0},{9,1},... | collective-permute-start | bytes 1179656 | tf_op jit(solution)/shard_map/weights_x_0/ppermute | solution.py:33
  43.9 7.4 %collective-permute-start.9 = (bf16[2,2,3,128,128]{4,3,2,1,0:T(8,128)(2,1)S(1)}, bf16[2,2,3,128,128]{4,3,2,1,0:T(8,128)(2,1)S(1)}, u32[]{:S(2)}, u32[]{:S(2)}) collective-permute-start(bf16[2,2,3,128,128]{4,3,2,1,0:T(8,128)(2,1)S(1)} %collective-permute-done.8.refs_4_), channel_id=1, source_target_pairs={{0,4},{1,5},{2,6},{3,7},{4,0},{5,1},{6,2},{7,3},{8,12},{9,13},{10,... | collective-permute-start | bytes 1179656 | tf_op jit(solution)/shard_map/weights_x_1/ppermute | solution.py:33
  43.9 20.8 %collective-permute-start.10 = (bf16[2,2,3,128,128]{4,3,2,1,0:T(8,128)(2,1)S(1)}, bf16[2,2,3,128,128]{4,3,2,1,0:T(8,128)(2,1)S(1)}, u32[]{:S(2)}, u32[]{:S(2)}) collective-permute-start(bf16[2,2,3,128,128]{4,3,2,1,0:T(8,128)(2,1)S(1)} %collective-permute-done.8.refs_4_), channel_id=1, source_target_pairs={{0,8},{1,9},{2,10},{3,11},{4,12},{5,13},{6,14},{7,15},{8,0},{9,1},... | collective-permute-start | bytes 1179656 | tf_op jit(solution)/shard_map/weights_x_1/ppermute | solution.py:33
  48.6 16.1 %collective-permute-start.11 = (bf16[2,2,3,128,128]{4,3,2,1,0:T(8,128)(2,1)S(1)}, bf16[2,2,3,128,128]{4,3,2,1,0:T(8,128)(2,1)S(1)}, u32[]{:S(2)}, u32[]{:S(2)}) collective-permute-start(bf16[2,2,3,128,128]{4,3,2,1,0:T(8,128)(2,1)S(1)} %collective-permute-done.8.refs_4_), channel_id=1, source_target_pairs={{0,12},{1,13},{2,14},{3,15},{4,8},{5,9},{6,10},{7,11},{8,4},{9,5},... | collective-permute-start | bytes 1179656 | tf_op jit(solution)/shard_map/weights_x_1/ppermute | solution.py:33
  65.8 7.1 %collective-permute-start.12 = (bf16[256,1536]{1,0:T(8,128)(2,1)S(1)}, bf16[256,1536]{1,0:T(8,128)(2,1)S(1)}, u32[]{:S(2)}, u32[]{:S(2)}) collective-permute-start(bf16[256,1536]{1,0:T(8,128)(2,1)S(1)} %get-tuple-element.47), channel_id=1, source_target_pairs={{0,1},{1,0},{2,3},{3,2},{4,5},{5,4},{6,7},{7,6},{8,9},{9,8},{10,11... | collective-permute-start | bytes 2359304 | tf_op jit(solution)/shard_map/ppermute | solution.py:33
  73.2 10.4 %collective-permute-start.15 = (bf16[64,1536]{1,0:T(8,128)(2,1)S(1)}, bf16[64,1536]{1,0:T(8,128)(2,1)S(1)}, u32[]{:S(2)}, u32[]{:S(2)}) collective-permute-start(bf16[64,1536]{1,0:T(8,128)(2,1)S(1)} %get-tuple-element.70), channel_id=1, source_target_pairs={{0,18},{1,19},{2,16},{3,17},{4,22},{5,23},{6,20},{7,21},{8,26},{9,... | collective-permute-start | bytes 589832 | tf_op jit(solution)/shard_map/ppermute | solution.py:33
  73.3 10.3 %collective-permute-start.14 = (bf16[64,1536]{1,0:T(8,128)(2,1)S(1)}, bf16[64,1536]{1,0:T(8,128)(2,1)S(1)}, u32[]{:S(2)}, u32[]{:S(2)}) collective-permute-start(bf16[64,1536]{1,0:T(8,128)(2,1)S(1)} %get-tuple-element.71), channel_id=1, source_target_pairs={{0,16},{1,17},{2,18},{3,19},{4,20},{5,21},{6,22},{7,23},{8,24},{9,... | collective-permute-start | bytes 589832 | tf_op jit(solution)/shard_map/ppermute | solution.py:33
  74.3 10.9 %collective-permute-start.13 = (bf16[64,1536]{1,0:T(8,128)(2,1)S(1)}, bf16[64,1536]{1,0:T(8,128)(2,1)S(1)}, u32[]{:S(2)}, u32[]{:S(2)}) collective-permute-start(bf16[64,1536]{1,0:T(8,128)(2,1)S(1)} %get-tuple-element.69), channel_id=1, source_target_pairs={{0,2},{1,3},{2,0},{3,1},{4,6},{5,7},{6,4},{7,5},{8,10},{9,11},{10,... | collective-permute-start | bytes 589832 | tf_op jit(solution)/shard_map/ppermute | solution.py:33
  85.3 7.6 %collective-permute-start.18 = (bf16[64,1536]{1,0:T(8,128)(2,1)S(1)}, bf16[64,1536]{1,0:T(8,128)(2,1)S(1)}, u32[]{:S(2)}, u32[]{:S(2)}) collective-permute-start(bf16[64,1536]{1,0:T(8,128)(2,1)S(1)} %pad_maximum_fusion.2), channel_id=1, source_target_pairs={{0,18},{1,19},{2,16},{3,17},{4,22},{5,23},{6,20},{7,21},{8,26},{9,... | collective-permute-start | bytes 589832 | tf_op jit(solution)/shard_map/ppermute | solution.py:33
  85.8 7.1 %collective-permute-start.17 = (bf16[64,1536]{1,0:T(8,128)(2,1)S(1)}, bf16[64,1536]{1,0:T(8,128)(2,1)S(1)}, u32[]{:S(2)}, u32[]{:S(2)}) collective-permute-start(bf16[64,1536]{1,0:T(8,128)(2,1)S(1)} %pad_maximum_fusion.2), channel_id=1, source_target_pairs={{0,16},{1,17},{2,18},{3,19},{4,20},{5,21},{6,22},{7,23},{8,24},{9,... | collective-permute-start | bytes 589832 | tf_op jit(solution)/shard_map/ppermute | solution.py:33
  86.7 9.5 %collective-permute-start.16 = (bf16[64,1536]{1,0:T(8,128)(2,1)S(1)}, bf16[64,1536]{1,0:T(8,128)(2,1)S(1)}, u32[]{:S(2)}, u32[]{:S(2)}) collective-permute-start(bf16[64,1536]{1,0:T(8,128)(2,1)S(1)} %pad_maximum_fusion.2), channel_id=1, source_target_pairs={{0,2},{1,3},{2,0},{3,1},{4,6},{5,7},{6,4},{7,5},{8,10},{9,11},{10,... | collective-permute-start | bytes 589832 | tf_op jit(solution)/shard_map/ppermute | solution.py:33
  96.2 4.6 %collective-permute-start.19 = (bf16[256,1536]{1,0:T(8,128)(2,1)S(1)}, bf16[256,1536]{1,0:T(8,128)(2,1)S(1)}, u32[]{:S(2)}, u32[]{:S(2)}) collective-permute-start(bf16[256,1536]{1,0:T(8,128)(2,1)S(1)} %pad_maximum_fusion.da), channel_id=1, source_target_pairs={{0,1},{1,0},{2,3},{3,2},{4,5},{5,4},{6,7},{7,6},{8,9},{9,8},{10,11... | collective-permute-start | bytes 2359304 | tf_op jit(solution)/shard_map/ppermute | solution.py:33
  102.2 12.0 %collective-permute-start.25 = (bf16[2,2,3,128,128]{4,3,2,1,0:T(8,128)(2,1)S(1)}, bf16[2,2,3,128,128]{4,3,2,1,0:T(8,128)(2,1)S(1)}, u32[]{:S(2)}, u32[]{:S(2)}) collective-permute-start(bf16[2,2,3,128,128]{4,3,2,1,0:T(8,128)(2,1)S(1)} %get-tuple-element.55), channel_id=1, source_target_pairs={{0,8},{1,9},{2,10},{3,11},{4,12},{5,13},{6,14},{7,15},{8,0},{9,1},... | collective-permute-start | bytes 1179656 | tf_op jit(solution)/shard_map/grads_x_1/ppermute | solution.py:33
  102.3 20.8 %collective-permute-start.24 = (bf16[2,2,3,128,128]{4,3,2,1,0:T(8,128)(2,1)S(1)}, bf16[2,2,3,128,128]{4,3,2,1,0:T(8,128)(2,1)S(1)}, u32[]{:S(2)}, u32[]{:S(2)}) collective-permute-start(bf16[2,2,3,128,128]{4,3,2,1,0:T(8,128)(2,1)S(1)} %get-tuple-element.54), channel_id=1, source_target_pairs={{0,12},{1,13},{2,14},{3,15},{4,8},{5,9},{6,10},{7,11},{8,4},{9,5},... | collective-permute-start | bytes 1179656 | tf_op jit(solution)/shard_map/grads_x_1/ppermute | solution.py:33
  102.8 20.3 %collective-permute-start.23 = (bf16[2,2,3,128,128]{4,3,2,1,0:T(8,128)(2,1)S(1)}, bf16[2,2,3,128,128]{4,3,2,1,0:T(8,128)(2,1)S(1)}, u32[]{:S(2)}, u32[]{:S(2)}) collective-permute-start(bf16[2,2,3,128,128]{4,3,2,1,0:T(8,128)(2,1)S(1)} %get-tuple-element.53), channel_id=1, source_target_pairs={{0,4},{1,5},{2,6},{3,7},{4,0},{5,1},{6,2},{7,3},{8,12},{9,13},{10,... | collective-permute-start | bytes 1179656 | tf_op jit(solution)/shard_map/grads_x_1/ppermute | solution.py:33
  106.7 33.3 %collective-permute-start.27 = (bf16[2,256,1024]{2,1,0:T(8,128)(2,1)S(1)}, bf16[2,256,1024]{2,1,0:T(8,128)(2,1)S(1)}, u32[]{:S(2)}, u32[]{:S(2)}) collective-permute-start(bf16[2,256,1024]{2,1,0:T(8,128)(2,1)S(1)} %get-tuple-element.56), channel_id=1, source_target_pairs={{0,16},{1,17},{2,18},{3,19},{4,20},{5,21},{6,22},{7,23},{8,24},{9,... | collective-permute-start | bytes 3145736 | tf_op jit(solution)/shard_map/output_swap/ppermute | solution.py:33
  109.0 22.1 %collective-permute-start.22 = (bf16[2,2,3,128,128]{4,3,2,1,0:T(8,128)(2,1)S(1)}, bf16[2,2,3,128,128]{4,3,2,1,0:T(8,128)(2,1)S(1)}, u32[]{:S(2)}, u32[]{:S(2)}) collective-permute-start(bf16[2,2,3,128,128]{4,3,2,1,0:T(8,128)(2,1)S(1)} %get-tuple-element.51), channel_id=1, source_target_pairs={{0,8},{1,9},{2,10},{3,11},{4,12},{5,13},{6,14},{7,15},{8,0},{9,1},... | collective-permute-start | bytes 1179656 | tf_op jit(solution)/shard_map/grads_x_0/ppermute | solution.py:33
  114.1 25.5 %collective-permute-start.21 = (bf16[2,2,3,128,128]{4,3,2,1,0:T(8,128)(2,1)S(1)}, bf16[2,2,3,128,128]{4,3,2,1,0:T(8,128)(2,1)S(1)}, u32[]{:S(2)}, u32[]{:S(2)}) collective-permute-start(bf16[2,2,3,128,128]{4,3,2,1,0:T(8,128)(2,1)S(1)} %get-tuple-element.50), channel_id=1, source_target_pairs={{0,12},{1,13},{2,14},{3,15},{4,8},{5,9},{6,10},{7,11},{8,4},{9,5},... | collective-permute-start | bytes 1179656 | tf_op jit(solution)/shard_map/grads_x_0/ppermute | solution.py:33
  123.1 16.6 %collective-permute-start.20 = (bf16[2,2,3,128,128]{4,3,2,1,0:T(8,128)(2,1)S(1)}, bf16[2,2,3,128,128]{4,3,2,1,0:T(8,128)(2,1)S(1)}, u32[]{:S(2)}, u32[]{:S(2)}) collective-permute-start(bf16[2,2,3,128,128]{4,3,2,1,0:T(8,128)(2,1)S(1)} %get-tuple-element.49), channel_id=1, source_target_pairs={{0,4},{1,5},{2,6},{3,7},{4,0},{5,1},{6,2},{7,3},{8,12},{9,13},{10,... | collective-permute-start | bytes 1179656 | tf_op jit(solution)/shard_map/grads_x_0/ppermute | solution.py:33
  123.3 16.4 %collective-permute-start.26 = (bf16[2,2,3,128,128]{4,3,2,1,0:T(8,128)(2,1)S(1)}, bf16[2,2,3,128,128]{4,3,2,1,0:T(8,128)(2,1)S(1)}, u32[]{:S(2)}, u32[]{:S(2)}) collective-permute-start(bf16[2,2,3,128,128]{4,3,2,1,0:T(8,128)(2,1)S(1)} %add_convert_fusion.1), channel_id=1, source_target_pairs={{0,32},{1,33},{2,34},{3,35},{4,36},{5,37},{6,38},{7,39},{8,40},{9,... | collective-permute-start | bytes 1179656 | tf_op jit(solution)/shard_map/grads_plane/ppermute | solution.py:33
  140.0 20.9 %collective-permute-start.28 = (bf16[3,128,128]{2,1,0:T(8,128)(2,1)S(1)}, bf16[3,128,128]{2,1,0:T(8,128)(2,1)S(1)}, u32[]{:S(2)}, u32[]{:S(2)}) collective-permute-start(bf16[3,128,128]{2,1,0:T(8,128)(2,1)S(1)} %get-tuple-element.75), channel_id=1, source_target_pairs={{0,0},{64,1},{128,2},{192,3},{4,4},{68,5},{132,6},{196,7},{8,8},{7... | collective-permute-start | bytes 294920 | tf_op jit(solution)/shard_map/grads_turn/ppermute | solution.py:37
  146.7 15.2 %collective-permute-start.29 = (bf16[3,128,128]{2,1,0:T(8,128)(2,1)S(1)}, bf16[3,128,128]{2,1,0:T(8,128)(2,1)S(1)}, u32[]{:S(2)}, u32[]{:S(2)}) collective-permute-start(bf16[3,128,128]{2,1,0:T(8,128)(2,1)S(1)} %get-tuple-element.74), channel_id=1, source_target_pairs={{64,0},{0,1},{192,2},{128,3},{68,4},{4,5},{196,6},{132,7},{72,8},{... | collective-permute-start | bytes 294920 | tf_op jit(solution)/shard_map/grads_turn/ppermute | solution.py:37
  146.8 16.2 %collective-permute-start.30 = (bf16[3,128,128]{2,1,0:T(8,128)(2,1)S(1)}, bf16[3,128,128]{2,1,0:T(8,128)(2,1)S(1)}, u32[]{:S(2)}, u32[]{:S(2)}) collective-permute-start(bf16[3,128,128]{2,1,0:T(8,128)(2,1)S(1)} %get-tuple-element.73), channel_id=1, source_target_pairs={{128,0},{192,1},{0,2},{64,3},{132,4},{196,5},{4,6},{68,7},{136,8},... | collective-permute-start | bytes 294920 | tf_op jit(solution)/shard_map/grads_turn/ppermute | solution.py:37
  146.9 17.1 %collective-permute-start.31 = (bf16[3,128,128]{2,1,0:T(8,128)(2,1)S(1)}, bf16[3,128,128]{2,1,0:T(8,128)(2,1)S(1)}, u32[]{:S(2)}, u32[]{:S(2)}) collective-permute-start(bf16[3,128,128]{2,1,0:T(8,128)(2,1)S(1)} %get-tuple-element.72), channel_id=1, source_target_pairs={{192,0},{128,1},{64,2},{0,3},{196,4},{132,5},{68,6},{4,7},{200,8},... | collective-permute-start | bytes 294920 | tf_op jit(solution)/shard_map/grads_turn/ppermute | solution.py:37
